TPU v7x, 256 devices: a whole 4x4x8 slice. The times are simulated.
256 devices in a mesh: dp: 64 (over y, x, z_lo, core), tensor: 4 (over z_hi).
Axes of the slice: x: 4, y: 4, z: 8 (z_hi: 4, z_lo: 2; z = z_hi * 2 + z_lo), core: 2. Of those that a mesh axis runs over, the one named last changes fastest.
Arguments:
- base_codes: int32 [4096, 14336], P('dp', 'tensor'), may hold values from 0 to 15
- block_scales: float32 [4096, 224], P('dp', 'tensor'), may hold values from 0.0008 to 0.0176, as said below
- input_adapter_factor: bfloat16 [4096, 64], replicated, may hold values from -0.09375 to 0.09375
- output_adapter_factor: bfloat16 [64, 14336], P(None, 'tensor'), may hold values from -0.046875 to 0.046875
- magnitude: float32 [14336], P('tensor'), may hold values from 0.5 to 2
- inputs: bfloat16 [12288, 4096], P('dp', 'tensor'), may hold values from -6 to 6
- grad_out: bfloat16 [12288, 14336], P('dp', 'tensor'), may hold values from -1.5 to 1.5
- pre_scale: bfloat16 [12288, 14336], P('dp', 'tensor'), may hold values from -6 to 6
Outputs:
- grad_inputs: bfloat16 [12288, 4096], P('dp', 'tensor')
- input_adapter_gradient: float32 [4096, 64], P('tensor')
- output_adapter_gradient: float32 [64, 14336], P(None, 'tensor')
- grad_magnitude: float32 [14336], P('tensor')
Inputs may be any that keep to these rules, and one draw needn't show every extreme that they name: `block_scales`: block scales of the 4-bit codes.
All inputs are finite; a program needn't handle non-finite values.
Results may differ from a plain program's by a relative error of at most 0.015.
Values may be sent and summed in bfloat16 or wider, within the bound.
No kernel may reach another device: no remote copies, remote signals or barrier semaphores. Data moves between devices by JAX's collectives and lax.ppermute only.
A program may use at most 192 MiB of HBM per device.

v0:
```python
import jax
import jax.numpy as jnp
from jax import lax
from jax.experimental import pallas as pl
from jax.experimental.pallas import tpu as pltpu
from jax.sharding import Mesh, PartitionSpec as P

SCALE = 0.5
BF = jnp.bfloat16
F32 = jnp.float32
SIZES = {"y": 4, "x": 4, "zl": 2, "co": 2, "t": 4}
DP = ("y", "x", "zl", "co")
N_DP = 64


def shift(value, axis, step):
    n = SIZES[axis]
    return lax.ppermute(value, axis, [(i, (i + step) % n) for i in range(n)])


def swap_all(value, axes):
    return lax.all_to_all(value, axes, 0, 0, tiled=True)


def merge_kernel(block, codes, scales, factor, out_factor, grad, pre, own, sums):
    width = codes.shape[1]
    count = scales.shape[1]
    start = pl.program_id(0) * width
    group = (start + lax.broadcasted_iota(jnp.int32, (count, width), 1)) // block
    pick = (group == lax.broadcasted_iota(jnp.int32, (count, width), 0)).astype(F32)
    spread = jnp.dot(
        scales[...], pick, precision=lax.Precision.HIGHEST, preferred_element_type=F32
    )
    low = jnp.dot(factor[...], out_factor[...], preferred_element_type=F32)
    merged = ((codes[...].astype(F32) - 7.5) * spread + SCALE * low).astype(BF)
    own[...] = merged
    wide = merged.astype(F32)
    sums[0:1, :] = jnp.sum(wide * wide, axis=0, keepdims=True)
    product = grad[...].astype(F32) * pre[...].astype(F32)
    sums[1:2, :] = jnp.sum(product, axis=0, keepdims=True)


def merge(codes, scales, factor, out_factor, grad, pre):
    rows, width = codes.shape
    tokens = grad.shape[0]
    rank = factor.shape[1]
    count = scales.shape[1]
    steps = 4
    part = width // steps

    def columns(n):
        return pl.BlockSpec((n, part), lambda i: (0, i))

    def whole(a, b):
        return pl.BlockSpec((a, b), lambda i: (0, 0))

    def body(*refs):
        merge_kernel(width // count, *refs)

    return pl.pallas_call(
        body,
        grid=(steps,),
        in_specs=[
            columns(rows),
            whole(rows, count),
            whole(rows, rank),
            columns(rank),
            columns(tokens),
            columns(tokens),
        ],
        out_specs=[columns(rows), columns(2)],
        out_shape=[
            jax.ShapeDtypeStruct((rows, width), BF),
            jax.ShapeDtypeStruct((2, width), F32),
        ],
        compiler_params=pltpu.CompilerParams(vmem_limit_bytes=32 * 1024 * 1024),
    )(codes, scales, factor, out_factor, grad, pre)


def on_device(codes, scales, in_factor, out_factor, magnitude, inputs, grad, pre):
    y, x, zl, co, t = (lax.axis_index(a) for a in ("y", "x", "zl", "co", "t"))
    rows, width = codes.shape
    tokens = grad.shape[0]
    half = tokens // 2
    features = inputs.shape[1]
    part = features // SIZES["x"]
    rank = in_factor.shape[1]

    g_left = shift(grad, "x", 1)
    g_right = shift(grad, "x", -1)

    first = (((y * 4 + x) * 2 + zl) * 2 + co) * rows
    factor_rows = lax.dynamic_slice_in_dim(in_factor, first, rows, 0)
    own, sums = merge(codes, scales, factor_rows, out_factor, grad, pre)
    other = shift(own, "zl", 1)

    sums = swap_all(sums.reshape(2, N_DP, -1).transpose(1, 0, 2).reshape(N_DP, -1), DP)
    sums = jnp.sum(sums, axis=0, keepdims=True)
    sums = swap_all(jnp.broadcast_to(sums, (N_DP, sums.shape[1])), DP)
    sums = sums.reshape(N_DP, 2, -1).transpose(1, 0, 2).reshape(2, width)
    col_norm = jnp.sqrt(sums[0] + 1e-06)
    mag_grad = sums[1] / col_norm
    ratio = magnitude / col_norm

    weight = jnp.zeros((4, 2, 2, rows, width), BF)

    def put(weight, block, step, zi):
        block = block.reshape(-1, rows, width)
        swapped = shift(block, "co", 1)
        row = (y + step) % 4
        for b, c in ((block, co), (swapped, 1 - co)):
            weight = lax.dynamic_update_slice(weight, b[None, :, None], (row, zi, c, 0, 0))
        return weight

    pair = jnp.where(zl == 0, jnp.stack([own, other]), jnp.stack([other, own]))
    down = shift(pair, "y", 1)
    up = shift(pair, "y", -1)
    weight = put(weight, pair, 0, 0)
    weight = put(weight, down, -1, 0)
    weight = put(weight, up, 1, 0)
    weight = put(weight, shift(down[0], "y", 1), 2, 0)
    weight = put(weight, shift(up[1], "y", -1), 2, 1)

    g_far = jnp.concatenate(
        [shift(g_left[:half], "x", 1), shift(g_right[half:], "x", -1)], axis=0
    )

    def scaled_of(g):
        return (g.astype(F32) * ratio).astype(BF)

    scaled_own = scaled_of(grad)
    scaled = jnp.zeros((4, tokens, width), BF)
    for e, g in ((0, scaled_own), (-1, scaled_of(g_left)), (1, scaled_of(g_right)), (2, scaled_of(g_far))):
        scaled = lax.dynamic_update_slice(scaled, g[None], ((x + e) % 4, 0, 0))

    factor_cols = lax.dynamic_slice_in_dim(in_factor, t * features, features, 0)
    hidden = jnp.dot(inputs, factor_cols, preferred_element_type=F32)
    back = lax.dot_general(
        scaled_own, out_factor, (((1,), (1,)), ((), ())), preferred_element_type=F32
    )
    low = jnp.concatenate([hidden, back], axis=1).astype(BF)
    low = swap_all(jnp.broadcast_to(low[None], (4,) + low.shape), "t")
    low = jnp.sum(low.astype(F32), axis=0).astype(BF)
    hidden, back = low[:, :rank], low[:, rank:]
    in_grad = SCALE * lax.dot_general(
        back, inputs, (((0,), (0,)), ((), ())), preferred_element_type=F32
    )
    out_grad = SCALE * lax.dot_general(
        hidden, scaled_own, (((0,), (0,)), ((), ())), preferred_element_type=F32
    )
    adapters = swap_all(jnp.concatenate([out_grad, in_grad], axis=1), DP)
    adapters = jnp.sum(adapters, axis=0, keepdims=True)
    adapters = swap_all(jnp.broadcast_to(adapters, (N_DP, adapters.shape[1])), DP)
    out_grad = adapters[:, :width]
    in_grad = adapters[:, width:].T

    tile = lax.dot_general(
        scaled.reshape(4 * tokens, width),
        weight.reshape(16 * rows, width),
        (((1,), (1,)), ((), ())),
        preferred_element_type=F32,
    ).astype(BF)
    tile = tile.reshape(4, tokens, 4, part).transpose(0, 2, 1, 3)
    tile = swap_all(tile.reshape(16, tokens, part), ("x", "t"))
    tile = jnp.sum(tile.reshape(4, 4, tokens, part).astype(F32), axis=1).astype(BF)
    grad_in = tile.transpose(1, 0, 2).reshape(tokens, features)
    return grad_in, in_grad, out_grad, mag_grad


def solution(mesh):
    fine = Mesh(mesh.devices.reshape(4, 4, 2, 2, 4), ("y", "x", "zl", "co", "t"))
    in_specs = (
        P(DP, "t"),
        P(DP, "t"),
        P(),
        P(None, "t"),
        P("t"),
        P(DP, "t"),
        P(DP, "t"),
        P(DP, "t"),
    )
    out_specs = (P(DP, "t"), P("t", None), P(None, "t"), P("t"))
    return jax.shard_map(
        on_device, mesh=fine, in_specs=in_specs, out_specs=out_specs, check_vma=False
    )
```

profile of v0, /device:TPU:8, one launch (start us, length us, event | category | flops | bytes accessed | tf_op | source)
XLA Modules:
  0.0 231.2 jit_solution(11311761329788573788)
XLA Ops:
  7.6 2.1 shard_map.111
  10.6 9.3 %all-to-all-start = ((f32[64,1,112]{2,1,0:T(1,128)}), f32[64,1,112]{2,1,0:T(1,128)S(1)}, u32[]{:S(2)}, u32[]{:S(2)}) async-start(f32[64,1,112]{2,1,0:T(1,128)} %bitcast.1), calls=%async_computation | async-start | bytes 65536 | tf_op jit(solution)/shard_map/all_to_all | solution.py:22
  19.9 1.6 collective-permute-start
  21.4 1.8 collective-permute-start.1
  23.2 1.5 collective-permute-start.4
  24.7 2.2 all-to-all-done
  27.6 5.6 %all-to-all-start.1 = ((f32[64,1,112]{2,1,0:T(1,128)}), f32[64,1,112]{2,1,0:T(1,128)S(1)}, u32[]{:S(2)}, u32[]{:S(2)}) async-start(f32[64,1,112]{2,1,0:T(1,128)} %broadcast_in_dim.61), calls=%async_computation.1 | async-start | bytes 65536 | tf_op jit(solution)/shard_map/all_to_all | solution.py:22
  34.6 21.9 %all-to-all-done.1 = f32[64,1,112]{2,1,0:T(1,128)S(1)} async-done(((f32[64,1,112]{2,1,0:T(1,128)}), f32[64,1,112]{2,1,0:T(1,128)S(1)}, u32[]{:S(2)}, u32[]{:S(2)}) %all-to-all-start.1) | async-done | bytes 28704 | tf_op jit(solution)/shard_map/all_to_all | solution.py:22
  60.3 7.6 %all-to-all-start.3 = ((bf16[4,192,128]{2,1,0:T(8,128)(2,1)}), bf16[4,192,128]{2,1,0:T(8,128)(2,1)S(1)}, u32[]{:S(2)}, u32[]{:S(2)}) async-start(bf16[4,192,128]{2,1,0:T(8,128)(2,1)} %broadcast_in_dim.73), calls=%async_computation.3 | async-start | bytes 393216 | tf_op jit(solution)/shard_map/all_to_all | solution.py:22
  67.9 2.8 %broadcast_in_dim.60 = bf16[4,192,3584]{2,1,0:T(8,128)(2,1)} broadcast(bf16[]{:T(256)} %constant.71.clone.1), dimensions={} | broadcast | bytes 5505026 | tf_op jit(solution)/shard_map/broadcast_in_dim | solution.py:132
  72.1 5.6 %all-to-all-done.3 = bf16[4,192,128]{2,1,0:T(8,128)(2,1)S(1)} async-done(((bf16[4,192,128]{2,1,0:T(8,128)(2,1)}), bf16[4,192,128]{2,1,0:T(8,128)(2,1)S(1)}, u32[]{:S(2)}, u32[]{:S(2)}) %all-to-all-start.3) | async-done | bytes 196640 | tf_op jit(solution)/shard_map/all_to_all | solution.py:22
  80.3 2.2 copy.67
  82.6 7.8 %all-to-all-start.4 = ((f32[64,1,4608]{2,1,0:T(1,128)}), f32[64,1,4608]{2,1,0:T(1,128)S(1)}, u32[]{:S(2)}, u32[]{:S(2)}) async-start(f32[64,1,4608]{2,1,0:T(1,128)} %copy.67), calls=%async_computation.4 | async-start | bytes 2359296 | tf_op jit(solution)/shard_map/all_to_all | solution.py:22
  91.2 3.7 %broadcast_in_dim.65 = bf16[4,2,2,64,3584]{4,3,2,1,0:T(8,128)(2,1)} broadcast(bf16[]{:T(256)} %constant.71.clone.1), dimensions={} | broadcast | bytes 7340034 | tf_op jit(solution)/shard_map/broadcast_in_dim | solution.py:105
  95.9 16.3 %collective-permute-done.6 = bf16[2,64,3584]{2,1,0:T(8,128)(2,1)} collective-permute-done((bf16[2,64,3584]{2,1,0:T(8,128)(2,1)}, bf16[2,64,3584]{2,1,0:T(8,128)(2,1)}, u32[]{:S(2)}, u32[]{:S(2)}) %collective-permute-start.6) | collective-permute-done | bytes 917536 | tf_op jit(solution)/shard_map/ppermute | solution.py:18
  113.3 1.9 collective-permute-start.10
  115.2 10.0 %collective-permute-done.8 = bf16[2,64,3584]{2,1,0:T(8,128)(2,1)S(1)} collective-permute-done((bf16[2,64,3584]{2,1,0:T(8,128)(2,1)}, bf16[2,64,3584]{2,1,0:T(8,128)(2,1)S(1)}, u32[]{:S(2)}, u32[]{:S(2)}) %collective-permute-start.8) | collective-permute-done | bytes 917536 | tf_op jit(solution)/shard_map/ppermute | solution.py:18
  126.8 1.6 collective-permute-start.2
  129.5 1.8 collective-permute-start.3
  131.4 2.7 %fusion.1 = bf16[4,192,3584]{2,1,0:T(8,128)(2,1)} fusion(bf16[4,192,3584]{2,1,0:T(8,128)(2,1)} %bitcast_dynamic-update-slice_fusion, s32[]{:T(128)S(6)} %select_n.110, bf16[192,3584]{1,0:T(8,128)(2,1)} %collective-permute-done, f32[3584]{0:T(1024)S(1)} %get-tuple-element.11), kind=kLoop, calls=%fused_computation.8 | loop fusion | flops 2064384 | bytes 2766852 | tf_op jit(solution)/shard_map/dynamic_update_slice | solution.py:134
  134.1 2.7 %fusion.3 = bf16[4,192,3584]{2,1,0:T(8,128)(2,1)} fusion(bf16[4,192,3584]{2,1,0:T(8,128)(2,1)} %fusion.1, s32[]{:T(128)S(6)} %select_n.112, bf16[192,3584]{1,0:T(8,128)(2,1)} %collective-permute-done.1, f32[3584]{0:T(1024)S(1)} %get-tuple-element.11), kind=kLoop, calls=%fused_computation.10 | loop fusion | flops 2064384 | bytes 2766852 | tf_op jit(solution)/shard_map/dynamic_update_slice | solution.py:134
  137.7 2.2 bitcast_dynamic-update-slice_fusion.4
  140.5 4.7 %collective-permute-done.2 = bf16[96,3584]{1,0:T(8,128)(2,1)S(1)} collective-permute-done((bf16[96,3584]{1,0:T(8,128)(2,1)S(1)}, bf16[96,3584]{1,0:T(8,128)(2,1)S(1)}, u32[]{:S(2)}, u32[]{:S(2)}) %collective-permute-start.2) | collective-permute-done | bytes 688160 | tf_op jit(solution)/shard_map/ppermute | solution.py:18
  152.4 1.8 bitcast_dynamic-update-slice_fusion.7
  154.9 1.6 broadcast_in_dim.74
  156.5 8.9 %all-to-all-start.5 = ((f32[64,1,4608]{2,1,0:T(1,128)}), f32[64,1,4608]{2,1,0:T(1,128)S(1)}, u32[]{:S(2)}, u32[]{:S(2)}) async-start(f32[64,1,4608]{2,1,0:T(1,128)} %broadcast_in_dim.74), calls=%async_computation.5 | async-start | bytes 2359296 | tf_op jit(solution)/shard_map/all_to_all | solution.py:22
  165.4 1.8 bitcast_dynamic-update-slice_fusion.6
  167.2 10.7 %convolution_convert_fusion = bf16[768,1024]{1,0:T(8,128)(2,1)} fusion(bf16[768,3584]{1,0:T(8,128)(2,1)} %bitcast.8, bf16[1024,3584]{1,0:T(8,128)(2,1)} %bitcast.31), kind=kOutput, calls=%fused_computation.5 | convolution fusion | flops 5637931008 | bytes 14417920 | tf_op jit(solution)/shard_map/dot_general | solution.py:157
  177.9 2.9 %reshape.201 = bf16[4,192,4,256]{3,2,1,0:T(4,128)(2,1)S(1)} reshape(bf16[768,1024]{1,0:T(8,128)(2,1)} %convolution_convert_fusion) | data formatting | bytes 3145728 | tf_op jit(solution)/shard_map/reshape | solution.py:163
  180.8 1.4 copy.64
  183.5 3.9 %all-to-all-start.2 = ((bf16[16,192,256]{2,1,0:T(8,128)(2,1)}), bf16[16,192,256]{2,1,0:T(8,128)(2,1)S(1)}, u32[]{:S(2)}, u32[]{:S(2)}) async-start(bf16[16,192,256]{2,1,0:T(8,128)(2,1)} %bitcast.33), calls=%async_computation.2 | async-start | bytes 3145728 | tf_op jit(solution)/shard_map/all_to_all | solution.py:22
  189.3 40.9 %all-to-all-done.2 = bf16[16,192,256]{2,1,0:T(8,128)(2,1)S(1)} async-done(((bf16[16,192,256]{2,1,0:T(8,128)(2,1)}), bf16[16,192,256]{2,1,0:T(8,128)(2,1)S(1)}, u32[]{:S(2)}, u32[]{:S(2)}) %all-to-all-start.2) | async-done | bytes 1572896 | tf_op jit(solution)/shard_map/all_to_all | solution.py:22
  (87 shorter events, 36.8 us)
Async XLA Ops:
  0.6 1.0 copy-start
  2.7 1.3 copy-start.1
  4.0 1.3 copy-start.3
  5.4 1.2 copy-start.4
  6.6 1.0 copy-start.5
  7.6 12.3 %copy-start.2 = (bf16[192,3584]{1,0:T(8,128)(2,1)S(1)}, bf16[192,3584]{1,0:T(8,128)(2,1)}, u32[]{:S(2)}) copy-start(bf16[192,3584]{1,0:T(8,128)(2,1)} %refs_4_.1) | copy-start | bytes 4128772
  7.6 50.7 %copy-start.10 = (f32[3584]{0:T(1024)S(1)}, f32[3584]{0:T(1024)}, u32[]{:S(2)}) copy-start(f32[3584]{0:T(1024)} %param.12) | copy-start | bytes 43012
  7.6 51.3 %copy-start.6 = (bf16[64,3584]{1,0:T(8,128)(2,1)S(1)}, bf16[64,3584]{1,0:T(8,128)(2,1)}, u32[]{:S(2)}) copy-start(bf16[64,3584]{1,0:T(8,128)(2,1)} %refs_3_.1) | copy-start | bytes 1376260
  10.6 16.3 %all-to-all-start = ((f32[64,1,112]{2,1,0:T(1,128)}), f32[64,1,112]{2,1,0:T(1,128)S(1)}, u32[]{:S(2)}, u32[]{:S(2)}) async-start(f32[64,1,112]{2,1,0:T(1,128)} %bitcast.1), calls=%async_computation | async-start | bytes 65536 | tf_op jit(solution)/shard_map/all_to_all | solution.py:22
  19.9 105.8 %collective-permute-start = (bf16[192,3584]{1,0:T(8,128)(2,1)S(1)}, bf16[192,3584]{1,0:T(8,128)(2,1)}, u32[]{:S(2)}, u32[]{:S(2)}) collective-permute-start(bf16[192,3584]{1,0:T(8,128)(2,1)S(1)} %copy-done.2), channel_id=1, source_target_pairs={{0,16},{16,32},{32,48},{48,0},{1,17},{17,33},{33,49},{49,1},{2,18}... | collective-permute-start | bytes 4128776 | tf_op jit(solution)/shard_map/ppermute | solution.py:18
  21.4 106.9 %collective-permute-start.1 = (bf16[192,3584]{1,0:T(8,128)(2,1)S(1)}, bf16[192,3584]{1,0:T(8,128)(2,1)}, u32[]{:S(2)}, u32[]{:S(2)}) collective-permute-start(bf16[192,3584]{1,0:T(8,128)(2,1)S(1)} %copy-done.2), channel_id=1, source_target_pairs={{0,48},{16,0},{32,16},{48,32},{1,49},{17,1},{33,17},{49,33},{2,50}... | collective-permute-start | bytes 4128776 | tf_op jit(solution)/shard_map/ppermute | solution.py:18
  23.2 55.3 %collective-permute-start.4 = (bf16[64,3584]{1,0:T(8,128)(2,1)S(1)}, bf16[64,3584]{1,0:T(8,128)(2,1)S(1)}, u32[]{:S(2)}, u32[]{:S(2)}) collective-permute-start(bf16[64,3584]{1,0:T(8,128)(2,1)S(1)} %get-tuple-element.7), channel_id=1, source_target_pairs={{0,8},{8,0},{1,9},{9,1},{2,10},{10,2},{3,11},{11,3},{4,12},{12,4},... | collective-permute-start | bytes 1376264 | tf_op jit(solution)/shard_map/ppermute | solution.py:18
  27.6 28.9 %all-to-all-start.1 = ((f32[64,1,112]{2,1,0:T(1,128)}), f32[64,1,112]{2,1,0:T(1,128)S(1)}, u32[]{:S(2)}, u32[]{:S(2)}) async-start(f32[64,1,112]{2,1,0:T(1,128)} %broadcast_in_dim.61), calls=%async_computation.1 | async-start | bytes 65536 | tf_op jit(solution)/shard_map/all_to_all | solution.py:22
  60.3 17.4 %all-to-all-start.3 = ((bf16[4,192,128]{2,1,0:T(8,128)(2,1)}), bf16[4,192,128]{2,1,0:T(8,128)(2,1)S(1)}, u32[]{:S(2)}, u32[]{:S(2)}) async-start(bf16[4,192,128]{2,1,0:T(8,128)(2,1)} %broadcast_in_dim.73), calls=%async_computation.3 | async-start | bytes 393216 | tf_op jit(solution)/shard_map/all_to_all | solution.py:22
  70.7 7.1 %copy-start.9 = (bf16[192,1024]{1,0:T(8,128)(2,1)S(1)}, bf16[192,1024]{1,0:T(8,128)(2,1)}, u32[]{:S(2)}) copy-start(bf16[192,1024]{1,0:T(8,128)(2,1)} %param.13) | copy-start | bytes 1179652
  78.5 4.0 %copy-start.7 = (bf16[64,3584]{1,0:T(8,128)(2,1)}, bf16[64,3584]{1,0:T(8,128)(2,1)S(1)}, u32[]{:S(2)}) copy-start(bf16[64,3584]{1,0:T(8,128)(2,1)S(1)} %collective-permute-done.4) | copy-start | bytes 1376260
  79.7 32.6 %collective-permute-start.6 = (bf16[2,64,3584]{2,1,0:T(8,128)(2,1)}, bf16[2,64,3584]{2,1,0:T(8,128)(2,1)}, u32[]{:S(2)}, u32[]{:S(2)}) collective-permute-start(bf16[2,64,3584]{2,1,0:T(8,128)(2,1)} %maximum_select_fusion.1), channel_id=1, source_target_pairs={{0,64},{64,128},{128,192},{192,0},{1,65},{65,129},{129,193},{193,1... | collective-permute-start | bytes 2752520 | tf_op jit(solution)/shard_map/ppermute | solution.py:18
  82.6 71.6 %all-to-all-start.4 = ((f32[64,1,4608]{2,1,0:T(1,128)}), f32[64,1,4608]{2,1,0:T(1,128)S(1)}, u32[]{:S(2)}, u32[]{:S(2)}) async-start(f32[64,1,4608]{2,1,0:T(1,128)} %copy.67), calls=%async_computation.4 | async-start | bytes 2359296 | tf_op jit(solution)/shard_map/all_to_all | solution.py:22
  90.4 46.4 %collective-permute-start.5 = (bf16[2,64,3584]{2,1,0:T(8,128)(2,1)}, bf16[2,64,3584]{2,1,0:T(8,128)(2,1)S(1)}, u32[]{:S(2)}, u32[]{:S(2)}) collective-permute-start(bf16[2,64,3584]{2,1,0:T(8,128)(2,1)} %maximum_select_fusion.1), channel_id=1, source_target_pairs={{0,4},{4,0},{1,5},{5,1},{2,6},{6,2},{3,7},{7,3},{8,12},{12,8},{9,1... | collective-permute-start | bytes 2752520 | tf_op jit(solution)/shard_map/ppermute | solution.py:18
  90.6 34.6 %collective-permute-start.8 = (bf16[2,64,3584]{2,1,0:T(8,128)(2,1)}, bf16[2,64,3584]{2,1,0:T(8,128)(2,1)S(1)}, u32[]{:S(2)}, u32[]{:S(2)}) collective-permute-start(bf16[2,64,3584]{2,1,0:T(8,128)(2,1)} %maximum_select_fusion.1), channel_id=1, source_target_pairs={{0,192},{64,0},{128,64},{192,128},{1,193},{65,1},{129,65},{193,129... | collective-permute-start | bytes 2752520 | tf_op jit(solution)/shard_map/ppermute | solution.py:18
  91.2 3.7 %copy-start.8 = (bf16[64,3584]{1,0:T(8,128)(2,1)S(1)}, bf16[64,3584]{1,0:T(8,128)(2,1)}, u32[]{:S(2)}) copy-start(bf16[64,3584]{1,0:T(8,128)(2,1)} %copy-done.7) | copy-start | bytes 1376260
  113.3 26.6 %collective-permute-start.10 = (bf16[64,3584]{1,0:T(8,128)(2,1)S(1)}, bf16[64,3584]{1,0:T(8,128)(2,1)S(1)}, u32[]{:S(2)}, u32[]{:S(2)}) collective-permute-start(bf16[64,3584]{1,0:T(8,128)(2,1)S(1)} %slice_bitcast_fusion.1), channel_id=1, source_target_pairs={{0,64},{64,128},{128,192},{192,0},{1,65},{65,129},{129,193},{193,1... | collective-permute-start | bytes 1376264 | tf_op jit(solution)/shard_map/ppermute | solution.py:18
  125.3 15.1 %collective-permute-start.12 = (bf16[64,3584]{1,0:T(8,128)(2,1)S(1)}, bf16[64,3584]{1,0:T(8,128)(2,1)}, u32[]{:S(2)}, u32[]{:S(2)}) collective-permute-start(bf16[64,3584]{1,0:T(8,128)(2,1)S(1)} %slice_bitcast_fusion), channel_id=1, source_target_pairs={{0,192},{64,0},{128,64},{192,128},{1,193},{65,1},{129,65},{193,129... | collective-permute-start | bytes 1376264 | tf_op jit(solution)/shard_map/ppermute | solution.py:18
  126.8 18.4 %collective-permute-start.2 = (bf16[96,3584]{1,0:T(8,128)(2,1)S(1)}, bf16[96,3584]{1,0:T(8,128)(2,1)S(1)}, u32[]{:S(2)}, u32[]{:S(2)}) collective-permute-start(bf16[96,3584]{1,0:T(8,128)(2,1)S(1)} %slice.43), channel_id=1, source_target_pairs={{0,16},{16,32},{32,48},{48,0},{1,17},{17,33},{33,49},{49,1},{2,18}... | collective-permute-start | bytes 2064392 | tf_op jit(solution)/shard_map/ppermute | solution.py:18
  129.5 16.9 %collective-permute-start.3 = (bf16[96,3584]{1,0:T(8,128)(2,1)S(1)}, bf16[96,3584]{1,0:T(8,128)(2,1)S(1)}, u32[]{:S(2)}, u32[]{:S(2)}) collective-permute-start(bf16[96,3584]{1,0:T(8,128)(2,1)S(1)} %slice.44), channel_id=1, source_target_pairs={{0,48},{16,0},{32,16},{48,32},{1,49},{17,1},{33,17},{49,33},{2,50}... | collective-permute-start | bytes 2064392 | tf_op jit(solution)/shard_map/ppermute | solution.py:18
  136.7 11.0 %collective-permute-start.7 = (bf16[2,64,3584]{2,1,0:T(8,128)(2,1)}, bf16[2,64,3584]{2,1,0:T(8,128)(2,1)S(1)}, u32[]{:S(2)}, u32[]{:S(2)}) collective-permute-start(bf16[2,64,3584]{2,1,0:T(8,128)(2,1)} %collective-permute-done.6), channel_id=1, source_target_pairs={{0,4},{4,0},{1,5},{5,1},{2,6},{6,2},{3,7},{7,3},{8,12},{12,8},{9,1... | collective-permute-start | bytes 2752520 | tf_op jit(solution)/shard_map/ppermute | solution.py:18
  139.9 9.9 %collective-permute-start.9 = (bf16[2,64,3584]{2,1,0:T(8,128)(2,1)S(1)}, bf16[2,64,3584]{2,1,0:T(8,128)(2,1)S(1)}, u32[]{:S(2)}, u32[]{:S(2)}) collective-permute-start(bf16[2,64,3584]{2,1,0:T(8,128)(2,1)S(1)} %collective-permute-done.8), channel_id=1, source_target_pairs={{0,4},{4,0},{1,5},{5,1},{2,6},{6,2},{3,7},{7,3},{8,12},{12,8},{9,1... | collective-permute-start | bytes 2752520 | tf_op jit(solution)/shard_map/ppermute | solution.py:18
  140.4 11.2 %collective-permute-start.11 = (bf16[1,64,3584]{2,1,0:T(8,128)(2,1)S(1)}, bf16[1,64,3584]{2,1,0:T(8,128)(2,1)S(1)}, u32[]{:S(2)}, u32[]{:S(2)}) collective-permute-start(bf16[1,64,3584]{2,1,0:T(8,128)(2,1)S(1)} %bitcast.86), channel_id=1, source_target_pairs={{0,4},{4,0},{1,5},{5,1},{2,6},{6,2},{3,7},{7,3},{8,12},{12,8},{9,1... | collective-permute-start | bytes 1376264 | tf_op jit(solution)/shard_map/ppermute | solution.py:18
  145.2 20.2 %collective-permute-start.13 = (bf16[1,64,3584]{2,1,0:T(8,128)(2,1)}, bf16[1,64,3584]{2,1,0:T(8,128)(2,1)}, u32[]{:S(2)}, u32[]{:S(2)}) collective-permute-start(bf16[1,64,3584]{2,1,0:T(8,128)(2,1)} %bitcast.29), channel_id=1, source_target_pairs={{0,4},{4,0},{1,5},{5,1},{2,6},{6,2},{3,7},{7,3},{8,12},{12,8},{9,1... | collective-permute-start | bytes 1376264 | tf_op jit(solution)/shard_map/ppermute | solution.py:18
  156.5 27.0 %all-to-all-start.5 = ((f32[64,1,4608]{2,1,0:T(1,128)}), f32[64,1,4608]{2,1,0:T(1,128)S(1)}, u32[]{:S(2)}, u32[]{:S(2)}) async-start(f32[64,1,4608]{2,1,0:T(1,128)} %broadcast_in_dim.74), calls=%async_computation.5 | async-start | bytes 2359296 | tf_op jit(solution)/shard_map/all_to_all | solution.py:22
  183.5 46.6 %all-to-all-start.2 = ((bf16[16,192,256]{2,1,0:T(8,128)(2,1)}), bf16[16,192,256]{2,1,0:T(8,128)(2,1)S(1)}, u32[]{:S(2)}, u32[]{:S(2)}) async-start(bf16[16,192,256]{2,1,0:T(8,128)(2,1)} %bitcast.33), calls=%async_computation.2 | async-start | bytes 3145728 | tf_op jit(solution)/shard_map/all_to_all | solution.py:22
where the time goes:
time: 232 us; the launch traced here: 231 us
  waiting for transfers between devices  104 us (45%)
  starting transfers between devices  55.6 us (24%)
  local copies, waits for them, and re-layouts  42 us (18%)
  matrix products  13.2 us (6%)
  other arithmetic  13 us (6%)
    all_to_all x6, waiting for transfers between devices, swap_all(): return lax.all_to_all(value, axes, 0, 0, tiled=True)  71.9 us
    all_to_all x6, starting transfers between devices, swap_all(): return lax.all_to_all(value, axes, 0, 0, tiled=True)  43.1 us
    ppermute x14, waiting for transfers between devices, shift(): return lax.ppermute(value, axis, [(i, (i + step) % n) for i in range(n)])  32.2 us
    ppermute x14, starting transfers between devices, shift(): return lax.ppermute(value, axis, [(i, (i + step) % n) for i in range(n)])  12.5 us
    dynamic_update_slice x9, local copies, waits for them, and re-layouts, put(): lax.dynamic_update_slice(weight, b[None, :, None], (row, zi, c, 0, 0))  11.4 us
    dot_general x1, matrix products, on_device(): lax.dot_general(scaled.reshape(4 * tokens, width), weight.reshape(16 * ro...  10.7 us
    dynamic_update_slice x4, other arithmetic, on_device(): scaled = lax.dynamic_update_slice(scaled, g[None], ((x + e) % 4, 0, 0))  8.1 us
    unnamed x25, local copies, waits for them, and re-layouts  6.93 us
  transfers between devices with their start and end apart: 20, of which 9 were waited for; matrix products, arithmetic and copies ran while one was open for 26% of the time, Pallas kernels for 0%

commit v1 on v0

v1 whole, which is shorter than its diff:
```python
import jax
import jax.numpy as jnp
from jax import lax
from jax.experimental import pallas as pl
from jax.experimental.pallas import tpu as pltpu
from jax.sharding import Mesh, PartitionSpec as P

SCALE = 0.5
BF = jnp.bfloat16
F32 = jnp.float32
SIZES = {"y": 4, "x": 4, "zl": 2, "co": 2, "t": 4}
DP = ("y", "x", "zl", "co")
N_DP = 64


def shift(value, axis, step):
    n = SIZES[axis]
    return lax.ppermute(value, axis, [(i, (i + step) % n) for i in range(n)])


def swap_all(value, axes):
    return lax.all_to_all(value, axes, 0, 0, tiled=True)


def after(value, *earlier):
    return lax.optimization_barrier((value,) + earlier)[0]


def merge_kernel(block, codes, scales, factor, out_factor, own, squares):
    width = codes.shape[1]
    count = scales.shape[1]
    start = pl.program_id(0) * width
    group = (start + lax.broadcasted_iota(jnp.int32, (count, width), 1)) // block
    pick = (group == lax.broadcasted_iota(jnp.int32, (count, width), 0)).astype(F32)
    spread = jnp.dot(
        scales[...], pick, precision=lax.Precision.HIGHEST, preferred_element_type=F32
    )
    low = jnp.dot(factor[...], out_factor[...], preferred_element_type=F32)
    merged = ((codes[...].astype(F32) - 7.5) * spread + SCALE * low).astype(BF)
    own[...] = merged
    wide = merged.astype(F32)
    squares[...] = jnp.sum(wide * wide, axis=0, keepdims=True)


def merge(codes, scales, factor, out_factor):
    rows, width = codes.shape
    rank = factor.shape[1]
    count = scales.shape[1]
    steps = 4
    part = width // steps

    def columns(n):
        return pl.BlockSpec((n, part), lambda i: (0, i))

    def whole(a, b):
        return pl.BlockSpec((a, b), lambda i: (0, 0))

    def body(*refs):
        merge_kernel(width // count, *refs)

    return pl.pallas_call(
        body,
        grid=(steps,),
        in_specs=[columns(rows), whole(rows, count), whole(rows, rank), columns(rank)],
        out_specs=[columns(rows), columns(1)],
        out_shape=[
            jax.ShapeDtypeStruct((rows, width), BF),
            jax.ShapeDtypeStruct((1, width), F32),
        ],
        compiler_params=pltpu.CompilerParams(vmem_limit_bytes=48 * 1024 * 1024),
    )(codes, scales, factor, out_factor)


def tile_kernel(where, grad, ratio, mine, swapped, out, scaled, wide):
    tokens = grad.shape[0]
    rows = mine.shape[2]
    co = where[0]

    @pl.when(pl.program_id(0) == 0)
    def _():
        @pl.loop(0, tokens, step=16)
        def _(r):
            r = pl.multiple_of(r, 16)
            value = grad[pl.ds(r, 16), :].astype(F32) * ratio[...]
            scaled[pl.ds(r, 16), :] = value.astype(BF)

    for zi in range(2):
        for source, c in ((mine, co), (swapped, 1 - co)):
            row = pl.multiple_of(zi * 2 * rows + c * rows, rows)
            wide[pl.ds(row, rows), :] = source[0, zi]
    n = tokens // 4
    for k in range(4):
        tile = lax.dot_general(
            scaled[k * n : (k + 1) * n, :],
            wide[...],
            (((1,), (1,)), ((), ())),
            preferred_element_type=F32,
        )
        out[k, 0] = tile.astype(BF)


def tile_of(where, grad, ratio, mine, swapped):
    tokens, width = grad.shape
    rows = mine.shape[2]
    n = tokens // 4

    def whole(shape):
        return pl.BlockSpec(shape, lambda i, w: (0, 0))

    weights = pl.BlockSpec((1, 2, rows, width), lambda i, w: (i, 0, 0, 0))
    return pl.pallas_call(
        tile_kernel,
        grid_spec=pltpu.PrefetchScalarGridSpec(
            num_scalar_prefetch=1,
            grid=(4,),
            in_specs=[whole(grad.shape), whole((1, width)), weights, weights],
            out_specs=pl.BlockSpec((4, 1, n, 4 * rows), lambda i, w: (0, i, 0, 0)),
            scratch_shapes=[
                pltpu.VMEM((tokens, width), BF),
                pltpu.VMEM((4 * rows, width), BF),
            ],
        ),
        out_shape=jax.ShapeDtypeStruct((4, 4, n, 4 * rows), BF),
        compiler_params=pltpu.CompilerParams(vmem_limit_bytes=48 * 1024 * 1024),
        cost_estimate=pl.CostEstimate(
            flops=2 * tokens * 16 * rows * width,
            bytes_accessed=2 * width * (tokens + 16 * rows),
            transcendentals=0,
        ),
    )(where, grad, ratio, mine, swapped)


def on_device(codes, scales, in_factor, out_factor, magnitude, inputs, grad, pre):
    y, x, zl, co, t = (lax.axis_index(a) for a in ("y", "x", "zl", "co", "t"))
    rows, width = codes.shape
    tokens = grad.shape[0]
    features = inputs.shape[1]
    part = features // SIZES["x"]
    rank = in_factor.shape[1]

    g_all = lax.all_gather(grad, "x", axis=0, tiled=True)

    first = (((y * 4 + x) * 2 + zl) * 2 + co) * rows
    factor_rows = lax.dynamic_slice_in_dim(in_factor, first, rows, 0)
    own, squares = merge(codes, scales, factor_rows, out_factor)

    other = shift(own, "zl", 1)
    mine = jnp.zeros((4, 2, rows, width), BF)

    def put(buffer, block, step, zi):
        return lax.dynamic_update_slice(buffer, block[None, None], ((y + step) % 4, zi, 0, 0))

    own_down, own_up = shift(own, "y", 1), shift(own, "y", -1)
    own_far = shift(own_down, "y", 1)
    other_down, other_up = shift(other, "y", 1), shift(other, "y", -1)
    other_far = shift(other_up, "y", -1)
    for zi, blocks in (
        (zl, ((own, 0), (own_down, -1), (own_up, 1), (own_far, 2))),
        (1 - zl, ((other, 0), (other_down, -1), (other_up, 1), (other_far, 2))),
    ):
        for block, step in blocks:
            mine = put(mine, block, step, zi)
    swapped = shift(mine, "co", 1)

    total = squares.reshape(-1, 128)
    for axis in ("y", "co", "zl", "x"):
        if axis == "x":
            total = after(total, own_down, own_up, other)
        steps = [shift(total, axis, k) for k in range(1, SIZES[axis])]
        for piece in steps:
            total = total + piece
    col_norm = jnp.sqrt(total.reshape(-1) + 1e-06)
    ratio = magnitude / col_norm

    scaled_own = (grad.astype(F32) * ratio).astype(BF)
    factor_cols = lax.dynamic_slice_in_dim(in_factor, t * features, features, 0)
    hidden = jnp.dot(inputs, factor_cols, preferred_element_type=F32)
    back = lax.dot_general(
        scaled_own, out_factor, (((1,), (1,)), ((), ())), preferred_element_type=F32
    )
    low = jnp.concatenate([hidden, back], axis=1).astype(BF)
    pieces = [shift(low, "t", k) for k in (1, 2, 3)]
    low = sum((p.astype(F32) for p in pieces), low.astype(F32)).astype(BF)
    hidden, back = low[:, :rank], low[:, rank:]
    in_grad = SCALE * lax.dot_general(
        back, inputs, (((0,), (0,)), ((), ())), preferred_element_type=F32
    )
    out_grad = SCALE * lax.dot_general(
        hidden, scaled_own, (((0,), (0,)), ((), ())), preferred_element_type=F32
    )
    mag_sum = jnp.sum(grad.astype(F32) * pre.astype(F32), axis=0).reshape(N_DP, -1)
    adapters = jnp.concatenate([out_grad, in_grad, mag_sum], axis=1)
    for axis, index in (("co", co), ("zl", zl)):
        side = adapters.shape[0] // 2
        keep = lax.dynamic_slice_in_dim(adapters, index * side, side, 0)
        give = lax.dynamic_slice_in_dim(adapters, (1 - index) * side, side, 0)
        adapters = keep + shift(give, axis, 1)
    adapters = swap_all(adapters, ("y", "x"))
    adapters = jnp.sum(adapters, axis=0, keepdims=True)
    adapters = swap_all(jnp.broadcast_to(adapters, (side, adapters.shape[1])), ("y", "x"))
    for axis, index in (("zl", zl), ("co", co)):
        across = shift(adapters, axis, 1)
        pair = (jnp.stack([adapters, across]), jnp.stack([across, adapters]))
        adapters = jnp.where(index == 0, *pair).reshape(-1, adapters.shape[1])
    out_grad = adapters[:, :width]
    in_grad = adapters[:, width : width + features].T
    mag_grad = adapters[:, width + features :].reshape(-1) / col_norm

    where = co.astype(jnp.int32).reshape(1)
    tile = tile_of(where, g_all, ratio.reshape(1, -1), mine, swapped)
    tile = swap_all(tile.reshape(16, tokens, part), ("x", "t"))

    tile = jnp.sum(tile.reshape(4, 4, tokens, part).astype(F32), axis=1).astype(BF)
    grad_in = tile.transpose(1, 0, 2).reshape(tokens, features)
    return grad_in, in_grad, out_grad, mag_grad


def solution(mesh):
    fine = Mesh(mesh.devices.reshape(4, 4, 2, 2, 4), ("y", "x", "zl", "co", "t"))
    in_specs = (
        P(DP, "t"),
        P(DP, "t"),
        P(),
        P(None, "t"),
        P("t"),
        P(DP, "t"),
        P(DP, "t"),
        P(DP, "t"),
    )
    out_specs = (P(DP, "t"), P("t", None), P(None, "t"), P("t"))
    return jax.shard_map(
        on_device, mesh=fine, in_specs=in_specs, out_specs=out_specs, check_vma=False
    )
```

time: 232 us -> 187 us (0.81)
  waiting for transfers between devices: 104 us -> 75.9 us
  local copies, waits for them, and re-layouts: 42 us -> 20.7 us
  Pallas kernels: 2.11 us -> 17.5 us
  between operations: 1.05 us -> 14.4 us
  matrix products: 13.2 us -> 1.44 us
  other arithmetic: 13 us -> 3.56 us
  starting transfers between devices: 55.6 us -> 51.3 us
    all_to_all x6 -> x3, waiting for transfers between devices: 71.9 us -> 7.14 us  [swap_all(): return lax.all_to_all(value, axes, 0, 0, tiled=True)]
    ppermute x14 -> x23, waiting for transfers between devices: 32.2 us -> 68.8 us  [shift(): return lax.ppermute(value, axis, [(i, (i + step) % n) for i in range(n)])]
    all_to_all x6 -> x3, starting transfers between devices: 43.1 us -> 20.1 us  [swap_all(): return lax.all_to_all(value, axes, 0, 0, tiled=True)]
    ppermute x14 -> x23, starting transfers between devices: 12.5 us -> 31.2 us  [shift(): return lax.ppermute(value, axis, [(i, (i + step) % n) for i in range(n)])]
    pallas_call x0 -> x1, Pallas kernels: none -> 15.7 us  [tile_of(): pl.pallas_call(tile_kernel, grid_spec=pltpu.PrefetchScalarGridSpec(num_sc...]
    dot_general x1 -> x0, matrix products: 10.7 us -> none  [on_device(): lax.dot_general(scaled.reshape(4 * tokens, width), weight.reshape(16 * ro...]
    dynamic_update_slice x5 -> x0, other arithmetic: 9.2 us -> none  [the longest x4 8.1 us: on_device(): scaled = lax.dynamic_update_slice(scaled, g[None], ((x + e) % 4, 0, 0))]
    broadcast_in_dim x5 -> x2, local copies, waits for them, and re-layouts: 9.44 us -> 3.07 us  [the longest x1 2.2 us: on_device(): mine = jnp.zeros((4, 2, rows, width), BF)]
  transfers between devices with their start and end apart: 20 -> 27, of which waited for: 9 -> 12; matrix products, arithmetic and copies ran while one was open for 26% -> 11% of each run, Pallas kernels for 0% -> 8%
where the time goes in v1:
time: 187 us; the launch traced here: 185 us
  waiting for transfers between devices  75.9 us (41%)
  starting transfers between devices  51.3 us (27%)
  local copies, waits for them, and re-layouts  20.7 us (11%)
  Pallas kernels  17.5 us (9%)
  between operations  14.4 us (8%)
  other arithmetic  3.56 us (2%)
    ppermute x23, waiting for transfers between devices, shift(): return lax.ppermute(value, axis, [(i, (i + step) % n) for i in range(n)])  68.8 us
    ppermute x23, starting transfers between devices, shift(): return lax.ppermute(value, axis, [(i, (i + step) % n) for i in range(n)])  31.2 us
    all_to_all x3, starting transfers between devices, swap_all(): return lax.all_to_all(value, axes, 0, 0, tiled=True)  20.1 us
    pallas_call x1, Pallas kernels, tile_of(): pl.pallas_call(tile_kernel, grid_spec=pltpu.PrefetchScalarGridSpec(num_sc...  15.7 us
    dynamic_update_slice x8, local copies, waits for them, and re-layouts, put(): lax.dynamic_update_slice(buffer, block[None, None], ((y + step) % 4, zi,...  9.56 us
    all_to_all x3, waiting for transfers between devices, swap_all(): return lax.all_to_all(value, axes, 0, 0, tiled=True)  7.14 us
    unnamed x23, local copies, waits for them, and re-layouts  4.16 us
  transfers between devices with their start and end apart: 27, of which 12 were waited for; matrix products, arithmetic and copies ran while one was open for 11% of the time, Pallas kernels for 8%

profile of v1, /device:TPU:8, one launch (start us, length us, event | category | flops | bytes accessed | tf_op | source)
XLA Modules:
  0.0 184.8 jit_solution(4208670269782175634)
XLA Ops:
  8.4 1.2 copy-done.1
  10.6 1.8 shard_map.111
  12.5 2.3 %collective-permute-start.2 = (f32[28,128]{1,0:T(8,128)S(1)}, f32[28,128]{1,0:T(8,128)S(1)}, u32[]{:S(2)}, u32[]{:S(2)}) collective-permute-start(f32[28,128]{1,0:T(8,128)S(1)} %bitcast.58), channel_id=1, source_target_pairs={{0,192},{64,0},{128,64},{192,128},{1,193},{65,1},{129,65},{193,129... | collective-permute-start | bytes 43016 | tf_op jit(solution)/shard_map/ppermute | solution.py:18
  15.6 1.9 %collective-permute-start = (f32[28,128]{1,0:T(8,128)S(1)}, f32[28,128]{1,0:T(8,128)S(1)}, u32[]{:S(2)}, u32[]{:S(2)}) collective-permute-start(f32[28,128]{1,0:T(8,128)S(1)} %bitcast.60), channel_id=1, source_target_pairs={{0,64},{64,128},{128,192},{192,0},{1,65},{65,129},{129,193},{193,1... | collective-permute-start | bytes 43016 | tf_op jit(solution)/shard_map/ppermute | solution.py:18
  17.5 1.4 collective-permute-start.5
  19.6 2.2 %broadcast_in_dim.34 = bf16[4,2,64,3584]{3,2,1,0:T(8,128)(2,1)} broadcast(bf16[]{:T(256)} %constant.72.clone.1), dimensions={} | broadcast | bytes 3670018 | tf_op jit(solution)/shard_map/broadcast_in_dim | solution.py:148
  22.6 1.9 %collective-permute-start.7 = (bf16[64,3584]{1,0:T(8,128)(2,1)S(1)}, bf16[64,3584]{1,0:T(8,128)(2,1)}, u32[]{:S(2)}, u32[]{:S(2)}) collective-permute-start(bf16[64,3584]{1,0:T(8,128)(2,1)S(1)} %get-tuple-element.8), channel_id=1, source_target_pairs={{0,8},{8,0},{1,9},{9,1},{2,10},{10,2},{3,11},{11,3},{4,12},{12,4},... | collective-permute-start | bytes 1376264 | tf_op jit(solution)/shard_map/ppermute | solution.py:18
  26.3 7.7 %collective-permute-done.4 = f32[28,128]{1,0:T(8,128)S(1)} collective-permute-done((f32[28,128]{1,0:T(8,128)S(1)}, f32[28,128]{1,0:T(8,128)S(1)}, u32[]{:S(2)}, u32[]{:S(2)}) %collective-permute-start.4) | collective-permute-done | bytes 14368 | tf_op jit(solution)/shard_map/ppermute | solution.py:18
  34.0 2.8 %collective-permute-start.10 = (f32[28,128]{1,0:T(8,128)S(1)}, f32[28,128]{1,0:T(8,128)S(1)}, u32[]{:S(2)}, u32[]{:S(2)}) collective-permute-start(f32[28,128]{1,0:T(8,128)S(1)} %add.139), channel_id=1, source_target_pairs={{0,48},{16,0},{32,16},{48,32},{1,49},{17,1},{33,17},{49,33},{2,50}... | collective-permute-start | bytes 43016 | tf_op jit(solution)/shard_map/ppermute | solution.py:18
  38.8 1.5 collective-permute-start.12
  40.3 1.8 bitcast_dynamic-update-slice_fusion.6
  43.5 6.2 %collective-permute-start.18 = (bf16[192,128]{0,1:T(8,128)(2,1)S(1)}, bf16[192,128]{0,1:T(8,128)(2,1)S(1)}, u32[]{:S(2)}, u32[]{:S(2)}) collective-permute-start(bf16[192,128]{0,1:T(8,128)(2,1)S(1)} %pad_maximum_fusion.1), channel_id=1, source_target_pairs={{0,3},{1,0},{2,1},{3,2},{4,7},{5,4},{6,5},{7,6},{8,11},{9,8},{10,9... | collective-permute-start | bytes 147464 | tf_op jit(solution)/shard_map/ppermute | solution.py:18
  49.7 1.2 collective-permute-start.17
  50.9 2.6 %collective-permute-start.16 = (bf16[192,128]{0,1:T(8,128)(2,1)S(1)}, bf16[192,128]{0,1:T(8,128)(2,1)S(1)}, u32[]{:S(2)}, u32[]{:S(2)}) collective-permute-start(bf16[192,128]{0,1:T(8,128)(2,1)S(1)} %pad_maximum_fusion.1), channel_id=1, source_target_pairs={{0,1},{1,2},{2,3},{3,0},{4,5},{5,6},{6,7},{7,4},{8,9},{9,10},{10,1... | collective-permute-start | bytes 147464 | tf_op jit(solution)/shard_map/ppermute | solution.py:18
  53.5 1.8 bitcast_dynamic-update-slice_fusion.5
  55.4 1.4 collective-permute-start.13
  56.7 1.4 collective-permute-done.17
  59.5 6.0 %collective-permute-done.13 = bf16[64,3584]{1,0:T(8,128)(2,1)S(1)} collective-permute-done((bf16[64,3584]{1,0:T(8,128)(2,1)}, bf16[64,3584]{1,0:T(8,128)(2,1)S(1)}, u32[]{:S(2)}, u32[]{:S(2)}) %collective-permute-start.13) | collective-permute-done | bytes 458784 | tf_op jit(solution)/shard_map/ppermute | solution.py:18
  65.5 1.4 collective-permute-start.14
  67.7 1.8 bitcast_dynamic-update-slice_fusion.3
  71.1 2.9 %collective-permute-done.14 = bf16[64,3584]{1,0:T(8,128)(2,1)S(1)} collective-permute-done((bf16[64,3584]{1,0:T(8,128)(2,1)S(1)}, bf16[64,3584]{1,0:T(8,128)(2,1)S(1)}, u32[]{:S(2)}, u32[]{:S(2)}) %collective-permute-start.14) | collective-permute-done | bytes 458784 | tf_op jit(solution)/shard_map/ppermute | solution.py:18
  74.9 1.7 collective-permute-start.20
  76.6 8.0 %collective-permute-done.20 = f32[16,4664]{1,0:T(8,128)S(1)} collective-permute-done((f32[16,4664]{1,0:T(8,128)S(1)}, f32[16,4664]{1,0:T(8,128)S(1)}, u32[]{:S(2)}, u32[]{:S(2)}) %collective-permute-start.20) | collective-permute-done | bytes 298528 | tf_op jit(solution)/shard_map/ppermute | solution.py:18
  85.7 8.2 %all-to-all-start.1 = ((f32[16,1,4664]{2,1,0:T(1,128)}), f32[16,1,4664]{2,1,0:T(1,128)S(1)}, u32[]{:S(2)}, u32[]{:S(2)}) async-start(f32[16,1,4664]{2,1,0:T(1,128)} %copy.22), calls=%async_computation.1 | async-start | bytes 606208 | tf_op jit(solution)/shard_map/all_to_all | solution.py:22
  93.9 7.1 %all-to-all-done.1 = f32[16,1,4664]{2,1,0:T(1,128)S(1)} async-done(((f32[16,1,4664]{2,1,0:T(1,128)}), f32[16,1,4664]{2,1,0:T(1,128)S(1)}, u32[]{:S(2)}, u32[]{:S(2)}) %all-to-all-start.1) | async-done | bytes 298528 | tf_op jit(solution)/shard_map/all_to_all | solution.py:22
  102.1 5.3 %all-to-all-start.2 = ((f32[16,1,4664]{2,1,0:T(1,128)}), f32[16,1,4664]{2,1,0:T(1,128)S(1)}, u32[]{:S(2)}, u32[]{:S(2)}) async-start(f32[16,1,4664]{2,1,0:T(1,128)} %broadcast_in_dim.43), calls=%async_computation.2 | async-start | bytes 606208 | tf_op jit(solution)/shard_map/all_to_all | solution.py:22
  107.5 15.7 %shard_map.112 = bf16[4,4,192,256]{3,2,1,0:T(8,128)(2,1)} custom-call(s32[1]{0:T(128)} %bitcast.where, bf16[768,3584]{1,0:T(8,128)(2,1)} %all-gather.2.cloned.1.call-done.grad, f32[1,3584]{1,0:T(1,128)S(1)} %reshape.77.ratio, bf16[4,2,64,3584]{3,2,1,0:T(8,128)(2,1)} %bitcast_dynamic-update-slice_fusion.mine, ...), custom_call_target="tpu_custom_call" | custom-call | flops 5637144576 | bytes 12845056 | tf_op jit(solution)/shard_map/pallas_call | solution.py:111
  123.2 6.6 %all-to-all-start = ((bf16[16,192,256]{2,1,0:T(8,128)(2,1)}), bf16[16,192,256]{2,1,0:T(8,128)(2,1)S(1)}, u32[]{:S(2)}, u32[]{:S(2)}) async-start(bf16[16,192,256]{2,1,0:T(8,128)(2,1)} %bitcast.10), calls=%async_computation | async-start | bytes 3145728 | tf_op jit(solution)/shard_map/all_to_all | solution.py:22
  129.7 1.1 collective-permute-start.21
  130.8 38.9 %collective-permute-done.21 = f32[16,4664]{1,0:T(8,128)S(1)} collective-permute-done((f32[16,4664]{1,0:T(8,128)S(1)}, f32[16,4664]{1,0:T(8,128)S(1)}, u32[]{:S(2)}, u32[]{:S(2)}) %collective-permute-start.21) | collective-permute-done | bytes 298528 | tf_op jit(solution)/shard_map/ppermute | solution.py:18
  169.9 2.0 %collective-permute-done.22 = f32[32,4664]{1,0:T(8,128)S(1)} collective-permute-done((f32[32,4664]{1,0:T(8,128)S(1)}, f32[32,4664]{1,0:T(8,128)S(1)}, u32[]{:S(2)}, u32[]{:S(2)}) %collective-permute-start.22) | collective-permute-done | bytes 597024 | tf_op jit(solution)/shard_map/ppermute | solution.py:18
  172.7 1.8 maximum_select_fusion
  (89 shorter events, 20.9 us)
Async XLA Ops:
  7.2 100.3 %all-gather.2.cloned.1.call-start = ((), (), s32[]{:S(2)}) async-start(), calls=%async_computation.3 | async-start | bytes 6881280 | tf_op jit(solution)/shard_map/all_gather | solution.py:141
  12.5 10.1 %collective-permute-start.2 = (f32[28,128]{1,0:T(8,128)S(1)}, f32[28,128]{1,0:T(8,128)S(1)}, u32[]{:S(2)}, u32[]{:S(2)}) collective-permute-start(f32[28,128]{1,0:T(8,128)S(1)} %bitcast.58), channel_id=1, source_target_pairs={{0,192},{64,0},{128,64},{192,128},{1,193},{65,1},{129,65},{193,129... | collective-permute-start | bytes 43016 | tf_op jit(solution)/shard_map/ppermute | solution.py:18
  14.7 9.8 %collective-permute-start.1 = (f32[28,128]{1,0:T(8,128)S(1)}, f32[28,128]{1,0:T(8,128)S(1)}, u32[]{:S(2)}, u32[]{:S(2)}) collective-permute-start(f32[28,128]{1,0:T(8,128)S(1)} %bitcast.59), channel_id=1, source_target_pairs={{0,128},{64,192},{128,0},{192,64},{1,129},{65,193},{129,1},{193,65... | collective-permute-start | bytes 43016 | tf_op jit(solution)/shard_map/ppermute | solution.py:18
  15.6 8.9 %collective-permute-start = (f32[28,128]{1,0:T(8,128)S(1)}, f32[28,128]{1,0:T(8,128)S(1)}, u32[]{:S(2)}, u32[]{:S(2)}) collective-permute-start(f32[28,128]{1,0:T(8,128)S(1)} %bitcast.60), channel_id=1, source_target_pairs={{0,64},{64,128},{128,192},{192,0},{1,65},{65,129},{129,193},{193,1... | collective-permute-start | bytes 43016 | tf_op jit(solution)/shard_map/ppermute | solution.py:18
  17.5 7.1 %copy-start.4 = (bf16[192,3584]{1,0:T(8,128)(2,1)S(1)}, bf16[192,3584]{1,0:T(8,128)(2,1)}, u32[]{:S(2)}) copy-start(bf16[192,3584]{1,0:T(8,128)(2,1)} %param.14) | copy-start | bytes 4128772
  17.5 16.5 %collective-permute-start.5 = (bf16[64,3584]{1,0:T(8,128)(2,1)S(1)}, bf16[64,3584]{1,0:T(8,128)(2,1)}, u32[]{:S(2)}, u32[]{:S(2)}) collective-permute-start(bf16[64,3584]{1,0:T(8,128)(2,1)S(1)} %get-tuple-element.8), channel_id=1, source_target_pairs={{0,64},{64,128},{128,192},{192,0},{1,65},{65,129},{129,193},{193,1... | collective-permute-start | bytes 1376264 | tf_op jit(solution)/shard_map/ppermute | solution.py:18
  18.8 15.1 %collective-permute-start.6 = (bf16[64,3584]{1,0:T(8,128)(2,1)S(1)}, bf16[64,3584]{1,0:T(8,128)(2,1)}, u32[]{:S(2)}, u32[]{:S(2)}) collective-permute-start(bf16[64,3584]{1,0:T(8,128)(2,1)S(1)} %get-tuple-element.8), channel_id=1, source_target_pairs={{0,192},{64,0},{128,64},{192,128},{1,193},{65,1},{129,65},{193,129... | collective-permute-start | bytes 1376264 | tf_op jit(solution)/shard_map/ppermute | solution.py:18
  19.5 5.1 %copy-start.7 = (bf16[192,3584]{1,0:T(8,128)(2,1)S(1)}, bf16[192,3584]{1,0:T(8,128)(2,1)}, u32[]{:S(2)}) copy-start(bf16[192,3584]{1,0:T(8,128)(2,1)} %param.15) | copy-start | bytes 4128772
  21.8 4.1 %copy-start.6 = (bf16[192,1024]{1,0:T(8,128)(2,1)S(1)}, bf16[192,1024]{1,0:T(8,128)(2,1)}, u32[]{:S(2)}) copy-start(bf16[192,1024]{1,0:T(8,128)(2,1)} %param.13) | copy-start | bytes 1179652
  21.8 21.1 %copy-start.9 = (f32[3584]{0:T(1024)S(1)}, f32[3584]{0:T(1024)}, u32[]{:S(2)}) copy-start(f32[3584]{0:T(1024)} %param.12) | copy-start | bytes 43012
  21.8 21.2 %copy-start.3 = (bf16[64,3584]{1,0:T(8,128)(2,1)S(1)}, bf16[64,3584]{1,0:T(8,128)(2,1)}, u32[]{:S(2)}) copy-start(bf16[64,3584]{1,0:T(8,128)(2,1)} %refs_3_.1) | copy-start | bytes 1376260
  22.6 11.4 %collective-permute-start.7 = (bf16[64,3584]{1,0:T(8,128)(2,1)S(1)}, bf16[64,3584]{1,0:T(8,128)(2,1)}, u32[]{:S(2)}, u32[]{:S(2)}) collective-permute-start(bf16[64,3584]{1,0:T(8,128)(2,1)S(1)} %get-tuple-element.8), channel_id=1, source_target_pairs={{0,8},{8,0},{1,9},{9,1},{2,10},{10,2},{3,11},{11,3},{4,12},{12,4},... | collective-permute-start | bytes 1376264 | tf_op jit(solution)/shard_map/ppermute | solution.py:18
  24.5 1.3 collective-permute-start.3
  25.8 8.2 %collective-permute-start.4 = (f32[28,128]{1,0:T(8,128)S(1)}, f32[28,128]{1,0:T(8,128)S(1)}, u32[]{:S(2)}, u32[]{:S(2)}) collective-permute-start(f32[28,128]{1,0:T(8,128)S(1)} %add.138), channel_id=1, source_target_pairs={{0,8},{8,0},{1,9},{9,1},{2,10},{10,2},{3,11},{11,3},{4,12},{12,4},... | collective-permute-start | bytes 43016 | tf_op jit(solution)/shard_map/ppermute | solution.py:18
  34.0 8.2 %collective-permute-start.10 = (f32[28,128]{1,0:T(8,128)S(1)}, f32[28,128]{1,0:T(8,128)S(1)}, u32[]{:S(2)}, u32[]{:S(2)}) collective-permute-start(f32[28,128]{1,0:T(8,128)S(1)} %add.139), channel_id=1, source_target_pairs={{0,48},{16,0},{32,16},{48,32},{1,49},{17,1},{33,17},{49,33},{2,50}... | collective-permute-start | bytes 43016 | tf_op jit(solution)/shard_map/ppermute | solution.py:18
  36.8 5.6 %collective-permute-start.9 = (f32[28,128]{1,0:T(8,128)S(1)}, f32[28,128]{1,0:T(8,128)S(1)}, u32[]{:S(2)}, u32[]{:S(2)}) collective-permute-start(f32[28,128]{1,0:T(8,128)S(1)} %add.139), channel_id=1, source_target_pairs={{0,32},{16,48},{32,0},{48,16},{1,33},{17,49},{33,1},{49,17},{2,34}... | collective-permute-start | bytes 43016 | tf_op jit(solution)/shard_map/ppermute | solution.py:18
  37.6 5.3 %collective-permute-start.8 = (f32[28,128]{1,0:T(8,128)S(1)}, f32[28,128]{1,0:T(8,128)S(1)}, u32[]{:S(2)}, u32[]{:S(2)}) collective-permute-start(f32[28,128]{1,0:T(8,128)S(1)} %add.139), channel_id=1, source_target_pairs={{0,16},{16,32},{32,48},{48,0},{1,17},{17,33},{33,49},{49,1},{2,18}... | collective-permute-start | bytes 43016 | tf_op jit(solution)/shard_map/ppermute | solution.py:18
  38.5 28.3 %collective-permute-start.11 = (bf16[64,3584]{1,0:T(8,128)(2,1)}, bf16[64,3584]{1,0:T(8,128)(2,1)S(1)}, u32[]{:S(2)}, u32[]{:S(2)}) collective-permute-start(bf16[64,3584]{1,0:T(8,128)(2,1)} %collective-permute-done.5), channel_id=1, source_target_pairs={{0,64},{64,128},{128,192},{192,0},{1,65},{65,129},{129,193},{193,1... | collective-permute-start | bytes 1376264 | tf_op jit(solution)/shard_map/ppermute | solution.py:18
  38.8 30.7 %collective-permute-start.12 = (bf16[64,3584]{1,0:T(8,128)(2,1)}, bf16[64,3584]{1,0:T(8,128)(2,1)S(1)}, u32[]{:S(2)}, u32[]{:S(2)}) collective-permute-start(bf16[64,3584]{1,0:T(8,128)(2,1)} %collective-permute-done.7), channel_id=1, source_target_pairs={{0,64},{64,128},{128,192},{192,0},{1,65},{65,129},{129,193},{193,1... | collective-permute-start | bytes 1376264 | tf_op jit(solution)/shard_map/ppermute | solution.py:18
  43.5 11.8 %collective-permute-start.18 = (bf16[192,128]{0,1:T(8,128)(2,1)S(1)}, bf16[192,128]{0,1:T(8,128)(2,1)S(1)}, u32[]{:S(2)}, u32[]{:S(2)}) collective-permute-start(bf16[192,128]{0,1:T(8,128)(2,1)S(1)} %pad_maximum_fusion.1), channel_id=1, source_target_pairs={{0,3},{1,0},{2,1},{3,2},{4,7},{5,4},{6,5},{7,6},{8,11},{9,8},{10,9... | collective-permute-start | bytes 147464 | tf_op jit(solution)/shard_map/ppermute | solution.py:18
  49.7 8.4 %collective-permute-start.17 = (bf16[192,128]{0,1:T(8,128)(2,1)S(1)}, bf16[192,128]{0,1:T(8,128)(2,1)S(1)}, u32[]{:S(2)}, u32[]{:S(2)}) collective-permute-start(bf16[192,128]{0,1:T(8,128)(2,1)S(1)} %pad_maximum_fusion.1), channel_id=1, source_target_pairs={{0,2},{1,3},{2,0},{3,1},{4,6},{5,7},{6,4},{7,5},{8,10},{9,11},{10,... | collective-permute-start | bytes 147464 | tf_op jit(solution)/shard_map/ppermute | solution.py:18
  50.9 7.6 %collective-permute-start.16 = (bf16[192,128]{0,1:T(8,128)(2,1)S(1)}, bf16[192,128]{0,1:T(8,128)(2,1)S(1)}, u32[]{:S(2)}, u32[]{:S(2)}) collective-permute-start(bf16[192,128]{0,1:T(8,128)(2,1)S(1)} %pad_maximum_fusion.1), channel_id=1, source_target_pairs={{0,1},{1,2},{2,3},{3,0},{4,5},{5,6},{6,7},{7,4},{8,9},{9,10},{10,1... | collective-permute-start | bytes 147464 | tf_op jit(solution)/shard_map/ppermute | solution.py:18
  55.4 10.1 %collective-permute-start.13 = (bf16[64,3584]{1,0:T(8,128)(2,1)}, bf16[64,3584]{1,0:T(8,128)(2,1)S(1)}, u32[]{:S(2)}, u32[]{:S(2)}) collective-permute-start(bf16[64,3584]{1,0:T(8,128)(2,1)} %collective-permute-done.7), channel_id=1, source_target_pairs={{0,192},{64,0},{128,64},{192,128},{1,193},{65,1},{129,65},{193,129... | collective-permute-start | bytes 1376264 | tf_op jit(solution)/shard_map/ppermute | solution.py:18
  59.4 15.5 %collective-permute-start.19 = (f32[32,4664]{1,0:T(8,128)S(1)}, f32[32,4664]{1,0:T(8,128)S(1)}, u32[]{:S(2)}, u32[]{:S(2)}) collective-permute-start(f32[32,4664]{1,0:T(8,128)S(1)} %constant_dynamic-slice_fusion.1), channel_id=1, source_target_pairs={{0,4},{4,0},{1,5},{5,1},{2,6},{6,2},{3,7},{7,3},{8,12},{12,8},{9,1... | collective-permute-start | bytes 1790984 | tf_op jit(solution)/shard_map/ppermute | solution.py:18
  65.5 8.5 %collective-permute-start.14 = (bf16[64,3584]{1,0:T(8,128)(2,1)S(1)}, bf16[64,3584]{1,0:T(8,128)(2,1)S(1)}, u32[]{:S(2)}, u32[]{:S(2)}) collective-permute-start(bf16[64,3584]{1,0:T(8,128)(2,1)S(1)} %collective-permute-done.13), channel_id=1, source_target_pairs={{0,192},{64,0},{128,64},{192,128},{1,193},{65,1},{129,65},{193,129... | collective-permute-start | bytes 1376264 | tf_op jit(solution)/shard_map/ppermute | solution.py:18
  74.8 32.6 %collective-permute-start.15 = (bf16[4,2,64,3584]{3,2,1,0:T(8,128)(2,1)}, bf16[4,2,64,3584]{3,2,1,0:T(8,128)(2,1)}, u32[]{:S(2)}, u32[]{:S(2)}) collective-permute-start(bf16[4,2,64,3584]{3,2,1,0:T(8,128)(2,1)} %bitcast_dynamic-update-slice_fusion.mine), channel_id=1, source_target_pairs={{0,4},{4,0},{1,5},{5,1},{2,6},{6,2},{3,7},{7,3},{8,12},{12,8},{9,1... | collective-permute-start | bytes 11010056 | tf_op jit(solution)/shard_map/ppermute | solution.py:18
  74.9 9.7 %collective-permute-start.20 = (f32[16,4664]{1,0:T(8,128)S(1)}, f32[16,4664]{1,0:T(8,128)S(1)}, u32[]{:S(2)}, u32[]{:S(2)}) collective-permute-start(f32[16,4664]{1,0:T(8,128)S(1)} %constant_dynamic-slice_fusion), channel_id=1, source_target_pairs={{0,8},{8,0},{1,9},{9,1},{2,10},{10,2},{3,11},{11,3},{4,12},{12,4},... | collective-permute-start | bytes 895496 | tf_op jit(solution)/shard_map/ppermute | solution.py:18
  85.7 15.4 %all-to-all-start.1 = ((f32[16,1,4664]{2,1,0:T(1,128)}), f32[16,1,4664]{2,1,0:T(1,128)S(1)}, u32[]{:S(2)}, u32[]{:S(2)}) async-start(f32[16,1,4664]{2,1,0:T(1,128)} %copy.22), calls=%async_computation.1 | async-start | bytes 606208 | tf_op jit(solution)/shard_map/all_to_all | solution.py:22
  102.1 21.0 %all-to-all-start.2 = ((f32[16,1,4664]{2,1,0:T(1,128)}), f32[16,1,4664]{2,1,0:T(1,128)S(1)}, u32[]{:S(2)}, u32[]{:S(2)}) async-start(f32[16,1,4664]{2,1,0:T(1,128)} %broadcast_in_dim.43), calls=%async_computation.2 | async-start | bytes 606208 | tf_op jit(solution)/shard_map/all_to_all | solution.py:22
  123.2 53.8 %all-to-all-start = ((bf16[16,192,256]{2,1,0:T(8,128)(2,1)}), bf16[16,192,256]{2,1,0:T(8,128)(2,1)S(1)}, u32[]{:S(2)}, u32[]{:S(2)}) async-start(bf16[16,192,256]{2,1,0:T(8,128)(2,1)} %bitcast.10), calls=%async_computation | async-start | bytes 3145728 | tf_op jit(solution)/shard_map/all_to_all | solution.py:22
  129.7 40.0 %collective-permute-start.21 = (f32[16,4664]{1,0:T(8,128)S(1)}, f32[16,4664]{1,0:T(8,128)S(1)}, u32[]{:S(2)}, u32[]{:S(2)}) collective-permute-start(f32[16,4664]{1,0:T(8,128)S(1)} %bitcast.53), channel_id=1, source_target_pairs={{0,8},{8,0},{1,9},{9,1},{2,10},{10,2},{3,11},{11,3},{4,12},{12,4},... | collective-permute-start | bytes 895496 | tf_op jit(solution)/shard_map/ppermute | solution.py:18
  169.8 2.1 %collective-permute-start.22 = (f32[32,4664]{1,0:T(8,128)S(1)}, f32[32,4664]{1,0:T(8,128)S(1)}, u32[]{:S(2)}, u32[]{:S(2)}) collective-permute-start(f32[32,4664]{1,0:T(8,128)S(1)} %bitcast.50), channel_id=1, source_target_pairs={{0,4},{4,0},{1,5},{5,1},{2,6},{6,2},{3,7},{7,3},{8,12},{12,8},{9,1... | collective-permute-start | bytes 1790984 | tf_op jit(solution)/shard_map/ppermute | solution.py:18
  (5 other events, 6.2 us)
Sparse Core Ops, SparseCore 0:
  19.6 64.0 all-gather.1

commit v2 on v1

v2 whole, which is shorter than its diff:
```python
import jax
import jax.numpy as jnp
from jax import lax
from jax.experimental import pallas as pl
from jax.experimental.pallas import tpu as pltpu
from jax.sharding import Mesh, PartitionSpec as P

SCALE = 0.5
BF = jnp.bfloat16
F32 = jnp.float32
SIZES = {"y": 4, "x": 4, "zl": 2, "co": 2, "t": 4}
DP = ("y", "x", "zl", "co")
N_DP = 64


def shift(value, axis, step):
    n = SIZES[axis]
    return lax.ppermute(value, axis, [(i, (i + step) % n) for i in range(n)])


def swap_all(value, axes):
    return lax.all_to_all(value, axes, 0, 0, tiled=True)


def after(value, *earlier):
    return lax.optimization_barrier((value,) + earlier)[0]


def merge_kernel(block, codes, scales, factor, out_factor, own, squares):
    width = codes.shape[1]
    count = scales.shape[0]
    start = pl.program_id(0) * width
    group = (start + lax.broadcasted_iota(jnp.int32, (count, width), 1)) // block
    pick = (group == lax.broadcasted_iota(jnp.int32, (count, width), 0)).astype(F32)
    spread = lax.dot_general(
        scales[...],
        pick,
        (((0,), (0,)), ((), ())),
        precision=lax.Precision.HIGHEST,
        preferred_element_type=F32,
    )
    low = jnp.dot(factor[...], out_factor[...], preferred_element_type=F32)
    merged = ((codes[...].astype(F32) - 7.5) * spread + SCALE * low).astype(BF)
    own[...] = merged
    wide = merged.astype(F32)
    squares[...] = jnp.sum(wide * wide, axis=0, keepdims=True)


def merge(codes, scales, factor, out_factor):
    rows, width = codes.shape
    rank = factor.shape[1]
    count = scales.shape[0]
    steps = 4
    part = width // steps

    def columns(n):
        return pl.BlockSpec((n, part), lambda i: (0, i))

    def whole(a, b):
        return pl.BlockSpec((a, b), lambda i: (0, 0))

    def body(*refs):
        merge_kernel(width // count, *refs)

    return pl.pallas_call(
        body,
        grid=(steps,),
        in_specs=[columns(rows), whole(count, rows), whole(rows, rank), columns(rank)],
        out_specs=[columns(rows), columns(1)],
        out_shape=[
            jax.ShapeDtypeStruct((rows, width), BF),
            jax.ShapeDtypeStruct((1, width), F32),
        ],
        compiler_params=pltpu.CompilerParams(vmem_limit_bytes=60 * 1024 * 1024),
    )(codes, scales, factor, out_factor)


def tile_kernel(where, scaled, own, other, own_swap, other_swap, out, wide):
    rows = own.shape[1]
    x, zl, co = where[0], where[1], where[2]
    for source, zi, c in (
        (own, zl, co),
        (other, 1 - zl, co),
        (own_swap, zl, 1 - co),
        (other_swap, 1 - zl, 1 - co),
    ):
        row = pl.multiple_of((zi * 2 + c) * rows, rows)
        wide[pl.ds(row, rows), :] = source[0]
    tile = lax.dot_general(
        scaled[...], wide[...], (((1,), (1,)), ((), ())), preferred_element_type=F32
    ).astype(BF)
    n = scaled.shape[0] // 4
    for k, e in enumerate((0, 3, 1, 2)):
        out[lax.rem(x + e, 4), 0] = tile[k * n : (k + 1) * n, :]


def tile_of(where, scaled, weights):
    tokens, width = scaled.shape
    rows = weights[0].shape[1]
    n = tokens // 4
    weight = pl.BlockSpec((1, rows, width), lambda i, w: (i, 0, 0))
    return pl.pallas_call(
        tile_kernel,
        grid_spec=pltpu.PrefetchScalarGridSpec(
            num_scalar_prefetch=1,
            grid=(4,),
            in_specs=[pl.BlockSpec((tokens, width), lambda i, w: (0, 0))] + [weight] * 4,
            out_specs=pl.BlockSpec((4, 1, n, 4 * rows), lambda i, w: (0, i, 0, 0)),
            scratch_shapes=[pltpu.VMEM((4 * rows, width), BF)],
        ),
        out_shape=jax.ShapeDtypeStruct((4, 4, n, 4 * rows), BF),
        compiler_params=pltpu.CompilerParams(vmem_limit_bytes=40 * 1024 * 1024),
        cost_estimate=pl.CostEstimate(
            flops=2 * tokens * 16 * rows * width,
            bytes_accessed=2 * width * (tokens + 16 * rows),
            transcendentals=0,
        ),
    )(where, scaled, *weights)


def on_device(codes, scales, in_factor, out_factor, magnitude, inputs, grad, pre):
    y, x, zl, co, t = (lax.axis_index(a) for a in ("y", "x", "zl", "co", "t"))
    rows, width = codes.shape
    tokens = grad.shape[0]
    half = tokens // 2
    features = inputs.shape[1]
    part = features // SIZES["x"]
    rank = in_factor.shape[1]

    low_half, high_half = grad[:half], grad[half:]
    left_low, right_high = shift(low_half, "x", 1), shift(high_half, "x", -1)
    left_high, right_low = shift(high_half, "x", 1), shift(low_half, "x", -1)
    far_low, far_high = shift(left_low, "x", 1), shift(right_high, "x", -1)

    first = (((y * 4 + x) * 2 + zl) * 2 + co) * rows
    factor_rows = lax.dynamic_slice_in_dim(in_factor, first, rows, 0)
    own, squares = merge(codes, scales.T, factor_rows, out_factor)

    other = shift(own, "zl", 1)
    own_down, own_up = shift(own, "y", 1), shift(own, "y", -1)
    own_far = shift(own_down, "y", 1)
    other_down, other_up = shift(other, "y", 1), shift(other, "y", -1)
    other_far = shift(other_up, "y", -1)

    def in_order(blocks):
        buffer = jnp.zeros((4, rows, width), BF)
        for block, step in zip(blocks, (0, -1, 1, 2)):
            buffer = lax.dynamic_update_slice(buffer, block[None], ((y + step) % 4, 0, 0))
        return buffer

    own_rows = in_order((own, own_down, own_up, own_far))
    own_swap = shift(own_rows, "co", 1)
    other_rows = in_order((other, other_down, other_up, other_far))
    other_swap = shift(other_rows, "co", 1)

    total = squares.reshape(-1, 128)
    for axis in ("y", "co", "zl", "x"):
        if axis == "x":
            total = after(total, own_down, own_up, left_low, right_high)
        steps = [shift(total, axis, k) for k in range(1, SIZES[axis])]
        for piece in steps:
            total = total + piece
    total = after(total, left_high, right_low)
    col_norm = jnp.sqrt(total.reshape(-1) + 1e-06)
    ratio = magnitude / col_norm

    def scaled_of(g):
        return (g.astype(F32) * ratio).astype(BF)

    scaled_own = scaled_of(grad)
    scaled = jnp.zeros((4 * tokens, width), BF)
    pieces = (grad, left_low, left_high, right_low, right_high, far_low, far_high)
    for k, g in zip((0, 2, 3, 4, 5, 6, 7), pieces):
        scaled = lax.dynamic_update_slice(scaled, scaled_of(g), (k * half, 0))

    factor_cols = lax.dynamic_slice_in_dim(in_factor, t * features, features, 0)
    hidden = jnp.dot(inputs, factor_cols, preferred_element_type=F32)
    back = lax.dot_general(
        scaled_own, out_factor, (((1,), (1,)), ((), ())), preferred_element_type=F32
    )
    low = jnp.concatenate([hidden, back], axis=1).astype(BF)
    low = after(low, own_far, other_down, other_up)
    pieces = [shift(low, "t", k) for k in (1, 2, 3)]
    low = sum((p.astype(F32) for p in pieces), low.astype(F32)).astype(BF)
    hidden, back = low[:, :rank], low[:, rank:]
    in_grad = SCALE * lax.dot_general(
        back, inputs, (((0,), (0,)), ((), ())), preferred_element_type=F32
    )
    out_grad = SCALE * lax.dot_general(
        hidden, scaled_own, (((0,), (0,)), ((), ())), preferred_element_type=F32
    )
    mag_sum = jnp.sum(grad.astype(F32) * pre.astype(F32), axis=0).reshape(N_DP, -1)
    adapters = jnp.concatenate([out_grad, in_grad, mag_sum], axis=1)
    adapters = after(adapters, other_far)
    side = adapters.shape[0] // 2
    keep = lax.dynamic_slice_in_dim(adapters, co * side, side, 0)
    give = lax.dynamic_slice_in_dim(adapters, (1 - co) * side, side, 0)
    adapters = keep + shift(give, "co", 1)
    adapters = adapters + shift(adapters, "zl", 1)
    adapters = after(adapters, far_low, far_high)
    for axis, index in (("y", y), ("x", x)):
        side = adapters.shape[0] // 4
        total = lax.dynamic_slice_in_dim(adapters, index * side, side, 0)
        for k in (1, 2, 3):
            give = lax.dynamic_slice_in_dim(adapters, ((index + k) % 4) * side, side, 0)
            total = total + shift(give, axis, k)
        adapters = total
    where = jnp.stack([x, zl, co]).astype(jnp.int32)
    tile = tile_of(where, scaled, (own_rows, other_rows, own_swap, other_swap))
    adapters = after(adapters, tile)
    tile = swap_all(tile.reshape(16, tokens, part), ("x", "t"))

    for axis, index in (("x", x), ("y", y), ("co", co)):
        n = SIZES[axis]
        side = adapters.shape[0]
        total = jnp.zeros((n * side, adapters.shape[1]), F32)
        for k in range(n):
            got = shift(adapters, axis, k) if k else adapters
            total = lax.dynamic_update_slice(total, got, (((index - k) % n) * side, 0))
        adapters = total
    out_grad = adapters[:, :width]
    in_grad = adapters[:, width : width + features].T
    mag_grad = adapters[:, width + features :].reshape(-1) / col_norm

    tile = jnp.sum(tile.reshape(4, 4, tokens, part).astype(F32), axis=1).astype(BF)
    grad_in = tile.transpose(1, 0, 2).reshape(tokens, features)
    return grad_in, in_grad, out_grad, mag_grad


def solution(mesh):
    fine = Mesh(mesh.devices.reshape(4, 4, 2, 2, 4), ("y", "x", "zl", "co", "t"))
    in_specs = (
        P(DP, "t"),
        P(DP, "t"),
        P(),
        P(None, "t"),
        P("t"),
        P(DP, "t"),
        P(DP, "t"),
        P(DP, "t"),
    )
    out_specs = (P(DP, "t"), P("t", None), P(None, "t"), P("t"))
    return jax.shard_map(
        on_device, mesh=fine, in_specs=in_specs, out_specs=out_specs, check_vma=False
    )
```

time: 187 us -> 211 us (1.13)
  between operations: 14.4 us -> 1.3 us
  starting transfers between devices: 51.3 us -> 64.1 us
  waiting for transfers between devices: 75.9 us -> 87.4 us
  other arithmetic: 3.56 us -> 12.9 us
  local copies, waits for them, and re-layouts: 20.7 us -> 26.9 us
  Pallas kernels: 17.5 us -> 14.7 us
    ppermute x23 -> x41, starting transfers between devices: 31.2 us -> 60.3 us  [shift(): return lax.ppermute(value, axis, [(i, (i + step) % n) for i in range(n)])]
    all_to_all x3 -> x1, starting transfers between devices: 20.1 us -> 3.75 us  [swap_all(): return lax.all_to_all(value, axes, 0, 0, tiled=True)]
    all_to_all x3 -> x1, waiting for transfers between devices: 7.14 us -> 22.8 us  [swap_all(): return lax.all_to_all(value, axes, 0, 0, tiled=True)]
    dynamic_update_slice x0 -> x6, other arithmetic: none -> 10.3 us  [on_device(): scaled = lax.dynamic_update_slice(scaled, scaled_of(g), (k * half, 0))]
    dynamic_update_slice x8 -> x19, local copies, waits for them, and re-layouts: 9.56 us -> 17.5 us  [the longest x8 9.63 us: in_order(): lax.dynamic_update_slice(buffer, block[None], ((y + step) % 4, 0, 0))]
    pallas_call x1, Pallas kernels: 15.7 us -> 10.4 us  [tile_of(): pl.pallas_call(tile_kernel, grid_spec=pltpu.PrefetchScalarGridSpec(num_sc...]
    ppermute x23 -> x41, waiting for transfers between devices: 68.8 us -> 64.6 us  [shift(): return lax.ppermute(value, axis, [(i, (i + step) % n) for i in range(n)])]
    pallas_call x1, Pallas kernels: 1.8 us -> 4.25 us  [merge(): pl.pallas_call(body, grid=(steps,), in_specs=[columns(rows), whole(count,...]
  transfers between devices with their start and end apart: 27 -> 42, of which waited for: 12 -> 13; matrix products, arithmetic and copies ran while one was open for 11% -> 18% of each run, Pallas kernels for 8% -> 0%
where the time goes in v2:
time: 211 us; the launch traced here: 210 us
  waiting for transfers between devices  87.4 us (41%)
  starting transfers between devices  64.1 us (30%)
  local copies, waits for them, and re-layouts  26.9 us (13%)
  Pallas kernels  14.7 us (7%)
  other arithmetic  12.9 us (6%)
  matrix products  2.8 us (1%)
    ppermute x41, waiting for transfers between devices, shift(): return lax.ppermute(value, axis, [(i, (i + step) % n) for i in range(n)])  64.6 us
    ppermute x41, starting transfers between devices, shift(): return lax.ppermute(value, axis, [(i, (i + step) % n) for i in range(n)])  60.3 us
    all_to_all x1, waiting for transfers between devices, swap_all(): return lax.all_to_all(value, axes, 0, 0, tiled=True)  22.8 us
    pallas_call x1, Pallas kernels, tile_of(): pl.pallas_call(tile_kernel, grid_spec=pltpu.PrefetchScalarGridSpec(num_sc...  10.4 us
    dynamic_update_slice x6, other arithmetic, on_device(): scaled = lax.dynamic_update_slice(scaled, scaled_of(g), (k * half, 0))  10.3 us
    dynamic_update_slice x8, local copies, waits for them, and re-layouts, in_order(): lax.dynamic_update_slice(buffer, block[None], ((y + step) % 4, 0, 0))  9.63 us
    dynamic_update_slice x10, local copies, waits for them, and re-layouts, on_device(): total = lax.dynamic_update_slice(total, got, ((index - k) % n * side, 0))  5.02 us
    pallas_call x1, Pallas kernels, merge(): pl.pallas_call(body, grid=(steps,), in_specs=[columns(rows), whole(count,...  4.25 us
  transfers between devices with their start and end apart: 42, of which 13 were waited for; matrix products, arithmetic and copies ran while one was open for 18% of the time, Pallas kernels for 0%

profile of v2, /device:TPU:8, one launch (start us, length us, event | category | flops | bytes accessed | tf_op | source)
XLA Modules:
  0.0 210.0 jit_solution(4793974215200233692)
XLA Ops:
  2.5 4.3 %shard_map.111 = (bf16[64,3584]{1,0:T(8,128)(2,1)}, f32[1,3584]{1,0:T(1,128)}) custom-call(s32[64,3584]{1,0:T(8,128)} %refs_0_.1, f32[56,64]{1,0:T(8,128)} %bitcast.46, bf16[64,64]{1,0:T(8,128)(2,1)} %copy.17.refs_2_, bf16[64,3584]{1,0:T(8,128)(2,1)} %refs_3_.1), custom_call_target="tpu_custom_call" | custom-call | tf_op jit(solution)/shard_map/pallas_call | solution.py:65
  9.1 2.7 %collective-permute-start.1 = (f32[28,128]{1,0:T(8,128)S(1)}, f32[28,128]{1,0:T(8,128)S(1)}, u32[]{:S(2)}, u32[]{:S(2)}) collective-permute-start(f32[28,128]{1,0:T(8,128)S(1)} %bitcast.44), channel_id=1, source_target_pairs={{0,128},{64,192},{128,0},{192,64},{1,129},{65,193},{129,1},{193,65... | collective-permute-start | bytes 43016 | tf_op jit(solution)/shard_map/ppermute | solution.py:18
  17.9 1.9 collective-permute-start.17
  19.8 2.7 %collective-permute-start.8 = (bf16[96,3584]{1,0:T(8,128)(2,1)}, bf16[96,3584]{1,0:T(8,128)(2,1)}, u32[]{:S(2)}, u32[]{:S(2)}) collective-permute-start(bf16[96,3584]{1,0:T(8,128)(2,1)} %get-tuple-element.22), channel_id=1, source_target_pairs={{0,48},{16,0},{32,16},{48,32},{1,49},{17,1},{33,17},{49,33},{2,50}... | collective-permute-start | bytes 2064392 | tf_op jit(solution)/shard_map/ppermute | solution.py:18
  24.2 5.0 %collective-permute-done.4 = f32[28,128]{1,0:T(8,128)S(1)} collective-permute-done((f32[28,128]{1,0:T(8,128)S(1)}, f32[28,128]{1,0:T(8,128)S(1)}, u32[]{:S(2)}, u32[]{:S(2)}) %collective-permute-start.4) | collective-permute-done | bytes 14368 | tf_op jit(solution)/shard_map/ppermute | solution.py:18
  33.7 1.8 collective-permute-start.13
  35.5 1.8 bitcast_dynamic-update-slice_fusion.6
  37.4 23.5 %collective-permute-done.7 = bf16[96,3584]{1,0:T(8,128)(2,1)} collective-permute-done((bf16[96,3584]{1,0:T(8,128)(2,1)}, bf16[96,3584]{1,0:T(8,128)(2,1)}, u32[]{:S(2)}, u32[]{:S(2)}) %collective-permute-start.7) | collective-permute-done | bytes 688160 | tf_op jit(solution)/shard_map/ppermute | solution.py:18
  64.5 1.8 bitcast_dynamic-update-slice_fusion.5
  66.3 2.6 %collective-permute-start.19 = (bf16[64,3584]{1,0:T(8,128)(2,1)}, bf16[64,3584]{1,0:T(8,128)(2,1)}, u32[]{:S(2)}, u32[]{:S(2)}) collective-permute-start(bf16[64,3584]{1,0:T(8,128)(2,1)} %collective-permute-done.17), channel_id=1, source_target_pairs={{0,192},{64,0},{128,64},{192,128},{1,193},{65,1},{129,65},{193,129... | collective-permute-start | bytes 1376264 | tf_op jit(solution)/shard_map/ppermute | solution.py:18
  69.7 2.8 %collective-permute-start.15 = (bf16[96,3584]{1,0:T(8,128)(2,1)}, bf16[96,3584]{1,0:T(8,128)(2,1)}, u32[]{:S(2)}, u32[]{:S(2)}) collective-permute-start(bf16[96,3584]{1,0:T(8,128)(2,1)} %collective-permute-done.8), channel_id=1, source_target_pairs={{0,48},{16,0},{32,16},{48,32},{1,49},{17,1},{33,17},{49,33},{2,50}... | collective-permute-start | bytes 2064392 | tf_op jit(solution)/shard_map/ppermute | solution.py:18
  73.1 2.9 %dynamic_update_slice.75 = bf16[768,3584]{1,0:T(8,128)(2,1)} pad(bf16[192,3584]{1,0:T(8,128)(2,1)S(1)} %get-tuple-element.21, bf16[]{:T(256)} %constant.148.clone.1), padding=0_576x0_0 | pad | bytes 6881282 | tf_op jit(solution)/shard_map/dynamic_update_slice | solution.py:174
  75.9 2.1 fusion.3
  80.0 2.1 fusion.6
  82.1 2.0 convolution_convert_fusion
  84.2 3.0 %collective-permute-done.18 = bf16[64,3584]{1,0:T(8,128)(2,1)} collective-permute-done((bf16[64,3584]{1,0:T(8,128)(2,1)}, bf16[64,3584]{1,0:T(8,128)(2,1)}, u32[]{:S(2)}, u32[]{:S(2)}) %collective-permute-start.18) | collective-permute-done | bytes 458784 | tf_op jit(solution)/shard_map/ppermute | solution.py:18
  87.2 3.3 %collective-permute-start.23 = (bf16[192,128]{0,1:T(8,128)(2,1)S(1)}, bf16[192,128]{0,1:T(8,128)(2,1)S(1)}, u32[]{:S(2)}, u32[]{:S(2)}) collective-permute-start(bf16[192,128]{0,1:T(8,128)(2,1)S(1)} %pad_maximum_fusion.1), channel_id=1, source_target_pairs={{0,1},{1,2},{2,3},{3,0},{4,5},{5,6},{6,7},{7,4},{8,9},{9,10},{10,1... | collective-permute-start | bytes 147464 | tf_op jit(solution)/shard_map/ppermute | solution.py:18
  90.5 4.8 %collective-permute-start.24 = (bf16[192,128]{0,1:T(8,128)(2,1)S(1)}, bf16[192,128]{0,1:T(8,128)(2,1)S(1)}, u32[]{:S(2)}, u32[]{:S(2)}) collective-permute-start(bf16[192,128]{0,1:T(8,128)(2,1)S(1)} %pad_maximum_fusion.1), channel_id=1, source_target_pairs={{0,2},{1,3},{2,0},{3,1},{4,6},{5,7},{6,4},{7,5},{8,10},{9,11},{10,... | collective-permute-start | bytes 147464 | tf_op jit(solution)/shard_map/ppermute | solution.py:18
  95.4 2.7 %collective-permute-start.25 = (bf16[192,128]{0,1:T(8,128)(2,1)S(1)}, bf16[192,128]{0,1:T(8,128)(2,1)S(1)}, u32[]{:S(2)}, u32[]{:S(2)}) collective-permute-start(bf16[192,128]{0,1:T(8,128)(2,1)S(1)} %pad_maximum_fusion.1), channel_id=1, source_target_pairs={{0,3},{1,0},{2,1},{3,2},{4,7},{5,4},{6,5},{7,6},{8,11},{9,8},{10,9... | collective-permute-start | bytes 147464 | tf_op jit(solution)/shard_map/ppermute | solution.py:18
  99.1 1.8 bitcast_dynamic-update-slice_fusion.4.own
  100.9 2.1 %collective-permute-start.20 = (bf16[64,3584]{1,0:T(8,128)(2,1)}, bf16[64,3584]{1,0:T(8,128)(2,1)S(1)}, u32[]{:S(2)}, u32[]{:S(2)}) collective-permute-start(bf16[64,3584]{1,0:T(8,128)(2,1)} %collective-permute-done.19), channel_id=1, source_target_pairs={{0,192},{64,0},{128,64},{192,128},{1,193},{65,1},{129,65},{193,129... | collective-permute-start | bytes 1376264 | tf_op jit(solution)/shard_map/ppermute | solution.py:18
  103.8 10.3 %collective-permute-done.20 = bf16[64,3584]{1,0:T(8,128)(2,1)S(1)} collective-permute-done((bf16[64,3584]{1,0:T(8,128)(2,1)}, bf16[64,3584]{1,0:T(8,128)(2,1)S(1)}, u32[]{:S(2)}, u32[]{:S(2)}) %collective-permute-start.20) | collective-permute-done | bytes 458784 | tf_op jit(solution)/shard_map/ppermute | solution.py:18
  117.5 14.6 %collective-permute-done.27 = f32[32,4664]{1,0:T(8,128)S(1)} collective-permute-done((f32[32,4664]{1,0:T(8,128)S(1)}, f32[32,4664]{1,0:T(8,128)S(1)}, u32[]{:S(2)}, u32[]{:S(2)}) %collective-permute-start.27) | collective-permute-done | bytes 597024 | tf_op jit(solution)/shard_map/ppermute | solution.py:18
  132.6 3.8 %collective-permute-start.29 = (f32[8,4664]{1,0:T(8,128)S(1)}, f32[8,4664]{1,0:T(8,128)S(1)}, u32[]{:S(2)}, u32[]{:S(2)}) collective-permute-start(f32[8,4664]{1,0:T(8,128)S(1)} %get-tuple-element.26), channel_id=1, source_target_pairs={{0,128},{64,192},{128,0},{192,64},{1,129},{65,193},{129,1},{193,65... | collective-permute-start | bytes 447752 | tf_op jit(solution)/shard_map/ppermute | solution.py:18
  137.6 2.1 %fusion.7 = bf16[768,3584]{1,0:T(8,128)(2,1)} fusion(bf16[768,3584]{1,0:T(8,128)(2,1)} %fusion.6, bf16[96,3584]{1,0:T(8,128)(2,1)} %collective-permute-done.14, f32[3584]{0:T(1024)S(1)} %bitcast_divide_fusion.1), kind=kLoop, calls=%fused_computation.21 | loop fusion | flops 1032192 | bytes 1390592 | tf_op jit(solution)/shard_map/dynamic_update_slice | solution.py:174
  143.6 3.2 %collective-permute-start.32 = (f32[2,4664]{1,0:T(2,128)S(1)}, f32[2,4664]{1,0:T(2,128)S(1)}, u32[]{:S(2)}, u32[]{:S(2)}) collective-permute-start(f32[2,4664]{1,0:T(2,128)S(1)} %get-tuple-element.29), channel_id=1, source_target_pairs={{0,32},{16,48},{32,0},{48,16},{1,33},{17,49},{33,1},{49,17},{2,34}... | collective-permute-start | bytes 111944 | tf_op jit(solution)/shard_map/ppermute | solution.py:18
  147.3 2.1 fusion.8.scaled
  150.8 10.4 %shard_map.112 = bf16[4,4,192,256]{3,2,1,0:T(8,128)(2,1)S(1)} custom-call(s32[3]{0:T(128)S(1)} %pad_add_fusion.where, bf16[768,3584]{1,0:T(8,128)(2,1)} %fusion.8.scaled, bf16[4,64,3584]{2,1,0:T(8,128)(2,1)} %bitcast_dynamic-update-slice_fusion.4.own, bf16[4,64,3584]{2,1,0:T(8,128)(2,1)S(1)} %bitcast_dynamic-update-slice_fusion.other, ...), custom_call_target="tpu_custom_call" | custom-call | flops 5637144576 | bytes 12845056 | tf_op jit(solution)/shard_map/pallas_call | solution.py:102
  162.7 2.9 %collective-permute-start.35 = (f32[2,4664]{1,0:T(2,128)S(1)}, f32[2,4664]{1,0:T(2,128)S(1)}, u32[]{:S(2)}, u32[]{:S(2)}) collective-permute-start(f32[2,4664]{1,0:T(2,128)S(1)} %add_add_fusion.1), channel_id=1, source_target_pairs={{0,32},{16,48},{32,0},{48,16},{1,33},{17,49},{33,1},{49,17},{2,34}... | collective-permute-start | bytes 111944 | tf_op jit(solution)/shard_map/ppermute | solution.py:18
  166.6 3.7 %all-to-all-start = ((bf16[16,192,256]{2,1,0:T(8,128)(2,1)}), bf16[16,192,256]{2,1,0:T(8,128)(2,1)S(1)}, u32[]{:S(2)}, u32[]{:S(2)}) async-start(bf16[16,192,256]{2,1,0:T(8,128)(2,1)} %bitcast.40), calls=%async_computation | async-start | bytes 3145728 | tf_op jit(solution)/shard_map/all_to_all | solution.py:22
  171.2 3.3 %collective-permute-start.38 = (f32[8,4664]{1,0:T(8,128)S(1)}, f32[8,4664]{1,0:T(8,128)S(1)}, u32[]{:S(2)}, u32[]{:S(2)}) collective-permute-start(f32[8,4664]{1,0:T(8,128)S(1)} %constant_dynamic-update-slice_fusion.6), channel_id=1, source_target_pairs={{0,128},{64,192},{128,0},{192,64},{1,129},{65,193},{129,1},{193,65... | collective-permute-start | bytes 447752 | tf_op jit(solution)/shard_map/ppermute | solution.py:18
  186.2 22.8 %all-to-all-done = bf16[16,192,256]{2,1,0:T(8,128)(2,1)S(1)} async-done(((bf16[16,192,256]{2,1,0:T(8,128)(2,1)}), bf16[16,192,256]{2,1,0:T(8,128)(2,1)S(1)}, u32[]{:S(2)}, u32[]{:S(2)}) %all-to-all-start) | async-done | bytes 1572896 | tf_op jit(solution)/shard_map/all_to_all | solution.py:22
  (139 shorter events, 51.8 us)
Async XLA Ops:
  7.5 10.4 %collective-permute-start = (f32[28,128]{1,0:T(8,128)S(1)}, f32[28,128]{1,0:T(8,128)S(1)}, u32[]{:S(2)}, u32[]{:S(2)}) collective-permute-start(f32[28,128]{1,0:T(8,128)S(1)} %bitcast.43), channel_id=1, source_target_pairs={{0,64},{64,128},{128,192},{192,0},{1,65},{65,129},{129,193},{193,1... | collective-permute-start | bytes 43016 | tf_op jit(solution)/shard_map/ppermute | solution.py:18
  9.1 10.7 %collective-permute-start.1 = (f32[28,128]{1,0:T(8,128)S(1)}, f32[28,128]{1,0:T(8,128)S(1)}, u32[]{:S(2)}, u32[]{:S(2)}) collective-permute-start(f32[28,128]{1,0:T(8,128)S(1)} %bitcast.44), channel_id=1, source_target_pairs={{0,128},{64,192},{128,0},{192,64},{1,129},{65,193},{129,1},{193,65... | collective-permute-start | bytes 43016 | tf_op jit(solution)/shard_map/ppermute | solution.py:18
  11.8 10.7 %collective-permute-start.2 = (f32[28,128]{1,0:T(8,128)S(1)}, f32[28,128]{1,0:T(8,128)S(1)}, u32[]{:S(2)}, u32[]{:S(2)}) collective-permute-start(f32[28,128]{1,0:T(8,128)S(1)} %bitcast.45), channel_id=1, source_target_pairs={{0,192},{64,0},{128,64},{192,128},{1,193},{65,1},{129,65},{193,129... | collective-permute-start | bytes 43016 | tf_op jit(solution)/shard_map/ppermute | solution.py:18
  12.5 21.2 %collective-permute-start.5 = (bf16[64,3584]{1,0:T(8,128)(2,1)}, bf16[64,3584]{1,0:T(8,128)(2,1)}, u32[]{:S(2)}, u32[]{:S(2)}) collective-permute-start(bf16[64,3584]{1,0:T(8,128)(2,1)} %get-tuple-element.13), channel_id=1, source_target_pairs={{0,64},{64,128},{128,192},{192,0},{1,65},{65,129},{129,193},{193,1... | collective-permute-start | bytes 1376264 | tf_op jit(solution)/shard_map/ppermute | solution.py:18
  13.8 23.5 %collective-permute-start.6 = (bf16[64,3584]{1,0:T(8,128)(2,1)}, bf16[64,3584]{1,0:T(8,128)(2,1)}, u32[]{:S(2)}, u32[]{:S(2)}) collective-permute-start(bf16[64,3584]{1,0:T(8,128)(2,1)} %get-tuple-element.13), channel_id=1, source_target_pairs={{0,192},{64,0},{128,64},{192,128},{1,193},{65,1},{129,65},{193,129... | collective-permute-start | bytes 1376264 | tf_op jit(solution)/shard_map/ppermute | solution.py:18
  17.9 12.9 %collective-permute-start.17 = (bf16[64,3584]{1,0:T(8,128)(2,1)S(1)}, bf16[64,3584]{1,0:T(8,128)(2,1)}, u32[]{:S(2)}, u32[]{:S(2)}) collective-permute-start(bf16[64,3584]{1,0:T(8,128)(2,1)S(1)} %copy-done.9), channel_id=1, source_target_pairs={{0,8},{8,0},{1,9},{9,1},{2,10},{10,2},{3,11},{11,3},{4,12},{12,4},... | collective-permute-start | bytes 1376264 | tf_op jit(solution)/shard_map/ppermute | solution.py:18
  19.8 41.1 %collective-permute-start.8 = (bf16[96,3584]{1,0:T(8,128)(2,1)}, bf16[96,3584]{1,0:T(8,128)(2,1)}, u32[]{:S(2)}, u32[]{:S(2)}) collective-permute-start(bf16[96,3584]{1,0:T(8,128)(2,1)} %get-tuple-element.22), channel_id=1, source_target_pairs={{0,48},{16,0},{32,16},{48,32},{1,49},{17,1},{33,17},{49,33},{2,50}... | collective-permute-start | bytes 2064392 | tf_op jit(solution)/shard_map/ppermute | solution.py:18
  29.2 39.9 %collective-permute-start.12 = (bf16[96,3584]{1,0:T(8,128)(2,1)}, bf16[96,3584]{1,0:T(8,128)(2,1)S(1)}, u32[]{:S(2)}, u32[]{:S(2)}) collective-permute-start(bf16[96,3584]{1,0:T(8,128)(2,1)} %get-tuple-element.22), channel_id=1, source_target_pairs={{0,16},{16,32},{32,48},{48,0},{1,17},{17,33},{33,49},{49,1},{2,18}... | collective-permute-start | bytes 2064392 | tf_op jit(solution)/shard_map/ppermute | solution.py:18
  30.8 30.1 %collective-permute-start.7 = (bf16[96,3584]{1,0:T(8,128)(2,1)}, bf16[96,3584]{1,0:T(8,128)(2,1)}, u32[]{:S(2)}, u32[]{:S(2)}) collective-permute-start(bf16[96,3584]{1,0:T(8,128)(2,1)} %get-tuple-element.23), channel_id=1, source_target_pairs={{0,16},{16,32},{32,48},{48,0},{1,17},{17,33},{33,49},{49,1},{2,18}... | collective-permute-start | bytes 2064392 | tf_op jit(solution)/shard_map/ppermute | solution.py:18
  33.7 36.0 %collective-permute-start.13 = (bf16[96,3584]{1,0:T(8,128)(2,1)}, bf16[96,3584]{1,0:T(8,128)(2,1)S(1)}, u32[]{:S(2)}, u32[]{:S(2)}) collective-permute-start(bf16[96,3584]{1,0:T(8,128)(2,1)} %get-tuple-element.23), channel_id=1, source_target_pairs={{0,48},{16,0},{32,16},{48,32},{1,49},{17,1},{33,17},{49,33},{2,50}... | collective-permute-start | bytes 2064392 | tf_op jit(solution)/shard_map/ppermute | solution.py:18
  62.5 6.4 %collective-permute-start.11 = (f32[28,128]{1,0:T(8,128)S(1)}, f32[28,128]{1,0:T(8,128)S(1)}, u32[]{:S(2)}, u32[]{:S(2)}) collective-permute-start(f32[28,128]{1,0:T(8,128)S(1)} %add.255), channel_id=1, source_target_pairs={{0,48},{16,0},{32,16},{48,32},{1,49},{17,1},{33,17},{49,33},{2,50}... | collective-permute-start | bytes 43016 | tf_op jit(solution)/shard_map/ppermute | solution.py:18
  66.3 17.8 %collective-permute-start.19 = (bf16[64,3584]{1,0:T(8,128)(2,1)}, bf16[64,3584]{1,0:T(8,128)(2,1)}, u32[]{:S(2)}, u32[]{:S(2)}) collective-permute-start(bf16[64,3584]{1,0:T(8,128)(2,1)} %collective-permute-done.17), channel_id=1, source_target_pairs={{0,192},{64,0},{128,64},{192,128},{1,193},{65,1},{129,65},{193,129... | collective-permute-start | bytes 1376264 | tf_op jit(solution)/shard_map/ppermute | solution.py:18
  68.9 15.3 %collective-permute-start.16 = (bf16[64,3584]{1,0:T(8,128)(2,1)}, bf16[64,3584]{1,0:T(8,128)(2,1)}, u32[]{:S(2)}, u32[]{:S(2)}) collective-permute-start(bf16[64,3584]{1,0:T(8,128)(2,1)} %collective-permute-done.5), channel_id=1, source_target_pairs={{0,64},{64,128},{128,192},{192,0},{1,65},{65,129},{129,193},{193,1... | collective-permute-start | bytes 1376264 | tf_op jit(solution)/shard_map/ppermute | solution.py:18
  68.9 18.3 %collective-permute-start.18 = (bf16[64,3584]{1,0:T(8,128)(2,1)}, bf16[64,3584]{1,0:T(8,128)(2,1)}, u32[]{:S(2)}, u32[]{:S(2)}) collective-permute-start(bf16[64,3584]{1,0:T(8,128)(2,1)} %collective-permute-done.17), channel_id=1, source_target_pairs={{0,64},{64,128},{128,192},{192,0},{1,65},{65,129},{129,193},{193,1... | collective-permute-start | bytes 1376264 | tf_op jit(solution)/shard_map/ppermute | solution.py:18
  69.1 63.0 %collective-permute-start.14 = (bf16[96,3584]{1,0:T(8,128)(2,1)}, bf16[96,3584]{1,0:T(8,128)(2,1)}, u32[]{:S(2)}, u32[]{:S(2)}) collective-permute-start(bf16[96,3584]{1,0:T(8,128)(2,1)} %collective-permute-done.7), channel_id=1, source_target_pairs={{0,16},{16,32},{32,48},{48,0},{1,17},{17,33},{33,49},{49,1},{2,18}... | collective-permute-start | bytes 2064392 | tf_op jit(solution)/shard_map/ppermute | solution.py:18
  69.7 62.5 %collective-permute-start.15 = (bf16[96,3584]{1,0:T(8,128)(2,1)}, bf16[96,3584]{1,0:T(8,128)(2,1)}, u32[]{:S(2)}, u32[]{:S(2)}) collective-permute-start(bf16[96,3584]{1,0:T(8,128)(2,1)} %collective-permute-done.8), channel_id=1, source_target_pairs={{0,48},{16,0},{32,16},{48,32},{1,49},{17,1},{33,17},{49,33},{2,50}... | collective-permute-start | bytes 2064392 | tf_op jit(solution)/shard_map/ppermute | solution.py:18
  87.2 13.7 %collective-permute-start.23 = (bf16[192,128]{0,1:T(8,128)(2,1)S(1)}, bf16[192,128]{0,1:T(8,128)(2,1)S(1)}, u32[]{:S(2)}, u32[]{:S(2)}) collective-permute-start(bf16[192,128]{0,1:T(8,128)(2,1)S(1)} %pad_maximum_fusion.1), channel_id=1, source_target_pairs={{0,1},{1,2},{2,3},{3,0},{4,5},{5,6},{6,7},{7,4},{8,9},{9,10},{10,1... | collective-permute-start | bytes 147464 | tf_op jit(solution)/shard_map/ppermute | solution.py:18
  90.5 10.4 %collective-permute-start.24 = (bf16[192,128]{0,1:T(8,128)(2,1)S(1)}, bf16[192,128]{0,1:T(8,128)(2,1)S(1)}, u32[]{:S(2)}, u32[]{:S(2)}) collective-permute-start(bf16[192,128]{0,1:T(8,128)(2,1)S(1)} %pad_maximum_fusion.1), channel_id=1, source_target_pairs={{0,2},{1,3},{2,0},{3,1},{4,6},{5,7},{6,4},{7,5},{8,10},{9,11},{10,... | collective-permute-start | bytes 147464 | tf_op jit(solution)/shard_map/ppermute | solution.py:18
  95.4 7.7 %collective-permute-start.25 = (bf16[192,128]{0,1:T(8,128)(2,1)S(1)}, bf16[192,128]{0,1:T(8,128)(2,1)S(1)}, u32[]{:S(2)}, u32[]{:S(2)}) collective-permute-start(bf16[192,128]{0,1:T(8,128)(2,1)S(1)} %pad_maximum_fusion.1), channel_id=1, source_target_pairs={{0,3},{1,0},{2,1},{3,2},{4,7},{5,4},{6,5},{7,6},{8,11},{9,8},{10,9... | collective-permute-start | bytes 147464 | tf_op jit(solution)/shard_map/ppermute | solution.py:18
  100.9 49.9 %collective-permute-start.21 = (bf16[4,64,3584]{2,1,0:T(8,128)(2,1)}, bf16[4,64,3584]{2,1,0:T(8,128)(2,1)S(1)}, u32[]{:S(2)}, u32[]{:S(2)}) collective-permute-start(bf16[4,64,3584]{2,1,0:T(8,128)(2,1)} %bitcast_dynamic-update-slice_fusion.4.own), channel_id=1, source_target_pairs={{0,4},{4,0},{1,5},{5,1},{2,6},{6,2},{3,7},{7,3},{8,12},{12,8},{9,1... | collective-permute-start | bytes 5505032 | tf_op jit(solution)/shard_map/ppermute | solution.py:18
  100.9 13.2 %collective-permute-start.20 = (bf16[64,3584]{1,0:T(8,128)(2,1)}, bf16[64,3584]{1,0:T(8,128)(2,1)S(1)}, u32[]{:S(2)}, u32[]{:S(2)}) collective-permute-start(bf16[64,3584]{1,0:T(8,128)(2,1)} %collective-permute-done.19), channel_id=1, source_target_pairs={{0,192},{64,0},{128,64},{192,128},{1,193},{65,1},{129,65},{193,129... | collective-permute-start | bytes 1376264 | tf_op jit(solution)/shard_map/ppermute | solution.py:18
  116.3 15.8 %collective-permute-start.27 = (f32[32,4664]{1,0:T(8,128)S(1)}, f32[32,4664]{1,0:T(8,128)S(1)}, u32[]{:S(2)}, u32[]{:S(2)}) collective-permute-start(f32[32,4664]{1,0:T(8,128)S(1)} %dynamic-slice_add_fusion), channel_id=1, source_target_pairs={{0,8},{8,0},{1,9},{9,1},{2,10},{10,2},{3,11},{11,3},{4,12},{12,4},... | collective-permute-start | bytes 1790984 | tf_op jit(solution)/shard_map/ppermute | solution.py:18
  117.4 33.4 %collective-permute-start.22 = (bf16[4,64,3584]{2,1,0:T(8,128)(2,1)S(1)}, bf16[4,64,3584]{2,1,0:T(8,128)(2,1)S(1)}, u32[]{:S(2)}, u32[]{:S(2)}) collective-permute-start(bf16[4,64,3584]{2,1,0:T(8,128)(2,1)S(1)} %bitcast_dynamic-update-slice_fusion.other), channel_id=1, source_target_pairs={{0,4},{4,0},{1,5},{5,1},{2,6},{6,2},{3,7},{7,3},{8,12},{12,8},{9,1... | collective-permute-start | bytes 5505032 | tf_op jit(solution)/shard_map/ppermute | solution.py:18
  132.2 7.4 %collective-permute-start.28 = (f32[8,4664]{1,0:T(8,128)S(1)}, f32[8,4664]{1,0:T(8,128)S(1)}, u32[]{:S(2)}, u32[]{:S(2)}) collective-permute-start(f32[8,4664]{1,0:T(8,128)S(1)} %get-tuple-element.24), channel_id=1, source_target_pairs={{0,64},{64,128},{128,192},{192,0},{1,65},{65,129},{129,193},{193,1... | collective-permute-start | bytes 447752 | tf_op jit(solution)/shard_map/ppermute | solution.py:18
  132.6 8.6 %collective-permute-start.29 = (f32[8,4664]{1,0:T(8,128)S(1)}, f32[8,4664]{1,0:T(8,128)S(1)}, u32[]{:S(2)}, u32[]{:S(2)}) collective-permute-start(f32[8,4664]{1,0:T(8,128)S(1)} %get-tuple-element.26), channel_id=1, source_target_pairs={{0,128},{64,192},{128,0},{192,64},{1,129},{65,193},{129,1},{193,65... | collective-permute-start | bytes 447752 | tf_op jit(solution)/shard_map/ppermute | solution.py:18
  136.4 6.4 %collective-permute-start.30 = (f32[8,4664]{1,0:T(8,128)S(1)}, f32[8,4664]{1,0:T(8,128)S(1)}, u32[]{:S(2)}, u32[]{:S(2)}) collective-permute-start(f32[8,4664]{1,0:T(8,128)S(1)} %get-tuple-element.25), channel_id=1, source_target_pairs={{0,192},{64,0},{128,64},{192,128},{1,193},{65,1},{129,65},{193,129... | collective-permute-start | bytes 447752 | tf_op jit(solution)/shard_map/ppermute | solution.py:18
  142.9 6.5 %collective-permute-start.31 = (f32[2,4664]{1,0:T(2,128)S(1)}, f32[2,4664]{1,0:T(2,128)S(1)}, u32[]{:S(2)}, u32[]{:S(2)}) collective-permute-start(f32[2,4664]{1,0:T(2,128)S(1)} %get-tuple-element.27), channel_id=1, source_target_pairs={{0,16},{16,32},{32,48},{48,0},{1,17},{17,33},{33,49},{49,1},{2,18}... | collective-permute-start | bytes 111944 | tf_op jit(solution)/shard_map/ppermute | solution.py:18
  162.4 8.0 %collective-permute-start.34 = (f32[2,4664]{1,0:T(2,128)S(1)}, f32[2,4664]{1,0:T(2,128)S(1)}, u32[]{:S(2)}, u32[]{:S(2)}) collective-permute-start(f32[2,4664]{1,0:T(2,128)S(1)} %add_add_fusion.1), channel_id=1, source_target_pairs={{0,16},{16,32},{32,48},{48,0},{1,17},{17,33},{33,49},{49,1},{2,18}... | collective-permute-start | bytes 111944 | tf_op jit(solution)/shard_map/ppermute | solution.py:18
  162.7 7.7 %collective-permute-start.35 = (f32[2,4664]{1,0:T(2,128)S(1)}, f32[2,4664]{1,0:T(2,128)S(1)}, u32[]{:S(2)}, u32[]{:S(2)}) collective-permute-start(f32[2,4664]{1,0:T(2,128)S(1)} %add_add_fusion.1), channel_id=1, source_target_pairs={{0,32},{16,48},{32,0},{48,16},{1,33},{17,49},{33,1},{49,17},{2,34}... | collective-permute-start | bytes 111944 | tf_op jit(solution)/shard_map/ppermute | solution.py:18
  166.6 42.4 %all-to-all-start = ((bf16[16,192,256]{2,1,0:T(8,128)(2,1)}), bf16[16,192,256]{2,1,0:T(8,128)(2,1)S(1)}, u32[]{:S(2)}, u32[]{:S(2)}) async-start(bf16[16,192,256]{2,1,0:T(8,128)(2,1)} %bitcast.40), calls=%async_computation | async-start | bytes 3145728 | tf_op jit(solution)/shard_map/all_to_all | solution.py:22
  170.5 7.2 %collective-permute-start.37 = (f32[8,4664]{1,0:T(8,128)S(1)}, f32[8,4664]{1,0:T(8,128)S(1)}, u32[]{:S(2)}, u32[]{:S(2)}) collective-permute-start(f32[8,4664]{1,0:T(8,128)S(1)} %constant_dynamic-update-slice_fusion.6), channel_id=1, source_target_pairs={{0,64},{64,128},{128,192},{192,0},{1,65},{65,129},{129,193},{193,1... | collective-permute-start | bytes 447752 | tf_op jit(solution)/shard_map/ppermute | solution.py:18
  171.2 7.2 %collective-permute-start.38 = (f32[8,4664]{1,0:T(8,128)S(1)}, f32[8,4664]{1,0:T(8,128)S(1)}, u32[]{:S(2)}, u32[]{:S(2)}) collective-permute-start(f32[8,4664]{1,0:T(8,128)S(1)} %constant_dynamic-update-slice_fusion.6), channel_id=1, source_target_pairs={{0,128},{64,192},{128,0},{192,64},{1,129},{65,193},{129,1},{193,65... | collective-permute-start | bytes 447752 | tf_op jit(solution)/shard_map/ppermute | solution.py:18
  (21 other events, 215.3 us)

commit v3 on v2

--- a/solution.py
+++ b/solution.py
@@ -75,9 +75,20 @@
     )(codes, scales, factor, out_factor)
 
 
-def tile_kernel(where, scaled, own, other, own_swap, other_swap, out, wide):
+def tile_kernel(
+    where, scaled, far_low, far_high, ratio, own, other, own_swap, other_swap, out, wide, far
+):
     rows = own.shape[1]
+    half = far_low.shape[0]
     x, zl, co = where[0], where[1], where[2]
+
+    @pl.when(pl.program_id(0) == 0)
+    def _():
+        for source, base in ((far_low, 0), (far_high, half)):
+            for r in range(0, half, 16):
+                value = source[r : r + 16, :].astype(F32) * ratio[...]
+                far[base + r : base + r + 16, :] = value.astype(BF)
+
     for source, zi, c in (
         (own, zl, co),
         (other, 1 - zl, co),
@@ -86,36 +97,48 @@
     ):
         row = pl.multiple_of((zi * 2 + c) * rows, rows)
         wide[pl.ds(row, rows), :] = source[0]
-    tile = lax.dot_general(
-        scaled[...], wide[...], (((1,), (1,)), ((), ())), preferred_element_type=F32
-    ).astype(BF)
-    n = scaled.shape[0] // 4
-    for k, e in enumerate((0, 3, 1, 2)):
+
+    def product(value):
+        return lax.dot_general(
+            value, wide[...], (((1,), (1,)), ((), ())), preferred_element_type=F32
+        ).astype(BF)
+
+    n = 2 * half
+    tile = product(scaled[...])
+    for k, e in enumerate((0, 3, 1)):
         out[lax.rem(x + e, 4), 0] = tile[k * n : (k + 1) * n, :]
-
-
-def tile_of(where, scaled, weights):
+    out[lax.rem(x + 2, 4), 0] = product(far[...])
+
+
+def tile_of(where, scaled, far_low, far_high, ratio, weights):
     tokens, width = scaled.shape
+    half = far_low.shape[0]
+    n = 2 * half
     rows = weights[0].shape[1]
-    n = tokens // 4
+
+    def whole(shape):
+        return pl.BlockSpec(shape, lambda i, w: (0, 0))
+
     weight = pl.BlockSpec((1, rows, width), lambda i, w: (i, 0, 0))
     return pl.pallas_call(
         tile_kernel,
         grid_spec=pltpu.PrefetchScalarGridSpec(
             num_scalar_prefetch=1,
             grid=(4,),
-            in_specs=[pl.BlockSpec((tokens, width), lambda i, w: (0, 0))] + [weight] * 4,
+            in_specs=[whole((tokens, width)), whole((half, width)), whole((half, width))]
+            + [whole((1, width))]
+            + [weight] * 4,
             out_specs=pl.BlockSpec((4, 1, n, 4 * rows), lambda i, w: (0, i, 0, 0)),
-            scratch_shapes=[pltpu.VMEM((4 * rows, width), BF)],
+            scratch_shapes=[pltpu.VMEM((4 * rows, width), BF), pltpu.VMEM((n, width), BF)],
         ),
         out_shape=jax.ShapeDtypeStruct((4, 4, n, 4 * rows), BF),
         compiler_params=pltpu.CompilerParams(vmem_limit_bytes=40 * 1024 * 1024),
         cost_estimate=pl.CostEstimate(
-            flops=2 * tokens * 16 * rows * width,
-            bytes_accessed=2 * width * (tokens + 16 * rows),
+            flops=8 * n * 16 * rows * width,
+            bytes_accessed=2 * width * (4 * n + 16 * rows),
             transcendentals=0,
         ),
-    )(where, scaled, *weights)
+    )(where, scaled, far_low, far_high, ratio, *weights)
 
 
 def on_device(codes, scales, in_factor, out_factor, magnitude, inputs, grad, pre):
@@ -129,7 +152,6 @@
 
     low_half, high_half = grad[:half], grad[half:]
     left_low, right_high = shift(low_half, "x", 1), shift(high_half, "x", -1)
-    left_high, right_low = shift(high_half, "x", 1), shift(low_half, "x", -1)
     far_low, far_high = shift(left_low, "x", 1), shift(right_high, "x", -1)
 
     first = (((y * 4 + x) * 2 + zl) * 2 + co) * rows
@@ -138,7 +160,7 @@
 
     other = shift(own, "zl", 1)
     own_down, own_up = shift(own, "y", 1), shift(own, "y", -1)
-    own_far = shift(own_down, "y", 1)
+    own_far = shift(after(own_down, left_low, right_high), "y", 1)
     other_down, other_up = shift(other, "y", 1), shift(other, "y", -1)
     other_far = shift(other_up, "y", -1)
 
@@ -154,13 +176,13 @@
     other_swap = shift(other_rows, "co", 1)
 
     total = squares.reshape(-1, 128)
-    for axis in ("y", "co", "zl", "x"):
-        if axis == "x":
-            total = after(total, own_down, own_up, left_low, right_high)
+    for axis in ("y", "x", "co", "zl"):
         steps = [shift(total, axis, k) for k in range(1, SIZES[axis])]
         for piece in steps:
             total = total + piece
-    total = after(total, left_high, right_low)
+        if axis == "x":
+            left_high = shift(after(high_half, total), "x", 1)
+            right_low = shift(after(low_half, total), "x", -1)
     col_norm = jnp.sqrt(total.reshape(-1) + 1e-06)
     ratio = magnitude / col_norm
 
@@ -168,10 +190,9 @@
         return (g.astype(F32) * ratio).astype(BF)
 
     scaled_own = scaled_of(grad)
-    scaled = jnp.zeros((4 * tokens, width), BF)
-    pieces = (grad, left_low, left_high, right_low, right_high, far_low, far_high)
-    for k, g in zip((0, 2, 3, 4, 5, 6, 7), pieces):
-        scaled = lax.dynamic_update_slice(scaled, scaled_of(g), (k * half, 0))
+    scaled = scaled_of(
+        jnp.concatenate([grad, left_low, left_high, right_low, right_high], axis=0)
+    )
 
     factor_cols = lax.dynamic_slice_in_dim(in_factor, t * features, features, 0)
     hidden = jnp.dot(inputs, factor_cols, preferred_element_type=F32)
@@ -196,32 +217,34 @@
     keep = lax.dynamic_slice_in_dim(adapters, co * side, side, 0)
     give = lax.dynamic_slice_in_dim(adapters, (1 - co) * side, side, 0)
     adapters = keep + shift(give, "co", 1)
-    adapters = adapters + shift(adapters, "zl", 1)
+    adapters = after(adapters, left_high, right_low).reshape(16, 2, -1)
+    keep = lax.dynamic_index_in_dim(adapters, zl, 1, False)
+    give = lax.dynamic_index_in_dim(adapters, 1 - zl, 1, False)
+    adapters = swap_all(keep + shift(give, "zl", 1), ("y", "x"))
+    adapters = jnp.sum(adapters, axis=0)
+    columns = adapters.shape[0]
+    across = shift(adapters.reshape(-1, 8), "zl", 1).reshape(-1)
+    adapters = jnp.where(
+        zl == 0,
+        jnp.concatenate([adapters, across]),
+        jnp.concatenate([across, adapters]),
+    )
     adapters = after(adapters, far_low, far_high)
-    for axis, index in (("y", y), ("x", x)):
-        side = adapters.shape[0] // 4
-        total = lax.dynamic_slice_in_dim(adapters, index * side, side, 0)
-        for k in (1, 2, 3):
-            give = lax.dynamic_slice_in_dim(adapters, ((index + k) % 4) * side, side, 0)
-            total = total + shift(give, axis, k)
-        adapters = total
-    where = jnp.stack([x, zl, co]).astype(jnp.int32)
-    tile = tile_of(where, scaled, (own_rows, other_rows, own_swap, other_swap))
-    adapters = after(adapters, tile)
-    tile = swap_all(tile.reshape(16, tokens, part), ("x", "t"))
-
-    for axis, index in (("x", x), ("y", y), ("co", co)):
-        n = SIZES[axis]
-        side = adapters.shape[0]
-        total = jnp.zeros((n * side, adapters.shape[1]), F32)
-        for k in range(n):
-            got = shift(adapters, axis, k) if k else adapters
-            total = lax.dynamic_update_slice(total, got, (((index - k) % n) * side, 0))
-        adapters = total
+    adapters = swap_all(jnp.broadcast_to(adapters[None], (16, 2 * columns)), ("y", "x"))
+    adapters = adapters.reshape(-1, columns)
+    across = shift(adapters, "co", 1)
+    adapters = jnp.where(
+        co == 0, jnp.stack([adapters, across]), jnp.stack([across, adapters])
+    ).reshape(N_DP, -1)
     out_grad = adapters[:, :width]
     in_grad = adapters[:, width : width + features].T
     mag_grad = adapters[:, width + features :].reshape(-1) / col_norm
 
+    where = jnp.stack([x, zl, co]).astype(jnp.int32)
+    weights = (own_rows, other_rows, own_swap, other_swap)
+    tile = tile_of(where, scaled, far_low, far_high, ratio.reshape(1, -1), weights)
+    tile = swap_all(tile.reshape(16, tokens, part), ("x", "t"))
+
     tile = jnp.sum(tile.reshape(4, 4, tokens, part).astype(F32), axis=1).astype(BF)
     grad_in = tile.transpose(1, 0, 2).reshape(tokens, features)
     return grad_in, in_grad, out_grad, mag_grad

time: 211 us -> 202 us (0.957)
  waiting for transfers between devices: 87.4 us -> 75.5 us
  local copies, waits for them, and re-layouts: 26.9 us -> 30.9 us
    ppermute x41 -> x30, waiting for transfers between devices: 64.6 us -> 40.9 us  [shift(): return lax.ppermute(value, axis, [(i, (i + step) % n) for i in range(n)])]
    all_to_all x1 -> x3, starting transfers between devices: 3.75 us -> 20.4 us  [swap_all(): return lax.all_to_all(value, axes, 0, 0, tiled=True)]
    ppermute x41 -> x30, starting transfers between devices: 60.3 us -> 44.7 us  [shift(): return lax.ppermute(value, axis, [(i, (i + step) % n) for i in range(n)])]
    all_to_all x1 -> x3, waiting for transfers between devices: 22.8 us -> 34.7 us  [swap_all(): return lax.all_to_all(value, axes, 0, 0, tiled=True)]
    dynamic_update_slice x6 -> x0, other arithmetic: 10.3 us -> none  [on_device(): scaled = lax.dynamic_update_slice(scaled, scaled_of(g), (k * half, 0))]
    dynamic_update_slice x11 -> x0, local copies, waits for them, and re-layouts: 7.88 us -> none  [the longest x10 5.02 us: on_device(): total = lax.dynamic_update_slice(total, got, ((index - k) % n * side, 0))]
    unnamed x23 -> x44, local copies, waits for them, and re-layouts: 2.93 us -> 9.63 us
    dynamic_update_slice x8, local copies, waits for them, and re-layouts: 9.63 us -> 4.48 us  [in_order(): lax.dynamic_update_slice(buffer, block[None], ((y + step) % 4, 0, 0))]
  transfers between devices with their start and end apart: 42 -> 33, of which waited for: 13 -> 13; matrix products, arithmetic and copies ran while one was open for 18% -> 19% of each run, Pallas kernels for 0% -> 5%
where the time goes in v3:
time: 202 us; the launch traced here: 201 us
  waiting for transfers between devices  75.5 us (37%)
  starting transfers between devices  65.1 us (32%)
  local copies, waits for them, and re-layouts  30.9 us (15%)
  Pallas kernels  14.6 us (7%)
  other arithmetic  11.3 us (6%)
  matrix products  2.47 us (1%)
    ppermute x30, starting transfers between devices, shift(): return lax.ppermute(value, axis, [(i, (i + step) % n) for i in range(n)])  44.7 us
    ppermute x30, waiting for transfers between devices, shift(): return lax.ppermute(value, axis, [(i, (i + step) % n) for i in range(n)])  40.9 us
    all_to_all x3, waiting for transfers between devices, swap_all(): return lax.all_to_all(value, axes, 0, 0, tiled=True)  34.7 us
    all_to_all x3, starting transfers between devices, swap_all(): return lax.all_to_all(value, axes, 0, 0, tiled=True)  20.4 us
    pallas_call x1, Pallas kernels, tile_of(): pl.pallas_call(tile_kernel, grid_spec=pltpu.PrefetchScalarGridSpec(num_sc...  10.3 us
    unnamed x44, local copies, waits for them, and re-layouts  9.63 us
    dynamic_update_slice x8, local copies, waits for them, and re-layouts, in_order(): lax.dynamic_update_slice(buffer, block[None], ((y + step) % 4, 0, 0))  4.48 us
    pallas_call x1, Pallas kernels, merge(): pl.pallas_call(body, grid=(steps,), in_specs=[columns(rows), whole(count,...  4.24 us
  transfers between devices with their start and end apart: 33, of which 13 were waited for; matrix products, arithmetic and copies ran while one was open for 19% of the time, Pallas kernels for 5%

profile of v3, /device:TPU:8, one launch (start us, length us, event | category | flops | bytes accessed | tf_op | source)
XLA Modules:
  0.0 200.9 jit_solution(18293209166005899046)
XLA Ops:
  2.5 4.2 %shard_map.111 = (bf16[64,3584]{1,0:T(8,128)(2,1)}, f32[1,3584]{1,0:T(1,128)}) custom-call(s32[64,3584]{1,0:T(8,128)} %refs_0_.1, f32[56,64]{1,0:T(8,128)} %bitcast.55, bf16[64,64]{1,0:T(8,128)(2,1)} %copy.19.refs_2_, bf16[64,3584]{1,0:T(8,128)(2,1)} %refs_3_.1), custom_call_target="tpu_custom_call" | custom-call | tf_op jit(solution)/shard_map/pallas_call | solution.py:65
  9.1 2.7 %collective-permute-start.2 = (f32[28,128]{1,0:T(8,128)S(1)}, f32[28,128]{1,0:T(8,128)S(1)}, u32[]{:S(2)}, u32[]{:S(2)}) collective-permute-start(f32[28,128]{1,0:T(8,128)S(1)} %bitcast.53), channel_id=1, source_target_pairs={{0,128},{64,192},{128,0},{192,64},{1,129},{65,193},{129,1},{193,65... | collective-permute-start | bytes 43016 | tf_op jit(solution)/shard_map/ppermute | solution.py:18
  20.7 2.7 %collective-permute-start.5 = (f32[28,128]{1,0:T(8,128)S(1)}, f32[28,128]{1,0:T(8,128)S(1)}, u32[]{:S(2)}, u32[]{:S(2)}) collective-permute-start(f32[28,128]{1,0:T(8,128)S(1)} %add_add_fusion.1), channel_id=1, source_target_pairs={{0,32},{16,48},{32,0},{48,16},{1,33},{17,49},{33,1},{49,17},{2,34}... | collective-permute-start | bytes 43016 | tf_op jit(solution)/shard_map/ppermute | solution.py:18
  25.9 2.6 %collective-permute-start.9 = (bf16[96,3584]{1,0:T(8,128)(2,1)}, bf16[96,3584]{1,0:T(8,128)(2,1)}, u32[]{:S(2)}, u32[]{:S(2)}) collective-permute-start(bf16[96,3584]{1,0:T(8,128)(2,1)} %get-tuple-element.14), channel_id=1, source_target_pairs={{0,48},{16,0},{32,16},{48,32},{1,49},{17,1},{33,17},{49,33},{2,50}... | collective-permute-start | bytes 2064392 | tf_op jit(solution)/shard_map/ppermute | solution.py:18
  31.2 2.4 %collective-permute-done.11 = f32[28,128]{1,0:T(8,128)S(1)} collective-permute-done((f32[28,128]{1,0:T(8,128)S(1)}, f32[28,128]{1,0:T(8,128)S(1)}, u32[]{:S(2)}, u32[]{:S(2)}) %collective-permute-start.11) | collective-permute-done | bytes 14368 | tf_op jit(solution)/shard_map/ppermute | solution.py:18
  33.6 2.0 collective-permute-start.15
  39.8 3.5 %collective-permute-start.8 = (bf16[96,3584]{1,0:T(8,128)(2,1)S(1)}, bf16[96,3584]{1,0:T(8,128)(2,1)}, u32[]{:S(2)}, u32[]{:S(2)}) collective-permute-start(bf16[96,3584]{1,0:T(8,128)(2,1)S(1)} %copy-done.7), channel_id=1, source_target_pairs={{0,48},{16,0},{32,16},{48,32},{1,49},{17,1},{33,17},{49,33},{2,50}... | collective-permute-start | bytes 2064392 | tf_op jit(solution)/shard_map/ppermute | solution.py:18
  43.3 1.8 bitcast_dynamic-update-slice_fusion.6
  45.6 2.2 %collective-permute-start.19 = (bf16[64,3584]{1,0:T(8,128)(2,1)S(1)}, bf16[64,3584]{1,0:T(8,128)(2,1)S(1)}, u32[]{:S(2)}, u32[]{:S(2)}) collective-permute-start(bf16[64,3584]{1,0:T(8,128)(2,1)S(1)} %copy-done.10), channel_id=1, source_target_pairs={{0,192},{64,0},{128,64},{192,128},{1,193},{65,1},{129,65},{193,129... | collective-permute-start | bytes 1376264 | tf_op jit(solution)/shard_map/ppermute | solution.py:18
  48.7 3.0 %collective-permute-start.16 = (bf16[64,3584]{1,0:T(8,128)(2,1)}, bf16[64,3584]{1,0:T(8,128)(2,1)S(1)}, u32[]{:S(2)}, u32[]{:S(2)}) collective-permute-start(bf16[64,3584]{1,0:T(8,128)(2,1)} %collective-permute-done.14), channel_id=1, source_target_pairs={{0,64},{64,128},{128,192},{192,0},{1,65},{65,129},{129,193},{193,1... | collective-permute-start | bytes 1376264 | tf_op jit(solution)/shard_map/ppermute | solution.py:18
  52.5 4.2 %collective-permute-done.7 = bf16[96,3584]{1,0:T(8,128)(2,1)S(1)} collective-permute-done((bf16[96,3584]{1,0:T(8,128)(2,1)S(1)}, bf16[96,3584]{1,0:T(8,128)(2,1)S(1)}, u32[]{:S(2)}, u32[]{:S(2)}) %collective-permute-start.7) | collective-permute-done | bytes 688160 | tf_op jit(solution)/shard_map/ppermute | solution.py:18
  57.6 6.1 %collective-permute-done.18 = bf16[64,3584]{1,0:T(8,128)(2,1)S(1)} collective-permute-done((bf16[64,3584]{1,0:T(8,128)(2,1)S(1)}, bf16[64,3584]{1,0:T(8,128)(2,1)S(1)}, u32[]{:S(2)}, u32[]{:S(2)}) %collective-permute-start.18) | collective-permute-done | bytes 458784 | tf_op jit(solution)/shard_map/ppermute | solution.py:18
  63.7 7.2 %collective-permute-done.16 = bf16[64,3584]{1,0:T(8,128)(2,1)S(1)} collective-permute-done((bf16[64,3584]{1,0:T(8,128)(2,1)}, bf16[64,3584]{1,0:T(8,128)(2,1)S(1)}, u32[]{:S(2)}, u32[]{:S(2)}) %collective-permute-start.16) | collective-permute-done | bytes 458784 | tf_op jit(solution)/shard_map/ppermute | solution.py:18
  71.0 3.3 %collective-permute-start.23 = (bf16[192,128]{0,1:T(8,128)(2,1)S(1)}, bf16[192,128]{0,1:T(8,128)(2,1)S(1)}, u32[]{:S(2)}, u32[]{:S(2)}) collective-permute-start(bf16[192,128]{0,1:T(8,128)(2,1)S(1)} %pad_maximum_fusion.1), channel_id=1, source_target_pairs={{0,1},{1,2},{2,3},{3,0},{4,5},{5,6},{6,7},{7,4},{8,9},{9,10},{10,1... | collective-permute-start | bytes 147464 | tf_op jit(solution)/shard_map/ppermute | solution.py:18
  74.2 4.5 %collective-permute-start.24 = (bf16[192,128]{0,1:T(8,128)(2,1)S(1)}, bf16[192,128]{0,1:T(8,128)(2,1)S(1)}, u32[]{:S(2)}, u32[]{:S(2)}) collective-permute-start(bf16[192,128]{0,1:T(8,128)(2,1)S(1)} %pad_maximum_fusion.1), channel_id=1, source_target_pairs={{0,2},{1,3},{2,0},{3,1},{4,6},{5,7},{6,4},{7,5},{8,10},{9,11},{10,... | collective-permute-start | bytes 147464 | tf_op jit(solution)/shard_map/ppermute | solution.py:18
  78.7 2.7 %collective-permute-start.25 = (bf16[192,128]{0,1:T(8,128)(2,1)S(1)}, bf16[192,128]{0,1:T(8,128)(2,1)S(1)}, u32[]{:S(2)}, u32[]{:S(2)}) collective-permute-start(bf16[192,128]{0,1:T(8,128)(2,1)S(1)} %pad_maximum_fusion.1), channel_id=1, source_target_pairs={{0,3},{1,0},{2,1},{3,2},{4,7},{5,4},{6,5},{7,6},{8,11},{9,8},{10,9... | collective-permute-start | bytes 147464 | tf_op jit(solution)/shard_map/ppermute | solution.py:18
  82.8 3.0 %collective-permute-start.20 = (bf16[64,3584]{1,0:T(8,128)(2,1)S(1)}, bf16[64,3584]{1,0:T(8,128)(2,1)S(1)}, u32[]{:S(2)}, u32[]{:S(2)}) collective-permute-start(bf16[64,3584]{1,0:T(8,128)(2,1)S(1)} %collective-permute-done.19), channel_id=1, source_target_pairs={{0,192},{64,0},{128,64},{192,128},{1,193},{65,1},{129,65},{193,129... | collective-permute-start | bytes 1376264 | tf_op jit(solution)/shard_map/ppermute | solution.py:18
  86.5 5.4 %collective-permute-done.20 = bf16[64,3584]{1,0:T(8,128)(2,1)S(1)} collective-permute-done((bf16[64,3584]{1,0:T(8,128)(2,1)S(1)}, bf16[64,3584]{1,0:T(8,128)(2,1)S(1)}, u32[]{:S(2)}, u32[]{:S(2)}) %collective-permute-start.20) | collective-permute-done | bytes 458784 | tf_op jit(solution)/shard_map/ppermute | solution.py:18
  95.0 2.3 %reshape.64 = f32[16,2,4664]{2,1,0:T(2,128)} reshape(f32[32,4664]{1,0:T(8,128)} %dynamic-slice_add_fusion) | data formatting | bytes 1193984 | tf_op jit(solution)/shard_map/reshape | solution.py:220
  97.3 2.0 %constant_dynamic-slice_fusion.1 = (f32[16,1,4664]{2,1,0:T(1,128)S(1)}, f32[16,1,4664]{2,1,0:T(1,128)S(1)}) fusion(f32[16,2,4664]{2,1,0:T(2,128)} %reshape.64, s32[]{:T(128)S(6)} %select_n.96, s32[]{:T(128)S(6)} %select_n.97), kind=kLoop, calls=%fused_computation.43 | loop fusion | bytes 1193992 | tf_op jit(solution)/shard_map/jit(dynamic_index_in_dim)/dynamic_slice | solution.py:221
  100.6 8.1 %collective-permute-done.27 = f32[16,4664]{1,0:T(8,128)S(1)} collective-permute-done((f32[16,4664]{1,0:T(8,128)S(1)}, f32[16,4664]{1,0:T(8,128)S(1)}, u32[]{:S(2)}, u32[]{:S(2)}) %collective-permute-start.27) | collective-permute-done | bytes 298528 | tf_op jit(solution)/shard_map/ppermute | solution.py:18
  109.7 6.0 %all-to-all-start.1 = ((f32[16,1,4664]{2,1,0:T(1,128)}), f32[16,1,4664]{2,1,0:T(1,128)S(1)}, u32[]{:S(2)}, u32[]{:S(2)}) async-start(f32[16,1,4664]{2,1,0:T(1,128)} %all_to_all.14), calls=%async_computation.1 | async-start | bytes 606208 | tf_op jit(solution)/shard_map/all_to_all | solution.py:22
  115.6 2.0 %constant_dynamic-update-slice_fusion.1 = bf16[576,3584]{1,0:T(8,128)(2,1)} fusion(bf16[576,3584]{1,0:T(8,128)(2,1)} %constant_dynamic-update-slice_fusion.2, bf16[96,3584]{1,0:T(8,128)(2,1)} %collective-permute-done.8), kind=kLoop, calls=%fused_computation.38 | loop fusion | bytes 1376256
  117.7 5.1 %all-to-all-done.1 = f32[16,1,4664]{2,1,0:T(1,128)S(1)} async-done(((f32[16,1,4664]{2,1,0:T(1,128)}), f32[16,1,4664]{2,1,0:T(1,128)S(1)}, u32[]{:S(2)}, u32[]{:S(2)}) %all-to-all-start.1) | async-done | bytes 298528 | tf_op jit(solution)/shard_map/all_to_all | solution.py:22
  124.8 2.0 constant_dynamic-update-slice_fusion
  126.8 4.2 %collective-permute-done.28 = f32[583,8]{1,0:T(8,128)S(1)} collective-permute-done((f32[583,8]{1,0:T(8,128)}, f32[583,8]{1,0:T(8,128)S(1)}, u32[]{:S(2)}, u32[]{:S(2)}) %collective-permute-start.28) | collective-permute-done | bytes 18688 | tf_op jit(solution)/shard_map/ppermute | solution.py:18
  132.4 6.2 %all-to-all-start.2 = ((f32[16,1,9328]{2,1,0:T(1,128)}), f32[16,1,9328]{2,1,0:T(1,128)}, u32[]{:S(2)}, u32[]{:S(2)}) async-start(f32[16,1,9328]{2,1,0:T(1,128)} %broadcast_in_dim.43), calls=%async_computation.2 | async-start | bytes 1196032 | tf_op jit(solution)/shard_map/all_to_all | solution.py:22
  138.6 2.9 %multiply_convert_fusion.scaled = bf16[576,3584]{1,0:T(8,128)(2,1)S(1)} fusion(bf16[576,3584]{1,0:T(8,128)(2,1)} %constant_dynamic-update-slice_fusion, f32[3584]{0:T(1024)S(1)} %bitcast_divide_fusion.1), kind=kLoop, calls=%fused_computation | loop fusion | flops 6193152 | bytes 8271872 | tf_op jit(solution)/shard_map/convert_element_type | solution.py:190
  141.5 10.3 %shard_map.112 = bf16[4,4,192,256]{3,2,1,0:T(8,128)(2,1)S(1)} custom-call(s32[3]{0:T(128)S(1)} %pad_add_fusion.where, bf16[576,3584]{1,0:T(8,128)(2,1)S(1)} %multiply_convert_fusion.scaled, bf16[96,3584]{1,0:T(8,128)(2,1)S(1)} %collective-permute-done.12.far_low, bf16[96,3584]{1,0:T(8,128)(2,1)} %collective-permute-done.13.far_high, ...), custom_call_target="tpu_custom_call" | custom-call | flops 5637144576 | bytes 12845056 | tf_op jit(solution)/shard_map/pallas_call | solution.py:123
  153.0 8.2 %all-to-all-start = ((bf16[16,192,256]{2,1,0:T(8,128)(2,1)}), bf16[16,192,256]{2,1,0:T(8,128)(2,1)S(1)}, u32[]{:S(2)}, u32[]{:S(2)}) async-start(bf16[16,192,256]{2,1,0:T(8,128)(2,1)} %bitcast.45), calls=%async_computation | async-start | bytes 3145728 | tf_op jit(solution)/shard_map/all_to_all | solution.py:22
  161.2 2.5 %reduce.3 = f32[16,9328]{1,0:T(8,128)S(1)} reduce(f32[16,1,9328]{2,1,0:T(1,128)} %all-to-all-done.2, f32[]{:T(128)} %constant.85), dimensions={1}, to_apply=%all_to_all.16.reduce_sub_computation | reduce | bytes 1193988 | tf_op jit(solution)/shard_map/all_to_all | solution.py:22
  170.4 29.6 %all-to-all-done = bf16[16,192,256]{2,1,0:T(8,128)(2,1)S(1)} async-done(((bf16[16,192,256]{2,1,0:T(8,128)(2,1)}), bf16[16,192,256]{2,1,0:T(8,128)(2,1)S(1)}, u32[]{:S(2)}, u32[]{:S(2)}) %all-to-all-start) | async-done | bytes 1572896 | tf_op jit(solution)/shard_map/all_to_all | solution.py:22
  (132 shorter events, 45.1 us)
Async XLA Ops:
  7.5 11.6 %collective-permute-start.1 = (f32[28,128]{1,0:T(8,128)S(1)}, f32[28,128]{1,0:T(8,128)S(1)}, u32[]{:S(2)}, u32[]{:S(2)}) collective-permute-start(f32[28,128]{1,0:T(8,128)S(1)} %bitcast.52), channel_id=1, source_target_pairs={{0,64},{64,128},{128,192},{192,0},{1,65},{65,129},{129,193},{193,1... | collective-permute-start | bytes 43016 | tf_op jit(solution)/shard_map/ppermute | solution.py:18
  9.1 10.0 %collective-permute-start.2 = (f32[28,128]{1,0:T(8,128)S(1)}, f32[28,128]{1,0:T(8,128)S(1)}, u32[]{:S(2)}, u32[]{:S(2)}) collective-permute-start(f32[28,128]{1,0:T(8,128)S(1)} %bitcast.53), channel_id=1, source_target_pairs={{0,128},{64,192},{128,0},{192,64},{1,129},{65,193},{129,1},{193,65... | collective-permute-start | bytes 43016 | tf_op jit(solution)/shard_map/ppermute | solution.py:18
  11.8 7.3 %collective-permute-start.3 = (f32[28,128]{1,0:T(8,128)S(1)}, f32[28,128]{1,0:T(8,128)S(1)}, u32[]{:S(2)}, u32[]{:S(2)}) collective-permute-start(f32[28,128]{1,0:T(8,128)S(1)} %bitcast.54), channel_id=1, source_target_pairs={{0,192},{64,0},{128,64},{192,128},{1,193},{65,1},{129,65},{193,129... | collective-permute-start | bytes 43016 | tf_op jit(solution)/shard_map/ppermute | solution.py:18
  12.5 27.4 %collective-permute-start.14 = (bf16[64,3584]{1,0:T(8,128)(2,1)}, bf16[64,3584]{1,0:T(8,128)(2,1)}, u32[]{:S(2)}, u32[]{:S(2)}) collective-permute-start(bf16[64,3584]{1,0:T(8,128)(2,1)} %get-tuple-element.16), channel_id=1, source_target_pairs={{0,64},{64,128},{128,192},{192,0},{1,65},{65,129},{129,193},{193,1... | collective-permute-start | bytes 1376264 | tf_op jit(solution)/shard_map/ppermute | solution.py:18
  13.8 24.1 %collective-permute-start.17 = (bf16[64,3584]{1,0:T(8,128)(2,1)}, bf16[64,3584]{1,0:T(8,128)(2,1)S(1)}, u32[]{:S(2)}, u32[]{:S(2)}) collective-permute-start(bf16[64,3584]{1,0:T(8,128)(2,1)} %get-tuple-element.16), channel_id=1, source_target_pairs={{0,8},{8,0},{1,9},{9,1},{2,10},{10,2},{3,11},{11,3},{4,12},{12,4},... | collective-permute-start | bytes 1376264 | tf_op jit(solution)/shard_map/ppermute | solution.py:18
  19.1 6.1 %collective-permute-start.4 = (f32[28,128]{1,0:T(8,128)S(1)}, f32[28,128]{1,0:T(8,128)S(1)}, u32[]{:S(2)}, u32[]{:S(2)}) collective-permute-start(f32[28,128]{1,0:T(8,128)S(1)} %add_add_fusion.1), channel_id=1, source_target_pairs={{0,16},{16,32},{32,48},{48,0},{1,17},{17,33},{33,49},{49,1},{2,18}... | collective-permute-start | bytes 43016 | tf_op jit(solution)/shard_map/ppermute | solution.py:18
  20.7 5.3 %collective-permute-start.5 = (f32[28,128]{1,0:T(8,128)S(1)}, f32[28,128]{1,0:T(8,128)S(1)}, u32[]{:S(2)}, u32[]{:S(2)}) collective-permute-start(f32[28,128]{1,0:T(8,128)S(1)} %add_add_fusion.1), channel_id=1, source_target_pairs={{0,32},{16,48},{32,0},{48,16},{1,33},{17,49},{33,1},{49,17},{2,34}... | collective-permute-start | bytes 43016 | tf_op jit(solution)/shard_map/ppermute | solution.py:18
  23.4 5.2 %collective-permute-start.6 = (f32[28,128]{1,0:T(8,128)S(1)}, f32[28,128]{1,0:T(8,128)S(1)}, u32[]{:S(2)}, u32[]{:S(2)}) collective-permute-start(f32[28,128]{1,0:T(8,128)S(1)} %add_add_fusion.1), channel_id=1, source_target_pairs={{0,48},{16,0},{32,16},{48,32},{1,49},{17,1},{33,17},{49,33},{2,50}... | collective-permute-start | bytes 43016 | tf_op jit(solution)/shard_map/ppermute | solution.py:18
  25.2 23.4 %collective-permute-start = (bf16[96,3584]{1,0:T(8,128)(2,1)}, bf16[96,3584]{1,0:T(8,128)(2,1)S(1)}, u32[]{:S(2)}, u32[]{:S(2)}) collective-permute-start(bf16[96,3584]{1,0:T(8,128)(2,1)} %get-tuple-element.15), channel_id=1, source_target_pairs={{0,16},{16,32},{32,48},{48,0},{1,17},{17,33},{33,49},{49,1},{2,18}... | collective-permute-start | bytes 2064392 | tf_op jit(solution)/shard_map/ppermute | solution.py:18
  25.9 22.7 %collective-permute-start.9 = (bf16[96,3584]{1,0:T(8,128)(2,1)}, bf16[96,3584]{1,0:T(8,128)(2,1)}, u32[]{:S(2)}, u32[]{:S(2)}) collective-permute-start(bf16[96,3584]{1,0:T(8,128)(2,1)} %get-tuple-element.14), channel_id=1, source_target_pairs={{0,48},{16,0},{32,16},{48,32},{1,49},{17,1},{33,17},{49,33},{2,50}... | collective-permute-start | bytes 2064392 | tf_op jit(solution)/shard_map/ppermute | solution.py:18
  29.9 3.7 %collective-permute-start.11 = (f32[28,128]{1,0:T(8,128)S(1)}, f32[28,128]{1,0:T(8,128)S(1)}, u32[]{:S(2)}, u32[]{:S(2)}) collective-permute-start(f32[28,128]{1,0:T(8,128)S(1)} %add.130), channel_id=1, source_target_pairs={{0,8},{8,0},{1,9},{9,1},{2,10},{10,2},{3,11},{11,3},{4,12},{12,4},... | collective-permute-start | bytes 43016 | tf_op jit(solution)/shard_map/ppermute | solution.py:18
  33.6 12.1 %collective-permute-start.15 = (bf16[64,3584]{1,0:T(8,128)(2,1)}, bf16[64,3584]{1,0:T(8,128)(2,1)S(1)}, u32[]{:S(2)}, u32[]{:S(2)}) collective-permute-start(bf16[64,3584]{1,0:T(8,128)(2,1)} %get-tuple-element.16), channel_id=1, source_target_pairs={{0,192},{64,0},{128,64},{192,128},{1,193},{65,1},{129,65},{193,129... | collective-permute-start | bytes 1376264 | tf_op jit(solution)/shard_map/ppermute | solution.py:18
  38.8 17.9 %collective-permute-start.7 = (bf16[96,3584]{1,0:T(8,128)(2,1)S(1)}, bf16[96,3584]{1,0:T(8,128)(2,1)S(1)}, u32[]{:S(2)}, u32[]{:S(2)}) collective-permute-start(bf16[96,3584]{1,0:T(8,128)(2,1)S(1)} %copy-done.8), channel_id=1, source_target_pairs={{0,16},{16,32},{32,48},{48,0},{1,17},{17,33},{33,49},{49,1},{2,18}... | collective-permute-start | bytes 2064392 | tf_op jit(solution)/shard_map/ppermute | solution.py:18
  39.8 55.2 %collective-permute-start.8 = (bf16[96,3584]{1,0:T(8,128)(2,1)S(1)}, bf16[96,3584]{1,0:T(8,128)(2,1)}, u32[]{:S(2)}, u32[]{:S(2)}) collective-permute-start(bf16[96,3584]{1,0:T(8,128)(2,1)S(1)} %copy-done.7), channel_id=1, source_target_pairs={{0,48},{16,0},{32,16},{48,32},{1,49},{17,1},{33,17},{49,33},{2,50}... | collective-permute-start | bytes 2064392 | tf_op jit(solution)/shard_map/ppermute | solution.py:18
  45.6 18.1 %collective-permute-start.19 = (bf16[64,3584]{1,0:T(8,128)(2,1)S(1)}, bf16[64,3584]{1,0:T(8,128)(2,1)S(1)}, u32[]{:S(2)}, u32[]{:S(2)}) collective-permute-start(bf16[64,3584]{1,0:T(8,128)(2,1)S(1)} %copy-done.10), channel_id=1, source_target_pairs={{0,192},{64,0},{128,64},{192,128},{1,193},{65,1},{129,65},{193,129... | collective-permute-start | bytes 1376264 | tf_op jit(solution)/shard_map/ppermute | solution.py:18
  48.6 15.1 %collective-permute-start.18 = (bf16[64,3584]{1,0:T(8,128)(2,1)S(1)}, bf16[64,3584]{1,0:T(8,128)(2,1)S(1)}, u32[]{:S(2)}, u32[]{:S(2)}) collective-permute-start(bf16[64,3584]{1,0:T(8,128)(2,1)S(1)} %copy-done.10), channel_id=1, source_target_pairs={{0,64},{64,128},{128,192},{192,0},{1,65},{65,129},{129,193},{193,1... | collective-permute-start | bytes 1376264 | tf_op jit(solution)/shard_map/ppermute | solution.py:18
  48.7 22.3 %collective-permute-start.16 = (bf16[64,3584]{1,0:T(8,128)(2,1)}, bf16[64,3584]{1,0:T(8,128)(2,1)S(1)}, u32[]{:S(2)}, u32[]{:S(2)}) collective-permute-start(bf16[64,3584]{1,0:T(8,128)(2,1)} %collective-permute-done.14), channel_id=1, source_target_pairs={{0,64},{64,128},{128,192},{192,0},{1,65},{65,129},{129,193},{193,1... | collective-permute-start | bytes 1376264 | tf_op jit(solution)/shard_map/ppermute | solution.py:18
  56.7 74.6 %collective-permute-start.12 = (bf16[96,3584]{1,0:T(8,128)(2,1)}, bf16[96,3584]{1,0:T(8,128)(2,1)S(1)}, u32[]{:S(2)}, u32[]{:S(2)}) collective-permute-start(bf16[96,3584]{1,0:T(8,128)(2,1)} %copy-done.6), channel_id=1, source_target_pairs={{0,16},{16,32},{32,48},{48,0},{1,17},{17,33},{33,49},{49,1},{2,18}... | collective-permute-start | bytes 2064392 | tf_op jit(solution)/shard_map/ppermute | solution.py:18
  71.0 10.5 %collective-permute-start.23 = (bf16[192,128]{0,1:T(8,128)(2,1)S(1)}, bf16[192,128]{0,1:T(8,128)(2,1)S(1)}, u32[]{:S(2)}, u32[]{:S(2)}) collective-permute-start(bf16[192,128]{0,1:T(8,128)(2,1)S(1)} %pad_maximum_fusion.1), channel_id=1, source_target_pairs={{0,1},{1,2},{2,3},{3,0},{4,5},{5,6},{6,7},{7,4},{8,9},{9,10},{10,1... | collective-permute-start | bytes 147464 | tf_op jit(solution)/shard_map/ppermute | solution.py:18
  74.2 8.5 %collective-permute-start.24 = (bf16[192,128]{0,1:T(8,128)(2,1)S(1)}, bf16[192,128]{0,1:T(8,128)(2,1)S(1)}, u32[]{:S(2)}, u32[]{:S(2)}) collective-permute-start(bf16[192,128]{0,1:T(8,128)(2,1)S(1)} %pad_maximum_fusion.1), channel_id=1, source_target_pairs={{0,2},{1,3},{2,0},{3,1},{4,6},{5,7},{6,4},{7,5},{8,10},{9,11},{10,... | collective-permute-start | bytes 147464 | tf_op jit(solution)/shard_map/ppermute | solution.py:18
  78.7 7.0 %collective-permute-start.25 = (bf16[192,128]{0,1:T(8,128)(2,1)S(1)}, bf16[192,128]{0,1:T(8,128)(2,1)S(1)}, u32[]{:S(2)}, u32[]{:S(2)}) collective-permute-start(bf16[192,128]{0,1:T(8,128)(2,1)S(1)} %pad_maximum_fusion.1), channel_id=1, source_target_pairs={{0,3},{1,0},{2,1},{3,2},{4,7},{5,4},{6,5},{7,6},{8,11},{9,8},{10,9... | collective-permute-start | bytes 147464 | tf_op jit(solution)/shard_map/ppermute | solution.py:18
  81.5 49.8 %collective-permute-start.13 = (bf16[96,3584]{1,0:T(8,128)(2,1)}, bf16[96,3584]{1,0:T(8,128)(2,1)}, u32[]{:S(2)}, u32[]{:S(2)}) collective-permute-start(bf16[96,3584]{1,0:T(8,128)(2,1)} %collective-permute-done.9), channel_id=1, source_target_pairs={{0,48},{16,0},{32,16},{48,32},{1,49},{17,1},{33,17},{49,33},{2,50}... | collective-permute-start | bytes 2064392 | tf_op jit(solution)/shard_map/ppermute | solution.py:18
  82.8 9.2 %collective-permute-start.20 = (bf16[64,3584]{1,0:T(8,128)(2,1)S(1)}, bf16[64,3584]{1,0:T(8,128)(2,1)S(1)}, u32[]{:S(2)}, u32[]{:S(2)}) collective-permute-start(bf16[64,3584]{1,0:T(8,128)(2,1)S(1)} %collective-permute-done.19), channel_id=1, source_target_pairs={{0,192},{64,0},{128,64},{192,128},{1,193},{65,1},{129,65},{193,129... | collective-permute-start | bytes 1376264 | tf_op jit(solution)/shard_map/ppermute | solution.py:18
  92.0 2.1 %collective-permute-start.26 = (f32[32,4664]{1,0:T(8,128)S(1)}, f32[32,4664]{1,0:T(8,128)S(1)}, u32[]{:S(2)}, u32[]{:S(2)}) collective-permute-start(f32[32,4664]{1,0:T(8,128)S(1)} %constant_dynamic-slice_fusion.2), channel_id=1, source_target_pairs={{0,4},{4,0},{1,5},{5,1},{2,6},{6,2},{3,7},{7,3},{8,12},{12,8},{9,1... | collective-permute-start | bytes 1790984 | tf_op jit(solution)/shard_map/ppermute | solution.py:18
  92.9 48.5 %collective-permute-start.21 = (bf16[4,64,3584]{2,1,0:T(8,128)(2,1)}, bf16[4,64,3584]{2,1,0:T(8,128)(2,1)}, u32[]{:S(2)}, u32[]{:S(2)}) collective-permute-start(bf16[4,64,3584]{2,1,0:T(8,128)(2,1)} %bitcast_dynamic-update-slice_fusion.4.own), channel_id=1, source_target_pairs={{0,4},{4,0},{1,5},{5,1},{2,6},{6,2},{3,7},{7,3},{8,12},{12,8},{9,1... | collective-permute-start | bytes 5505032 | tf_op jit(solution)/shard_map/ppermute | solution.py:18
  99.4 9.3 %collective-permute-start.27 = (f32[16,4664]{1,0:T(8,128)S(1)}, f32[16,4664]{1,0:T(8,128)S(1)}, u32[]{:S(2)}, u32[]{:S(2)}) collective-permute-start(f32[16,4664]{1,0:T(8,128)S(1)} %bitcast.51), channel_id=1, source_target_pairs={{0,8},{8,0},{1,9},{9,1},{2,10},{10,2},{3,11},{11,3},{4,12},{12,4},... | collective-permute-start | bytes 895496 | tf_op jit(solution)/shard_map/ppermute | solution.py:18
  100.5 40.9 %collective-permute-start.22 = (bf16[4,64,3584]{2,1,0:T(8,128)(2,1)S(1)}, bf16[4,64,3584]{2,1,0:T(8,128)(2,1)}, u32[]{:S(2)}, u32[]{:S(2)}) collective-permute-start(bf16[4,64,3584]{2,1,0:T(8,128)(2,1)S(1)} %bitcast_dynamic-update-slice_fusion.other), channel_id=1, source_target_pairs={{0,4},{4,0},{1,5},{5,1},{2,6},{6,2},{3,7},{7,3},{8,12},{12,8},{9,1... | collective-permute-start | bytes 5505032 | tf_op jit(solution)/shard_map/ppermute | solution.py:18
  109.7 13.1 %all-to-all-start.1 = ((f32[16,1,4664]{2,1,0:T(1,128)}), f32[16,1,4664]{2,1,0:T(1,128)S(1)}, u32[]{:S(2)}, u32[]{:S(2)}) async-start(f32[16,1,4664]{2,1,0:T(1,128)} %all_to_all.14), calls=%async_computation.1 | async-start | bytes 606208 | tf_op jit(solution)/shard_map/all_to_all | solution.py:22
  123.9 7.1 %collective-permute-start.28 = (f32[583,8]{1,0:T(8,128)}, f32[583,8]{1,0:T(8,128)S(1)}, u32[]{:S(2)}, u32[]{:S(2)}) collective-permute-start(f32[583,8]{1,0:T(8,128)} %reshape.65), channel_id=1, source_target_pairs={{0,8},{8,0},{1,9},{9,1},{2,10},{10,2},{3,11},{11,3},{4,12},{12,4},... | collective-permute-start | bytes 55976 | tf_op jit(solution)/shard_map/ppermute | solution.py:18
  132.4 20.6 %all-to-all-start.2 = ((f32[16,1,9328]{2,1,0:T(1,128)}), f32[16,1,9328]{2,1,0:T(1,128)}, u32[]{:S(2)}, u32[]{:S(2)}) async-start(f32[16,1,9328]{2,1,0:T(1,128)} %broadcast_in_dim.43), calls=%async_computation.2 | async-start | bytes 1196032 | tf_op jit(solution)/shard_map/all_to_all | solution.py:22
  153.0 46.9 %all-to-all-start = ((bf16[16,192,256]{2,1,0:T(8,128)(2,1)}), bf16[16,192,256]{2,1,0:T(8,128)(2,1)S(1)}, u32[]{:S(2)}, u32[]{:S(2)}) async-start(bf16[16,192,256]{2,1,0:T(8,128)(2,1)} %bitcast.45), calls=%async_computation | async-start | bytes 3145728 | tf_op jit(solution)/shard_map/all_to_all | solution.py:22
  163.9 2.2 %collective-permute-start.29 = (f32[32,4664]{1,0:T(8,128)S(1)}, f32[32,4664]{1,0:T(8,128)}, u32[]{:S(2)}, u32[]{:S(2)}) collective-permute-start(f32[32,4664]{1,0:T(8,128)S(1)} %reshape.67), channel_id=1, source_target_pairs={{0,4},{4,0},{1,5},{5,1},{2,6},{6,2},{3,7},{7,3},{8,12},{12,8},{9,1... | collective-permute-start | bytes 1790984 | tf_op jit(solution)/shard_map/ppermute | solution.py:18
  (20 other events, 116.1 us)

commit v4 on v3

--- a/solution.py
+++ b/solution.py
@@ -116,6 +116,10 @@
     n = 2 * half
     rows = weights[0].shape[1]
 
+    def place(i, where):
+        step = jnp.where(i == 0, 0, jnp.where(i == 1, 3, i - 1))
+        return 0, lax.rem(where[3] + step, 4), 0, 0
+
     def whole(shape):
         return pl.BlockSpec(shape, lambda i, w: (0, 0))
 
@@ -128,7 +132,7 @@
             in_specs=[whole((tokens, width)), whole((half, width)), whole((half, width))]
             + [whole((1, width))]
             + [weight] * 4,
-            out_specs=pl.BlockSpec((4, 1, n, 4 * rows), lambda i, w: (0, i, 0, 0)),
+            out_specs=pl.BlockSpec((4, 1, n, 4 * rows), place),
             scratch_shapes=[pltpu.VMEM((4 * rows, width), BF), pltpu.VMEM((n, width), BF)],
         ),
         out_shape=jax.ShapeDtypeStruct((4, 4, n, 4 * rows), BF),
@@ -150,39 +154,40 @@
     part = features // SIZES["x"]
     rank = in_factor.shape[1]
 
-    low_half, high_half = grad[:half], grad[half:]
-    left_low, right_high = shift(low_half, "x", 1), shift(high_half, "x", -1)
-    far_low, far_high = shift(left_low, "x", 1), shift(right_high, "x", -1)
+    def gather_sum(value, axis):
+        steps = [shift(value, axis, k) for k in range(1, SIZES[axis])]
+        for piece in steps:
+            value = value + piece
+        return value
 
     first = (((y * 4 + x) * 2 + zl) * 2 + co) * rows
     factor_rows = lax.dynamic_slice_in_dim(in_factor, first, rows, 0)
     own, squares = merge(codes, scales.T, factor_rows, out_factor)
 
+    low_half, high_half = grad[:half], grad[half:]
+    left_low, right_high = shift(low_half, "x", 1), shift(high_half, "x", -1)
     other = shift(own, "zl", 1)
     own_down, own_up = shift(own, "y", 1), shift(own, "y", -1)
-    own_far = shift(after(own_down, left_low, right_high), "y", 1)
+    total = gather_sum(gather_sum(squares.reshape(-1, 128), "y"), "co")
+    phase = (left_low, right_high, other, own_down, own_up, total, low_half, high_half)
+    phase = lax.optimization_barrier(phase)
+    left_low, right_high, other, own_down, own_up, total, low_half, high_half = phase
+
+    left_high, right_low = shift(high_half, "x", 1), shift(low_half, "x", -1)
     other_down, other_up = shift(other, "y", 1), shift(other, "y", -1)
+    own_far = shift(own_down, "y", 1)
+    total = after(gather_sum(total, "zl"), other_down, other_up, own_far)
+    total = gather_sum(total, "x")
+    phase = (left_low, right_high, left_high, right_low, other_down, other_up, own_far, total)
+    phase = lax.optimization_barrier(phase)
+    left_low, right_high, left_high, right_low, other_down, other_up, own_far, total = phase
+
+    far_low, far_high = shift(left_low, "x", 1), shift(right_high, "x", -1)
     other_far = shift(other_up, "y", -1)
-
-    def in_order(blocks):
-        buffer = jnp.zeros((4, rows, width), BF)
-        for block, step in zip(blocks, (0, -1, 1, 2)):
-            buffer = lax.dynamic_update_slice(buffer, block[None], ((y + step) % 4, 0, 0))
-        return buffer
-
-    own_rows = in_order((own, own_down, own_up, own_far))
+    own_rows = jnp.stack([own, own_down, own_up, own_far])
     own_swap = shift(own_rows, "co", 1)
-    other_rows = in_order((other, other_down, other_up, other_far))
+    other_rows = jnp.stack([other, other_down, other_up, other_far])
     other_swap = shift(other_rows, "co", 1)
-
-    total = squares.reshape(-1, 128)
-    for axis in ("y", "x", "co", "zl"):
-        steps = [shift(total, axis, k) for k in range(1, SIZES[axis])]
-        for piece in steps:
-            total = total + piece
-        if axis == "x":
-            left_high = shift(after(high_half, total), "x", 1)
-            right_low = shift(after(low_half, total), "x", -1)
     col_norm = jnp.sqrt(total.reshape(-1) + 1e-06)
     ratio = magnitude / col_norm
 
@@ -200,9 +205,9 @@
         scaled_own, out_factor, (((1,), (1,)), ((), ())), preferred_element_type=F32
     )
     low = jnp.concatenate([hidden, back], axis=1).astype(BF)
-    low = after(low, own_far, other_down, other_up)
     pieces = [shift(low, "t", k) for k in (1, 2, 3)]
     low = sum((p.astype(F32) for p in pieces), low.astype(F32)).astype(BF)
+    low = after(low, far_low, far_high, other_far)
     hidden, back = low[:, :rank], low[:, rank:]
     in_grad = SCALE * lax.dot_general(
         back, inputs, (((0,), (0,)), ((), ())), preferred_element_type=F32
@@ -212,39 +217,37 @@
     )
     mag_sum = jnp.sum(grad.astype(F32) * pre.astype(F32), axis=0).reshape(N_DP, -1)
     adapters = jnp.concatenate([out_grad, in_grad, mag_sum], axis=1)
-    adapters = after(adapters, other_far)
     side = adapters.shape[0] // 2
     keep = lax.dynamic_slice_in_dim(adapters, co * side, side, 0)
     give = lax.dynamic_slice_in_dim(adapters, (1 - co) * side, side, 0)
     adapters = keep + shift(give, "co", 1)
-    adapters = after(adapters, left_high, right_low).reshape(16, 2, -1)
-    keep = lax.dynamic_index_in_dim(adapters, zl, 1, False)
-    give = lax.dynamic_index_in_dim(adapters, 1 - zl, 1, False)
-    adapters = swap_all(keep + shift(give, "zl", 1), ("y", "x"))
-    adapters = jnp.sum(adapters, axis=0)
-    columns = adapters.shape[0]
-    across = shift(adapters.reshape(-1, 8), "zl", 1).reshape(-1)
-    adapters = jnp.where(
-        zl == 0,
-        jnp.concatenate([adapters, across]),
-        jnp.concatenate([across, adapters]),
-    )
-    adapters = after(adapters, far_low, far_high)
-    adapters = swap_all(jnp.broadcast_to(adapters[None], (16, 2 * columns)), ("y", "x"))
-    adapters = adapters.reshape(-1, columns)
-    across = shift(adapters, "co", 1)
-    adapters = jnp.where(
-        co == 0, jnp.stack([adapters, across]), jnp.stack([across, adapters])
-    ).reshape(N_DP, -1)
+    for axis, index in (("y", y), ("x", x)):
+        side = adapters.shape[0] // 4
+        total = lax.dynamic_slice_in_dim(adapters, index * side, side, 0)
+        for k in (1, 2, 3):
+            give = lax.dynamic_slice_in_dim(adapters, ((index + k) % 4) * side, side, 0)
+            total = total + shift(give, axis, k)
+        adapters = total
+    adapters = adapters + shift(adapters, "zl", 1)
+
+    where = jnp.stack([x, zl, co, y]).astype(jnp.int32)
+    weights = (own_rows, other_rows, own_swap, other_swap)
+    tile = tile_of(where, scaled, far_low, far_high, ratio.reshape(1, -1), weights)
+    adapters = after(adapters, tile)
+    tile = swap_all(tile.reshape(16, tokens, part), ("x", "t"))
+
+    for axis, index in (("x", x), ("y", y), ("co", co)):
+        n = SIZES[axis]
+        side = adapters.shape[0]
+        total = jnp.zeros((n * side, adapters.shape[1]), F32)
+        for k in range(n):
+            got = shift(adapters, axis, k) if k else adapters
+            total = lax.dynamic_update_slice(total, got, (((index - k) % n) * side, 0))
+        adapters = total
     out_grad = adapters[:, :width]
     in_grad = adapters[:, width : width + features].T
     mag_grad = adapters[:, width + features :].reshape(-1) / col_norm
 
-    where = jnp.stack([x, zl, co]).astype(jnp.int32)
-    weights = (own_rows, other_rows, own_swap, other_swap)
-    tile = tile_of(where, scaled, far_low, far_high, ratio.reshape(1, -1), weights)
-    tile = swap_all(tile.reshape(16, tokens, part), ("x", "t"))
-
     tile = jnp.sum(tile.reshape(4, 4, tokens, part).astype(F32), axis=1).astype(BF)
     grad_in = tile.transpose(1, 0, 2).reshape(tokens, features)
     return grad_in, in_grad, out_grad, mag_grad

time: 202 us -> 179 us (0.89)
  the two profiles are of different devices: /device:TPU:8 before, /device:TPU:32 now
where the time goes in v4:
time: 179 us; the launch traced here: 178 us
  waiting for transfers between devices  76.1 us (43%)
  starting transfers between devices  58.8 us (33%)
  local copies, waits for them, and re-layouts  19.5 us (11%)
  Pallas kernels  13.6 us (8%)
  other arithmetic  6.46 us (4%)
  matrix products  2.53 us (1%)
    ppermute x41, waiting for transfers between devices, shift(): return lax.ppermute(value, axis, [(i, (i + step) % n) for i in range(n)])  54.6 us
    ppermute x41, starting transfers between devices, shift(): return lax.ppermute(value, axis, [(i, (i + step) % n) for i in range(n)])  53.7 us
    all_to_all x1, waiting for transfers between devices, swap_all(): return lax.all_to_all(value, axes, 0, 0, tiled=True)  21.5 us
    unnamed x41, local copies, waits for them, and re-layouts  9.42 us
    pallas_call x1, Pallas kernels, tile_of(): pl.pallas_call(tile_kernel, grid_spec=pltpu.PrefetchScalarGridSpec(num_sc...  9.35 us
    all_to_all x1, starting transfers between devices, swap_all(): return lax.all_to_all(value, axes, 0, 0, tiled=True)  5.1 us
    dynamic_update_slice x10, local copies, waits for them, and re-layouts, on_device(): total = lax.dynamic_update_slice(total, got, ((index - k) % n * side, 0))  5.02 us
    pallas_call x1, Pallas kernels, merge(): pl.pallas_call(body, grid=(steps,), in_specs=[columns(rows), whole(count,...  4.23 us
  transfers between devices with their start and end apart: 42, of which 19 were waited for; matrix products, arithmetic and copies ran while one was open for 11% of the time, Pallas kernels for 0%

profile of v4, /device:TPU:32, one launch (start us, length us, event | category | flops | bytes accessed | tf_op | source)
XLA Modules:
  0.0 178.3 jit_solution(7889003161462115755)
XLA Ops:
  2.5 4.2 %shard_map.111 = (bf16[64,3584]{1,0:T(8,128)(2,1)}, f32[1,3584]{1,0:T(1,128)}) custom-call(s32[64,3584]{1,0:T(8,128)} %refs_0_.1, f32[56,64]{1,0:T(8,128)} %bitcast.44, bf16[64,64]{1,0:T(8,128)(2,1)} %copy.17.refs_2_, bf16[64,3584]{1,0:T(8,128)(2,1)} %refs_3_.1), custom_call_target="tpu_custom_call" | custom-call | tf_op jit(solution)/shard_map/pallas_call | solution.py:65
  7.5 3.1 %collective-permute-start.7 = (f32[28,128]{1,0:T(8,128)S(1)}, f32[28,128]{1,0:T(8,128)S(1)}, u32[]{:S(2)}, u32[]{:S(2)}) collective-permute-start(f32[28,128]{1,0:T(8,128)S(1)} %bitcast.41), channel_id=1, source_target_pairs={{0,192},{64,0},{128,64},{192,128},{1,193},{65,1},{129,65},{193,129... | collective-permute-start | bytes 43016 | tf_op jit(solution)/shard_map/ppermute | solution.py:18
  14.8 1.7 collective-permute-start.1
  16.9 1.9 %collective-permute-start.3 = (bf16[64,3584]{1,0:T(8,128)(2,1)S(1)}, bf16[64,3584]{1,0:T(8,128)(2,1)S(1)}, u32[]{:S(2)}, u32[]{:S(2)}) collective-permute-start(bf16[64,3584]{1,0:T(8,128)(2,1)S(1)} %copy-done.6), channel_id=1, source_target_pairs={{0,64},{64,128},{128,192},{192,0},{1,65},{65,129},{129,193},{193,1... | collective-permute-start | bytes 1376264 | tf_op jit(solution)/shard_map/ppermute | solution.py:18
  20.1 9.5 %collective-permute-done.2 = bf16[64,3584]{1,0:T(8,128)(2,1)S(1)} collective-permute-done((bf16[64,3584]{1,0:T(8,128)(2,1)S(1)}, bf16[64,3584]{1,0:T(8,128)(2,1)S(1)}, u32[]{:S(2)}, u32[]{:S(2)}) %collective-permute-start.2) | collective-permute-done | bytes 458784 | tf_op jit(solution)/shard_map/ppermute | solution.py:18
  32.2 1.8 collective-permute-start.14
  35.6 2.8 %collective-permute-start.12 = (bf16[64,3584]{1,0:T(8,128)(2,1)S(1)}, bf16[64,3584]{1,0:T(8,128)(2,1)S(1)}, u32[]{:S(2)}, u32[]{:S(2)}) collective-permute-start(bf16[64,3584]{1,0:T(8,128)(2,1)S(1)} %collective-permute-done.2), channel_id=1, source_target_pairs={{0,192},{64,0},{128,64},{192,128},{1,193},{65,1},{129,65},{193,129... | collective-permute-start | bytes 1376264 | tf_op jit(solution)/shard_map/ppermute | solution.py:18
  39.1 2.5 %collective-permute-start.10 = (bf16[96,3584]{1,0:T(8,128)(2,1)}, bf16[96,3584]{1,0:T(8,128)(2,1)}, u32[]{:S(2)}, u32[]{:S(2)}) collective-permute-start(bf16[96,3584]{1,0:T(8,128)(2,1)} %get-tuple-element.30), channel_id=1, source_target_pairs={{0,48},{16,0},{32,16},{48,32},{1,49},{17,1},{33,17},{49,33},{2,50}... | collective-permute-start | bytes 2064392 | tf_op jit(solution)/shard_map/ppermute | solution.py:18
  41.9 1.7 fusion.1
  43.7 6.2 %collective-permute-done.11 = bf16[64,3584]{1,0:T(8,128)(2,1)S(1)} collective-permute-done((bf16[64,3584]{1,0:T(8,128)(2,1)S(1)}, bf16[64,3584]{1,0:T(8,128)(2,1)S(1)}, u32[]{:S(2)}, u32[]{:S(2)}) %collective-permute-start.11) | collective-permute-done | bytes 458784 | tf_op jit(solution)/shard_map/ppermute | solution.py:18
  49.9 7.6 %collective-permute-done.13 = bf16[64,3584]{1,0:T(8,128)(2,1)S(1)} collective-permute-done((bf16[64,3584]{1,0:T(8,128)(2,1)}, bf16[64,3584]{1,0:T(8,128)(2,1)S(1)}, u32[]{:S(2)}, u32[]{:S(2)}) %collective-permute-start.13) | collective-permute-done | bytes 458784 | tf_op jit(solution)/shard_map/ppermute | solution.py:18
  57.5 2.2 %collective-permute-start.17 = (f32[28,128]{1,0:T(8,128)S(1)}, f32[28,128]{1,0:T(8,128)}, u32[]{:S(2)}, u32[]{:S(2)}) collective-permute-start(f32[28,128]{1,0:T(8,128)S(1)} %add.221), channel_id=1, source_target_pairs={{0,48},{16,0},{32,16},{48,32},{1,49},{17,1},{33,17},{49,33},{2,50}... | collective-permute-start | bytes 43016 | tf_op jit(solution)/shard_map/ppermute | solution.py:18
  61.8 3.2 %collective-permute-done.16 = f32[28,128]{1,0:T(8,128)} collective-permute-done((f32[28,128]{1,0:T(8,128)S(1)}, f32[28,128]{1,0:T(8,128)}, u32[]{:S(2)}, u32[]{:S(2)}) %collective-permute-start.16) | collective-permute-done | bytes 14368 | tf_op jit(solution)/shard_map/ppermute | solution.py:18
  67.0 1.6 fusion.5
  68.7 5.5 %collective-permute-start.25 = (bf16[192,128]{0,1:T(8,128)(2,1)S(1)}, bf16[192,128]{0,1:T(8,128)(2,1)S(1)}, u32[]{:S(2)}, u32[]{:S(2)}) collective-permute-start(bf16[192,128]{0,1:T(8,128)(2,1)S(1)} %pad_maximum_fusion.3), channel_id=1, source_target_pairs={{0,3},{1,0},{2,1},{3,2},{4,7},{5,4},{6,5},{7,6},{8,11},{9,8},{10,9... | collective-permute-start | bytes 147464 | tf_op jit(solution)/shard_map/ppermute | solution.py:18
  75.6 2.4 %collective-permute-start.23 = (bf16[192,128]{0,1:T(8,128)(2,1)S(1)}, bf16[192,128]{0,1:T(8,128)(2,1)S(1)}, u32[]{:S(2)}, u32[]{:S(2)}) collective-permute-start(bf16[192,128]{0,1:T(8,128)(2,1)S(1)} %pad_maximum_fusion.3), channel_id=1, source_target_pairs={{0,1},{1,2},{2,3},{3,0},{4,5},{5,6},{6,7},{7,4},{8,9},{9,10},{10,1... | collective-permute-start | bytes 147464 | tf_op jit(solution)/shard_map/ppermute | solution.py:18
  78.9 3.2 %collective-permute-start.19 = (bf16[96,3584]{1,0:T(8,128)(2,1)S(1)}, bf16[96,3584]{1,0:T(8,128)(2,1)S(1)}, u32[]{:S(2)}, u32[]{:S(2)}) collective-permute-start(bf16[96,3584]{1,0:T(8,128)(2,1)S(1)} %collective-permute-done.1), channel_id=1, source_target_pairs={{0,48},{16,0},{32,16},{48,32},{1,49},{17,1},{33,17},{49,33},{2,50}... | collective-permute-start | bytes 2064392 | tf_op jit(solution)/shard_map/ppermute | solution.py:18
  83.4 2.0 %constant_dynamic-update-slice_fusion.2 = bf16[576,3584]{1,0:T(8,128)(2,1)} fusion(bf16[576,3584]{1,0:T(8,128)(2,1)} %constant_dynamic-update-slice_fusion.3, bf16[96,3584]{1,0:T(8,128)(2,1)} %collective-permute-done.9), kind=kLoop, calls=%fused_computation.31 | loop fusion | bytes 1376256
  85.5 5.2 %collective-permute-done.20 = bf16[64,3584]{1,0:T(8,128)(2,1)S(1)} collective-permute-done((bf16[64,3584]{1,0:T(8,128)(2,1)S(1)}, bf16[64,3584]{1,0:T(8,128)(2,1)S(1)}, u32[]{:S(2)}, u32[]{:S(2)}) %collective-permute-start.20) | collective-permute-done | bytes 458784 | tf_op jit(solution)/shard_map/ppermute | solution.py:18
  98.5 4.6 %collective-permute-done.29 = f32[8,4664]{1,0:T(8,128)S(1)} collective-permute-done((f32[8,4664]{1,0:T(8,128)S(1)}, f32[8,4664]{1,0:T(8,128)S(1)}, u32[]{:S(2)}, u32[]{:S(2)}) %collective-permute-start.29) | collective-permute-done | bytes 149280 | tf_op jit(solution)/shard_map/ppermute | solution.py:18
  103.1 2.3 %collective-permute-done.28 = f32[8,4664]{1,0:T(8,128)S(1)} collective-permute-done((f32[8,4664]{1,0:T(8,128)S(1)}, f32[8,4664]{1,0:T(8,128)S(1)}, u32[]{:S(2)}, u32[]{:S(2)}) %collective-permute-start.28) | collective-permute-done | bytes 149280 | tf_op jit(solution)/shard_map/ppermute | solution.py:18
  105.4 1.6 collective-permute-done.27
  107.1 3.8 %collective-permute-start.32 = (f32[2,4664]{1,0:T(2,128)S(1)}, f32[2,4664]{1,0:T(2,128)S(1)}, u32[]{:S(2)}, u32[]{:S(2)}) collective-permute-start(f32[2,4664]{1,0:T(2,128)S(1)} %get-tuple-element.52), channel_id=1, source_target_pairs={{0,48},{16,0},{32,16},{48,32},{1,49},{17,1},{33,17},{49,33},{2,50}... | collective-permute-start | bytes 111944 | tf_op jit(solution)/shard_map/ppermute | solution.py:18
  112.5 3.9 %collective-permute-done.31 = f32[2,4664]{1,0:T(2,128)S(1)} collective-permute-done((f32[2,4664]{1,0:T(2,128)S(1)}, f32[2,4664]{1,0:T(2,128)S(1)}, u32[]{:S(2)}, u32[]{:S(2)}) %collective-permute-start.31) | collective-permute-done | bytes 37344 | tf_op jit(solution)/shard_map/ppermute | solution.py:18
  118.4 2.2 %collective-permute-done.33 = f32[2,4664]{1,0:T(2,128)S(1)} collective-permute-done((f32[2,4664]{1,0:T(2,128)S(1)}, f32[2,4664]{1,0:T(2,128)S(1)}, u32[]{:S(2)}, u32[]{:S(2)}) %collective-permute-start.33) | collective-permute-done | bytes 37344 | tf_op jit(solution)/shard_map/ppermute | solution.py:18
  120.6 9.3 %shard_map.112 = bf16[4,4,192,256]{3,2,1,0:T(8,128)(2,1)} custom-call(s32[4]{0:T(128)S(1)} %pad_add_fusion.where, bf16[576,3584]{1,0:T(8,128)(2,1)S(1)} %multiply_convert_fusion.scaled, bf16[96,3584]{1,0:T(8,128)(2,1)S(1)} %collective-permute-done.18.far_low, bf16[96,3584]{1,0:T(8,128)(2,1)S(1)} %collective-permute-done.19.far_high, ...), custom_call_target="tpu_custom_call" | custom-call | flops 5637144576 | bytes 12845056 | tf_op jit(solution)/shard_map/pallas_call | solution.py:127
  129.9 2.3 %collective-permute-start.35 = (f32[2,4664]{1,0:T(2,128)S(1)}, f32[2,4664]{1,0:T(2,128)S(1)}, u32[]{:S(2)}, u32[]{:S(2)}) collective-permute-start(f32[2,4664]{1,0:T(2,128)S(1)} %add.260), channel_id=1, source_target_pairs={{0,32},{16,48},{32,0},{48,16},{1,33},{17,49},{33,1},{49,17},{2,34}... | collective-permute-start | bytes 111944 | tf_op jit(solution)/shard_map/ppermute | solution.py:18
  132.3 2.2 %collective-permute-start.36 = (f32[2,4664]{1,0:T(2,128)S(1)}, f32[2,4664]{1,0:T(2,128)S(1)}, u32[]{:S(2)}, u32[]{:S(2)}) collective-permute-start(f32[2,4664]{1,0:T(2,128)S(1)} %add.260), channel_id=1, source_target_pairs={{0,48},{16,0},{32,16},{48,32},{1,49},{17,1},{33,17},{49,33},{2,50}... | collective-permute-start | bytes 111944 | tf_op jit(solution)/shard_map/ppermute | solution.py:18
  134.5 5.1 %all-to-all-start = ((bf16[16,192,256]{2,1,0:T(8,128)(2,1)}), bf16[16,192,256]{2,1,0:T(8,128)(2,1)S(1)}, u32[]{:S(2)}, u32[]{:S(2)}) async-start(bf16[16,192,256]{2,1,0:T(8,128)(2,1)} %bitcast.14), calls=%async_computation | async-start | bytes 3145728 | tf_op jit(solution)/shard_map/all_to_all | solution.py:22
  139.9 2.1 %collective-permute-start.38 = (f32[8,4664]{1,0:T(8,128)S(1)}, f32[8,4664]{1,0:T(8,128)S(1)}, u32[]{:S(2)}, u32[]{:S(2)}) collective-permute-start(f32[8,4664]{1,0:T(8,128)S(1)} %constant_dynamic-update-slice_fusion.11), channel_id=1, source_target_pairs={{0,128},{64,192},{128,0},{192,64},{1,129},{65,193},{129,1},{193,65... | collective-permute-start | bytes 447752 | tf_op jit(solution)/shard_map/ppermute | solution.py:18
  144.6 3.2 %collective-permute-done.37 = f32[8,4664]{1,0:T(8,128)S(1)} collective-permute-done((f32[8,4664]{1,0:T(8,128)S(1)}, f32[8,4664]{1,0:T(8,128)S(1)}, u32[]{:S(2)}, u32[]{:S(2)}) %collective-permute-start.37) | collective-permute-done | bytes 149280 | tf_op jit(solution)/shard_map/ppermute | solution.py:18
  155.8 21.5 %all-to-all-done = bf16[16,192,256]{2,1,0:T(8,128)(2,1)S(1)} async-done(((bf16[16,192,256]{2,1,0:T(8,128)(2,1)}), bf16[16,192,256]{2,1,0:T(8,128)(2,1)S(1)}, u32[]{:S(2)}, u32[]{:S(2)}) %all-to-all-start) | async-done | bytes 1572896 | tf_op jit(solution)/shard_map/all_to_all | solution.py:22
  (145 shorter events, 44.5 us)
Async XLA Ops:
  7.5 9.1 %collective-permute-start.7 = (f32[28,128]{1,0:T(8,128)S(1)}, f32[28,128]{1,0:T(8,128)S(1)}, u32[]{:S(2)}, u32[]{:S(2)}) collective-permute-start(f32[28,128]{1,0:T(8,128)S(1)} %bitcast.41), channel_id=1, source_target_pairs={{0,192},{64,0},{128,64},{192,128},{1,193},{65,1},{129,65},{193,129... | collective-permute-start | bytes 43016 | tf_op jit(solution)/shard_map/ppermute | solution.py:18
  10.5 6.0 %collective-permute-start.6 = (f32[28,128]{1,0:T(8,128)S(1)}, f32[28,128]{1,0:T(8,128)S(1)}, u32[]{:S(2)}, u32[]{:S(2)}) collective-permute-start(f32[28,128]{1,0:T(8,128)S(1)} %bitcast.42), channel_id=1, source_target_pairs={{0,128},{64,192},{128,0},{192,64},{1,129},{65,193},{129,1},{193,65... | collective-permute-start | bytes 43016 | tf_op jit(solution)/shard_map/ppermute | solution.py:18
  13.3 17.9 %collective-permute-start = (bf16[96,3584]{1,0:T(8,128)(2,1)}, bf16[96,3584]{1,0:T(8,128)(2,1)S(1)}, u32[]{:S(2)}, u32[]{:S(2)}) collective-permute-start(bf16[96,3584]{1,0:T(8,128)(2,1)} %get-tuple-element.30), channel_id=1, source_target_pairs={{0,16},{16,32},{32,48},{48,0},{1,17},{17,33},{33,49},{49,1},{2,18}... | collective-permute-start | bytes 2064392 | tf_op jit(solution)/shard_map/ppermute | solution.py:18
  14.8 16.4 %collective-permute-start.1 = (bf16[96,3584]{1,0:T(8,128)(2,1)}, bf16[96,3584]{1,0:T(8,128)(2,1)S(1)}, u32[]{:S(2)}, u32[]{:S(2)}) collective-permute-start(bf16[96,3584]{1,0:T(8,128)(2,1)} %get-tuple-element.29), channel_id=1, source_target_pairs={{0,48},{16,0},{32,16},{48,32},{1,49},{17,1},{33,17},{49,33},{2,50}... | collective-permute-start | bytes 2064392 | tf_op jit(solution)/shard_map/ppermute | solution.py:18
  16.7 12.9 %collective-permute-start.2 = (bf16[64,3584]{1,0:T(8,128)(2,1)S(1)}, bf16[64,3584]{1,0:T(8,128)(2,1)S(1)}, u32[]{:S(2)}, u32[]{:S(2)}) collective-permute-start(bf16[64,3584]{1,0:T(8,128)(2,1)S(1)} %copy-done.6), channel_id=1, source_target_pairs={{0,8},{8,0},{1,9},{9,1},{2,10},{10,2},{3,11},{11,3},{4,12},{12,4},... | collective-permute-start | bytes 1376264 | tf_op jit(solution)/shard_map/ppermute | solution.py:18
  16.9 13.9 %collective-permute-start.3 = (bf16[64,3584]{1,0:T(8,128)(2,1)S(1)}, bf16[64,3584]{1,0:T(8,128)(2,1)S(1)}, u32[]{:S(2)}, u32[]{:S(2)}) collective-permute-start(bf16[64,3584]{1,0:T(8,128)(2,1)S(1)} %copy-done.6), channel_id=1, source_target_pairs={{0,64},{64,128},{128,192},{192,0},{1,65},{65,129},{129,193},{193,1... | collective-permute-start | bytes 1376264 | tf_op jit(solution)/shard_map/ppermute | solution.py:18
  18.8 12.4 %collective-permute-start.4 = (bf16[64,3584]{1,0:T(8,128)(2,1)S(1)}, bf16[64,3584]{1,0:T(8,128)(2,1)S(1)}, u32[]{:S(2)}, u32[]{:S(2)}) collective-permute-start(bf16[64,3584]{1,0:T(8,128)(2,1)S(1)} %copy-done.6), channel_id=1, source_target_pairs={{0,192},{64,0},{128,64},{192,128},{1,193},{65,1},{129,65},{193,129... | collective-permute-start | bytes 1376264 | tf_op jit(solution)/shard_map/ppermute | solution.py:18
  32.2 9.5 %collective-permute-start.14 = (f32[28,128]{1,0:T(8,128)S(1)}, f32[28,128]{1,0:T(8,128)S(1)}, u32[]{:S(2)}, u32[]{:S(2)}) collective-permute-start(f32[28,128]{1,0:T(8,128)S(1)} %add.220), channel_id=1, source_target_pairs={{0,8},{8,0},{1,9},{9,1},{2,10},{10,2},{3,11},{11,3},{4,12},{12,4},... | collective-permute-start | bytes 43016 | tf_op jit(solution)/shard_map/ppermute | solution.py:18
  35.2 14.7 %collective-permute-start.11 = (bf16[64,3584]{1,0:T(8,128)(2,1)S(1)}, bf16[64,3584]{1,0:T(8,128)(2,1)S(1)}, u32[]{:S(2)}, u32[]{:S(2)}) collective-permute-start(bf16[64,3584]{1,0:T(8,128)(2,1)S(1)} %collective-permute-done.2), channel_id=1, source_target_pairs={{0,64},{64,128},{128,192},{192,0},{1,65},{65,129},{129,193},{193,1... | collective-permute-start | bytes 1376264 | tf_op jit(solution)/shard_map/ppermute | solution.py:18
  35.6 14.2 %collective-permute-start.12 = (bf16[64,3584]{1,0:T(8,128)(2,1)S(1)}, bf16[64,3584]{1,0:T(8,128)(2,1)S(1)}, u32[]{:S(2)}, u32[]{:S(2)}) collective-permute-start(bf16[64,3584]{1,0:T(8,128)(2,1)S(1)} %collective-permute-done.2), channel_id=1, source_target_pairs={{0,192},{64,0},{128,64},{192,128},{1,193},{65,1},{129,65},{193,129... | collective-permute-start | bytes 1376264 | tf_op jit(solution)/shard_map/ppermute | solution.py:18
  38.4 27.9 %collective-permute-start.9 = (bf16[96,3584]{1,0:T(8,128)(2,1)}, bf16[96,3584]{1,0:T(8,128)(2,1)}, u32[]{:S(2)}, u32[]{:S(2)}) collective-permute-start(bf16[96,3584]{1,0:T(8,128)(2,1)} %get-tuple-element.29), channel_id=1, source_target_pairs={{0,16},{16,32},{32,48},{48,0},{1,17},{17,33},{33,49},{49,1},{2,18}... | collective-permute-start | bytes 2064392 | tf_op jit(solution)/shard_map/ppermute | solution.py:18
  39.1 27.2 %collective-permute-start.10 = (bf16[96,3584]{1,0:T(8,128)(2,1)}, bf16[96,3584]{1,0:T(8,128)(2,1)}, u32[]{:S(2)}, u32[]{:S(2)}) collective-permute-start(bf16[96,3584]{1,0:T(8,128)(2,1)} %get-tuple-element.30), channel_id=1, source_target_pairs={{0,48},{16,0},{32,16},{48,32},{1,49},{17,1},{33,17},{49,33},{2,50}... | collective-permute-start | bytes 2064392 | tf_op jit(solution)/shard_map/ppermute | solution.py:18
  41.7 15.8 %collective-permute-start.13 = (bf16[64,3584]{1,0:T(8,128)(2,1)}, bf16[64,3584]{1,0:T(8,128)(2,1)S(1)}, u32[]{:S(2)}, u32[]{:S(2)}) collective-permute-start(bf16[64,3584]{1,0:T(8,128)(2,1)} %copy-done.12), channel_id=1, source_target_pairs={{0,64},{64,128},{128,192},{192,0},{1,65},{65,129},{129,193},{193,1... | collective-permute-start | bytes 1376264 | tf_op jit(solution)/shard_map/ppermute | solution.py:18
  68.7 13.4 %collective-permute-start.25 = (bf16[192,128]{0,1:T(8,128)(2,1)S(1)}, bf16[192,128]{0,1:T(8,128)(2,1)S(1)}, u32[]{:S(2)}, u32[]{:S(2)}) collective-permute-start(bf16[192,128]{0,1:T(8,128)(2,1)S(1)} %pad_maximum_fusion.3), channel_id=1, source_target_pairs={{0,3},{1,0},{2,1},{3,2},{4,7},{5,4},{6,5},{7,6},{8,11},{9,8},{10,9... | collective-permute-start | bytes 147464 | tf_op jit(solution)/shard_map/ppermute | solution.py:18
  74.2 11.2 %collective-permute-start.24 = (bf16[192,128]{0,1:T(8,128)(2,1)S(1)}, bf16[192,128]{0,1:T(8,128)(2,1)S(1)}, u32[]{:S(2)}, u32[]{:S(2)}) collective-permute-start(bf16[192,128]{0,1:T(8,128)(2,1)S(1)} %pad_maximum_fusion.3), channel_id=1, source_target_pairs={{0,2},{1,3},{2,0},{3,1},{4,6},{5,7},{6,4},{7,5},{8,10},{9,11},{10,... | collective-permute-start | bytes 147464 | tf_op jit(solution)/shard_map/ppermute | solution.py:18
  75.6 9.8 %collective-permute-start.23 = (bf16[192,128]{0,1:T(8,128)(2,1)S(1)}, bf16[192,128]{0,1:T(8,128)(2,1)S(1)}, u32[]{:S(2)}, u32[]{:S(2)}) collective-permute-start(bf16[192,128]{0,1:T(8,128)(2,1)S(1)} %pad_maximum_fusion.3), channel_id=1, source_target_pairs={{0,1},{1,2},{2,3},{3,0},{4,5},{5,6},{6,7},{7,4},{8,9},{9,10},{10,1... | collective-permute-start | bytes 147464 | tf_op jit(solution)/shard_map/ppermute | solution.py:18
  78.0 14.2 %collective-permute-start.18 = (bf16[96,3584]{1,0:T(8,128)(2,1)S(1)}, bf16[96,3584]{1,0:T(8,128)(2,1)S(1)}, u32[]{:S(2)}, u32[]{:S(2)}) collective-permute-start(bf16[96,3584]{1,0:T(8,128)(2,1)S(1)} %copy-done.5), channel_id=1, source_target_pairs={{0,16},{16,32},{32,48},{48,0},{1,17},{17,33},{33,49},{49,1},{2,18}... | collective-permute-start | bytes 2064392 | tf_op jit(solution)/shard_map/ppermute | solution.py:18
  78.9 13.4 %collective-permute-start.19 = (bf16[96,3584]{1,0:T(8,128)(2,1)S(1)}, bf16[96,3584]{1,0:T(8,128)(2,1)S(1)}, u32[]{:S(2)}, u32[]{:S(2)}) collective-permute-start(bf16[96,3584]{1,0:T(8,128)(2,1)S(1)} %collective-permute-done.1), channel_id=1, source_target_pairs={{0,48},{16,0},{32,16},{48,32},{1,49},{17,1},{33,17},{49,33},{2,50}... | collective-permute-start | bytes 2064392 | tf_op jit(solution)/shard_map/ppermute | solution.py:18
  82.1 8.5 %collective-permute-start.20 = (bf16[64,3584]{1,0:T(8,128)(2,1)S(1)}, bf16[64,3584]{1,0:T(8,128)(2,1)S(1)}, u32[]{:S(2)}, u32[]{:S(2)}) collective-permute-start(bf16[64,3584]{1,0:T(8,128)(2,1)S(1)} %copy-done.11), channel_id=1, source_target_pairs={{0,192},{64,0},{128,64},{192,128},{1,193},{65,1},{129,65},{193,129... | collective-permute-start | bytes 1376264 | tf_op jit(solution)/shard_map/ppermute | solution.py:18
  96.3 6.8 %collective-permute-start.29 = (f32[8,4664]{1,0:T(8,128)S(1)}, f32[8,4664]{1,0:T(8,128)S(1)}, u32[]{:S(2)}, u32[]{:S(2)}) collective-permute-start(f32[8,4664]{1,0:T(8,128)S(1)} %get-tuple-element.49), channel_id=1, source_target_pairs={{0,192},{64,0},{128,64},{192,128},{1,193},{65,1},{129,65},{193,129... | collective-permute-start | bytes 447752 | tf_op jit(solution)/shard_map/ppermute | solution.py:18
  97.4 8.0 %collective-permute-start.28 = (f32[8,4664]{1,0:T(8,128)S(1)}, f32[8,4664]{1,0:T(8,128)S(1)}, u32[]{:S(2)}, u32[]{:S(2)}) collective-permute-start(f32[8,4664]{1,0:T(8,128)S(1)} %get-tuple-element.50), channel_id=1, source_target_pairs={{0,128},{64,192},{128,0},{192,64},{1,129},{65,193},{129,1},{193,65... | collective-permute-start | bytes 447752 | tf_op jit(solution)/shard_map/ppermute | solution.py:18
  97.4 9.6 %collective-permute-start.27 = (f32[8,4664]{1,0:T(8,128)S(1)}, f32[8,4664]{1,0:T(8,128)S(1)}, u32[]{:S(2)}, u32[]{:S(2)}) collective-permute-start(f32[8,4664]{1,0:T(8,128)S(1)} %get-tuple-element.48), channel_id=1, source_target_pairs={{0,64},{64,128},{128,192},{192,0},{1,65},{65,129},{129,193},{193,1... | collective-permute-start | bytes 447752 | tf_op jit(solution)/shard_map/ppermute | solution.py:18
  98.4 22.1 %collective-permute-start.21 = (bf16[4,64,3584]{2,1,0:T(8,128)(2,1)S(1)}, bf16[4,64,3584]{2,1,0:T(8,128)(2,1)S(1)}, u32[]{:S(2)}, u32[]{:S(2)}) collective-permute-start(bf16[4,64,3584]{2,1,0:T(8,128)(2,1)S(1)} %pad_maximum_fusion.own), channel_id=1, source_target_pairs={{0,4},{4,0},{1,5},{5,1},{2,6},{6,2},{3,7},{7,3},{8,12},{12,8},{9,1... | collective-permute-start | bytes 5505032 | tf_op jit(solution)/shard_map/ppermute | solution.py:18
  110.8 5.6 %collective-permute-start.30 = (f32[2,4664]{1,0:T(2,128)S(1)}, f32[2,4664]{1,0:T(2,128)S(1)}, u32[]{:S(2)}, u32[]{:S(2)}) collective-permute-start(f32[2,4664]{1,0:T(2,128)S(1)} %get-tuple-element.51), channel_id=1, source_target_pairs={{0,16},{16,32},{32,48},{48,0},{1,17},{17,33},{33,49},{49,1},{2,18}... | collective-permute-start | bytes 111944 | tf_op jit(solution)/shard_map/ppermute | solution.py:18
  112.3 8.3 %collective-permute-start.22 = (bf16[4,64,3584]{2,1,0:T(8,128)(2,1)S(1)}, bf16[4,64,3584]{2,1,0:T(8,128)(2,1)S(1)}, u32[]{:S(2)}, u32[]{:S(2)}) collective-permute-start(bf16[4,64,3584]{2,1,0:T(8,128)(2,1)S(1)} %pad_maximum_fusion.1.other), channel_id=1, source_target_pairs={{0,4},{4,0},{1,5},{5,1},{2,6},{6,2},{3,7},{7,3},{8,12},{12,8},{9,1... | collective-permute-start | bytes 5505032 | tf_op jit(solution)/shard_map/ppermute | solution.py:18
  129.9 9.7 %collective-permute-start.34 = (f32[2,4664]{1,0:T(2,128)S(1)}, f32[2,4664]{1,0:T(2,128)S(1)}, u32[]{:S(2)}, u32[]{:S(2)}) collective-permute-start(f32[2,4664]{1,0:T(2,128)S(1)} %add.260), channel_id=1, source_target_pairs={{0,16},{16,32},{32,48},{48,0},{1,17},{17,33},{33,49},{49,1},{2,18}... | collective-permute-start | bytes 111944 | tf_op jit(solution)/shard_map/ppermute | solution.py:18
  129.9 9.7 %collective-permute-start.35 = (f32[2,4664]{1,0:T(2,128)S(1)}, f32[2,4664]{1,0:T(2,128)S(1)}, u32[]{:S(2)}, u32[]{:S(2)}) collective-permute-start(f32[2,4664]{1,0:T(2,128)S(1)} %add.260), channel_id=1, source_target_pairs={{0,32},{16,48},{32,0},{48,16},{1,33},{17,49},{33,1},{49,17},{2,34}... | collective-permute-start | bytes 111944 | tf_op jit(solution)/shard_map/ppermute | solution.py:18
  132.3 7.5 %collective-permute-start.36 = (f32[2,4664]{1,0:T(2,128)S(1)}, f32[2,4664]{1,0:T(2,128)S(1)}, u32[]{:S(2)}, u32[]{:S(2)}) collective-permute-start(f32[2,4664]{1,0:T(2,128)S(1)} %add.260), channel_id=1, source_target_pairs={{0,48},{16,0},{32,16},{48,32},{1,49},{17,1},{33,17},{49,33},{2,50}... | collective-permute-start | bytes 111944 | tf_op jit(solution)/shard_map/ppermute | solution.py:18
  134.5 42.8 %all-to-all-start = ((bf16[16,192,256]{2,1,0:T(8,128)(2,1)}), bf16[16,192,256]{2,1,0:T(8,128)(2,1)S(1)}, u32[]{:S(2)}, u32[]{:S(2)}) async-start(bf16[16,192,256]{2,1,0:T(8,128)(2,1)} %bitcast.14), calls=%async_computation | async-start | bytes 3145728 | tf_op jit(solution)/shard_map/all_to_all | solution.py:22
  139.8 8.1 %collective-permute-start.37 = (f32[8,4664]{1,0:T(8,128)S(1)}, f32[8,4664]{1,0:T(8,128)S(1)}, u32[]{:S(2)}, u32[]{:S(2)}) collective-permute-start(f32[8,4664]{1,0:T(8,128)S(1)} %constant_dynamic-update-slice_fusion.11), channel_id=1, source_target_pairs={{0,64},{64,128},{128,192},{192,0},{1,65},{65,129},{129,193},{193,1... | collective-permute-start | bytes 447752 | tf_op jit(solution)/shard_map/ppermute | solution.py:18
  139.9 8.7 %collective-permute-start.38 = (f32[8,4664]{1,0:T(8,128)S(1)}, f32[8,4664]{1,0:T(8,128)S(1)}, u32[]{:S(2)}, u32[]{:S(2)}) collective-permute-start(f32[8,4664]{1,0:T(8,128)S(1)} %constant_dynamic-update-slice_fusion.11), channel_id=1, source_target_pairs={{0,128},{64,192},{128,0},{192,64},{1,129},{65,193},{129,1},{193,65... | collective-permute-start | bytes 447752 | tf_op jit(solution)/shard_map/ppermute | solution.py:18
  141.9 7.3 %collective-permute-start.39 = (f32[8,4664]{1,0:T(8,128)S(1)}, f32[8,4664]{1,0:T(8,128)S(1)}, u32[]{:S(2)}, u32[]{:S(2)}) collective-permute-start(f32[8,4664]{1,0:T(8,128)S(1)} %constant_dynamic-update-slice_fusion.11), channel_id=1, source_target_pairs={{0,192},{64,0},{128,64},{192,128},{1,193},{65,1},{129,65},{193,129... | collective-permute-start | bytes 447752 | tf_op jit(solution)/shard_map/ppermute | solution.py:18
  (28 other events, 182.8 us)

commit v5 on v4

--- a/solution.py
+++ b/solution.py
@@ -76,7 +76,7 @@
 
 
 def tile_kernel(
-    where, scaled, far_low, far_high, ratio, own, other, own_swap, other_swap, out, wide, far
+    where, scaled, far_low, far_high, ratio, own, other, own_swap, other_swap, first, second, wide, far
 ):
     rows = own.shape[1]
     half = far_low.shape[0]
@@ -106,8 +106,11 @@
     n = 2 * half
     tile = product(scaled[...])
     for k, e in enumerate((0, 3, 1)):
-        out[lax.rem(x + e, 4), 0] = tile[k * n : (k + 1) * n, :]
-    out[lax.rem(x + 2, 4), 0] = product(far[...])
+        first[lax.rem(x + e, 4), 0] = tile[k * n : k * n + half, :]
+        second[lax.rem(x + e, 4), 0] = tile[k * n + half : (k + 1) * n, :]
+    tile = product(far[...])
+    first[lax.rem(x + 2, 4), 0] = tile[:half, :]
+    second[lax.rem(x + 2, 4), 0] = tile[half:, :]
 
 
 def tile_of(where, scaled, far_low, far_high, ratio, weights):
@@ -132,10 +135,10 @@
             in_specs=[whole((tokens, width)), whole((half, width)), whole((half, width))]
             + [whole((1, width))]
             + [weight] * 4,
-            out_specs=pl.BlockSpec((4, 1, n, 4 * rows), place),
+            out_specs=[pl.BlockSpec((4, 1, half, 4 * rows), place)] * 2,
             scratch_shapes=[pltpu.VMEM((4 * rows, width), BF), pltpu.VMEM((n, width), BF)],
         ),
-        out_shape=jax.ShapeDtypeStruct((4, 4, n, 4 * rows), BF),
+        out_shape=[jax.ShapeDtypeStruct((4, 4, half, 4 * rows), BF)] * 2,
         compiler_params=pltpu.CompilerParams(vmem_limit_bytes=40 * 1024 * 1024),
         cost_estimate=pl.CostEstimate(
             flops=8 * n * 16 * rows * width,
@@ -168,7 +171,7 @@
     left_low, right_high = shift(low_half, "x", 1), shift(high_half, "x", -1)
     other = shift(own, "zl", 1)
     own_down, own_up = shift(own, "y", 1), shift(own, "y", -1)
-    total = gather_sum(gather_sum(squares.reshape(-1, 128), "y"), "co")
+    total = gather_sum(gather_sum(squares.reshape(-1, 128), "x"), "y")
     phase = (left_low, right_high, other, own_down, own_up, total, low_half, high_half)
     phase = lax.optimization_barrier(phase)
     left_low, right_high, other, own_down, own_up, total, low_half, high_half = phase
@@ -176,51 +179,59 @@
     left_high, right_low = shift(high_half, "x", 1), shift(low_half, "x", -1)
     other_down, other_up = shift(other, "y", 1), shift(other, "y", -1)
     own_far = shift(own_down, "y", 1)
-    total = after(gather_sum(total, "zl"), other_down, other_up, own_far)
-    total = gather_sum(total, "x")
+    total = gather_sum(gather_sum(total, "co"), "zl")
     phase = (left_low, right_high, left_high, right_low, other_down, other_up, own_far, total)
     phase = lax.optimization_barrier(phase)
     left_low, right_high, left_high, right_low, other_down, other_up, own_far, total = phase
 
     far_low, far_high = shift(left_low, "x", 1), shift(right_high, "x", -1)
     other_far = shift(other_up, "y", -1)
+    col_norm = jnp.sqrt(total.reshape(-1) + 1e-06)
+    ratio = magnitude / col_norm
+
+    def scaled_of(g):
+        return (g.astype(F32) * ratio).astype(BF)
+
+    scaled_own = scaled_of(grad)
+    scaled = scaled_of(
+        jnp.concatenate([grad, left_low, left_high, right_low, right_high], axis=0)
+    )
+
+    factor_cols = lax.dynamic_slice_in_dim(in_factor, t * features, features, 0)
+    hidden = jnp.dot(inputs, factor_cols, preferred_element_type=F32)
+    back = lax.dot_general(
+        scaled_own, out_factor, (((1,), (1,)), ((), ())), preferred_element_type=F32
+    )
+    low = jnp.concatenate([hidden, back], axis=1).astype(BF)
+    pieces = [shift(low, "t", k) for k in (1, 2, 3)]
+    low = sum((p.astype(F32) for p in pieces), low.astype(F32)).astype(BF)
+    hidden, back = low[:, :rank], low[:, rank:]
+    in_grad = SCALE * lax.dot_general(
+        back, inputs, (((0,), (0,)), ((), ())), preferred_element_type=F32
+    )
+    out_grad = SCALE * lax.dot_general(
+        hidden, scaled_own, (((0,), (0,)), ((), ())), preferred_element_type=F32
+    )
+    mag_sum = jnp.sum(grad.astype(F32) * pre.astype(F32), axis=0).reshape(N_DP, -1)
+    adapters = jnp.concatenate([out_grad, in_grad, mag_sum], axis=1)
+    phase = lax.optimization_barrier((far_low, far_high, other_far, adapters))
+    far_low, far_high, other_far, adapters = phase
     own_rows = jnp.stack([own, own_down, own_up, own_far])
     own_swap = shift(own_rows, "co", 1)
     other_rows = jnp.stack([other, other_down, other_up, other_far])
     other_swap = shift(other_rows, "co", 1)
-    col_norm = jnp.sqrt(total.reshape(-1) + 1e-06)
-    ratio = magnitude / col_norm
-
-    def scaled_of(g):
-        return (g.astype(F32) * ratio).astype(BF)
-
-    scaled_own = scaled_of(grad)
-    scaled = scaled_of(
-        jnp.concatenate([grad, left_low, left_high, right_low, right_high], axis=0)
-    )
-
-    factor_cols = lax.dynamic_slice_in_dim(in_factor, t * features, features, 0)
-    hidden = jnp.dot(inputs, factor_cols, preferred_element_type=F32)
-    back = lax.dot_general(
-        scaled_own, out_factor, (((1,), (1,)), ((), ())), preferred_element_type=F32
-    )
-    low = jnp.concatenate([hidden, back], axis=1).astype(BF)
-    pieces = [shift(low, "t", k) for k in (1, 2, 3)]
-    low = sum((p.astype(F32) for p in pieces), low.astype(F32)).astype(BF)
-    low = after(low, far_low, far_high, other_far)
-    hidden, back = low[:, :rank], low[:, rank:]
-    in_grad = SCALE * lax.dot_general(
-        back, inputs, (((0,), (0,)), ((), ())), preferred_element_type=F32
-    )
-    out_grad = SCALE * lax.dot_general(
-        hidden, scaled_own, (((0,), (0,)), ((), ())), preferred_element_type=F32
-    )
-    mag_sum = jnp.sum(grad.astype(F32) * pre.astype(F32), axis=0).reshape(N_DP, -1)
-    adapters = jnp.concatenate([out_grad, in_grad, mag_sum], axis=1)
     side = adapters.shape[0] // 2
     keep = lax.dynamic_slice_in_dim(adapters, co * side, side, 0)
     give = lax.dynamic_slice_in_dim(adapters, (1 - co) * side, side, 0)
     adapters = keep + shift(give, "co", 1)
+    adapters = adapters + shift(adapters, "zl", 1)
+
+    where = jnp.stack([x, zl, co, y]).astype(jnp.int32)
+    weights = (own_rows, other_rows, own_swap, other_swap)
+    tiles = tile_of(where, scaled, far_low, far_high, ratio.reshape(1, -1), weights)
+    adapters = after(adapters, tiles[0])
+    tiles = [swap_all(v.reshape(16, half, part), ("x", "t")) for v in tiles]
+
     for axis, index in (("y", y), ("x", x)):
         side = adapters.shape[0] // 4
         total = lax.dynamic_slice_in_dim(adapters, index * side, side, 0)
@@ -228,15 +239,10 @@
             give = lax.dynamic_slice_in_dim(adapters, ((index + k) % 4) * side, side, 0)
             total = total + shift(give, axis, k)
         adapters = total
-    adapters = adapters + shift(adapters, "zl", 1)
-
-    where = jnp.stack([x, zl, co, y]).astype(jnp.int32)
-    weights = (own_rows, other_rows, own_swap, other_swap)
-    tile = tile_of(where, scaled, far_low, far_high, ratio.reshape(1, -1), weights)
-    adapters = after(adapters, tile)
-    tile = swap_all(tile.reshape(16, tokens, part), ("x", "t"))
-
+    adapters = after(adapters, tiles[0])
     for axis, index in (("x", x), ("y", y), ("co", co)):
+        if axis == "co":
+            tiles[1] = after(tiles[1], adapters)
         n = SIZES[axis]
         side = adapters.shape[0]
         total = jnp.zeros((n * side, adapters.shape[1]), F32)
@@ -248,8 +254,10 @@
     in_grad = adapters[:, width : width + features].T
     mag_grad = adapters[:, width + features :].reshape(-1) / col_norm
 
-    tile = jnp.sum(tile.reshape(4, 4, tokens, part).astype(F32), axis=1).astype(BF)
-    grad_in = tile.transpose(1, 0, 2).reshape(tokens, features)
+    tiles = [jnp.sum(v.reshape(4, 4, half, part).astype(F32), axis=1).astype(BF) for v in tiles]
+    grad_in = jnp.concatenate(
+        [v.transpose(1, 0, 2).reshape(half, features) for v in tiles], axis=0
+    )
     return grad_in, in_grad, out_grad, mag_grad
 
 

time: 179 us -> 183 us (1.022)
  the two profiles are of different devices: /device:TPU:32 before, /device:TPU:8 now
where the time goes in v5:
time: 183 us; the launch traced here: 181 us
  starting transfers between devices  75.8 us (41%)
  waiting for transfers between devices  73.5 us (40%)
  Pallas kernels  13.6 us (7%)
  local copies, waits for them, and re-layouts  9.03 us (5%)
  other arithmetic  6.49 us (4%)
    ppermute x41, starting transfers between devices, shift(): return lax.ppermute(value, axis, [(i, (i + step) % n) for i in range(n)])  66.2 us
    ppermute x41, waiting for transfers between devices, shift(): return lax.ppermute(value, axis, [(i, (i + step) % n) for i in range(n)])  61.2 us
    all_to_all x2, waiting for transfers between devices, swap_all(): return lax.all_to_all(value, axes, 0, 0, tiled=True)  12.3 us
    all_to_all x2, starting transfers between devices, swap_all(): return lax.all_to_all(value, axes, 0, 0, tiled=True)  9.65 us
    pallas_call x1, Pallas kernels, tile_of(): pl.pallas_call(tile_kernel, grid_spec=pltpu.PrefetchScalarGridSpec(num_sc...  9.34 us
    unnamed x29, local copies, waits for them, and re-layouts  5.31 us
    pallas_call x1, Pallas kernels, merge(): pl.pallas_call(body, grid=(steps,), in_specs=[columns(rows), whole(count,...  4.25 us
  transfers between devices with their start and end apart: 43, of which 20 were waited for; matrix products, arithmetic and copies ran while one was open for 6% of the time, Pallas kernels for 0%

profile of v5, /device:TPU:8, one launch (start us, length us, event | category | flops | bytes accessed | tf_op | source)
XLA Modules:
  0.0 181.0 jit_solution(79020581072533282)
XLA Ops:
  2.5 4.3 %shard_map.111 = (bf16[64,3584]{1,0:T(8,128)(2,1)}, f32[1,3584]{1,0:T(1,128)}) custom-call(s32[64,3584]{1,0:T(8,128)} %refs_0_.1, f32[56,64]{1,0:T(8,128)} %bitcast.52, bf16[64,64]{1,0:T(8,128)(2,1)} %copy.18.refs_2_, bf16[64,3584]{1,0:T(8,128)(2,1)} %refs_3_.1), custom_call_target="tpu_custom_call" | custom-call | tf_op jit(solution)/shard_map/pallas_call | solution.py:65
  7.5 2.8 %collective-permute-start.7 = (f32[28,128]{1,0:T(8,128)S(1)}, f32[28,128]{1,0:T(8,128)S(1)}, u32[]{:S(2)}, u32[]{:S(2)}) collective-permute-start(f32[28,128]{1,0:T(8,128)S(1)} %bitcast.49), channel_id=1, source_target_pairs={{0,48},{16,0},{32,16},{48,32},{1,49},{17,1},{33,17},{49,33},{2,50}... | collective-permute-start | bytes 43016 | tf_op jit(solution)/shard_map/ppermute | solution.py:18
  13.2 1.8 collective-permute-start
  17.0 2.6 %collective-permute-start.9 = (f32[28,128]{1,0:T(8,128)S(1)}, f32[28,128]{1,0:T(8,128)S(1)}, u32[]{:S(2)}, u32[]{:S(2)}) collective-permute-start(f32[28,128]{1,0:T(8,128)S(1)} %add_add_fusion.3), channel_id=1, source_target_pairs={{0,128},{64,192},{128,0},{192,64},{1,129},{65,193},{129,1},{193,65... | collective-permute-start | bytes 43016 | tf_op jit(solution)/shard_map/ppermute | solution.py:18
  19.6 1.9 %collective-permute-start.8 = (f32[28,128]{1,0:T(8,128)S(1)}, f32[28,128]{1,0:T(8,128)S(1)}, u32[]{:S(2)}, u32[]{:S(2)}) collective-permute-start(f32[28,128]{1,0:T(8,128)S(1)} %add_add_fusion.3), channel_id=1, source_target_pairs={{0,64},{64,128},{128,192},{192,0},{1,65},{65,129},{129,193},{193,1... | collective-permute-start | bytes 43016 | tf_op jit(solution)/shard_map/ppermute | solution.py:18
  21.5 1.9 %collective-permute-start.2 = (bf16[64,3584]{1,0:T(8,128)(2,1)S(1)}, bf16[64,3584]{1,0:T(8,128)(2,1)S(1)}, u32[]{:S(2)}, u32[]{:S(2)}) collective-permute-start(bf16[64,3584]{1,0:T(8,128)(2,1)S(1)} %copy-done.3), channel_id=1, source_target_pairs={{0,8},{8,0},{1,9},{9,1},{2,10},{10,2},{3,11},{11,3},{4,12},{12,4},... | collective-permute-start | bytes 1376264 | tf_op jit(solution)/shard_map/ppermute | solution.py:18
  23.8 1.8 collective-permute-start.4
  27.4 4.3 %collective-permute-done.2 = bf16[64,3584]{1,0:T(8,128)(2,1)S(1)} collective-permute-done((bf16[64,3584]{1,0:T(8,128)(2,1)S(1)}, bf16[64,3584]{1,0:T(8,128)(2,1)S(1)}, u32[]{:S(2)}, u32[]{:S(2)}) %collective-permute-start.2) | collective-permute-done | bytes 458784 | tf_op jit(solution)/shard_map/ppermute | solution.py:18
  34.4 3.0 %collective-permute-start.12 = (bf16[96,3584]{1,0:T(8,128)(2,1)}, bf16[96,3584]{1,0:T(8,128)(2,1)}, u32[]{:S(2)}, u32[]{:S(2)}) collective-permute-start(bf16[96,3584]{1,0:T(8,128)(2,1)} %get-tuple-element.36), channel_id=1, source_target_pairs={{0,48},{16,0},{32,16},{48,32},{1,49},{17,1},{33,17},{49,33},{2,50}... | collective-permute-start | bytes 2064392 | tf_op jit(solution)/shard_map/ppermute | solution.py:18
  40.0 2.2 %collective-permute-start.13 = (bf16[64,3584]{1,0:T(8,128)(2,1)}, bf16[64,3584]{1,0:T(8,128)(2,1)S(1)}, u32[]{:S(2)}, u32[]{:S(2)}) collective-permute-start(bf16[64,3584]{1,0:T(8,128)(2,1)} %copy-done.4), channel_id=1, source_target_pairs={{0,64},{64,128},{128,192},{192,0},{1,65},{65,129},{129,193},{193,1... | collective-permute-start | bytes 1376264 | tf_op jit(solution)/shard_map/ppermute | solution.py:18
  42.9 2.3 %collective-permute-start.15 = (bf16[64,3584]{1,0:T(8,128)(2,1)}, bf16[64,3584]{1,0:T(8,128)(2,1)S(1)}, u32[]{:S(2)}, u32[]{:S(2)}) collective-permute-start(bf16[64,3584]{1,0:T(8,128)(2,1)} %copy-done.6), channel_id=1, source_target_pairs={{0,64},{64,128},{128,192},{192,0},{1,65},{65,129},{129,193},{193,1... | collective-permute-start | bytes 1376264 | tf_op jit(solution)/shard_map/ppermute | solution.py:18
  46.0 8.4 %collective-permute-done.13 = bf16[64,3584]{1,0:T(8,128)(2,1)S(1)} collective-permute-done((bf16[64,3584]{1,0:T(8,128)(2,1)}, bf16[64,3584]{1,0:T(8,128)(2,1)S(1)}, u32[]{:S(2)}, u32[]{:S(2)}) %collective-permute-start.13) | collective-permute-done | bytes 458784 | tf_op jit(solution)/shard_map/ppermute | solution.py:18
  55.7 7.7 %collective-permute-done.15 = bf16[64,3584]{1,0:T(8,128)(2,1)S(1)} collective-permute-done((bf16[64,3584]{1,0:T(8,128)(2,1)}, bf16[64,3584]{1,0:T(8,128)(2,1)S(1)}, u32[]{:S(2)}, u32[]{:S(2)}) %collective-permute-start.15) | collective-permute-done | bytes 458784 | tf_op jit(solution)/shard_map/ppermute | solution.py:18
  64.1 5.5 %collective-permute-start.23 = (bf16[192,128]{0,1:T(8,128)(2,1)S(1)}, bf16[192,128]{0,1:T(8,128)(2,1)S(1)}, u32[]{:S(2)}, u32[]{:S(2)}) collective-permute-start(bf16[192,128]{0,1:T(8,128)(2,1)S(1)} %pad_maximum_fusion.4), channel_id=1, source_target_pairs={{0,3},{1,0},{2,1},{3,2},{4,7},{5,4},{6,5},{7,6},{8,11},{9,8},{10,9... | collective-permute-start | bytes 147464 | tf_op jit(solution)/shard_map/ppermute | solution.py:18
  71.0 2.4 %collective-permute-start.21 = (bf16[192,128]{0,1:T(8,128)(2,1)S(1)}, bf16[192,128]{0,1:T(8,128)(2,1)S(1)}, u32[]{:S(2)}, u32[]{:S(2)}) collective-permute-start(bf16[192,128]{0,1:T(8,128)(2,1)S(1)} %pad_maximum_fusion.4), channel_id=1, source_target_pairs={{0,1},{1,2},{2,3},{3,0},{4,5},{5,6},{6,7},{7,4},{8,9},{9,10},{10,1... | collective-permute-start | bytes 147464 | tf_op jit(solution)/shard_map/ppermute | solution.py:18
  74.6 3.3 %collective-permute-start.19 = (bf16[96,3584]{1,0:T(8,128)(2,1)S(1)}, bf16[96,3584]{1,0:T(8,128)(2,1)S(1)}, u32[]{:S(2)}, u32[]{:S(2)}) collective-permute-start(bf16[96,3584]{1,0:T(8,128)(2,1)S(1)} %collective-permute-done.1), channel_id=1, source_target_pairs={{0,48},{16,0},{32,16},{48,32},{1,49},{17,1},{33,17},{49,33},{2,50}... | collective-permute-start | bytes 2064392 | tf_op jit(solution)/shard_map/ppermute | solution.py:18
  80.5 3.0 %collective-permute-start.20 = (bf16[64,3584]{1,0:T(8,128)(2,1)S(1)}, bf16[64,3584]{1,0:T(8,128)(2,1)S(1)}, u32[]{:S(2)}, u32[]{:S(2)}) collective-permute-start(bf16[64,3584]{1,0:T(8,128)(2,1)S(1)} %collective-permute-done.14), channel_id=1, source_target_pairs={{0,192},{64,0},{128,64},{192,128},{1,193},{65,1},{129,65},{193,129... | collective-permute-start | bytes 1376264 | tf_op jit(solution)/shard_map/ppermute | solution.py:18
  84.3 6.8 %collective-permute-done.20 = bf16[64,3584]{1,0:T(8,128)(2,1)S(1)} collective-permute-done((bf16[64,3584]{1,0:T(8,128)(2,1)S(1)}, bf16[64,3584]{1,0:T(8,128)(2,1)S(1)}, u32[]{:S(2)}, u32[]{:S(2)}) %collective-permute-start.20) | collective-permute-done | bytes 458784 | tf_op jit(solution)/shard_map/ppermute | solution.py:18
  95.3 14.0 %collective-permute-done.27 = f32[32,4664]{1,0:T(8,128)S(1)} collective-permute-done((f32[32,4664]{1,0:T(8,128)S(1)}, f32[32,4664]{1,0:T(8,128)S(1)}, u32[]{:S(2)}, u32[]{:S(2)}) %collective-permute-start.27) | collective-permute-done | bytes 597024 | tf_op jit(solution)/shard_map/ppermute | solution.py:18
  109.4 9.3 %shard_map.112 = (bf16[4,4,96,256]{3,2,1,0:T(8,128)(2,1)}, bf16[4,4,96,256]{3,2,1,0:T(8,128)(2,1)}) custom-call(s32[4]{0:T(128)S(1)} %pad_add_fusion.where, bf16[576,3584]{1,0:T(8,128)(2,1)S(1)} %multiply_convert_fusion.scaled, bf16[96,3584]{1,0:T(8,128)(2,1)S(1)} %collective-permute-done.18.far_low, bf16[96,3584]{1,0:T(8,128)(2,1)S(1)} %collective-permute-done.19.far_high, ...), custom_call_target="tpu_custom_call" | custom-call | flops 5637144576 | bytes 12845056 | tf_op jit(solution)/shard_map/pallas_call | solution.py:130
  118.8 2.6 %collective-permute-start.30 = (f32[8,4664]{1,0:T(8,128)S(1)}, f32[8,4664]{1,0:T(8,128)S(1)}, u32[]{:S(2)}, u32[]{:S(2)}) collective-permute-start(f32[8,4664]{1,0:T(8,128)S(1)} %get-tuple-element.61), channel_id=1, source_target_pairs={{0,192},{64,0},{128,64},{192,128},{1,193},{65,1},{129,65},{193,129... | collective-permute-start | bytes 447752 | tf_op jit(solution)/shard_map/ppermute | solution.py:18
  121.4 1.8 %collective-permute-start.29 = (f32[8,4664]{1,0:T(8,128)S(1)}, f32[8,4664]{1,0:T(8,128)S(1)}, u32[]{:S(2)}, u32[]{:S(2)}) collective-permute-start(f32[8,4664]{1,0:T(8,128)S(1)} %get-tuple-element.62), channel_id=1, source_target_pairs={{0,128},{64,192},{128,0},{192,64},{1,129},{65,193},{129,1},{193,65... | collective-permute-start | bytes 447752 | tf_op jit(solution)/shard_map/ppermute | solution.py:18
  123.2 2.5 %collective-permute-start.28 = (f32[8,4664]{1,0:T(8,128)S(1)}, f32[8,4664]{1,0:T(8,128)S(1)}, u32[]{:S(2)}, u32[]{:S(2)}) collective-permute-start(f32[8,4664]{1,0:T(8,128)S(1)} %get-tuple-element.60), channel_id=1, source_target_pairs={{0,64},{64,128},{128,192},{192,0},{1,65},{65,129},{129,193},{193,1... | collective-permute-start | bytes 447752 | tf_op jit(solution)/shard_map/ppermute | solution.py:18
  125.8 6.0 %all-to-all-start = ((bf16[16,96,256]{2,1,0:T(8,128)(2,1)}), bf16[16,96,256]{2,1,0:T(8,128)(2,1)S(1)}, u32[]{:S(2)}, u32[]{:S(2)}) async-start(bf16[16,96,256]{2,1,0:T(8,128)(2,1)} %bitcast.15), calls=%async_computation | async-start | bytes 1572864 | tf_op jit(solution)/shard_map/all_to_all | solution.py:22
  131.9 3.2 %collective-permute-start.33 = (f32[2,4664]{1,0:T(2,128)S(1)}, f32[2,4664]{1,0:T(2,128)S(1)}, u32[]{:S(2)}, u32[]{:S(2)}) collective-permute-start(f32[2,4664]{1,0:T(2,128)S(1)} %get-tuple-element.64), channel_id=1, source_target_pairs={{0,48},{16,0},{32,16},{48,32},{1,49},{17,1},{33,17},{49,33},{2,50}... | collective-permute-start | bytes 111944 | tf_op jit(solution)/shard_map/ppermute | solution.py:18
  138.0 2.6 %collective-permute-done.32 = f32[2,4664]{1,0:T(2,128)S(1)} collective-permute-done((f32[2,4664]{1,0:T(2,128)S(1)}, f32[2,4664]{1,0:T(2,128)S(1)}, u32[]{:S(2)}, u32[]{:S(2)}) %collective-permute-start.32) | collective-permute-done | bytes 37344 | tf_op jit(solution)/shard_map/ppermute | solution.py:18
  142.2 12.3 %all-to-all-done = bf16[16,96,256]{2,1,0:T(8,128)(2,1)S(1)} async-done(((bf16[16,96,256]{2,1,0:T(8,128)(2,1)}), bf16[16,96,256]{2,1,0:T(8,128)(2,1)S(1)}, u32[]{:S(2)}, u32[]{:S(2)}) %all-to-all-start) | async-done | bytes 786464 | tf_op jit(solution)/shard_map/all_to_all | solution.py:22
  154.5 3.6 %all-to-all-start.1 = ((bf16[16,96,256]{2,1,0:T(8,128)(2,1)}), bf16[16,96,256]{2,1,0:T(8,128)(2,1)S(1)}, u32[]{:S(2)}, u32[]{:S(2)}) async-start(bf16[16,96,256]{2,1,0:T(8,128)(2,1)} %bitcast.18), calls=%async_computation.1 | async-start | bytes 1572864 | tf_op jit(solution)/shard_map/all_to_all | solution.py:22
  158.1 1.8 %collective-permute-start.34 = (f32[2,4664]{1,0:T(2,128)S(1)}, f32[2,4664]{1,0:T(2,128)S(1)}, u32[]{:S(2)}, u32[]{:S(2)}) collective-permute-start(f32[2,4664]{1,0:T(2,128)S(1)} %add_add_fusion.1), channel_id=1, source_target_pairs={{0,16},{16,32},{32,48},{48,0},{1,17},{17,33},{33,49},{49,1},{2,18}... | collective-permute-start | bytes 111944 | tf_op jit(solution)/shard_map/ppermute | solution.py:18
  159.9 2.7 %collective-permute-start.35 = (f32[2,4664]{1,0:T(2,128)S(1)}, f32[2,4664]{1,0:T(2,128)S(1)}, u32[]{:S(2)}, u32[]{:S(2)}) collective-permute-start(f32[2,4664]{1,0:T(2,128)S(1)} %add_add_fusion.1), channel_id=1, source_target_pairs={{0,32},{16,48},{32,0},{48,16},{1,33},{17,49},{33,1},{49,17},{2,34}... | collective-permute-start | bytes 111944 | tf_op jit(solution)/shard_map/ppermute | solution.py:18
  164.3 2.3 %collective-permute-done.34 = f32[2,4664]{1,0:T(2,128)S(1)} collective-permute-done((f32[2,4664]{1,0:T(2,128)S(1)}, f32[2,4664]{1,0:T(2,128)S(1)}, u32[]{:S(2)}, u32[]{:S(2)}) %collective-permute-start.34) | collective-permute-done | bytes 37344 | tf_op jit(solution)/shard_map/ppermute | solution.py:18
  172.7 2.5 %collective-permute-done.38 = f32[8,4664]{1,0:T(8,128)S(1)} collective-permute-done((f32[8,4664]{1,0:T(8,128)S(1)}, f32[8,4664]{1,0:T(8,128)S(1)}, u32[]{:S(2)}, u32[]{:S(2)}) %collective-permute-start.38) | collective-permute-done | bytes 149280 | tf_op jit(solution)/shard_map/ppermute | solution.py:18
  (138 shorter events, 46.6 us)
Async XLA Ops:
  7.5 8.9 %collective-permute-start.7 = (f32[28,128]{1,0:T(8,128)S(1)}, f32[28,128]{1,0:T(8,128)S(1)}, u32[]{:S(2)}, u32[]{:S(2)}) collective-permute-start(f32[28,128]{1,0:T(8,128)S(1)} %bitcast.49), channel_id=1, source_target_pairs={{0,48},{16,0},{32,16},{48,32},{1,49},{17,1},{33,17},{49,33},{2,50}... | collective-permute-start | bytes 43016 | tf_op jit(solution)/shard_map/ppermute | solution.py:18
  13.2 20.9 %collective-permute-start = (bf16[96,3584]{1,0:T(8,128)(2,1)}, bf16[96,3584]{1,0:T(8,128)(2,1)}, u32[]{:S(2)}, u32[]{:S(2)}) collective-permute-start(bf16[96,3584]{1,0:T(8,128)(2,1)} %get-tuple-element.36), channel_id=1, source_target_pairs={{0,16},{16,32},{32,48},{48,0},{1,17},{17,33},{33,49},{49,1},{2,18}... | collective-permute-start | bytes 2064392 | tf_op jit(solution)/shard_map/ppermute | solution.py:18
  15.0 19.1 %collective-permute-start.1 = (bf16[96,3584]{1,0:T(8,128)(2,1)}, bf16[96,3584]{1,0:T(8,128)(2,1)S(1)}, u32[]{:S(2)}, u32[]{:S(2)}) collective-permute-start(bf16[96,3584]{1,0:T(8,128)(2,1)} %get-tuple-element.35), channel_id=1, source_target_pairs={{0,48},{16,0},{32,16},{48,32},{1,49},{17,1},{33,17},{49,33},{2,50}... | collective-permute-start | bytes 2064392 | tf_op jit(solution)/shard_map/ppermute | solution.py:18
  17.0 6.4 %collective-permute-start.9 = (f32[28,128]{1,0:T(8,128)S(1)}, f32[28,128]{1,0:T(8,128)S(1)}, u32[]{:S(2)}, u32[]{:S(2)}) collective-permute-start(f32[28,128]{1,0:T(8,128)S(1)} %add_add_fusion.3), channel_id=1, source_target_pairs={{0,128},{64,192},{128,0},{192,64},{1,129},{65,193},{129,1},{193,65... | collective-permute-start | bytes 43016 | tf_op jit(solution)/shard_map/ppermute | solution.py:18
  21.5 10.2 %collective-permute-start.2 = (bf16[64,3584]{1,0:T(8,128)(2,1)S(1)}, bf16[64,3584]{1,0:T(8,128)(2,1)S(1)}, u32[]{:S(2)}, u32[]{:S(2)}) collective-permute-start(bf16[64,3584]{1,0:T(8,128)(2,1)S(1)} %copy-done.3), channel_id=1, source_target_pairs={{0,8},{8,0},{1,9},{9,1},{2,10},{10,2},{3,11},{11,3},{4,12},{12,4},... | collective-permute-start | bytes 1376264 | tf_op jit(solution)/shard_map/ppermute | solution.py:18
  23.4 9.8 %collective-permute-start.3 = (bf16[64,3584]{1,0:T(8,128)(2,1)S(1)}, bf16[64,3584]{1,0:T(8,128)(2,1)S(1)}, u32[]{:S(2)}, u32[]{:S(2)}) collective-permute-start(bf16[64,3584]{1,0:T(8,128)(2,1)S(1)} %copy-done.3), channel_id=1, source_target_pairs={{0,64},{64,128},{128,192},{192,0},{1,65},{65,129},{129,193},{193,1... | collective-permute-start | bytes 1376264 | tf_op jit(solution)/shard_map/ppermute | solution.py:18
  23.8 10.3 %collective-permute-start.4 = (bf16[64,3584]{1,0:T(8,128)(2,1)S(1)}, bf16[64,3584]{1,0:T(8,128)(2,1)S(1)}, u32[]{:S(2)}, u32[]{:S(2)}) collective-permute-start(bf16[64,3584]{1,0:T(8,128)(2,1)S(1)} %copy-done.3), channel_id=1, source_target_pairs={{0,192},{64,0},{128,64},{192,128},{1,193},{65,1},{129,65},{193,129... | collective-permute-start | bytes 1376264 | tf_op jit(solution)/shard_map/ppermute | solution.py:18
  34.1 29.3 %collective-permute-start.11 = (bf16[96,3584]{1,0:T(8,128)(2,1)}, bf16[96,3584]{1,0:T(8,128)(2,1)}, u32[]{:S(2)}, u32[]{:S(2)}) collective-permute-start(bf16[96,3584]{1,0:T(8,128)(2,1)} %get-tuple-element.35), channel_id=1, source_target_pairs={{0,16},{16,32},{32,48},{48,0},{1,17},{17,33},{33,49},{49,1},{2,18}... | collective-permute-start | bytes 2064392 | tf_op jit(solution)/shard_map/ppermute | solution.py:18
  34.4 29.1 %collective-permute-start.12 = (bf16[96,3584]{1,0:T(8,128)(2,1)}, bf16[96,3584]{1,0:T(8,128)(2,1)}, u32[]{:S(2)}, u32[]{:S(2)}) collective-permute-start(bf16[96,3584]{1,0:T(8,128)(2,1)} %get-tuple-element.36), channel_id=1, source_target_pairs={{0,48},{16,0},{32,16},{48,32},{1,49},{17,1},{33,17},{49,33},{2,50}... | collective-permute-start | bytes 2064392 | tf_op jit(solution)/shard_map/ppermute | solution.py:18
  40.0 14.4 %collective-permute-start.13 = (bf16[64,3584]{1,0:T(8,128)(2,1)}, bf16[64,3584]{1,0:T(8,128)(2,1)S(1)}, u32[]{:S(2)}, u32[]{:S(2)}) collective-permute-start(bf16[64,3584]{1,0:T(8,128)(2,1)} %copy-done.4), channel_id=1, source_target_pairs={{0,64},{64,128},{128,192},{192,0},{1,65},{65,129},{129,193},{193,1... | collective-permute-start | bytes 1376264 | tf_op jit(solution)/shard_map/ppermute | solution.py:18
  42.2 13.5 %collective-permute-start.14 = (bf16[64,3584]{1,0:T(8,128)(2,1)}, bf16[64,3584]{1,0:T(8,128)(2,1)S(1)}, u32[]{:S(2)}, u32[]{:S(2)}) collective-permute-start(bf16[64,3584]{1,0:T(8,128)(2,1)} %copy-done.4), channel_id=1, source_target_pairs={{0,192},{64,0},{128,64},{192,128},{1,193},{65,1},{129,65},{193,129... | collective-permute-start | bytes 1376264 | tf_op jit(solution)/shard_map/ppermute | solution.py:18
  42.9 20.5 %collective-permute-start.15 = (bf16[64,3584]{1,0:T(8,128)(2,1)}, bf16[64,3584]{1,0:T(8,128)(2,1)S(1)}, u32[]{:S(2)}, u32[]{:S(2)}) collective-permute-start(bf16[64,3584]{1,0:T(8,128)(2,1)} %copy-done.6), channel_id=1, source_target_pairs={{0,64},{64,128},{128,192},{192,0},{1,65},{65,129},{129,193},{193,1... | collective-permute-start | bytes 1376264 | tf_op jit(solution)/shard_map/ppermute | solution.py:18
  64.1 16.3 %collective-permute-start.23 = (bf16[192,128]{0,1:T(8,128)(2,1)S(1)}, bf16[192,128]{0,1:T(8,128)(2,1)S(1)}, u32[]{:S(2)}, u32[]{:S(2)}) collective-permute-start(bf16[192,128]{0,1:T(8,128)(2,1)S(1)} %pad_maximum_fusion.4), channel_id=1, source_target_pairs={{0,3},{1,0},{2,1},{3,2},{4,7},{5,4},{6,5},{7,6},{8,11},{9,8},{10,9... | collective-permute-start | bytes 147464 | tf_op jit(solution)/shard_map/ppermute | solution.py:18
  69.6 13.9 %collective-permute-start.22 = (bf16[192,128]{0,1:T(8,128)(2,1)S(1)}, bf16[192,128]{0,1:T(8,128)(2,1)S(1)}, u32[]{:S(2)}, u32[]{:S(2)}) collective-permute-start(bf16[192,128]{0,1:T(8,128)(2,1)S(1)} %pad_maximum_fusion.4), channel_id=1, source_target_pairs={{0,2},{1,3},{2,0},{3,1},{4,6},{5,7},{6,4},{7,5},{8,10},{9,11},{10,... | collective-permute-start | bytes 147464 | tf_op jit(solution)/shard_map/ppermute | solution.py:18
  71.0 12.5 %collective-permute-start.21 = (bf16[192,128]{0,1:T(8,128)(2,1)S(1)}, bf16[192,128]{0,1:T(8,128)(2,1)S(1)}, u32[]{:S(2)}, u32[]{:S(2)}) collective-permute-start(bf16[192,128]{0,1:T(8,128)(2,1)S(1)} %pad_maximum_fusion.4), channel_id=1, source_target_pairs={{0,1},{1,2},{2,3},{3,0},{4,5},{5,6},{6,7},{7,4},{8,9},{9,10},{10,1... | collective-permute-start | bytes 147464 | tf_op jit(solution)/shard_map/ppermute | solution.py:18
  73.4 17.7 %collective-permute-start.18 = (bf16[96,3584]{1,0:T(8,128)(2,1)}, bf16[96,3584]{1,0:T(8,128)(2,1)S(1)}, u32[]{:S(2)}, u32[]{:S(2)}) collective-permute-start(bf16[96,3584]{1,0:T(8,128)(2,1)} %collective-permute-done), channel_id=1, source_target_pairs={{0,16},{16,32},{32,48},{48,0},{1,17},{17,33},{33,49},{49,1},{2,18}... | collective-permute-start | bytes 2064392 | tf_op jit(solution)/shard_map/ppermute | solution.py:18
  74.6 16.5 %collective-permute-start.19 = (bf16[96,3584]{1,0:T(8,128)(2,1)S(1)}, bf16[96,3584]{1,0:T(8,128)(2,1)S(1)}, u32[]{:S(2)}, u32[]{:S(2)}) collective-permute-start(bf16[96,3584]{1,0:T(8,128)(2,1)S(1)} %collective-permute-done.1), channel_id=1, source_target_pairs={{0,48},{16,0},{32,16},{48,32},{1,49},{17,1},{33,17},{49,33},{2,50}... | collective-permute-start | bytes 2064392 | tf_op jit(solution)/shard_map/ppermute | solution.py:18
  80.5 10.6 %collective-permute-start.20 = (bf16[64,3584]{1,0:T(8,128)(2,1)S(1)}, bf16[64,3584]{1,0:T(8,128)(2,1)S(1)}, u32[]{:S(2)}, u32[]{:S(2)}) collective-permute-start(bf16[64,3584]{1,0:T(8,128)(2,1)S(1)} %collective-permute-done.14), channel_id=1, source_target_pairs={{0,192},{64,0},{128,64},{192,128},{1,193},{65,1},{129,65},{193,129... | collective-permute-start | bytes 1376264 | tf_op jit(solution)/shard_map/ppermute | solution.py:18
  91.3 18.1 %collective-permute-start.24 = (bf16[4,64,3584]{2,1,0:T(8,128)(2,1)S(1)}, bf16[4,64,3584]{2,1,0:T(8,128)(2,1)S(1)}, u32[]{:S(2)}, u32[]{:S(2)}) collective-permute-start(bf16[4,64,3584]{2,1,0:T(8,128)(2,1)S(1)} %pad_maximum_fusion.own), channel_id=1, source_target_pairs={{0,4},{4,0},{1,5},{5,1},{2,6},{6,2},{3,7},{7,3},{8,12},{12,8},{9,1... | collective-permute-start | bytes 5505032 | tf_op jit(solution)/shard_map/ppermute | solution.py:18
  92.1 17.3 %collective-permute-start.25 = (bf16[4,64,3584]{2,1,0:T(8,128)(2,1)S(1)}, bf16[4,64,3584]{2,1,0:T(8,128)(2,1)S(1)}, u32[]{:S(2)}, u32[]{:S(2)}) collective-permute-start(bf16[4,64,3584]{2,1,0:T(8,128)(2,1)S(1)} %pad_maximum_fusion.1.other), channel_id=1, source_target_pairs={{0,4},{4,0},{1,5},{5,1},{2,6},{6,2},{3,7},{7,3},{8,12},{12,8},{9,1... | collective-permute-start | bytes 5505032 | tf_op jit(solution)/shard_map/ppermute | solution.py:18
  93.3 16.0 %collective-permute-start.27 = (f32[32,4664]{1,0:T(8,128)S(1)}, f32[32,4664]{1,0:T(8,128)S(1)}, u32[]{:S(2)}, u32[]{:S(2)}) collective-permute-start(f32[32,4664]{1,0:T(8,128)S(1)} %dynamic-slice_add_fusion), channel_id=1, source_target_pairs={{0,8},{8,0},{1,9},{9,1},{2,10},{10,2},{3,11},{11,3},{4,12},{12,4},... | collective-permute-start | bytes 1790984 | tf_op jit(solution)/shard_map/ppermute | solution.py:18
  118.8 13.0 %collective-permute-start.30 = (f32[8,4664]{1,0:T(8,128)S(1)}, f32[8,4664]{1,0:T(8,128)S(1)}, u32[]{:S(2)}, u32[]{:S(2)}) collective-permute-start(f32[8,4664]{1,0:T(8,128)S(1)} %get-tuple-element.61), channel_id=1, source_target_pairs={{0,192},{64,0},{128,64},{192,128},{1,193},{65,1},{129,65},{193,129... | collective-permute-start | bytes 447752 | tf_op jit(solution)/shard_map/ppermute | solution.py:18
  121.4 10.4 %collective-permute-start.29 = (f32[8,4664]{1,0:T(8,128)S(1)}, f32[8,4664]{1,0:T(8,128)S(1)}, u32[]{:S(2)}, u32[]{:S(2)}) collective-permute-start(f32[8,4664]{1,0:T(8,128)S(1)} %get-tuple-element.62), channel_id=1, source_target_pairs={{0,128},{64,192},{128,0},{192,64},{1,129},{65,193},{129,1},{193,65... | collective-permute-start | bytes 447752 | tf_op jit(solution)/shard_map/ppermute | solution.py:18
  123.2 8.6 %collective-permute-start.28 = (f32[8,4664]{1,0:T(8,128)S(1)}, f32[8,4664]{1,0:T(8,128)S(1)}, u32[]{:S(2)}, u32[]{:S(2)}) collective-permute-start(f32[8,4664]{1,0:T(8,128)S(1)} %get-tuple-element.60), channel_id=1, source_target_pairs={{0,64},{64,128},{128,192},{192,0},{1,65},{65,129},{129,193},{193,1... | collective-permute-start | bytes 447752 | tf_op jit(solution)/shard_map/ppermute | solution.py:18
  125.8 28.7 %all-to-all-start = ((bf16[16,96,256]{2,1,0:T(8,128)(2,1)}), bf16[16,96,256]{2,1,0:T(8,128)(2,1)S(1)}, u32[]{:S(2)}, u32[]{:S(2)}) async-start(bf16[16,96,256]{2,1,0:T(8,128)(2,1)} %bitcast.15), calls=%async_computation | async-start | bytes 1572864 | tf_op jit(solution)/shard_map/all_to_all | solution.py:22
  131.9 6.1 %collective-permute-start.33 = (f32[2,4664]{1,0:T(2,128)S(1)}, f32[2,4664]{1,0:T(2,128)S(1)}, u32[]{:S(2)}, u32[]{:S(2)}) collective-permute-start(f32[2,4664]{1,0:T(2,128)S(1)} %get-tuple-element.64), channel_id=1, source_target_pairs={{0,48},{16,0},{32,16},{48,32},{1,49},{17,1},{33,17},{49,33},{2,50}... | collective-permute-start | bytes 111944 | tf_op jit(solution)/shard_map/ppermute | solution.py:18
  136.0 6.1 %collective-permute-start.31 = (f32[2,4664]{1,0:T(2,128)S(1)}, f32[2,4664]{1,0:T(2,128)S(1)}, u32[]{:S(2)}, u32[]{:S(2)}) collective-permute-start(f32[2,4664]{1,0:T(2,128)S(1)} %get-tuple-element.63), channel_id=1, source_target_pairs={{0,16},{16,32},{32,48},{48,0},{1,17},{17,33},{33,49},{49,1},{2,18}... | collective-permute-start | bytes 111944 | tf_op jit(solution)/shard_map/ppermute | solution.py:18
  154.5 22.1 %all-to-all-start.1 = ((bf16[16,96,256]{2,1,0:T(8,128)(2,1)}), bf16[16,96,256]{2,1,0:T(8,128)(2,1)S(1)}, u32[]{:S(2)}, u32[]{:S(2)}) async-start(bf16[16,96,256]{2,1,0:T(8,128)(2,1)} %bitcast.18), calls=%async_computation.1 | async-start | bytes 1572864 | tf_op jit(solution)/shard_map/all_to_all | solution.py:22
  158.1 8.4 %collective-permute-start.34 = (f32[2,4664]{1,0:T(2,128)S(1)}, f32[2,4664]{1,0:T(2,128)S(1)}, u32[]{:S(2)}, u32[]{:S(2)}) collective-permute-start(f32[2,4664]{1,0:T(2,128)S(1)} %add_add_fusion.1), channel_id=1, source_target_pairs={{0,16},{16,32},{32,48},{48,0},{1,17},{17,33},{33,49},{49,1},{2,18}... | collective-permute-start | bytes 111944 | tf_op jit(solution)/shard_map/ppermute | solution.py:18
  159.9 7.4 %collective-permute-start.35 = (f32[2,4664]{1,0:T(2,128)S(1)}, f32[2,4664]{1,0:T(2,128)S(1)}, u32[]{:S(2)}, u32[]{:S(2)}) collective-permute-start(f32[2,4664]{1,0:T(2,128)S(1)} %add_add_fusion.1), channel_id=1, source_target_pairs={{0,32},{16,48},{32,0},{48,16},{1,33},{17,49},{33,1},{49,17},{2,34}... | collective-permute-start | bytes 111944 | tf_op jit(solution)/shard_map/ppermute | solution.py:18
  168.4 6.8 %collective-permute-start.38 = (f32[8,4664]{1,0:T(8,128)S(1)}, f32[8,4664]{1,0:T(8,128)S(1)}, u32[]{:S(2)}, u32[]{:S(2)}) collective-permute-start(f32[8,4664]{1,0:T(8,128)S(1)} %constant_dynamic-update-slice_fusion.11), channel_id=1, source_target_pairs={{0,128},{64,192},{128,0},{192,64},{1,129},{65,193},{129,1},{193,65... | collective-permute-start | bytes 447752 | tf_op jit(solution)/shard_map/ppermute | solution.py:18
  169.6 6.8 %collective-permute-start.39 = (f32[8,4664]{1,0:T(8,128)S(1)}, f32[8,4664]{1,0:T(8,128)S(1)}, u32[]{:S(2)}, u32[]{:S(2)}) collective-permute-start(f32[8,4664]{1,0:T(8,128)S(1)} %constant_dynamic-update-slice_fusion.11), channel_id=1, source_target_pairs={{0,192},{64,0},{128,64},{192,128},{1,193},{65,1},{129,65},{193,129... | collective-permute-start | bytes 447752 | tf_op jit(solution)/shard_map/ppermute | solution.py:18
  (23 other events, 202.2 us)

commit v6 on v4

--- a/solution.py
+++ b/solution.py
@@ -8,7 +8,7 @@
 SCALE = 0.5
 BF = jnp.bfloat16
 F32 = jnp.float32
-SIZES = {"y": 4, "x": 4, "zl": 2, "co": 2, "t": 4}
+SIZES = {"y": 4, "x": 4, "zl": 2, "co": 2, "t": 4, ("zl", "co"): 4}
 DP = ("y", "x", "zl", "co")
 N_DP = 64
 
@@ -72,6 +72,11 @@
             jax.ShapeDtypeStruct((1, width), F32),
         ],
         compiler_params=pltpu.CompilerParams(vmem_limit_bytes=60 * 1024 * 1024),
+        cost_estimate=pl.CostEstimate(
+            flops=2 * rows * width * (rank + 8 * count),
+            bytes_accessed=8 * rows * width,
+            transcendentals=0,
+        ),
     )(codes, scales, factor, out_factor)
 
 
@@ -168,78 +173,70 @@
     left_low, right_high = shift(low_half, "x", 1), shift(high_half, "x", -1)
     other = shift(own, "zl", 1)
     own_down, own_up = shift(own, "y", 1), shift(own, "y", -1)
-    total = gather_sum(gather_sum(squares.reshape(-1, 128), "y"), "co")
+    total = gather_sum(squares.reshape(-1, 128), "y")
     phase = (left_low, right_high, other, own_down, own_up, total, low_half, high_half)
     phase = lax.optimization_barrier(phase)
     left_low, right_high, other, own_down, own_up, total, low_half, high_half = phase
 
     left_high, right_low = shift(high_half, "x", 1), shift(low_half, "x", -1)
     other_down, other_up = shift(other, "y", 1), shift(other, "y", -1)
+    total = gather_sum(gather_sum(total, "x"), ("zl", "co"))
+    phase = (left_low, right_high, left_high, right_low, other_down, other_up, own_down, total)
+    phase = lax.optimization_barrier(phase)
+    left_low, right_high, left_high, right_low, other_down, other_up, own_down, total = phase
+
+    far_low, far_high = shift(left_low, "x", 1), shift(right_high, "x", -1)
     own_far = shift(own_down, "y", 1)
-    total = after(gather_sum(total, "zl"), other_down, other_up, own_far)
-    total = gather_sum(total, "x")
-    phase = (left_low, right_high, left_high, right_low, other_down, other_up, own_far, total)
+    other_far = shift(other_up, "y", -1)
+    col_norm = jnp.sqrt(total.reshape(-1) + 1e-06)
+    ratio = magnitude / col_norm
+
+    def scaled_of(g):
+        return (g.astype(F32) * ratio).astype(BF)
+
+    scaled_own = scaled_of(grad)
+    scaled = scaled_of(
+        jnp.concatenate([grad, left_low, left_high, right_low, right_high], axis=0)
+    )
+
+    factor_cols = lax.dynamic_slice_in_dim(in_factor, t * features, features, 0)
+    hidden = jnp.dot(inputs, factor_cols, preferred_element_type=F32)
+    back = lax.dot_general(
+        scaled_own, out_factor, (((1,), (1,)), ((), ())), preferred_element_type=F32
+    )
+    low = jnp.concatenate([hidden, back], axis=1).astype(BF)
+    pieces = [shift(low, "t", k) for k in (1, 2, 3)]
+    low = sum((p.astype(F32) for p in pieces), low.astype(F32)).astype(BF)
+    hidden, back = low[:, :rank], low[:, rank:]
+    in_grad = SCALE * lax.dot_general(
+        back, inputs, (((0,), (0,)), ((), ())), preferred_element_type=F32
+    )
+    out_grad = SCALE * lax.dot_general(
+        hidden, scaled_own, (((0,), (0,)), ((), ())), preferred_element_type=F32
+    )
+    mag_sum = jnp.sum(grad.astype(F32) * pre.astype(F32), axis=0).reshape(N_DP, -1)
+    adapters = jnp.concatenate([out_grad, in_grad, mag_sum], axis=1)
+    phase = (far_low, far_high, own_far, other_far, adapters, scaled)
     phase = lax.optimization_barrier(phase)
-    left_low, right_high, left_high, right_low, other_down, other_up, own_far, total = phase
-
-    far_low, far_high = shift(left_low, "x", 1), shift(right_high, "x", -1)
-    other_far = shift(other_up, "y", -1)
+    far_low, far_high, own_far, other_far, adapters, scaled = phase
     own_rows = jnp.stack([own, own_down, own_up, own_far])
     own_swap = shift(own_rows, "co", 1)
     other_rows = jnp.stack([other, other_down, other_up, other_far])
     other_swap = shift(other_rows, "co", 1)
-    col_norm = jnp.sqrt(total.reshape(-1) + 1e-06)
-    ratio = magnitude / col_norm
-
-    def scaled_of(g):
-        return (g.astype(F32) * ratio).astype(BF)
-
-    scaled_own = scaled_of(grad)
-    scaled = scaled_of(
-        jnp.concatenate([grad, left_low, left_high, right_low, right_high], axis=0)
-    )
-
-    factor_cols = lax.dynamic_slice_in_dim(in_factor, t * features, features, 0)
-    hidden = jnp.dot(inputs, factor_cols, preferred_element_type=F32)
-    back = lax.dot_general(
-        scaled_own, out_factor, (((1,), (1,)), ((), ())), preferred_element_type=F32
-    )
-    low = jnp.concatenate([hidden, back], axis=1).astype(BF)
-    pieces = [shift(low, "t", k) for k in (1, 2, 3)]
-    low = sum((p.astype(F32) for p in pieces), low.astype(F32)).astype(BF)
-    low = after(low, far_low, far_high, other_far)
-    hidden, back = low[:, :rank], low[:, rank:]
-    in_grad = SCALE * lax.dot_general(
-        back, inputs, (((0,), (0,)), ((), ())), preferred_element_type=F32
-    )
-    out_grad = SCALE * lax.dot_general(
-        hidden, scaled_own, (((0,), (0,)), ((), ())), preferred_element_type=F32
-    )
-    mag_sum = jnp.sum(grad.astype(F32) * pre.astype(F32), axis=0).reshape(N_DP, -1)
-    adapters = jnp.concatenate([out_grad, in_grad, mag_sum], axis=1)
-    side = adapters.shape[0] // 2
-    keep = lax.dynamic_slice_in_dim(adapters, co * side, side, 0)
-    give = lax.dynamic_slice_in_dim(adapters, (1 - co) * side, side, 0)
-    adapters = keep + shift(give, "co", 1)
-    for axis, index in (("y", y), ("x", x)):
-        side = adapters.shape[0] // 4
-        total = lax.dynamic_slice_in_dim(adapters, index * side, side, 0)
-        for k in (1, 2, 3):
-            give = lax.dynamic_slice_in_dim(adapters, ((index + k) % 4) * side, side, 0)
-            total = total + shift(give, axis, k)
-        adapters = total
-    adapters = adapters + shift(adapters, "zl", 1)
+    columns = adapters.shape[1]
+    adapters = swap_all(adapters.reshape(N_DP // 2, -1), ("y", "x", "co"))
 
     where = jnp.stack([x, zl, co, y]).astype(jnp.int32)
     weights = (own_rows, other_rows, own_swap, other_swap)
     tile = tile_of(where, scaled, far_low, far_high, ratio.reshape(1, -1), weights)
-    adapters = after(adapters, tile)
-    tile = swap_all(tile.reshape(16, tokens, part), ("x", "t"))
-
-    for axis, index in (("x", x), ("y", y), ("co", co)):
+    adapters = jnp.sum(adapters, axis=0).reshape(-1, columns)
+    adapters = adapters + shift(adapters, "zl", 1)
+    tile = swap_all(after(tile, adapters).reshape(16, tokens, part), ("x", "t"))
+
+    for axis, index in (("co", co), ("x", x), ("y", y)):
         n = SIZES[axis]
         side = adapters.shape[0]
-        total = jnp.zeros((n * side, adapters.shape[1]), F32)
+        total = jnp.zeros((n * side, columns), F32)
         for k in range(n):
             got = shift(adapters, axis, k) if k else adapters
             total = lax.dynamic_update_slice(total, got, (((index - k) % n) * side, 0))

time: 179 us -> 198 us (1.11)
  the two profiles are of different devices: /device:TPU:32 before, /device:TPU:8 now
where the time goes in v6:
time: 198 us; the launch traced here: 196 us
  waiting for transfers between devices  81.6 us (41%)
  starting transfers between devices  62.4 us (32%)
  local copies, waits for them, and re-layouts  23.5 us (12%)
  Pallas kernels  13.6 us (7%)
  other arithmetic  11.2 us (6%)
  matrix products  2.53 us (1%)
    ppermute x35, starting transfers between devices, shift(): return lax.ppermute(value, axis, [(i, (i + step) % n) for i in range(n)])  53.2 us
    ppermute x35, waiting for transfers between devices, shift(): return lax.ppermute(value, axis, [(i, (i + step) % n) for i in range(n)])  46.2 us
    all_to_all x2, waiting for transfers between devices, swap_all(): return lax.all_to_all(value, axes, 0, 0, tiled=True)  35.4 us
    unnamed x45, local copies, waits for them, and re-layouts  9.44 us
    pallas_call x1, Pallas kernels, tile_of(): pl.pallas_call(tile_kernel, grid_spec=pltpu.PrefetchScalarGridSpec(num_sc...  9.3 us
    all_to_all x2, starting transfers between devices, swap_all(): return lax.all_to_all(value, axes, 0, 0, tiled=True)  9.24 us
    convert_element_type x1, other arithmetic, scaled_of(): return (g.astype(F32) * ratio).astype(BF)  4.86 us
    dynamic_update_slice x9, local copies, waits for them, and re-layouts, on_device(): total = lax.dynamic_update_slice(total, got, ((index - k) % n * side, 0))  4.58 us
  transfers between devices with their start and end apart: 37, of which 16 were waited for; matrix products, arithmetic and copies ran while one was open for 14% of the time, Pallas kernels for 7%

profile of v6, /device:TPU:8, one launch (start us, length us, event | category | flops | bytes accessed | tf_op | source)
XLA Modules:
  0.0 196.0 jit_solution(11122810383699584775)
XLA Ops:
  0.7 2.4 %fusion.13 = (bf16[96,3584]{1,0:T(8,128)(2,1)}, bf16[96,3584]{1,0:T(8,128)(2,1)S(1)}) fusion(bf16[192,3584]{1,0:T(8,128)(2,1)} %param.14), kind=kLoop, calls=%fused_computation.45 | loop fusion | bytes 2752512 | tf_op jit(solution)/shard_map/slice | solution.py:172
  7.1 4.3 %shard_map.111 = (bf16[64,3584]{1,0:T(8,128)(2,1)}, f32[1,3584]{1,0:T(1,128)}) custom-call(s32[64,3584]{1,0:T(8,128)} %refs_0_.1, f32[56,64]{1,0:T(8,128)} %bitcast.42, bf16[64,64]{1,0:T(8,128)(2,1)} %copy.19.refs_2_, bf16[64,3584]{1,0:T(8,128)(2,1)} %refs_3_.1), custom_call_target="tpu_custom_call" | custom-call | flops 234881024 | bytes 1835008 | tf_op jit(solution)/shard_map/pallas_call | solution.py:65
  13.7 2.7 %collective-permute-start.6 = (f32[28,128]{1,0:T(8,128)S(1)}, f32[28,128]{1,0:T(8,128)S(1)}, u32[]{:S(2)}, u32[]{:S(2)}) collective-permute-start(f32[28,128]{1,0:T(8,128)S(1)} %bitcast.40), channel_id=1, source_target_pairs={{0,128},{64,192},{128,0},{192,64},{1,129},{65,193},{129,1},{193,65... | collective-permute-start | bytes 43016 | tf_op jit(solution)/shard_map/ppermute | solution.py:18
  17.1 1.9 collective-permute-start.2
  21.0 7.3 %collective-permute-done.2 = bf16[64,3584]{1,0:T(8,128)(2,1)S(1)} collective-permute-done((bf16[64,3584]{1,0:T(8,128)(2,1)}, bf16[64,3584]{1,0:T(8,128)(2,1)S(1)}, u32[]{:S(2)}, u32[]{:S(2)}) %collective-permute-start.2) | collective-permute-done | bytes 458784 | tf_op jit(solution)/shard_map/ppermute | solution.py:18
  31.7 2.2 %collective-permute-start.13 = (f32[28,128]{1,0:T(8,128)S(1)}, f32[28,128]{1,0:T(8,128)S(1)}, u32[]{:S(2)}, u32[]{:S(2)}) collective-permute-start(f32[28,128]{1,0:T(8,128)S(1)} %add_add_fusion.2), channel_id=1, source_target_pairs={{0,32},{16,48},{32,0},{48,16},{1,33},{17,49},{33,1},{49,17},{2,34}... | collective-permute-start | bytes 43016 | tf_op jit(solution)/shard_map/ppermute | solution.py:18
  37.1 2.4 %collective-permute-start.9 = (bf16[96,3584]{1,0:T(8,128)(2,1)S(1)}, bf16[96,3584]{1,0:T(8,128)(2,1)}, u32[]{:S(2)}, u32[]{:S(2)}) collective-permute-start(bf16[96,3584]{1,0:T(8,128)(2,1)S(1)} %get-tuple-element.34), channel_id=1, source_target_pairs={{0,48},{16,0},{32,16},{48,32},{1,49},{17,1},{33,17},{49,33},{2,50}... | collective-permute-start | bytes 2064392 | tf_op jit(solution)/shard_map/ppermute | solution.py:18
  39.6 2.0 %collective-permute-start.16 = (f32[28,128]{1,0:T(8,128)S(1)}, f32[28,128]{1,0:T(8,128)S(1)}, u32[]{:S(2)}, u32[]{:S(2)}) collective-permute-start(f32[28,128]{1,0:T(8,128)S(1)} %add_add_fusion.1), channel_id=1, source_target_pairs={{0,8},{4,12},{8,0},{12,4},{1,9},{5,13},{9,1},{13,5},{2,10},{6,14},... | collective-permute-start | bytes 43016 | tf_op jit(solution)/shard_map/ppermute | solution.py:18
  47.9 9.1 %collective-permute-done.10 = bf16[64,3584]{1,0:T(8,128)(2,1)} collective-permute-done((bf16[64,3584]{1,0:T(8,128)(2,1)}, bf16[64,3584]{1,0:T(8,128)(2,1)}, u32[]{:S(2)}, u32[]{:S(2)}) %collective-permute-start.10) | collective-permute-done | bytes 458784 | tf_op jit(solution)/shard_map/ppermute | solution.py:18
  60.1 3.4 %collective-permute-start.22 = (bf16[192,128]{0,1:T(8,128)(2,1)S(1)}, bf16[192,128]{0,1:T(8,128)(2,1)S(1)}, u32[]{:S(2)}, u32[]{:S(2)}) collective-permute-start(bf16[192,128]{0,1:T(8,128)(2,1)S(1)} %pad_maximum_fusion.3), channel_id=1, source_target_pairs={{0,1},{1,2},{2,3},{3,0},{4,5},{5,6},{6,7},{7,4},{8,9},{9,10},{10,1... | collective-permute-start | bytes 147464 | tf_op jit(solution)/shard_map/ppermute | solution.py:18
  63.5 5.1 %collective-permute-start.23 = (bf16[192,128]{0,1:T(8,128)(2,1)S(1)}, bf16[192,128]{0,1:T(8,128)(2,1)S(1)}, u32[]{:S(2)}, u32[]{:S(2)}) collective-permute-start(bf16[192,128]{0,1:T(8,128)(2,1)S(1)} %pad_maximum_fusion.3), channel_id=1, source_target_pairs={{0,2},{1,3},{2,0},{3,1},{4,6},{5,7},{6,4},{7,5},{8,10},{9,11},{10,... | collective-permute-start | bytes 147464 | tf_op jit(solution)/shard_map/ppermute | solution.py:18
  68.6 2.7 %collective-permute-start.24 = (bf16[192,128]{0,1:T(8,128)(2,1)S(1)}, bf16[192,128]{0,1:T(8,128)(2,1)S(1)}, u32[]{:S(2)}, u32[]{:S(2)}) collective-permute-start(bf16[192,128]{0,1:T(8,128)(2,1)S(1)} %pad_maximum_fusion.3), channel_id=1, source_target_pairs={{0,3},{1,0},{2,1},{3,2},{4,7},{5,4},{6,5},{7,6},{8,11},{9,8},{10,9... | collective-permute-start | bytes 147464 | tf_op jit(solution)/shard_map/ppermute | solution.py:18
  71.3 2.0 %constant_dynamic-update-slice_fusion.3 = bf16[576,3584]{1,0:T(8,128)(2,1)} fusion(bf16[576,3584]{1,0:T(8,128)(2,1)} %constant_dynamic-update-slice_fusion.4, bf16[96,3584]{1,0:T(8,128)(2,1)} %collective-permute-done), kind=kLoop, calls=%fused_computation.30 | loop fusion | bytes 1376256
  73.3 3.2 %collective-permute-start.19 = (bf16[96,3584]{1,0:T(8,128)(2,1)S(1)}, bf16[96,3584]{1,0:T(8,128)(2,1)S(1)}, u32[]{:S(2)}, u32[]{:S(2)}) collective-permute-start(bf16[96,3584]{1,0:T(8,128)(2,1)S(1)} %copy-done.6), channel_id=1, source_target_pairs={{0,48},{16,0},{32,16},{48,32},{1,49},{17,1},{33,17},{49,33},{2,50}... | collective-permute-start | bytes 2064392 | tf_op jit(solution)/shard_map/ppermute | solution.py:18
  76.6 2.0 %constant_dynamic-update-slice_fusion.2 = bf16[576,3584]{1,0:T(8,128)(2,1)} fusion(bf16[576,3584]{1,0:T(8,128)(2,1)} %constant_dynamic-update-slice_fusion.3, bf16[96,3584]{1,0:T(8,128)(2,1)} %collective-permute-done.8), kind=kLoop, calls=%fused_computation.29 | loop fusion | bytes 1376256
  78.6 2.0 %constant_dynamic-update-slice_fusion.1 = bf16[576,3584]{1,0:T(8,128)(2,1)} fusion(bf16[576,3584]{1,0:T(8,128)(2,1)} %constant_dynamic-update-slice_fusion.2, bf16[96,3584]{1,0:T(8,128)(2,1)} %collective-permute-done.9), kind=kLoop, calls=%fused_computation.28 | loop fusion | bytes 1376256
  81.5 4.9 %multiply_convert_fusion.scaled = bf16[576,3584]{1,0:T(8,128)(2,1)} fusion(bf16[576,3584]{1,0:T(8,128)(2,1)} %constant_dynamic-update-slice_fusion, f32[3584]{0:T(1024)S(1)} %bitcast_divide_fusion.1), kind=kLoop, calls=%fused_computation | loop fusion | flops 6193152 | bytes 8271872 | tf_op jit(solution)/shard_map/convert_element_type | solution.py:195
  86.4 1.8 collective-permute-start.20
  89.3 8.1 %collective-permute-done.20 = bf16[64,3584]{1,0:T(8,128)(2,1)S(1)} collective-permute-done((bf16[64,3584]{1,0:T(8,128)(2,1)S(1)}, bf16[64,3584]{1,0:T(8,128)(2,1)S(1)}, u32[]{:S(2)}, u32[]{:S(2)}) %collective-permute-start.20) | collective-permute-done | bytes 458784 | tf_op jit(solution)/shard_map/ppermute | solution.py:18
  99.6 2.4 %all_to_all.12 = f32[32,1,9328]{2,1,0:T(1,128)} reshape(f32[64,4664]{1,0:T(8,128)S(1)} %pad_maximum_fusion.2) | data formatting | bytes 2387968 | tf_op jit(solution)/shard_map/all_to_all | solution.py:22
  102.1 5.3 %all-to-all-start = ((f32[32,1,9328]{2,1,0:T(1,128)}), f32[32,1,9328]{2,1,0:T(1,128)S(1)}, u32[]{:S(2)}, u32[]{:S(2)}) async-start(f32[32,1,9328]{2,1,0:T(1,128)} %all_to_all.12), calls=%async_computation | async-start | bytes 2392064 | tf_op jit(solution)/shard_map/all_to_all | solution.py:22
  107.7 16.2 %all-to-all-done = f32[32,1,9328]{2,1,0:T(1,128)S(1)} async-done(((f32[32,1,9328]{2,1,0:T(1,128)}), f32[32,1,9328]{2,1,0:T(1,128)S(1)}, u32[]{:S(2)}, u32[]{:S(2)}) %all-to-all-start) | async-done | bytes 1194016 | tf_op jit(solution)/shard_map/all_to_all | solution.py:22
  125.9 1.8 pad_maximum_fusion.1.other
  133.2 2.3 %collective-permute-start.30 = (f32[4,4664]{1,0:T(4,128)S(1)}, f32[4,4664]{1,0:T(4,128)S(1)}, u32[]{:S(2)}, u32[]{:S(2)}) collective-permute-start(f32[4,4664]{1,0:T(4,128)S(1)} %constant_dynamic-update-slice_fusion.13), channel_id=1, source_target_pairs={{0,32},{16,48},{32,0},{48,16},{1,33},{17,49},{33,1},{49,17},{2,34}... | collective-permute-start | bytes 223880 | tf_op jit(solution)/shard_map/ppermute | solution.py:18
  140.4 9.3 %shard_map.112 = bf16[4,4,192,256]{3,2,1,0:T(8,128)(2,1)} custom-call(s32[4]{0:T(128)S(1)} %pad_add_fusion.where, bf16[576,3584]{1,0:T(8,128)(2,1)S(1)} %copy-done.1, bf16[96,3584]{1,0:T(8,128)(2,1)S(1)} %collective-permute-done.18.far_low, bf16[96,3584]{1,0:T(8,128)(2,1)S(1)} %collective-permute-done.19.far_high, f32[1,3584]{1,0:T(1,128)S(1)} %broadcast_in_dim.13.ratio, ...), custom_call_target="tpu_custom_call" | custom-call | flops 5637144576 | bytes 12845056 | tf_op jit(solution)/shard_map/pallas_call | solution.py:132
  149.7 4.0 %all-to-all-start.1 = ((bf16[16,192,256]{2,1,0:T(8,128)(2,1)}), bf16[16,192,256]{2,1,0:T(8,128)(2,1)S(1)}, u32[]{:S(2)}, u32[]{:S(2)}) async-start(bf16[16,192,256]{2,1,0:T(8,128)(2,1)} %bitcast.15), calls=%async_computation.1 | async-start | bytes 3145728 | tf_op jit(solution)/shard_map/all_to_all | solution.py:22
  155.2 1.8 collective-permute-start.32
  157.0 3.2 %collective-permute-start.33 = (f32[16,4664]{1,0:T(8,128)}, f32[16,4664]{1,0:T(8,128)S(1)}, u32[]{:S(2)}, u32[]{:S(2)}) collective-permute-start(f32[16,4664]{1,0:T(8,128)} %constant_dynamic-update-slice_fusion.9), channel_id=1, source_target_pairs={{0,128},{64,192},{128,0},{192,64},{1,129},{65,193},{129,1},{193,65... | collective-permute-start | bytes 895496 | tf_op jit(solution)/shard_map/ppermute | solution.py:18
  161.3 5.1 %collective-permute-done.32 = f32[16,4664]{1,0:T(8,128)S(1)} collective-permute-done((f32[16,4664]{1,0:T(8,128)}, f32[16,4664]{1,0:T(8,128)S(1)}, u32[]{:S(2)}, u32[]{:S(2)}) %collective-permute-start.32) | collective-permute-done | bytes 298528 | tf_op jit(solution)/shard_map/ppermute | solution.py:18
  166.4 2.4 %collective-permute-done.33 = f32[16,4664]{1,0:T(8,128)S(1)} collective-permute-done((f32[16,4664]{1,0:T(8,128)}, f32[16,4664]{1,0:T(8,128)S(1)}, u32[]{:S(2)}, u32[]{:S(2)}) %collective-permute-start.33) | collective-permute-done | bytes 298528 | tf_op jit(solution)/shard_map/ppermute | solution.py:18
  168.9 4.4 %collective-permute-done.34 = f32[16,4664]{1,0:T(8,128)S(1)} collective-permute-done((f32[16,4664]{1,0:T(8,128)}, f32[16,4664]{1,0:T(8,128)S(1)}, u32[]{:S(2)}, u32[]{:S(2)}) %collective-permute-start.34) | collective-permute-done | bytes 298528 | tf_op jit(solution)/shard_map/ppermute | solution.py:18
  175.7 19.2 %all-to-all-done.1 = bf16[16,192,256]{2,1,0:T(8,128)(2,1)S(1)} async-done(((bf16[16,192,256]{2,1,0:T(8,128)(2,1)}), bf16[16,192,256]{2,1,0:T(8,128)(2,1)S(1)}, u32[]{:S(2)}, u32[]{:S(2)}) %all-to-all-start.1) | async-done | bytes 1572896 | tf_op jit(solution)/shard_map/all_to_all | solution.py:22
  (134 shorter events, 47.9 us)
Async XLA Ops:
  3.0 27.8 %collective-permute-start = (bf16[96,3584]{1,0:T(8,128)(2,1)S(1)}, bf16[96,3584]{1,0:T(8,128)(2,1)}, u32[]{:S(2)}, u32[]{:S(2)}) collective-permute-start(bf16[96,3584]{1,0:T(8,128)(2,1)S(1)} %get-tuple-element.34), channel_id=1, source_target_pairs={{0,16},{16,32},{32,48},{48,0},{1,17},{17,33},{33,49},{49,1},{2,18}... | collective-permute-start | bytes 2064392 | tf_op jit(solution)/shard_map/ppermute | solution.py:18
  4.5 26.3 %collective-permute-start.1 = (bf16[96,3584]{1,0:T(8,128)(2,1)}, bf16[96,3584]{1,0:T(8,128)(2,1)S(1)}, u32[]{:S(2)}, u32[]{:S(2)}) collective-permute-start(bf16[96,3584]{1,0:T(8,128)(2,1)} %get-tuple-element.33), channel_id=1, source_target_pairs={{0,48},{16,0},{32,16},{48,32},{1,49},{17,1},{33,17},{49,33},{2,50}... | collective-permute-start | bytes 2064392 | tf_op jit(solution)/shard_map/ppermute | solution.py:18
  13.7 5.3 %collective-permute-start.6 = (f32[28,128]{1,0:T(8,128)S(1)}, f32[28,128]{1,0:T(8,128)S(1)}, u32[]{:S(2)}, u32[]{:S(2)}) collective-permute-start(f32[28,128]{1,0:T(8,128)S(1)} %bitcast.40), channel_id=1, source_target_pairs={{0,128},{64,192},{128,0},{192,64},{1,129},{65,193},{129,1},{193,65... | collective-permute-start | bytes 43016 | tf_op jit(solution)/shard_map/ppermute | solution.py:18
  17.1 11.3 %collective-permute-start.2 = (bf16[64,3584]{1,0:T(8,128)(2,1)}, bf16[64,3584]{1,0:T(8,128)(2,1)S(1)}, u32[]{:S(2)}, u32[]{:S(2)}) collective-permute-start(bf16[64,3584]{1,0:T(8,128)(2,1)} %get-tuple-element.29), channel_id=1, source_target_pairs={{0,8},{8,0},{1,9},{9,1},{2,10},{10,2},{3,11},{11,3},{4,12},{12,4},... | collective-permute-start | bytes 1376264 | tf_op jit(solution)/shard_map/ppermute | solution.py:18
  19.0 10.8 %collective-permute-start.3 = (bf16[64,3584]{1,0:T(8,128)(2,1)}, bf16[64,3584]{1,0:T(8,128)(2,1)S(1)}, u32[]{:S(2)}, u32[]{:S(2)}) collective-permute-start(bf16[64,3584]{1,0:T(8,128)(2,1)} %get-tuple-element.29), channel_id=1, source_target_pairs={{0,64},{64,128},{128,192},{192,0},{1,65},{65,129},{129,193},{193,1... | collective-permute-start | bytes 1376264 | tf_op jit(solution)/shard_map/ppermute | solution.py:18
  20.3 10.6 %collective-permute-start.4 = (bf16[64,3584]{1,0:T(8,128)(2,1)}, bf16[64,3584]{1,0:T(8,128)(2,1)S(1)}, u32[]{:S(2)}, u32[]{:S(2)}) collective-permute-start(bf16[64,3584]{1,0:T(8,128)(2,1)} %get-tuple-element.29), channel_id=1, source_target_pairs={{0,192},{64,0},{128,64},{192,128},{1,193},{65,1},{129,65},{193,129... | collective-permute-start | bytes 1376264 | tf_op jit(solution)/shard_map/ppermute | solution.py:18
  30.9 8.6 %collective-permute-start.12 = (f32[28,128]{1,0:T(8,128)S(1)}, f32[28,128]{1,0:T(8,128)S(1)}, u32[]{:S(2)}, u32[]{:S(2)}) collective-permute-start(f32[28,128]{1,0:T(8,128)S(1)} %add_add_fusion.2), channel_id=1, source_target_pairs={{0,16},{16,32},{32,48},{48,0},{1,17},{17,33},{33,49},{49,1},{2,18}... | collective-permute-start | bytes 43016 | tf_op jit(solution)/shard_map/ppermute | solution.py:18
  31.7 7.8 %collective-permute-start.13 = (f32[28,128]{1,0:T(8,128)S(1)}, f32[28,128]{1,0:T(8,128)S(1)}, u32[]{:S(2)}, u32[]{:S(2)}) collective-permute-start(f32[28,128]{1,0:T(8,128)S(1)} %add_add_fusion.2), channel_id=1, source_target_pairs={{0,32},{16,48},{32,0},{48,16},{1,33},{17,49},{33,1},{49,17},{2,34}... | collective-permute-start | bytes 43016 | tf_op jit(solution)/shard_map/ppermute | solution.py:18
  33.9 5.6 %collective-permute-start.14 = (f32[28,128]{1,0:T(8,128)S(1)}, f32[28,128]{1,0:T(8,128)S(1)}, u32[]{:S(2)}, u32[]{:S(2)}) collective-permute-start(f32[28,128]{1,0:T(8,128)S(1)} %add_add_fusion.2), channel_id=1, source_target_pairs={{0,48},{16,0},{32,16},{48,32},{1,49},{17,1},{33,17},{49,33},{2,50}... | collective-permute-start | bytes 43016 | tf_op jit(solution)/shard_map/ppermute | solution.py:18
  36.2 22.2 %collective-permute-start.8 = (bf16[96,3584]{1,0:T(8,128)(2,1)}, bf16[96,3584]{1,0:T(8,128)(2,1)}, u32[]{:S(2)}, u32[]{:S(2)}) collective-permute-start(bf16[96,3584]{1,0:T(8,128)(2,1)} %get-tuple-element.33), channel_id=1, source_target_pairs={{0,16},{16,32},{32,48},{48,0},{1,17},{17,33},{33,49},{49,1},{2,18}... | collective-permute-start | bytes 2064392 | tf_op jit(solution)/shard_map/ppermute | solution.py:18
  37.1 21.3 %collective-permute-start.9 = (bf16[96,3584]{1,0:T(8,128)(2,1)S(1)}, bf16[96,3584]{1,0:T(8,128)(2,1)}, u32[]{:S(2)}, u32[]{:S(2)}) collective-permute-start(bf16[96,3584]{1,0:T(8,128)(2,1)S(1)} %get-tuple-element.34), channel_id=1, source_target_pairs={{0,48},{16,0},{32,16},{48,32},{1,49},{17,1},{33,17},{49,33},{2,50}... | collective-permute-start | bytes 2064392 | tf_op jit(solution)/shard_map/ppermute | solution.py:18
  39.5 5.2 %collective-permute-start.15 = (f32[28,128]{1,0:T(8,128)S(1)}, f32[28,128]{1,0:T(8,128)S(1)}, u32[]{:S(2)}, u32[]{:S(2)}) collective-permute-start(f32[28,128]{1,0:T(8,128)S(1)} %add_add_fusion.1), channel_id=1, source_target_pairs={{0,4},{4,8},{8,12},{12,0},{1,5},{5,9},{9,13},{13,1},{2,6},{6,10},{... | collective-permute-start | bytes 43016 | tf_op jit(solution)/shard_map/ppermute | solution.py:18
  39.6 6.0 %collective-permute-start.16 = (f32[28,128]{1,0:T(8,128)S(1)}, f32[28,128]{1,0:T(8,128)S(1)}, u32[]{:S(2)}, u32[]{:S(2)}) collective-permute-start(f32[28,128]{1,0:T(8,128)S(1)} %add_add_fusion.1), channel_id=1, source_target_pairs={{0,8},{4,12},{8,0},{12,4},{1,9},{5,13},{9,1},{13,5},{2,10},{6,14},... | collective-permute-start | bytes 43016 | tf_op jit(solution)/shard_map/ppermute | solution.py:18
  43.3 13.7 %collective-permute-start.10 = (bf16[64,3584]{1,0:T(8,128)(2,1)}, bf16[64,3584]{1,0:T(8,128)(2,1)}, u32[]{:S(2)}, u32[]{:S(2)}) collective-permute-start(bf16[64,3584]{1,0:T(8,128)(2,1)} %copy-done.13), channel_id=1, source_target_pairs={{0,64},{64,128},{128,192},{192,0},{1,65},{65,129},{129,193},{193,1... | collective-permute-start | bytes 1376264 | tf_op jit(solution)/shard_map/ppermute | solution.py:18
  44.7 13.8 %collective-permute-start.11 = (bf16[64,3584]{1,0:T(8,128)(2,1)}, bf16[64,3584]{1,0:T(8,128)(2,1)}, u32[]{:S(2)}, u32[]{:S(2)}) collective-permute-start(bf16[64,3584]{1,0:T(8,128)(2,1)} %copy-done.13), channel_id=1, source_target_pairs={{0,192},{64,0},{128,64},{192,128},{1,193},{65,1},{129,65},{193,129... | collective-permute-start | bytes 1376264 | tf_op jit(solution)/shard_map/ppermute | solution.py:18
  60.1 26.3 %collective-permute-start.22 = (bf16[192,128]{0,1:T(8,128)(2,1)S(1)}, bf16[192,128]{0,1:T(8,128)(2,1)S(1)}, u32[]{:S(2)}, u32[]{:S(2)}) collective-permute-start(bf16[192,128]{0,1:T(8,128)(2,1)S(1)} %pad_maximum_fusion.3), channel_id=1, source_target_pairs={{0,1},{1,2},{2,3},{3,0},{4,5},{5,6},{6,7},{7,4},{8,9},{9,10},{10,1... | collective-permute-start | bytes 147464 | tf_op jit(solution)/shard_map/ppermute | solution.py:18
  63.5 24.7 %collective-permute-start.23 = (bf16[192,128]{0,1:T(8,128)(2,1)S(1)}, bf16[192,128]{0,1:T(8,128)(2,1)S(1)}, u32[]{:S(2)}, u32[]{:S(2)}) collective-permute-start(bf16[192,128]{0,1:T(8,128)(2,1)S(1)} %pad_maximum_fusion.3), channel_id=1, source_target_pairs={{0,2},{1,3},{2,0},{3,1},{4,6},{5,7},{6,4},{7,5},{8,10},{9,11},{10,... | collective-permute-start | bytes 147464 | tf_op jit(solution)/shard_map/ppermute | solution.py:18
  68.6 19.9 %collective-permute-start.24 = (bf16[192,128]{0,1:T(8,128)(2,1)S(1)}, bf16[192,128]{0,1:T(8,128)(2,1)S(1)}, u32[]{:S(2)}, u32[]{:S(2)}) collective-permute-start(bf16[192,128]{0,1:T(8,128)(2,1)S(1)} %pad_maximum_fusion.3), channel_id=1, source_target_pairs={{0,3},{1,0},{2,1},{3,2},{4,7},{5,4},{6,5},{7,6},{8,11},{9,8},{10,9... | collective-permute-start | bytes 147464 | tf_op jit(solution)/shard_map/ppermute | solution.py:18
  71.3 27.6 %collective-permute-start.18 = (bf16[96,3584]{1,0:T(8,128)(2,1)}, bf16[96,3584]{1,0:T(8,128)(2,1)S(1)}, u32[]{:S(2)}, u32[]{:S(2)}) collective-permute-start(bf16[96,3584]{1,0:T(8,128)(2,1)} %collective-permute-done), channel_id=1, source_target_pairs={{0,16},{16,32},{32,48},{48,0},{1,17},{17,33},{33,49},{49,1},{2,18}... | collective-permute-start | bytes 2064392 | tf_op jit(solution)/shard_map/ppermute | solution.py:18
  73.3 26.3 %collective-permute-start.19 = (bf16[96,3584]{1,0:T(8,128)(2,1)S(1)}, bf16[96,3584]{1,0:T(8,128)(2,1)S(1)}, u32[]{:S(2)}, u32[]{:S(2)}) collective-permute-start(bf16[96,3584]{1,0:T(8,128)(2,1)S(1)} %copy-done.6), channel_id=1, source_target_pairs={{0,48},{16,0},{32,16},{48,32},{1,49},{17,1},{33,17},{49,33},{2,50}... | collective-permute-start | bytes 2064392 | tf_op jit(solution)/shard_map/ppermute | solution.py:18
  86.4 11.0 %collective-permute-start.20 = (bf16[64,3584]{1,0:T(8,128)(2,1)S(1)}, bf16[64,3584]{1,0:T(8,128)(2,1)S(1)}, u32[]{:S(2)}, u32[]{:S(2)}) collective-permute-start(bf16[64,3584]{1,0:T(8,128)(2,1)S(1)} %copy-done.9), channel_id=1, source_target_pairs={{0,64},{64,128},{128,192},{192,0},{1,65},{65,129},{129,193},{193,1... | collective-permute-start | bytes 1376264 | tf_op jit(solution)/shard_map/ppermute | solution.py:18
  88.2 10.7 %collective-permute-start.21 = (bf16[64,3584]{1,0:T(8,128)(2,1)}, bf16[64,3584]{1,0:T(8,128)(2,1)S(1)}, u32[]{:S(2)}, u32[]{:S(2)}) collective-permute-start(bf16[64,3584]{1,0:T(8,128)(2,1)} %collective-permute-done.11), channel_id=1, source_target_pairs={{0,192},{64,0},{128,64},{192,128},{1,193},{65,1},{129,65},{193,129... | collective-permute-start | bytes 1376264 | tf_op jit(solution)/shard_map/ppermute | solution.py:18
  102.1 21.8 %all-to-all-start = ((f32[32,1,9328]{2,1,0:T(1,128)}), f32[32,1,9328]{2,1,0:T(1,128)S(1)}, u32[]{:S(2)}, u32[]{:S(2)}) async-start(f32[32,1,9328]{2,1,0:T(1,128)} %all_to_all.12), calls=%async_computation | async-start | bytes 2392064 | tf_op jit(solution)/shard_map/all_to_all | solution.py:22
  127.7 12.6 %collective-permute-start.26 = (bf16[4,64,3584]{2,1,0:T(8,128)(2,1)S(1)}, bf16[4,64,3584]{2,1,0:T(8,128)(2,1)S(1)}, u32[]{:S(2)}, u32[]{:S(2)}) collective-permute-start(bf16[4,64,3584]{2,1,0:T(8,128)(2,1)S(1)} %pad_maximum_fusion.1.other), channel_id=1, source_target_pairs={{0,4},{4,0},{1,5},{5,1},{2,6},{6,2},{3,7},{7,3},{8,12},{12,8},{9,1... | collective-permute-start | bytes 5505032 | tf_op jit(solution)/shard_map/ppermute | solution.py:18
  129.7 10.7 %collective-permute-start.25 = (bf16[4,64,3584]{2,1,0:T(8,128)(2,1)S(1)}, bf16[4,64,3584]{2,1,0:T(8,128)(2,1)S(1)}, u32[]{:S(2)}, u32[]{:S(2)}) collective-permute-start(bf16[4,64,3584]{2,1,0:T(8,128)(2,1)S(1)} %pad_maximum_fusion.own), channel_id=1, source_target_pairs={{0,4},{4,0},{1,5},{5,1},{2,6},{6,2},{3,7},{7,3},{8,12},{12,8},{9,1... | collective-permute-start | bytes 5505032 | tf_op jit(solution)/shard_map/ppermute | solution.py:18
  131.8 6.5 %collective-permute-start.29 = (f32[4,4664]{1,0:T(4,128)S(1)}, f32[4,4664]{1,0:T(4,128)S(1)}, u32[]{:S(2)}, u32[]{:S(2)}) collective-permute-start(f32[4,4664]{1,0:T(4,128)S(1)} %constant_dynamic-update-slice_fusion.13), channel_id=1, source_target_pairs={{0,16},{16,32},{32,48},{48,0},{1,17},{17,33},{33,49},{49,1},{2,18}... | collective-permute-start | bytes 223880 | tf_op jit(solution)/shard_map/ppermute | solution.py:18
  133.2 6.5 %collective-permute-start.30 = (f32[4,4664]{1,0:T(4,128)S(1)}, f32[4,4664]{1,0:T(4,128)S(1)}, u32[]{:S(2)}, u32[]{:S(2)}) collective-permute-start(f32[4,4664]{1,0:T(4,128)S(1)} %constant_dynamic-update-slice_fusion.13), channel_id=1, source_target_pairs={{0,32},{16,48},{32,0},{48,16},{1,33},{17,49},{33,1},{49,17},{2,34}... | collective-permute-start | bytes 223880 | tf_op jit(solution)/shard_map/ppermute | solution.py:18
  135.5 18.1 %collective-permute-start.31 = (f32[4,4664]{1,0:T(4,128)S(1)}, f32[4,4664]{1,0:T(4,128)}, u32[]{:S(2)}, u32[]{:S(2)}) collective-permute-start(f32[4,4664]{1,0:T(4,128)S(1)} %constant_dynamic-update-slice_fusion.13), channel_id=1, source_target_pairs={{0,48},{16,0},{32,16},{48,32},{1,49},{17,1},{33,17},{49,33},{2,50}... | collective-permute-start | bytes 223880 | tf_op jit(solution)/shard_map/ppermute | solution.py:18
  149.7 45.3 %all-to-all-start.1 = ((bf16[16,192,256]{2,1,0:T(8,128)(2,1)}), bf16[16,192,256]{2,1,0:T(8,128)(2,1)S(1)}, u32[]{:S(2)}, u32[]{:S(2)}) async-start(bf16[16,192,256]{2,1,0:T(8,128)(2,1)} %bitcast.15), calls=%async_computation.1 | async-start | bytes 3145728 | tf_op jit(solution)/shard_map/all_to_all | solution.py:22
  155.2 11.2 %collective-permute-start.32 = (f32[16,4664]{1,0:T(8,128)}, f32[16,4664]{1,0:T(8,128)S(1)}, u32[]{:S(2)}, u32[]{:S(2)}) collective-permute-start(f32[16,4664]{1,0:T(8,128)} %constant_dynamic-update-slice_fusion.9), channel_id=1, source_target_pairs={{0,64},{64,128},{128,192},{192,0},{1,65},{65,129},{129,193},{193,1... | collective-permute-start | bytes 895496 | tf_op jit(solution)/shard_map/ppermute | solution.py:18
  157.0 11.9 %collective-permute-start.33 = (f32[16,4664]{1,0:T(8,128)}, f32[16,4664]{1,0:T(8,128)S(1)}, u32[]{:S(2)}, u32[]{:S(2)}) collective-permute-start(f32[16,4664]{1,0:T(8,128)} %constant_dynamic-update-slice_fusion.9), channel_id=1, source_target_pairs={{0,128},{64,192},{128,0},{192,64},{1,129},{65,193},{129,1},{193,65... | collective-permute-start | bytes 895496 | tf_op jit(solution)/shard_map/ppermute | solution.py:18
  160.2 13.1 %collective-permute-start.34 = (f32[16,4664]{1,0:T(8,128)}, f32[16,4664]{1,0:T(8,128)S(1)}, u32[]{:S(2)}, u32[]{:S(2)}) collective-permute-start(f32[16,4664]{1,0:T(8,128)} %constant_dynamic-update-slice_fusion.9), channel_id=1, source_target_pairs={{0,192},{64,0},{128,64},{192,128},{1,193},{65,1},{129,65},{193,129... | collective-permute-start | bytes 895496 | tf_op jit(solution)/shard_map/ppermute | solution.py:18
  (25 other events, 188.1 us)

commit v7 on v5

--- a/solution.py
+++ b/solution.py
@@ -8,7 +8,7 @@
 SCALE = 0.5
 BF = jnp.bfloat16
 F32 = jnp.float32
-SIZES = {"y": 4, "x": 4, "zl": 2, "co": 2, "t": 4}
+SIZES = {"y": 4, "x": 4, "zl": 2, "co": 2, "t": 4, ("zl", "co"): 4}
 DP = ("y", "x", "zl", "co")
 N_DP = 64
 
@@ -72,59 +72,58 @@
             jax.ShapeDtypeStruct((1, width), F32),
         ],
         compiler_params=pltpu.CompilerParams(vmem_limit_bytes=60 * 1024 * 1024),
+        cost_estimate=pl.CostEstimate(
+            flops=2 * rows * width * (rank + 8 * count),
+            bytes_accessed=8 * rows * width,
+            transcendentals=0,
+        ),
     )(codes, scales, factor, out_factor)
 
 
-def tile_kernel(
-    where, scaled, far_low, far_high, ratio, own, other, own_swap, other_swap, first, second, wide, far
-):
-    rows = own.shape[1]
-    half = far_low.shape[0]
+def tile_kernel(where, *refs):
+    tokens, (ratio, *weights), (first, second), (wide, scaled) = (
+        refs[:7],
+        refs[7:12],
+        refs[12:14],
+        refs[14:],
+    )
+    rows = weights[0].shape[1]
+    half = tokens[1].shape[0]
     x, zl, co = where[0], where[1], where[2]
 
     @pl.when(pl.program_id(0) == 0)
     def _():
-        for source, base in ((far_low, 0), (far_high, half)):
-            for r in range(0, half, 16):
+        base = 0
+        for source in tokens:
+            for r in range(0, source.shape[0], 16):
                 value = source[r : r + 16, :].astype(F32) * ratio[...]
-                far[base + r : base + r + 16, :] = value.astype(BF)
-
-    for source, zi, c in (
-        (own, zl, co),
-        (other, 1 - zl, co),
-        (own_swap, zl, 1 - co),
-        (other_swap, 1 - zl, 1 - co),
-    ):
+                scaled[base + r : base + r + 16, :] = value.astype(BF)
+            base += source.shape[0]
+
+    places = ((zl, co), (1 - zl, co), (zl, 1 - co), (1 - zl, 1 - co))
+    for source, (zi, c) in zip(weights, places):
         row = pl.multiple_of((zi * 2 + c) * rows, rows)
         wide[pl.ds(row, rows), :] = source[0]
-
-    def product(value):
-        return lax.dot_general(
-            value, wide[...], (((1,), (1,)), ((), ())), preferred_element_type=F32
-        ).astype(BF)
-
+    tile = lax.dot_general(
+        scaled[...], wide[...], (((1,), (1,)), ((), ())), preferred_element_type=F32
+    ).astype(BF)
     n = 2 * half
-    tile = product(scaled[...])
-    for k, e in enumerate((0, 3, 1)):
+    for k, e in enumerate((0, 3, 1, 2)):
         first[lax.rem(x + e, 4), 0] = tile[k * n : k * n + half, :]
         second[lax.rem(x + e, 4), 0] = tile[k * n + half : (k + 1) * n, :]
-    tile = product(far[...])
-    first[lax.rem(x + 2, 4), 0] = tile[:half, :]
-    second[lax.rem(x + 2, 4), 0] = tile[half:, :]
-
-
-def tile_of(where, scaled, far_low, far_high, ratio, weights):
-    tokens, width = scaled.shape
-    half = far_low.shape[0]
-    n = 2 * half
+
+
+def tile_of(where, tokens, ratio, weights):
+    width = ratio.shape[1]
+    half = tokens[1].shape[0]
     rows = weights[0].shape[1]
 
     def place(i, where):
         step = jnp.where(i == 0, 0, jnp.where(i == 1, 3, i - 1))
         return 0, lax.rem(where[3] + step, 4), 0, 0
 
-    def whole(shape):
-        return pl.BlockSpec(shape, lambda i, w: (0, 0))
+    def whole(value):
+        return pl.BlockSpec(value.shape, lambda i, w: (0, 0))
 
     weight = pl.BlockSpec((1, rows, width), lambda i, w: (i, 0, 0))
     return pl.pallas_call(
@@ -132,20 +131,21 @@
         grid_spec=pltpu.PrefetchScalarGridSpec(
             num_scalar_prefetch=1,
             grid=(4,),
-            in_specs=[whole((tokens, width)), whole((half, width)), whole((half, width))]
-            + [whole((1, width))]
-            + [weight] * 4,
+            in_specs=[whole(v) for v in tokens] + [whole(ratio)] + [weight] * 4,
             out_specs=[pl.BlockSpec((4, 1, half, 4 * rows), place)] * 2,
-            scratch_shapes=[pltpu.VMEM((4 * rows, width), BF), pltpu.VMEM((n, width), BF)],
+            scratch_shapes=[
+                pltpu.VMEM((4 * rows, width), BF),
+                pltpu.VMEM((8 * half, width), BF),
+            ],
         ),
         out_shape=[jax.ShapeDtypeStruct((4, 4, half, 4 * rows), BF)] * 2,
         compiler_params=pltpu.CompilerParams(vmem_limit_bytes=40 * 1024 * 1024),
         cost_estimate=pl.CostEstimate(
-            flops=8 * n * 16 * rows * width,
-            bytes_accessed=2 * width * (4 * n + 16 * rows),
+            flops=16 * half * 16 * rows * width,
+            bytes_accessed=2 * width * (8 * half + 16 * rows),
             transcendentals=0,
         ),
-    )(where, scaled, far_low, far_high, ratio, *weights)
+    )(where, *tokens, ratio, *weights)
 
 
 def on_device(codes, scales, in_factor, out_factor, magnitude, inputs, grad, pre):
@@ -171,7 +171,7 @@
     left_low, right_high = shift(low_half, "x", 1), shift(high_half, "x", -1)
     other = shift(own, "zl", 1)
     own_down, own_up = shift(own, "y", 1), shift(own, "y", -1)
-    total = gather_sum(gather_sum(squares.reshape(-1, 128), "x"), "y")
+    total = gather_sum(squares.reshape(-1, 128), "y")
     phase = (left_low, right_high, other, own_down, own_up, total, low_half, high_half)
     phase = lax.optimization_barrier(phase)
     left_low, right_high, other, own_down, own_up, total, low_half, high_half = phase
@@ -179,7 +179,8 @@
     left_high, right_low = shift(high_half, "x", 1), shift(low_half, "x", -1)
     other_down, other_up = shift(other, "y", 1), shift(other, "y", -1)
     own_far = shift(own_down, "y", 1)
-    total = gather_sum(gather_sum(total, "co"), "zl")
+    total = after(gather_sum(total, "x"), other_down, other_up)
+    total = gather_sum(total, ("zl", "co"))
     phase = (left_low, right_high, left_high, right_low, other_down, other_up, own_far, total)
     phase = lax.optimization_barrier(phase)
     left_low, right_high, left_high, right_low, other_down, other_up, own_far, total = phase
@@ -193,10 +194,6 @@
         return (g.astype(F32) * ratio).astype(BF)
 
     scaled_own = scaled_of(grad)
-    scaled = scaled_of(
-        jnp.concatenate([grad, left_low, left_high, right_low, right_high], axis=0)
-    )
-
     factor_cols = lax.dynamic_slice_in_dim(in_factor, t * features, features, 0)
     hidden = jnp.dot(inputs, factor_cols, preferred_element_type=F32)
     back = lax.dot_general(
@@ -224,12 +221,14 @@
     keep = lax.dynamic_slice_in_dim(adapters, co * side, side, 0)
     give = lax.dynamic_slice_in_dim(adapters, (1 - co) * side, side, 0)
     adapters = keep + shift(give, "co", 1)
-    adapters = adapters + shift(adapters, "zl", 1)
+    got = shift(adapters, "zl", 1)
 
     where = jnp.stack([x, zl, co, y]).astype(jnp.int32)
+    tokens_all = (grad, left_low, left_high, right_low, right_high, far_low, far_high)
     weights = (own_rows, other_rows, own_swap, other_swap)
-    tiles = tile_of(where, scaled, far_low, far_high, ratio.reshape(1, -1), weights)
-    adapters = after(adapters, tiles[0])
+    tiles = tile_of(where, tokens_all, ratio.reshape(1, -1), weights)
+    adapters, got, *tiles = lax.optimization_barrier((adapters, got, *tiles))
+    adapters = adapters + got
     tiles = [swap_all(v.reshape(16, half, part), ("x", "t")) for v in tiles]
 
     for axis, index in (("y", y), ("x", x)):

time: 183 us -> 173 us (0.945)
  waiting for transfers between devices: 73.5 us -> 60.5 us
  starting transfers between devices: 75.8 us -> 72 us
  other arithmetic: 6.49 us -> 9.9 us
  Pallas kernels: 13.6 us -> 15.9 us
  matrix products: 1.45 us -> 3.46 us
    ppermute x41 -> x42, waiting for transfers between devices: 61.2 us -> 46.1 us  [shift(): return lax.ppermute(value, axis, [(i, (i + step) % n) for i in range(n)])]
    ppermute x41 -> x42, starting transfers between devices: 66.2 us -> 62.5 us  [shift(): return lax.ppermute(value, axis, [(i, (i + step) % n) for i in range(n)])]
    unnamed x29 -> x41, local copies, waits for them, and re-layouts: 5.31 us -> 2.31 us
    another operation x1, other arithmetic: 0.23 us -> 2.58 us  [on_device(): own_rows = jnp.stack([own, own_down, own_up, own_far])]
    pallas_call x1, Pallas kernels: 9.34 us -> 11.6 us  [tile_of(): pl.pallas_call(tile_kernel, grid_spec=pltpu.PrefetchScalarGridSpec(num_sc...]
    all_to_all x2, waiting for transfers between devices: 12.3 us -> 14.4 us  [swap_all(): return lax.all_to_all(value, axes, 0, 0, tiled=True)]
  transfers between devices with their start and end apart: 43 -> 44, of which waited for: 20 -> 26; matrix products, arithmetic and copies ran while one was open for 6% -> 8% of each run, Pallas kernels for 0% -> 9%
where the time goes in v7:
time: 173 us; the launch traced here: 171 us
  starting transfers between devices  72 us (42%)
  waiting for transfers between devices  60.5 us (35%)
  Pallas kernels  15.9 us (9%)
  other arithmetic  9.9 us (6%)
  local copies, waits for them, and re-layouts  8.26 us (5%)
  matrix products  3.46 us (2%)
    ppermute x42, starting transfers between devices, shift(): return lax.ppermute(value, axis, [(i, (i + step) % n) for i in range(n)])  62.5 us
    ppermute x42, waiting for transfers between devices, shift(): return lax.ppermute(value, axis, [(i, (i + step) % n) for i in range(n)])  46.1 us
    all_to_all x2, waiting for transfers between devices, swap_all(): return lax.all_to_all(value, axes, 0, 0, tiled=True)  14.4 us
    pallas_call x1, Pallas kernels, tile_of(): pl.pallas_call(tile_kernel, grid_spec=pltpu.PrefetchScalarGridSpec(num_sc...  11.6 us
    all_to_all x2, starting transfers between devices, swap_all(): return lax.all_to_all(value, axes, 0, 0, tiled=True)  9.54 us
    pallas_call x1, Pallas kernels, merge(): pl.pallas_call(body, grid=(steps,), in_specs=[columns(rows), whole(count,...  4.25 us
  transfers between devices with their start and end apart: 44, of which 26 were waited for; matrix products, arithmetic and copies ran while one was open for 8% of the time, Pallas kernels for 9%

profile of v7, /device:TPU:8, one launch (start us, length us, event | category | flops | bytes accessed | tf_op | source)
XLA Modules:
  0.0 171.1 jit_solution(17368861710032701723)
XLA Ops:
  0.6 2.5 %fusion.13 = (bf16[96,3584]{1,0:T(8,128)(2,1)}, bf16[96,3584]{1,0:T(8,128)(2,1)}) fusion(bf16[192,3584]{1,0:T(8,128)(2,1)} %refs_0_.3), kind=kLoop, calls=%fused_computation.51 | loop fusion | bytes 2752512 | tf_op jit(solution)/shard_map/slice | solution.py:170
  4.7 1.7 %collective-permute-start.1 = (bf16[96,3584]{1,0:T(8,128)(2,1)}, bf16[96,3584]{1,0:T(8,128)(2,1)S(1)}, u32[]{:S(2)}, u32[]{:S(2)}) collective-permute-start(bf16[96,3584]{1,0:T(8,128)(2,1)} %get-tuple-element.39), channel_id=1, source_target_pairs={{0,48},{16,0},{32,16},{48,32},{1,49},{17,1},{33,17},{49,33},{2,50}... | collective-permute-start | bytes 2064392 | tf_op jit(solution)/shard_map/ppermute | solution.py:18
  7.2 4.3 %shard_map.111 = (bf16[64,3584]{1,0:T(8,128)(2,1)}, f32[1,3584]{1,0:T(1,128)}) custom-call(s32[64,3584]{1,0:T(8,128)} %refs_0_.2, f32[56,64]{1,0:T(8,128)} %bitcast.51, bf16[64,64]{1,0:T(8,128)(2,1)} %copy.18.refs_2_, bf16[64,3584]{1,0:T(8,128)(2,1)} %refs_3_.1), custom_call_target="tpu_custom_call" | custom-call | flops 234881024 | bytes 1835008 | tf_op jit(solution)/shard_map/pallas_call | solution.py:65
  12.2 2.3 %collective-permute-start.7 = (f32[28,128]{1,0:T(8,128)S(1)}, f32[28,128]{1,0:T(8,128)S(1)}, u32[]{:S(2)}, u32[]{:S(2)}) collective-permute-start(f32[28,128]{1,0:T(8,128)S(1)} %bitcast.48), channel_id=1, source_target_pairs={{0,192},{64,0},{128,64},{192,128},{1,193},{65,1},{129,65},{193,129... | collective-permute-start | bytes 43016 | tf_op jit(solution)/shard_map/ppermute | solution.py:18
  15.3 1.9 %collective-permute-start.5 = (f32[28,128]{1,0:T(8,128)S(1)}, f32[28,128]{1,0:T(8,128)S(1)}, u32[]{:S(2)}, u32[]{:S(2)}) collective-permute-start(f32[28,128]{1,0:T(8,128)S(1)} %bitcast.50), channel_id=1, source_target_pairs={{0,64},{64,128},{128,192},{192,0},{1,65},{65,129},{129,193},{193,1... | collective-permute-start | bytes 43016 | tf_op jit(solution)/shard_map/ppermute | solution.py:18
  17.2 1.9 %collective-permute-start.2 = (bf16[64,3584]{1,0:T(8,128)(2,1)}, bf16[64,3584]{1,0:T(8,128)(2,1)S(1)}, u32[]{:S(2)}, u32[]{:S(2)}) collective-permute-start(bf16[64,3584]{1,0:T(8,128)(2,1)} %get-tuple-element.35), channel_id=1, source_target_pairs={{0,8},{8,0},{1,9},{9,1},{2,10},{10,2},{3,11},{11,3},{4,12},{12,4},... | collective-permute-start | bytes 1376264 | tf_op jit(solution)/shard_map/ppermute | solution.py:18
  19.7 2.0 %collective-permute-start.4 = (bf16[64,3584]{1,0:T(8,128)(2,1)}, bf16[64,3584]{1,0:T(8,128)(2,1)S(1)}, u32[]{:S(2)}, u32[]{:S(2)}) collective-permute-start(bf16[64,3584]{1,0:T(8,128)(2,1)} %get-tuple-element.35), channel_id=1, source_target_pairs={{0,192},{64,0},{128,64},{192,128},{1,193},{65,1},{129,65},{193,129... | collective-permute-start | bytes 1376264 | tf_op jit(solution)/shard_map/ppermute | solution.py:18
  21.8 6.7 %collective-permute-done.2 = bf16[64,3584]{1,0:T(8,128)(2,1)S(1)} collective-permute-done((bf16[64,3584]{1,0:T(8,128)(2,1)}, bf16[64,3584]{1,0:T(8,128)(2,1)S(1)}, u32[]{:S(2)}, u32[]{:S(2)}) %collective-permute-start.2) | collective-permute-done | bytes 458784 | tf_op jit(solution)/shard_map/ppermute | solution.py:18
  38.7 2.0 %collective-permute-done.14 = f32[28,128]{1,0:T(8,128)S(1)} collective-permute-done((f32[28,128]{1,0:T(8,128)S(1)}, f32[28,128]{1,0:T(8,128)S(1)}, u32[]{:S(2)}, u32[]{:S(2)}) %collective-permute-start.14) | collective-permute-done | bytes 14368 | tf_op jit(solution)/shard_map/ppermute | solution.py:18
  45.4 1.8 %collective-permute-start.12 = (bf16[64,3584]{1,0:T(8,128)(2,1)}, bf16[64,3584]{1,0:T(8,128)(2,1)}, u32[]{:S(2)}, u32[]{:S(2)}) collective-permute-start(bf16[64,3584]{1,0:T(8,128)(2,1)} %copy-done.15), channel_id=1, source_target_pairs={{0,64},{64,128},{128,192},{192,0},{1,65},{65,129},{129,193},{193,1... | collective-permute-start | bytes 1376264 | tf_op jit(solution)/shard_map/ppermute | solution.py:18
  47.2 1.9 %collective-permute-start.17 = (f32[28,128]{1,0:T(8,128)S(1)}, f32[28,128]{1,0:T(8,128)S(1)}, u32[]{:S(2)}, u32[]{:S(2)}) collective-permute-start(f32[28,128]{1,0:T(8,128)S(1)} %add_add_fusion.3), channel_id=1, source_target_pairs={{0,8},{4,12},{8,0},{12,4},{1,9},{5,13},{9,1},{13,5},{2,10},{6,14},... | collective-permute-start | bytes 43016 | tf_op jit(solution)/shard_map/ppermute | solution.py:18
  52.3 7.2 %collective-permute-done.12 = bf16[64,3584]{1,0:T(8,128)(2,1)} collective-permute-done((bf16[64,3584]{1,0:T(8,128)(2,1)}, bf16[64,3584]{1,0:T(8,128)(2,1)}, u32[]{:S(2)}, u32[]{:S(2)}) %collective-permute-start.12) | collective-permute-done | bytes 458784 | tf_op jit(solution)/shard_map/ppermute | solution.py:18
  61.2 6.4 %collective-permute-start.24 = (bf16[192,128]{0,1:T(8,128)(2,1)S(1)}, bf16[192,128]{0,1:T(8,128)(2,1)S(1)}, u32[]{:S(2)}, u32[]{:S(2)}) collective-permute-start(bf16[192,128]{0,1:T(8,128)(2,1)S(1)} %pad_maximum_fusion.4), channel_id=1, source_target_pairs={{0,3},{1,0},{2,1},{3,2},{4,7},{5,4},{6,5},{7,6},{8,11},{9,8},{10,9... | collective-permute-start | bytes 147464 | tf_op jit(solution)/shard_map/ppermute | solution.py:18
  68.6 2.8 %collective-permute-start.22 = (bf16[192,128]{0,1:T(8,128)(2,1)S(1)}, bf16[192,128]{0,1:T(8,128)(2,1)S(1)}, u32[]{:S(2)}, u32[]{:S(2)}) collective-permute-start(bf16[192,128]{0,1:T(8,128)(2,1)S(1)} %pad_maximum_fusion.4), channel_id=1, source_target_pairs={{0,1},{1,2},{2,3},{3,0},{4,5},{5,6},{6,7},{7,4},{8,9},{9,10},{10,1... | collective-permute-start | bytes 147464 | tf_op jit(solution)/shard_map/ppermute | solution.py:18
  72.7 2.0 %collective-permute-start.20 = (bf16[96,3584]{1,0:T(8,128)(2,1)S(1)}, bf16[96,3584]{1,0:T(8,128)(2,1)S(1)}, u32[]{:S(2)}, u32[]{:S(2)}) collective-permute-start(bf16[96,3584]{1,0:T(8,128)(2,1)S(1)} %collective-permute-done.1.refs_4_), channel_id=1, source_target_pairs={{0,48},{16,0},{32,16},{48,32},{1,49},{17,1},{33,17},{49,33},{2,50}... | collective-permute-start | bytes 2064392 | tf_op jit(solution)/shard_map/ppermute | solution.py:18
  74.7 2.6 %pad_maximum_fusion.refs_8_ = bf16[4,64,3584]{2,1,0:T(8,128)(2,1)} fusion(bf16[1,64,3584]{2,1,0:T(8,128)(2,1)} %bitcast.10, bf16[1,64,3584]{2,1,0:T(8,128)(2,1)S(1)} %bitcast.46, bf16[1,64,3584]{2,1,0:T(8,128)(2,1)S(1)} %bitcast.45, bf16[1,64,3584]{2,1,0:T(8,128)(2,1)S(1)} %bitcast.42), kind=kLoop, calls=%fused_computation.5 | loop fusion | flops 2752512 | bytes 3670016 | tf_op jit(solution)/shard_map/stack | solution.py:216
  77.3 3.0 %collective-permute-start.21 = (bf16[64,3584]{1,0:T(8,128)(2,1)S(1)}, bf16[64,3584]{1,0:T(8,128)(2,1)S(1)}, u32[]{:S(2)}, u32[]{:S(2)}) collective-permute-start(bf16[64,3584]{1,0:T(8,128)(2,1)S(1)} %copy-done.14), channel_id=1, source_target_pairs={{0,192},{64,0},{128,64},{192,128},{1,193},{65,1},{129,65},{193,129... | collective-permute-start | bytes 1376264 | tf_op jit(solution)/shard_map/ppermute | solution.py:18
  81.1 7.4 %collective-permute-done.21 = bf16[64,3584]{1,0:T(8,128)(2,1)S(1)} collective-permute-done((bf16[64,3584]{1,0:T(8,128)(2,1)S(1)}, bf16[64,3584]{1,0:T(8,128)(2,1)S(1)}, u32[]{:S(2)}, u32[]{:S(2)}) %collective-permute-start.21) | collective-permute-done | bytes 458784 | tf_op jit(solution)/shard_map/ppermute | solution.py:18
  95.8 11.6 %shard_map.112 = (bf16[4,4,96,256]{3,2,1,0:T(8,128)(2,1)}, bf16[4,4,96,256]{3,2,1,0:T(8,128)(2,1)}) custom-call(s32[4]{0:T(128)S(1)} %pad_add_fusion.where, bf16[192,3584]{1,0:T(8,128)(2,1)S(1)} %copy-done.1, bf16[96,3584]{1,0:T(8,128)(2,1)S(1)} %collective-permute-done.refs_1_, bf16[96,3584]{1,0:T(8,128)(2,1)} %collective-permute-done.8.refs_2_, ...), custom_call_target="tpu_custom_call" | custom-call | flops 5637144576 | bytes 12845056 | tf_op jit(solution)/shard_map/pallas_call | solution.py:129
  107.4 2.3 %collective-permute-done.26 = f32[32,4664]{1,0:T(8,128)S(1)} collective-permute-done((f32[32,4664]{1,0:T(8,128)S(1)}, f32[32,4664]{1,0:T(8,128)S(1)}, u32[]{:S(2)}, u32[]{:S(2)}) %collective-permute-start.26) | collective-permute-done | bytes 597024 | tf_op jit(solution)/shard_map/ppermute | solution.py:18
  109.9 2.8 %collective-permute-start.31 = (f32[8,4664]{1,0:T(8,128)S(1)}, f32[8,4664]{1,0:T(8,128)S(1)}, u32[]{:S(2)}, u32[]{:S(2)}) collective-permute-start(f32[8,4664]{1,0:T(8,128)S(1)} %get-tuple-element.69), channel_id=1, source_target_pairs={{0,192},{64,0},{128,64},{192,128},{1,193},{65,1},{129,65},{193,129... | collective-permute-start | bytes 447752 | tf_op jit(solution)/shard_map/ppermute | solution.py:18
  112.7 2.4 %collective-permute-start.29 = (f32[8,4664]{1,0:T(8,128)S(1)}, f32[8,4664]{1,0:T(8,128)S(1)}, u32[]{:S(2)}, u32[]{:S(2)}) collective-permute-start(f32[8,4664]{1,0:T(8,128)S(1)} %get-tuple-element.68), channel_id=1, source_target_pairs={{0,64},{64,128},{128,192},{192,0},{1,65},{65,129},{129,193},{193,1... | collective-permute-start | bytes 447752 | tf_op jit(solution)/shard_map/ppermute | solution.py:18
  115.1 5.9 %all-to-all-start = ((bf16[16,96,256]{2,1,0:T(8,128)(2,1)}), bf16[16,96,256]{2,1,0:T(8,128)(2,1)S(1)}, u32[]{:S(2)}, u32[]{:S(2)}) async-start(bf16[16,96,256]{2,1,0:T(8,128)(2,1)} %bitcast.15), calls=%async_computation | async-start | bytes 1572864 | tf_op jit(solution)/shard_map/all_to_all | solution.py:22
  121.2 3.2 %collective-permute-start.34 = (f32[2,4664]{1,0:T(2,128)S(1)}, f32[2,4664]{1,0:T(2,128)S(1)}, u32[]{:S(2)}, u32[]{:S(2)}) collective-permute-start(f32[2,4664]{1,0:T(2,128)S(1)} %get-tuple-element.72), channel_id=1, source_target_pairs={{0,48},{16,0},{32,16},{48,32},{1,49},{17,1},{33,17},{49,33},{2,50}... | collective-permute-start | bytes 111944 | tf_op jit(solution)/shard_map/ppermute | solution.py:18
  127.3 2.6 %collective-permute-done.33 = f32[2,4664]{1,0:T(2,128)S(1)} collective-permute-done((f32[2,4664]{1,0:T(2,128)S(1)}, f32[2,4664]{1,0:T(2,128)S(1)}, u32[]{:S(2)}, u32[]{:S(2)}) %collective-permute-start.33) | collective-permute-done | bytes 37344 | tf_op jit(solution)/shard_map/ppermute | solution.py:18
  131.4 13.0 %all-to-all-done = bf16[16,96,256]{2,1,0:T(8,128)(2,1)S(1)} async-done(((bf16[16,96,256]{2,1,0:T(8,128)(2,1)}), bf16[16,96,256]{2,1,0:T(8,128)(2,1)S(1)}, u32[]{:S(2)}, u32[]{:S(2)}) %all-to-all-start) | async-done | bytes 786464 | tf_op jit(solution)/shard_map/all_to_all | solution.py:22
  144.3 3.6 %all-to-all-start.1 = ((bf16[16,96,256]{2,1,0:T(8,128)(2,1)}), bf16[16,96,256]{2,1,0:T(8,128)(2,1)S(1)}, u32[]{:S(2)}, u32[]{:S(2)}) async-start(bf16[16,96,256]{2,1,0:T(8,128)(2,1)} %bitcast.18), calls=%async_computation.1 | async-start | bytes 1572864 | tf_op jit(solution)/shard_map/all_to_all | solution.py:22
  148.0 1.8 %collective-permute-start.35 = (f32[2,4664]{1,0:T(2,128)S(1)}, f32[2,4664]{1,0:T(2,128)S(1)}, u32[]{:S(2)}, u32[]{:S(2)}) collective-permute-start(f32[2,4664]{1,0:T(2,128)S(1)} %add_add_fusion.1), channel_id=1, source_target_pairs={{0,16},{16,32},{32,48},{48,0},{1,17},{17,33},{33,49},{49,1},{2,18}... | collective-permute-start | bytes 111944 | tf_op jit(solution)/shard_map/ppermute | solution.py:18
  149.8 2.7 %collective-permute-start.36 = (f32[2,4664]{1,0:T(2,128)S(1)}, f32[2,4664]{1,0:T(2,128)S(1)}, u32[]{:S(2)}, u32[]{:S(2)}) collective-permute-start(f32[2,4664]{1,0:T(2,128)S(1)} %add_add_fusion.1), channel_id=1, source_target_pairs={{0,32},{16,48},{32,0},{48,16},{1,33},{17,49},{33,1},{49,17},{2,34}... | collective-permute-start | bytes 111944 | tf_op jit(solution)/shard_map/ppermute | solution.py:18
  156.5 2.2 %collective-permute-start.38 = (f32[8,4664]{1,0:T(8,128)S(1)}, f32[8,4664]{1,0:T(8,128)S(1)}, u32[]{:S(2)}, u32[]{:S(2)}) collective-permute-start(f32[8,4664]{1,0:T(8,128)S(1)} %constant_dynamic-update-slice_fusion.6), channel_id=1, source_target_pairs={{0,64},{64,128},{128,192},{192,0},{1,65},{65,129},{129,193},{193,1... | collective-permute-start | bytes 447752 | tf_op jit(solution)/shard_map/ppermute | solution.py:18
  159.2 2.1 %collective-permute-start.40 = (f32[8,4664]{1,0:T(8,128)S(1)}, f32[8,4664]{1,0:T(8,128)S(1)}, u32[]{:S(2)}, u32[]{:S(2)}) collective-permute-start(f32[8,4664]{1,0:T(8,128)S(1)} %constant_dynamic-update-slice_fusion.6), channel_id=1, source_target_pairs={{0,192},{64,0},{128,64},{192,128},{1,193},{65,1},{129,65},{193,129... | collective-permute-start | bytes 447752 | tf_op jit(solution)/shard_map/ppermute | solution.py:18
  161.8 3.7 %collective-permute-done.39 = f32[8,4664]{1,0:T(8,128)S(1)} collective-permute-done((f32[8,4664]{1,0:T(8,128)S(1)}, f32[8,4664]{1,0:T(8,128)S(1)}, u32[]{:S(2)}, u32[]{:S(2)}) %collective-permute-start.39) | collective-permute-done | bytes 149280 | tf_op jit(solution)/shard_map/ppermute | solution.py:18
  (149 shorter events, 49.5 us)
Async XLA Ops:
  3.2 27.6 %collective-permute-start = (bf16[96,3584]{1,0:T(8,128)(2,1)}, bf16[96,3584]{1,0:T(8,128)(2,1)S(1)}, u32[]{:S(2)}, u32[]{:S(2)}) collective-permute-start(bf16[96,3584]{1,0:T(8,128)(2,1)} %get-tuple-element.40), channel_id=1, source_target_pairs={{0,16},{16,32},{32,48},{48,0},{1,17},{17,33},{33,49},{49,1},{2,18}... | collective-permute-start | bytes 2064392 | tf_op jit(solution)/shard_map/ppermute | solution.py:18
  4.7 26.1 %collective-permute-start.1 = (bf16[96,3584]{1,0:T(8,128)(2,1)}, bf16[96,3584]{1,0:T(8,128)(2,1)S(1)}, u32[]{:S(2)}, u32[]{:S(2)}) collective-permute-start(bf16[96,3584]{1,0:T(8,128)(2,1)} %get-tuple-element.39), channel_id=1, source_target_pairs={{0,48},{16,0},{32,16},{48,32},{1,49},{17,1},{33,17},{49,33},{2,50}... | collective-permute-start | bytes 2064392 | tf_op jit(solution)/shard_map/ppermute | solution.py:18
  17.2 11.2 %collective-permute-start.2 = (bf16[64,3584]{1,0:T(8,128)(2,1)}, bf16[64,3584]{1,0:T(8,128)(2,1)S(1)}, u32[]{:S(2)}, u32[]{:S(2)}) collective-permute-start(bf16[64,3584]{1,0:T(8,128)(2,1)} %get-tuple-element.35), channel_id=1, source_target_pairs={{0,8},{8,0},{1,9},{9,1},{2,10},{10,2},{3,11},{11,3},{4,12},{12,4},... | collective-permute-start | bytes 1376264 | tf_op jit(solution)/shard_map/ppermute | solution.py:18
  19.7 10.2 %collective-permute-start.3 = (bf16[64,3584]{1,0:T(8,128)(2,1)}, bf16[64,3584]{1,0:T(8,128)(2,1)S(1)}, u32[]{:S(2)}, u32[]{:S(2)}) collective-permute-start(bf16[64,3584]{1,0:T(8,128)(2,1)} %get-tuple-element.35), channel_id=1, source_target_pairs={{0,64},{64,128},{128,192},{192,0},{1,65},{65,129},{129,193},{193,1... | collective-permute-start | bytes 1376264 | tf_op jit(solution)/shard_map/ppermute | solution.py:18
  19.7 11.1 %collective-permute-start.4 = (bf16[64,3584]{1,0:T(8,128)(2,1)}, bf16[64,3584]{1,0:T(8,128)(2,1)S(1)}, u32[]{:S(2)}, u32[]{:S(2)}) collective-permute-start(bf16[64,3584]{1,0:T(8,128)(2,1)} %get-tuple-element.35), channel_id=1, source_target_pairs={{0,192},{64,0},{128,64},{192,128},{1,193},{65,1},{129,65},{193,129... | collective-permute-start | bytes 1376264 | tf_op jit(solution)/shard_map/ppermute | solution.py:18
  31.6 9.8 %collective-permute-start.10 = (bf16[64,3584]{1,0:T(8,128)(2,1)S(1)}, bf16[64,3584]{1,0:T(8,128)(2,1)S(1)}, u32[]{:S(2)}, u32[]{:S(2)}) collective-permute-start(bf16[64,3584]{1,0:T(8,128)(2,1)S(1)} %collective-permute-done.2), channel_id=1, source_target_pairs={{0,64},{64,128},{128,192},{192,0},{1,65},{65,129},{129,193},{193,1... | collective-permute-start | bytes 1376264 | tf_op jit(solution)/shard_map/ppermute | solution.py:18
  33.3 9.6 %collective-permute-start.11 = (bf16[64,3584]{1,0:T(8,128)(2,1)S(1)}, bf16[64,3584]{1,0:T(8,128)(2,1)S(1)}, u32[]{:S(2)}, u32[]{:S(2)}) collective-permute-start(bf16[64,3584]{1,0:T(8,128)(2,1)S(1)} %collective-permute-done.2), channel_id=1, source_target_pairs={{0,192},{64,0},{128,64},{192,128},{1,193},{65,1},{129,65},{193,129... | collective-permute-start | bytes 1376264 | tf_op jit(solution)/shard_map/ppermute | solution.py:18
  35.2 5.5 %collective-permute-start.14 = (f32[28,128]{1,0:T(8,128)S(1)}, f32[28,128]{1,0:T(8,128)S(1)}, u32[]{:S(2)}, u32[]{:S(2)}) collective-permute-start(f32[28,128]{1,0:T(8,128)S(1)} %add_add_fusion.4), channel_id=1, source_target_pairs={{0,32},{16,48},{32,0},{48,16},{1,33},{17,49},{33,1},{49,17},{2,34}... | collective-permute-start | bytes 43016 | tf_op jit(solution)/shard_map/ppermute | solution.py:18
  37.4 22.2 %collective-permute-start.8 = (bf16[96,3584]{1,0:T(8,128)(2,1)}, bf16[96,3584]{1,0:T(8,128)(2,1)}, u32[]{:S(2)}, u32[]{:S(2)}) collective-permute-start(bf16[96,3584]{1,0:T(8,128)(2,1)} %get-tuple-element.39), channel_id=1, source_target_pairs={{0,16},{16,32},{32,48},{48,0},{1,17},{17,33},{33,49},{49,1},{2,18}... | collective-permute-start | bytes 2064392 | tf_op jit(solution)/shard_map/ppermute | solution.py:18
  40.7 18.9 %collective-permute-start.9 = (bf16[96,3584]{1,0:T(8,128)(2,1)}, bf16[96,3584]{1,0:T(8,128)(2,1)}, u32[]{:S(2)}, u32[]{:S(2)}) collective-permute-start(bf16[96,3584]{1,0:T(8,128)(2,1)} %get-tuple-element.40), channel_id=1, source_target_pairs={{0,48},{16,0},{32,16},{48,32},{1,49},{17,1},{33,17},{49,33},{2,50}... | collective-permute-start | bytes 2064392 | tf_op jit(solution)/shard_map/ppermute | solution.py:18
  43.7 5.5 %collective-permute-start.18 = (f32[28,128]{1,0:T(8,128)S(1)}, f32[28,128]{1,0:T(8,128)S(1)}, u32[]{:S(2)}, u32[]{:S(2)}) collective-permute-start(f32[28,128]{1,0:T(8,128)S(1)} %add_add_fusion.3), channel_id=1, source_target_pairs={{0,12},{4,0},{8,4},{12,8},{1,13},{5,1},{9,5},{13,9},{2,14},{6,2},{... | collective-permute-start | bytes 43016 | tf_op jit(solution)/shard_map/ppermute | solution.py:18
  45.4 14.2 %collective-permute-start.12 = (bf16[64,3584]{1,0:T(8,128)(2,1)}, bf16[64,3584]{1,0:T(8,128)(2,1)}, u32[]{:S(2)}, u32[]{:S(2)}) collective-permute-start(bf16[64,3584]{1,0:T(8,128)(2,1)} %copy-done.15), channel_id=1, source_target_pairs={{0,64},{64,128},{128,192},{192,0},{1,65},{65,129},{129,193},{193,1... | collective-permute-start | bytes 1376264 | tf_op jit(solution)/shard_map/ppermute | solution.py:18
  61.2 16.0 %collective-permute-start.24 = (bf16[192,128]{0,1:T(8,128)(2,1)S(1)}, bf16[192,128]{0,1:T(8,128)(2,1)S(1)}, u32[]{:S(2)}, u32[]{:S(2)}) collective-permute-start(bf16[192,128]{0,1:T(8,128)(2,1)S(1)} %pad_maximum_fusion.4), channel_id=1, source_target_pairs={{0,3},{1,0},{2,1},{3,2},{4,7},{5,4},{6,5},{7,6},{8,11},{9,8},{10,9... | collective-permute-start | bytes 147464 | tf_op jit(solution)/shard_map/ppermute | solution.py:18
  67.6 12.7 %collective-permute-start.23 = (bf16[192,128]{0,1:T(8,128)(2,1)S(1)}, bf16[192,128]{0,1:T(8,128)(2,1)S(1)}, u32[]{:S(2)}, u32[]{:S(2)}) collective-permute-start(bf16[192,128]{0,1:T(8,128)(2,1)S(1)} %pad_maximum_fusion.4), channel_id=1, source_target_pairs={{0,2},{1,3},{2,0},{3,1},{4,6},{5,7},{6,4},{7,5},{8,10},{9,11},{10,... | collective-permute-start | bytes 147464 | tf_op jit(solution)/shard_map/ppermute | solution.py:18
  68.6 11.7 %collective-permute-start.22 = (bf16[192,128]{0,1:T(8,128)(2,1)S(1)}, bf16[192,128]{0,1:T(8,128)(2,1)S(1)}, u32[]{:S(2)}, u32[]{:S(2)}) collective-permute-start(bf16[192,128]{0,1:T(8,128)(2,1)S(1)} %pad_maximum_fusion.4), channel_id=1, source_target_pairs={{0,1},{1,2},{2,3},{3,0},{4,5},{5,6},{6,7},{7,4},{8,9},{9,10},{10,1... | collective-permute-start | bytes 147464 | tf_op jit(solution)/shard_map/ppermute | solution.py:18
  71.4 17.6 %collective-permute-start.19 = (bf16[96,3584]{1,0:T(8,128)(2,1)S(1)}, bf16[96,3584]{1,0:T(8,128)(2,1)S(1)}, u32[]{:S(2)}, u32[]{:S(2)}) collective-permute-start(bf16[96,3584]{1,0:T(8,128)(2,1)S(1)} %collective-permute-done.refs_1_), channel_id=1, source_target_pairs={{0,16},{16,32},{32,48},{48,0},{1,17},{17,33},{33,49},{49,1},{2,18}... | collective-permute-start | bytes 2064392 | tf_op jit(solution)/shard_map/ppermute | solution.py:18
  72.7 16.4 %collective-permute-start.20 = (bf16[96,3584]{1,0:T(8,128)(2,1)S(1)}, bf16[96,3584]{1,0:T(8,128)(2,1)S(1)}, u32[]{:S(2)}, u32[]{:S(2)}) collective-permute-start(bf16[96,3584]{1,0:T(8,128)(2,1)S(1)} %collective-permute-done.1.refs_4_), channel_id=1, source_target_pairs={{0,48},{16,0},{32,16},{48,32},{1,49},{17,1},{33,17},{49,33},{2,50}... | collective-permute-start | bytes 2064392 | tf_op jit(solution)/shard_map/ppermute | solution.py:18
  77.3 11.3 %collective-permute-start.21 = (bf16[64,3584]{1,0:T(8,128)(2,1)S(1)}, bf16[64,3584]{1,0:T(8,128)(2,1)S(1)}, u32[]{:S(2)}, u32[]{:S(2)}) collective-permute-start(bf16[64,3584]{1,0:T(8,128)(2,1)S(1)} %copy-done.14), channel_id=1, source_target_pairs={{0,192},{64,0},{128,64},{192,128},{1,193},{65,1},{129,65},{193,129... | collective-permute-start | bytes 1376264 | tf_op jit(solution)/shard_map/ppermute | solution.py:18
  80.3 14.9 %collective-permute-start.27 = (bf16[4,64,3584]{2,1,0:T(8,128)(2,1)}, bf16[4,64,3584]{2,1,0:T(8,128)(2,1)}, u32[]{:S(2)}, u32[]{:S(2)}) collective-permute-start(bf16[4,64,3584]{2,1,0:T(8,128)(2,1)} %pad_maximum_fusion.refs_8_), channel_id=1, source_target_pairs={{0,4},{4,0},{1,5},{5,1},{2,6},{6,2},{3,7},{7,3},{8,12},{12,8},{9,1... | collective-permute-start | bytes 5505032 | tf_op jit(solution)/shard_map/ppermute | solution.py:18
  93.8 16.0 %collective-permute-start.26 = (f32[32,4664]{1,0:T(8,128)S(1)}, f32[32,4664]{1,0:T(8,128)S(1)}, u32[]{:S(2)}, u32[]{:S(2)}) collective-permute-start(f32[32,4664]{1,0:T(8,128)S(1)} %dynamic-slice_add_fusion), channel_id=1, source_target_pairs={{0,8},{8,0},{1,9},{9,1},{2,10},{10,2},{3,11},{11,3},{4,12},{12,4},... | collective-permute-start | bytes 1790984 | tf_op jit(solution)/shard_map/ppermute | solution.py:18
  109.9 11.2 %collective-permute-start.31 = (f32[8,4664]{1,0:T(8,128)S(1)}, f32[8,4664]{1,0:T(8,128)S(1)}, u32[]{:S(2)}, u32[]{:S(2)}) collective-permute-start(f32[8,4664]{1,0:T(8,128)S(1)} %get-tuple-element.69), channel_id=1, source_target_pairs={{0,192},{64,0},{128,64},{192,128},{1,193},{65,1},{129,65},{193,129... | collective-permute-start | bytes 447752 | tf_op jit(solution)/shard_map/ppermute | solution.py:18
  112.7 8.4 %collective-permute-start.30 = (f32[8,4664]{1,0:T(8,128)S(1)}, f32[8,4664]{1,0:T(8,128)S(1)}, u32[]{:S(2)}, u32[]{:S(2)}) collective-permute-start(f32[8,4664]{1,0:T(8,128)S(1)} %get-tuple-element.70), channel_id=1, source_target_pairs={{0,128},{64,192},{128,0},{192,64},{1,129},{65,193},{129,1},{193,65... | collective-permute-start | bytes 447752 | tf_op jit(solution)/shard_map/ppermute | solution.py:18
  112.7 8.4 %collective-permute-start.29 = (f32[8,4664]{1,0:T(8,128)S(1)}, f32[8,4664]{1,0:T(8,128)S(1)}, u32[]{:S(2)}, u32[]{:S(2)}) collective-permute-start(f32[8,4664]{1,0:T(8,128)S(1)} %get-tuple-element.68), channel_id=1, source_target_pairs={{0,64},{64,128},{128,192},{192,0},{1,65},{65,129},{129,193},{193,1... | collective-permute-start | bytes 447752 | tf_op jit(solution)/shard_map/ppermute | solution.py:18
  115.1 29.3 %all-to-all-start = ((bf16[16,96,256]{2,1,0:T(8,128)(2,1)}), bf16[16,96,256]{2,1,0:T(8,128)(2,1)S(1)}, u32[]{:S(2)}, u32[]{:S(2)}) async-start(bf16[16,96,256]{2,1,0:T(8,128)(2,1)} %bitcast.15), calls=%async_computation | async-start | bytes 1572864 | tf_op jit(solution)/shard_map/all_to_all | solution.py:22
  121.2 6.1 %collective-permute-start.34 = (f32[2,4664]{1,0:T(2,128)S(1)}, f32[2,4664]{1,0:T(2,128)S(1)}, u32[]{:S(2)}, u32[]{:S(2)}) collective-permute-start(f32[2,4664]{1,0:T(2,128)S(1)} %get-tuple-element.72), channel_id=1, source_target_pairs={{0,48},{16,0},{32,16},{48,32},{1,49},{17,1},{33,17},{49,33},{2,50}... | collective-permute-start | bytes 111944 | tf_op jit(solution)/shard_map/ppermute | solution.py:18
  124.4 5.5 %collective-permute-start.33 = (f32[2,4664]{1,0:T(2,128)S(1)}, f32[2,4664]{1,0:T(2,128)S(1)}, u32[]{:S(2)}, u32[]{:S(2)}) collective-permute-start(f32[2,4664]{1,0:T(2,128)S(1)} %get-tuple-element.73), channel_id=1, source_target_pairs={{0,32},{16,48},{32,0},{48,16},{1,33},{17,49},{33,1},{49,17},{2,34}... | collective-permute-start | bytes 111944 | tf_op jit(solution)/shard_map/ppermute | solution.py:18
  125.2 6.1 %collective-permute-start.32 = (f32[2,4664]{1,0:T(2,128)S(1)}, f32[2,4664]{1,0:T(2,128)S(1)}, u32[]{:S(2)}, u32[]{:S(2)}) collective-permute-start(f32[2,4664]{1,0:T(2,128)S(1)} %get-tuple-element.71), channel_id=1, source_target_pairs={{0,16},{16,32},{32,48},{48,0},{1,17},{17,33},{33,49},{49,1},{2,18}... | collective-permute-start | bytes 111944 | tf_op jit(solution)/shard_map/ppermute | solution.py:18
  144.3 23.2 %all-to-all-start.1 = ((bf16[16,96,256]{2,1,0:T(8,128)(2,1)}), bf16[16,96,256]{2,1,0:T(8,128)(2,1)S(1)}, u32[]{:S(2)}, u32[]{:S(2)}) async-start(bf16[16,96,256]{2,1,0:T(8,128)(2,1)} %bitcast.18), calls=%async_computation.1 | async-start | bytes 1572864 | tf_op jit(solution)/shard_map/all_to_all | solution.py:22
  148.0 7.8 %collective-permute-start.35 = (f32[2,4664]{1,0:T(2,128)S(1)}, f32[2,4664]{1,0:T(2,128)S(1)}, u32[]{:S(2)}, u32[]{:S(2)}) collective-permute-start(f32[2,4664]{1,0:T(2,128)S(1)} %add_add_fusion.1), channel_id=1, source_target_pairs={{0,16},{16,32},{32,48},{48,0},{1,17},{17,33},{33,49},{49,1},{2,18}... | collective-permute-start | bytes 111944 | tf_op jit(solution)/shard_map/ppermute | solution.py:18
  149.8 6.1 %collective-permute-start.36 = (f32[2,4664]{1,0:T(2,128)S(1)}, f32[2,4664]{1,0:T(2,128)S(1)}, u32[]{:S(2)}, u32[]{:S(2)}) collective-permute-start(f32[2,4664]{1,0:T(2,128)S(1)} %add_add_fusion.1), channel_id=1, source_target_pairs={{0,32},{16,48},{32,0},{48,16},{1,33},{17,49},{33,1},{49,17},{2,34}... | collective-permute-start | bytes 111944 | tf_op jit(solution)/shard_map/ppermute | solution.py:18
  158.7 6.8 %collective-permute-start.39 = (f32[8,4664]{1,0:T(8,128)S(1)}, f32[8,4664]{1,0:T(8,128)S(1)}, u32[]{:S(2)}, u32[]{:S(2)}) collective-permute-start(f32[8,4664]{1,0:T(8,128)S(1)} %constant_dynamic-update-slice_fusion.6), channel_id=1, source_target_pairs={{0,128},{64,192},{128,0},{192,64},{1,129},{65,193},{129,1},{193,65... | collective-permute-start | bytes 447752 | tf_op jit(solution)/shard_map/ppermute | solution.py:18
  159.2 6.8 %collective-permute-start.40 = (f32[8,4664]{1,0:T(8,128)S(1)}, f32[8,4664]{1,0:T(8,128)S(1)}, u32[]{:S(2)}, u32[]{:S(2)}) collective-permute-start(f32[8,4664]{1,0:T(8,128)S(1)} %constant_dynamic-update-slice_fusion.6), channel_id=1, source_target_pairs={{0,192},{64,0},{128,64},{192,128},{1,193},{65,1},{129,65},{193,129... | collective-permute-start | bytes 447752 | tf_op jit(solution)/shard_map/ppermute | solution.py:18
  (32 other events, 239.4 us)

commit v8 on v7

--- a/solution.py
+++ b/solution.py
@@ -171,15 +171,17 @@
     left_low, right_high = shift(low_half, "x", 1), shift(high_half, "x", -1)
     other = shift(own, "zl", 1)
     own_down, own_up = shift(own, "y", 1), shift(own, "y", -1)
-    total = gather_sum(squares.reshape(-1, 128), "y")
-    phase = (left_low, right_high, other, own_down, own_up, total, low_half, high_half)
+    total = squares.reshape(-1, 128)
+    sums = [shift(total, "y", k) for k in (1, 2, 3)]
+    phase = (left_low, right_high, other, own_down, own_up, low_half, high_half, total, *sums)
     phase = lax.optimization_barrier(phase)
-    left_low, right_high, other, own_down, own_up, total, low_half, high_half = phase
+    left_low, right_high, other, own_down, own_up, low_half, high_half, *sums = phase
+    total = sum(sums[1:], sums[0])
 
     left_high, right_low = shift(high_half, "x", 1), shift(low_half, "x", -1)
     other_down, other_up = shift(other, "y", 1), shift(other, "y", -1)
     own_far = shift(own_down, "y", 1)
-    total = after(gather_sum(total, "x"), other_down, other_up)
+    total = after(gather_sum(total, "x"), other_down, other_up, own_far)
     total = gather_sum(total, ("zl", "co"))
     phase = (left_low, right_high, left_high, right_low, other_down, other_up, own_far, total)
     phase = lax.optimization_barrier(phase)
@@ -201,6 +203,8 @@
     )
     low = jnp.concatenate([hidden, back], axis=1).astype(BF)
     pieces = [shift(low, "t", k) for k in (1, 2, 3)]
+    phase = lax.optimization_barrier((far_low, far_high, other_far, low, *pieces))
+    far_low, far_high, other_far, low, *pieces = phase
     low = sum((p.astype(F32) for p in pieces), low.astype(F32)).astype(BF)
     hidden, back = low[:, :rank], low[:, rank:]
     in_grad = SCALE * lax.dot_general(
@@ -211,8 +215,6 @@
     )
     mag_sum = jnp.sum(grad.astype(F32) * pre.astype(F32), axis=0).reshape(N_DP, -1)
     adapters = jnp.concatenate([out_grad, in_grad, mag_sum], axis=1)
-    phase = lax.optimization_barrier((far_low, far_high, other_far, adapters))
-    far_low, far_high, other_far, adapters = phase
     own_rows = jnp.stack([own, own_down, own_up, own_far])
     own_swap = shift(own_rows, "co", 1)
     other_rows = jnp.stack([other, other_down, other_up, other_far])

time: 173 us -> 172 us (level)
  waiting for transfers between devices: 60.5 us -> 56.9 us
    ppermute x42, waiting for transfers between devices: 46.1 us -> 42.6 us  [shift(): return lax.ppermute(value, axis, [(i, (i + step) % n) for i in range(n)])]
    ppermute x42, starting transfers between devices: 62.5 us -> 64.9 us  [shift(): return lax.ppermute(value, axis, [(i, (i + step) % n) for i in range(n)])]
    all_to_all x2, starting transfers between devices: 9.54 us -> 7.55 us  [swap_all(): return lax.all_to_all(value, axes, 0, 0, tiled=True)]
  transfers between devices with their start and end apart: 44 -> 44, of which waited for: 26 -> 25; matrix products, arithmetic and copies ran while one was open for 8% -> 9% of each run, Pallas kernels for 9% -> 10%
where the time goes in v8:
time: 172 us; the launch traced here: 168 us
  starting transfers between devices  72.4 us (42%)
  waiting for transfers between devices  56.9 us (33%)
  Pallas kernels  16.1 us (9%)
  other arithmetic  10.2 us (6%)
  local copies, waits for them, and re-layouts  8.46 us (5%)
  matrix products  3.46 us (2%)
    ppermute x42, starting transfers between devices, shift(): return lax.ppermute(value, axis, [(i, (i + step) % n) for i in range(n)])  64.9 us
    ppermute x42, waiting for transfers between devices, shift(): return lax.ppermute(value, axis, [(i, (i + step) % n) for i in range(n)])  42.6 us
    all_to_all x2, waiting for transfers between devices, swap_all(): return lax.all_to_all(value, axes, 0, 0, tiled=True)  14.2 us
    pallas_call x1, Pallas kernels, tile_of(): pl.pallas_call(tile_kernel, grid_spec=pltpu.PrefetchScalarGridSpec(num_sc...  11.9 us
    all_to_all x2, starting transfers between devices, swap_all(): return lax.all_to_all(value, axes, 0, 0, tiled=True)  7.55 us
    pallas_call x1, Pallas kernels, merge(): pl.pallas_call(body, grid=(steps,), in_specs=[columns(rows), whole(count,...  4.26 us
  transfers between devices with their start and end apart: 44, of which 25 were waited for; matrix products, arithmetic and copies ran while one was open for 9% of the time, Pallas kernels for 10%

profile of v8, /device:TPU:8, one launch (start us, length us, event | category | flops | bytes accessed | tf_op | source)
XLA Modules:
  0.0 168.5 jit_solution(14623963012768160969)
XLA Ops:
  0.6 2.5 %fusion.13 = (bf16[96,3584]{1,0:T(8,128)(2,1)}, bf16[96,3584]{1,0:T(8,128)(2,1)}) fusion(bf16[192,3584]{1,0:T(8,128)(2,1)} %refs_0_.3), kind=kLoop, calls=%fused_computation.51 | loop fusion | bytes 2752512 | tf_op jit(solution)/shard_map/slice | solution.py:170
  4.7 1.7 %collective-permute-start.1 = (bf16[96,3584]{1,0:T(8,128)(2,1)}, bf16[96,3584]{1,0:T(8,128)(2,1)S(1)}, u32[]{:S(2)}, u32[]{:S(2)}) collective-permute-start(bf16[96,3584]{1,0:T(8,128)(2,1)} %get-tuple-element.45), channel_id=1, source_target_pairs={{0,48},{16,0},{32,16},{48,32},{1,49},{17,1},{33,17},{49,33},{2,50}... | collective-permute-start | bytes 2064392 | tf_op jit(solution)/shard_map/ppermute | solution.py:18
  7.2 4.3 %shard_map.111 = (bf16[64,3584]{1,0:T(8,128)(2,1)}, f32[1,3584]{1,0:T(1,128)}) custom-call(s32[64,3584]{1,0:T(8,128)} %refs_0_.2, f32[56,64]{1,0:T(8,128)} %bitcast.47, bf16[64,64]{1,0:T(8,128)(2,1)} %copy.18.refs_2_, bf16[64,3584]{1,0:T(8,128)(2,1)} %refs_3_.1), custom_call_target="tpu_custom_call" | custom-call | flops 234881024 | bytes 1835008 | tf_op jit(solution)/shard_map/pallas_call | solution.py:65
  13.9 2.7 %collective-permute-start.6 = (f32[28,128]{1,0:T(8,128)S(1)}, f32[28,128]{1,0:T(8,128)S(1)}, u32[]{:S(2)}, u32[]{:S(2)}) collective-permute-start(f32[28,128]{1,0:T(8,128)S(1)} %bitcast.44), channel_id=1, source_target_pairs={{0,128},{64,192},{128,0},{192,64},{1,129},{65,193},{129,1},{193,65... | collective-permute-start | bytes 43016 | tf_op jit(solution)/shard_map/ppermute | solution.py:18
  17.2 1.9 %collective-permute-start.2 = (bf16[64,3584]{1,0:T(8,128)(2,1)}, bf16[64,3584]{1,0:T(8,128)(2,1)}, u32[]{:S(2)}, u32[]{:S(2)}) collective-permute-start(bf16[64,3584]{1,0:T(8,128)(2,1)} %get-tuple-element.41), channel_id=1, source_target_pairs={{0,8},{8,0},{1,9},{9,1},{2,10},{10,2},{3,11},{11,3},{4,12},{12,4},... | collective-permute-start | bytes 1376264 | tf_op jit(solution)/shard_map/ppermute | solution.py:18
  21.2 7.4 %collective-permute-done.2 = bf16[64,3584]{1,0:T(8,128)(2,1)} collective-permute-done((bf16[64,3584]{1,0:T(8,128)(2,1)}, bf16[64,3584]{1,0:T(8,128)(2,1)}, u32[]{:S(2)}, u32[]{:S(2)}) %collective-permute-start.2) | collective-permute-done | bytes 458784 | tf_op jit(solution)/shard_map/ppermute | solution.py:18
  33.7 1.9 %collective-permute-start.12 = (bf16[64,3584]{1,0:T(8,128)(2,1)}, bf16[64,3584]{1,0:T(8,128)(2,1)}, u32[]{:S(2)}, u32[]{:S(2)}) collective-permute-start(bf16[64,3584]{1,0:T(8,128)(2,1)} %collective-permute-done.3), channel_id=1, source_target_pairs={{0,64},{64,128},{128,192},{192,0},{1,65},{65,129},{129,193},{193,1... | collective-permute-start | bytes 1376264 | tf_op jit(solution)/shard_map/ppermute | solution.py:18
  36.0 2.7 %collective-permute-start.14 = (f32[28,128]{1,0:T(8,128)S(1)}, f32[28,128]{1,0:T(8,128)S(1)}, u32[]{:S(2)}, u32[]{:S(2)}) collective-permute-start(f32[28,128]{1,0:T(8,128)S(1)} %add_add_fusion.4), channel_id=1, source_target_pairs={{0,32},{16,48},{32,0},{48,16},{1,33},{17,49},{33,1},{49,17},{2,34}... | collective-permute-start | bytes 43016 | tf_op jit(solution)/shard_map/ppermute | solution.py:18
  38.7 2.1 %collective-permute-done.13 = f32[28,128]{1,0:T(8,128)S(1)} collective-permute-done((f32[28,128]{1,0:T(8,128)S(1)}, f32[28,128]{1,0:T(8,128)S(1)}, u32[]{:S(2)}, u32[]{:S(2)}) %collective-permute-start.13) | collective-permute-done | bytes 14368 | tf_op jit(solution)/shard_map/ppermute | solution.py:18
  42.9 1.9 %collective-permute-done.15 = f32[28,128]{1,0:T(8,128)S(1)} collective-permute-done((f32[28,128]{1,0:T(8,128)S(1)}, f32[28,128]{1,0:T(8,128)S(1)}, u32[]{:S(2)}, u32[]{:S(2)}) %collective-permute-start.15) | collective-permute-done | bytes 14368 | tf_op jit(solution)/shard_map/ppermute | solution.py:18
  46.2 5.3 %collective-permute-done.12 = bf16[64,3584]{1,0:T(8,128)(2,1)} collective-permute-done((bf16[64,3584]{1,0:T(8,128)(2,1)}, bf16[64,3584]{1,0:T(8,128)(2,1)}, u32[]{:S(2)}, u32[]{:S(2)}) %collective-permute-start.12) | collective-permute-done | bytes 458784 | tf_op jit(solution)/shard_map/ppermute | solution.py:18
  51.5 1.8 %collective-permute-start.17 = (f32[28,128]{1,0:T(8,128)S(1)}, f32[28,128]{1,0:T(8,128)S(1)}, u32[]{:S(2)}, u32[]{:S(2)}) collective-permute-start(f32[28,128]{1,0:T(8,128)S(1)} %add_add_fusion.3), channel_id=1, source_target_pairs={{0,8},{4,12},{8,0},{12,4},{1,9},{5,13},{9,1},{13,5},{2,10},{6,14},... | collective-permute-start | bytes 43016 | tf_op jit(solution)/shard_map/ppermute | solution.py:18
  56.7 3.2 %collective-permute-start.20 = (bf16[96,3584]{1,0:T(8,128)(2,1)S(1)}, bf16[96,3584]{1,0:T(8,128)(2,1)}, u32[]{:S(2)}, u32[]{:S(2)}) collective-permute-start(bf16[96,3584]{1,0:T(8,128)(2,1)S(1)} %collective-permute-done.1.refs_4_), channel_id=1, source_target_pairs={{0,48},{16,0},{32,16},{48,32},{1,49},{17,1},{33,17},{49,33},{2,50}... | collective-permute-start | bytes 2064392 | tf_op jit(solution)/shard_map/ppermute | solution.py:18
  61.6 3.3 %collective-permute-start.22 = (bf16[192,128]{0,1:T(8,128)(2,1)S(1)}, bf16[192,128]{0,1:T(8,128)(2,1)S(1)}, u32[]{:S(2)}, u32[]{:S(2)}) collective-permute-start(bf16[192,128]{0,1:T(8,128)(2,1)S(1)} %pad_maximum_fusion.4), channel_id=1, source_target_pairs={{0,1},{1,2},{2,3},{3,0},{4,5},{5,6},{6,7},{7,4},{8,9},{9,10},{10,1... | collective-permute-start | bytes 147464 | tf_op jit(solution)/shard_map/ppermute | solution.py:18
  65.4 5.5 %collective-permute-start.23 = (bf16[192,128]{0,1:T(8,128)(2,1)S(1)}, bf16[192,128]{0,1:T(8,128)(2,1)S(1)}, u32[]{:S(2)}, u32[]{:S(2)}) collective-permute-start(bf16[192,128]{0,1:T(8,128)(2,1)S(1)} %pad_maximum_fusion.4), channel_id=1, source_target_pairs={{0,2},{1,3},{2,0},{3,1},{4,6},{5,7},{6,4},{7,5},{8,10},{9,11},{10,... | collective-permute-start | bytes 147464 | tf_op jit(solution)/shard_map/ppermute | solution.py:18
  70.9 2.7 %collective-permute-start.24 = (bf16[192,128]{0,1:T(8,128)(2,1)S(1)}, bf16[192,128]{0,1:T(8,128)(2,1)S(1)}, u32[]{:S(2)}, u32[]{:S(2)}) collective-permute-start(bf16[192,128]{0,1:T(8,128)(2,1)S(1)} %pad_maximum_fusion.4), channel_id=1, source_target_pairs={{0,3},{1,0},{2,1},{3,2},{4,7},{5,4},{6,5},{7,6},{8,11},{9,8},{10,9... | collective-permute-start | bytes 147464 | tf_op jit(solution)/shard_map/ppermute | solution.py:18
  74.9 3.0 %pad_maximum_fusion.refs_8_ = bf16[4,64,3584]{2,1,0:T(8,128)(2,1)} fusion(bf16[1,64,3584]{2,1,0:T(8,128)(2,1)} %bitcast.10, bf16[1,64,3584]{2,1,0:T(8,128)(2,1)} %bitcast.41, bf16[1,64,3584]{2,1,0:T(8,128)(2,1)} %bitcast.8, bf16[1,64,3584]{2,1,0:T(8,128)(2,1)} %bitcast.40), kind=kLoop, calls=%fused_computation.5 | loop fusion | flops 2752512 | bytes 3670016 | tf_op jit(solution)/shard_map/stack | solution.py:218
  77.9 7.0 %collective-permute-done.21 = bf16[64,3584]{1,0:T(8,128)(2,1)S(1)} collective-permute-done((bf16[64,3584]{1,0:T(8,128)(2,1)}, bf16[64,3584]{1,0:T(8,128)(2,1)S(1)}, u32[]{:S(2)}, u32[]{:S(2)}) %collective-permute-start.21) | collective-permute-done | bytes 458784 | tf_op jit(solution)/shard_map/ppermute | solution.py:18
  87.7 2.8 %pad_maximum_fusion.1.refs_9_ = bf16[4,64,3584]{2,1,0:T(8,128)(2,1)} fusion(bf16[1,64,3584]{2,1,0:T(8,128)(2,1)S(1)} %bitcast.42, bf16[1,64,3584]{2,1,0:T(8,128)(2,1)} %bitcast.13, bf16[1,64,3584]{2,1,0:T(8,128)(2,1)} %bitcast.12, bf16[1,64,3584]{2,1,0:T(8,128)(2,1)} %bitcast.11), kind=kLoop, calls=%fused_computation.6 | loop fusion | flops 2752512 | bytes 3670016 | tf_op jit(solution)/shard_map/stack | solution.py:220
  94.7 11.9 %shard_map.112 = (bf16[4,4,96,256]{3,2,1,0:T(8,128)(2,1)}, bf16[4,4,96,256]{3,2,1,0:T(8,128)(2,1)}) custom-call(s32[4]{0:T(128)S(1)} %pad_add_fusion.where, bf16[192,3584]{1,0:T(8,128)(2,1)S(1)} %copy-done.1, bf16[96,3584]{1,0:T(8,128)(2,1)S(1)} %collective-permute-done.refs_1_, bf16[96,3584]{1,0:T(8,128)(2,1)} %collective-permute-done.8.refs_2_, ...), custom_call_target="tpu_custom_call" | custom-call | flops 5637144576 | bytes 12845056 | tf_op jit(solution)/shard_map/pallas_call | solution.py:129
  108.3 1.8 %collective-permute-start.29 = (f32[8,4664]{1,0:T(8,128)S(1)}, f32[8,4664]{1,0:T(8,128)S(1)}, u32[]{:S(2)}, u32[]{:S(2)}) collective-permute-start(f32[8,4664]{1,0:T(8,128)S(1)} %get-tuple-element.80), channel_id=1, source_target_pairs={{0,64},{64,128},{128,192},{192,0},{1,65},{65,129},{129,193},{193,1... | collective-permute-start | bytes 447752 | tf_op jit(solution)/shard_map/ppermute | solution.py:18
  110.1 2.7 %collective-permute-start.30 = (f32[8,4664]{1,0:T(8,128)S(1)}, f32[8,4664]{1,0:T(8,128)S(1)}, u32[]{:S(2)}, u32[]{:S(2)}) collective-permute-start(f32[8,4664]{1,0:T(8,128)S(1)} %get-tuple-element.82), channel_id=1, source_target_pairs={{0,128},{64,192},{128,0},{192,64},{1,129},{65,193},{129,1},{193,65... | collective-permute-start | bytes 447752 | tf_op jit(solution)/shard_map/ppermute | solution.py:18
  112.8 2.3 %collective-permute-start.31 = (f32[8,4664]{1,0:T(8,128)S(1)}, f32[8,4664]{1,0:T(8,128)S(1)}, u32[]{:S(2)}, u32[]{:S(2)}) collective-permute-start(f32[8,4664]{1,0:T(8,128)S(1)} %get-tuple-element.81), channel_id=1, source_target_pairs={{0,192},{64,0},{128,64},{192,128},{1,193},{65,1},{129,65},{193,129... | collective-permute-start | bytes 447752 | tf_op jit(solution)/shard_map/ppermute | solution.py:18
  115.1 3.9 %all-to-all-start = ((bf16[16,96,256]{2,1,0:T(8,128)(2,1)}), bf16[16,96,256]{2,1,0:T(8,128)(2,1)S(1)}, u32[]{:S(2)}, u32[]{:S(2)}) async-start(bf16[16,96,256]{2,1,0:T(8,128)(2,1)} %bitcast.15), calls=%async_computation | async-start | bytes 1572864 | tf_op jit(solution)/shard_map/all_to_all | solution.py:22
  121.2 2.7 %collective-permute-start.33 = (f32[2,4664]{1,0:T(2,128)S(1)}, f32[2,4664]{1,0:T(2,128)S(1)}, u32[]{:S(2)}, u32[]{:S(2)}) collective-permute-start(f32[2,4664]{1,0:T(2,128)S(1)} %get-tuple-element.85), channel_id=1, source_target_pairs={{0,32},{16,48},{32,0},{48,16},{1,33},{17,49},{33,1},{49,17},{2,34}... | collective-permute-start | bytes 111944 | tf_op jit(solution)/shard_map/ppermute | solution.py:18
  125.5 2.2 %collective-permute-done.33 = f32[2,4664]{1,0:T(2,128)S(1)} collective-permute-done((f32[2,4664]{1,0:T(2,128)S(1)}, f32[2,4664]{1,0:T(2,128)S(1)}, u32[]{:S(2)}, u32[]{:S(2)}) %collective-permute-start.33) | collective-permute-done | bytes 37344 | tf_op jit(solution)/shard_map/ppermute | solution.py:18
  127.9 13.8 %all-to-all-done = bf16[16,96,256]{2,1,0:T(8,128)(2,1)S(1)} async-done(((bf16[16,96,256]{2,1,0:T(8,128)(2,1)}), bf16[16,96,256]{2,1,0:T(8,128)(2,1)S(1)}, u32[]{:S(2)}, u32[]{:S(2)}) %all-to-all-start) | async-done | bytes 786464 | tf_op jit(solution)/shard_map/all_to_all | solution.py:22
  141.7 3.6 %all-to-all-start.1 = ((bf16[16,96,256]{2,1,0:T(8,128)(2,1)}), bf16[16,96,256]{2,1,0:T(8,128)(2,1)S(1)}, u32[]{:S(2)}, u32[]{:S(2)}) async-start(bf16[16,96,256]{2,1,0:T(8,128)(2,1)} %bitcast.18), calls=%async_computation.1 | async-start | bytes 1572864 | tf_op jit(solution)/shard_map/all_to_all | solution.py:22
  145.3 1.8 %collective-permute-start.35 = (f32[2,4664]{1,0:T(2,128)S(1)}, f32[2,4664]{1,0:T(2,128)S(1)}, u32[]{:S(2)}, u32[]{:S(2)}) collective-permute-start(f32[2,4664]{1,0:T(2,128)S(1)} %add_add_fusion.1), channel_id=1, source_target_pairs={{0,16},{16,32},{32,48},{48,0},{1,17},{17,33},{33,49},{49,1},{2,18}... | collective-permute-start | bytes 111944 | tf_op jit(solution)/shard_map/ppermute | solution.py:18
  147.1 2.7 %collective-permute-start.36 = (f32[2,4664]{1,0:T(2,128)S(1)}, f32[2,4664]{1,0:T(2,128)S(1)}, u32[]{:S(2)}, u32[]{:S(2)}) collective-permute-start(f32[2,4664]{1,0:T(2,128)S(1)} %add_add_fusion.1), channel_id=1, source_target_pairs={{0,32},{16,48},{32,0},{48,16},{1,33},{17,49},{33,1},{49,17},{2,34}... | collective-permute-start | bytes 111944 | tf_op jit(solution)/shard_map/ppermute | solution.py:18
  157.8 2.3 %collective-permute-done.38 = f32[8,4664]{1,0:T(8,128)S(1)} collective-permute-done((f32[8,4664]{1,0:T(8,128)S(1)}, f32[8,4664]{1,0:T(8,128)S(1)}, u32[]{:S(2)}, u32[]{:S(2)}) %collective-permute-start.38) | collective-permute-done | bytes 149280 | tf_op jit(solution)/shard_map/ppermute | solution.py:18
  160.2 2.2 %collective-permute-done.39 = f32[8,4664]{1,0:T(8,128)S(1)} collective-permute-done((f32[8,4664]{1,0:T(8,128)S(1)}, f32[8,4664]{1,0:T(8,128)S(1)}, u32[]{:S(2)}, u32[]{:S(2)}) %collective-permute-start.39) | collective-permute-done | bytes 149280 | tf_op jit(solution)/shard_map/ppermute | solution.py:18
  (123 shorter events, 49.7 us)
Async XLA Ops:
  3.2 27.7 %collective-permute-start = (bf16[96,3584]{1,0:T(8,128)(2,1)}, bf16[96,3584]{1,0:T(8,128)(2,1)S(1)}, u32[]{:S(2)}, u32[]{:S(2)}) collective-permute-start(bf16[96,3584]{1,0:T(8,128)(2,1)} %get-tuple-element.46), channel_id=1, source_target_pairs={{0,16},{16,32},{32,48},{48,0},{1,17},{17,33},{33,49},{49,1},{2,18}... | collective-permute-start | bytes 2064392 | tf_op jit(solution)/shard_map/ppermute | solution.py:18
  4.7 26.2 %collective-permute-start.1 = (bf16[96,3584]{1,0:T(8,128)(2,1)}, bf16[96,3584]{1,0:T(8,128)(2,1)S(1)}, u32[]{:S(2)}, u32[]{:S(2)}) collective-permute-start(bf16[96,3584]{1,0:T(8,128)(2,1)} %get-tuple-element.45), channel_id=1, source_target_pairs={{0,48},{16,0},{32,16},{48,32},{1,49},{17,1},{33,17},{49,33},{2,50}... | collective-permute-start | bytes 2064392 | tf_op jit(solution)/shard_map/ppermute | solution.py:18
  13.9 5.3 %collective-permute-start.6 = (f32[28,128]{1,0:T(8,128)S(1)}, f32[28,128]{1,0:T(8,128)S(1)}, u32[]{:S(2)}, u32[]{:S(2)}) collective-permute-start(f32[28,128]{1,0:T(8,128)S(1)} %bitcast.44), channel_id=1, source_target_pairs={{0,128},{64,192},{128,0},{192,64},{1,129},{65,193},{129,1},{193,65... | collective-permute-start | bytes 43016 | tf_op jit(solution)/shard_map/ppermute | solution.py:18
  17.2 11.3 %collective-permute-start.2 = (bf16[64,3584]{1,0:T(8,128)(2,1)}, bf16[64,3584]{1,0:T(8,128)(2,1)}, u32[]{:S(2)}, u32[]{:S(2)}) collective-permute-start(bf16[64,3584]{1,0:T(8,128)(2,1)} %get-tuple-element.41), channel_id=1, source_target_pairs={{0,8},{8,0},{1,9},{9,1},{2,10},{10,2},{3,11},{11,3},{4,12},{12,4},... | collective-permute-start | bytes 1376264 | tf_op jit(solution)/shard_map/ppermute | solution.py:18
  19.1 10.9 %collective-permute-start.3 = (bf16[64,3584]{1,0:T(8,128)(2,1)}, bf16[64,3584]{1,0:T(8,128)(2,1)}, u32[]{:S(2)}, u32[]{:S(2)}) collective-permute-start(bf16[64,3584]{1,0:T(8,128)(2,1)} %get-tuple-element.41), channel_id=1, source_target_pairs={{0,64},{64,128},{128,192},{192,0},{1,65},{65,129},{129,193},{193,1... | collective-permute-start | bytes 1376264 | tf_op jit(solution)/shard_map/ppermute | solution.py:18
  20.4 10.5 %collective-permute-start.4 = (bf16[64,3584]{1,0:T(8,128)(2,1)}, bf16[64,3584]{1,0:T(8,128)(2,1)S(1)}, u32[]{:S(2)}, u32[]{:S(2)}) collective-permute-start(bf16[64,3584]{1,0:T(8,128)(2,1)} %get-tuple-element.41), channel_id=1, source_target_pairs={{0,192},{64,0},{128,64},{192,128},{1,193},{65,1},{129,65},{193,129... | collective-permute-start | bytes 1376264 | tf_op jit(solution)/shard_map/ppermute | solution.py:18
  31.7 14.4 %collective-permute-start.10 = (bf16[64,3584]{1,0:T(8,128)(2,1)}, bf16[64,3584]{1,0:T(8,128)(2,1)}, u32[]{:S(2)}, u32[]{:S(2)}) collective-permute-start(bf16[64,3584]{1,0:T(8,128)(2,1)} %collective-permute-done.2), channel_id=1, source_target_pairs={{0,64},{64,128},{128,192},{192,0},{1,65},{65,129},{129,193},{193,1... | collective-permute-start | bytes 1376264 | tf_op jit(solution)/shard_map/ppermute | solution.py:18
  32.7 13.4 %collective-permute-start.11 = (bf16[64,3584]{1,0:T(8,128)(2,1)}, bf16[64,3584]{1,0:T(8,128)(2,1)}, u32[]{:S(2)}, u32[]{:S(2)}) collective-permute-start(bf16[64,3584]{1,0:T(8,128)(2,1)} %collective-permute-done.2), channel_id=1, source_target_pairs={{0,192},{64,0},{128,64},{192,128},{1,193},{65,1},{129,65},{193,129... | collective-permute-start | bytes 1376264 | tf_op jit(solution)/shard_map/ppermute | solution.py:18
  33.7 17.7 %collective-permute-start.12 = (bf16[64,3584]{1,0:T(8,128)(2,1)}, bf16[64,3584]{1,0:T(8,128)(2,1)}, u32[]{:S(2)}, u32[]{:S(2)}) collective-permute-start(bf16[64,3584]{1,0:T(8,128)(2,1)} %collective-permute-done.3), channel_id=1, source_target_pairs={{0,64},{64,128},{128,192},{192,0},{1,65},{65,129},{129,193},{193,1... | collective-permute-start | bytes 1376264 | tf_op jit(solution)/shard_map/ppermute | solution.py:18
  36.0 5.3 %collective-permute-start.14 = (f32[28,128]{1,0:T(8,128)S(1)}, f32[28,128]{1,0:T(8,128)S(1)}, u32[]{:S(2)}, u32[]{:S(2)}) collective-permute-start(f32[28,128]{1,0:T(8,128)S(1)} %add_add_fusion.4), channel_id=1, source_target_pairs={{0,32},{16,48},{32,0},{48,16},{1,33},{17,49},{33,1},{49,17},{2,34}... | collective-permute-start | bytes 43016 | tf_op jit(solution)/shard_map/ppermute | solution.py:18
  41.3 14.9 %collective-permute-start.8 = (bf16[96,3584]{1,0:T(8,128)(2,1)}, bf16[96,3584]{1,0:T(8,128)(2,1)}, u32[]{:S(2)}, u32[]{:S(2)}) collective-permute-start(bf16[96,3584]{1,0:T(8,128)(2,1)} %get-tuple-element.45), channel_id=1, source_target_pairs={{0,16},{16,32},{32,48},{48,0},{1,17},{17,33},{33,49},{49,1},{2,18}... | collective-permute-start | bytes 2064392 | tf_op jit(solution)/shard_map/ppermute | solution.py:18
  44.8 11.9 %collective-permute-start.9 = (bf16[96,3584]{1,0:T(8,128)(2,1)}, bf16[96,3584]{1,0:T(8,128)(2,1)}, u32[]{:S(2)}, u32[]{:S(2)}) collective-permute-start(bf16[96,3584]{1,0:T(8,128)(2,1)} %get-tuple-element.46), channel_id=1, source_target_pairs={{0,48},{16,0},{32,16},{48,32},{1,49},{17,1},{33,17},{49,33},{2,50}... | collective-permute-start | bytes 2064392 | tf_op jit(solution)/shard_map/ppermute | solution.py:18
  56.7 28.2 %collective-permute-start.19 = (bf16[96,3584]{1,0:T(8,128)(2,1)S(1)}, bf16[96,3584]{1,0:T(8,128)(2,1)}, u32[]{:S(2)}, u32[]{:S(2)}) collective-permute-start(bf16[96,3584]{1,0:T(8,128)(2,1)S(1)} %collective-permute-done.refs_1_), channel_id=1, source_target_pairs={{0,16},{16,32},{32,48},{48,0},{1,17},{17,33},{33,49},{49,1},{2,18}... | collective-permute-start | bytes 2064392 | tf_op jit(solution)/shard_map/ppermute | solution.py:18
  56.7 28.2 %collective-permute-start.20 = (bf16[96,3584]{1,0:T(8,128)(2,1)S(1)}, bf16[96,3584]{1,0:T(8,128)(2,1)}, u32[]{:S(2)}, u32[]{:S(2)}) collective-permute-start(bf16[96,3584]{1,0:T(8,128)(2,1)S(1)} %collective-permute-done.1.refs_4_), channel_id=1, source_target_pairs={{0,48},{16,0},{32,16},{48,32},{1,49},{17,1},{33,17},{49,33},{2,50}... | collective-permute-start | bytes 2064392 | tf_op jit(solution)/shard_map/ppermute | solution.py:18
  61.6 12.0 %collective-permute-start.22 = (bf16[192,128]{0,1:T(8,128)(2,1)S(1)}, bf16[192,128]{0,1:T(8,128)(2,1)S(1)}, u32[]{:S(2)}, u32[]{:S(2)}) collective-permute-start(bf16[192,128]{0,1:T(8,128)(2,1)S(1)} %pad_maximum_fusion.4), channel_id=1, source_target_pairs={{0,1},{1,2},{2,3},{3,0},{4,5},{5,6},{6,7},{7,4},{8,9},{9,10},{10,1... | collective-permute-start | bytes 147464 | tf_op jit(solution)/shard_map/ppermute | solution.py:18
  65.4 12.5 %collective-permute-start.23 = (bf16[192,128]{0,1:T(8,128)(2,1)S(1)}, bf16[192,128]{0,1:T(8,128)(2,1)S(1)}, u32[]{:S(2)}, u32[]{:S(2)}) collective-permute-start(bf16[192,128]{0,1:T(8,128)(2,1)S(1)} %pad_maximum_fusion.4), channel_id=1, source_target_pairs={{0,2},{1,3},{2,0},{3,1},{4,6},{5,7},{6,4},{7,5},{8,10},{9,11},{10,... | collective-permute-start | bytes 147464 | tf_op jit(solution)/shard_map/ppermute | solution.py:18
  70.9 7.0 %collective-permute-start.24 = (bf16[192,128]{0,1:T(8,128)(2,1)S(1)}, bf16[192,128]{0,1:T(8,128)(2,1)S(1)}, u32[]{:S(2)}, u32[]{:S(2)}) collective-permute-start(bf16[192,128]{0,1:T(8,128)(2,1)S(1)} %pad_maximum_fusion.4), channel_id=1, source_target_pairs={{0,3},{1,0},{2,1},{3,2},{4,7},{5,4},{6,5},{7,6},{8,11},{9,8},{10,9... | collective-permute-start | bytes 147464 | tf_op jit(solution)/shard_map/ppermute | solution.py:18
  73.6 11.4 %collective-permute-start.21 = (bf16[64,3584]{1,0:T(8,128)(2,1)}, bf16[64,3584]{1,0:T(8,128)(2,1)S(1)}, u32[]{:S(2)}, u32[]{:S(2)}) collective-permute-start(bf16[64,3584]{1,0:T(8,128)(2,1)} %collective-permute-done.11), channel_id=1, source_target_pairs={{0,192},{64,0},{128,64},{192,128},{1,193},{65,1},{129,65},{193,129... | collective-permute-start | bytes 1376264 | tf_op jit(solution)/shard_map/ppermute | solution.py:18
  77.9 15.8 %collective-permute-start.27 = (bf16[4,64,3584]{2,1,0:T(8,128)(2,1)}, bf16[4,64,3584]{2,1,0:T(8,128)(2,1)}, u32[]{:S(2)}, u32[]{:S(2)}) collective-permute-start(bf16[4,64,3584]{2,1,0:T(8,128)(2,1)} %pad_maximum_fusion.refs_8_), channel_id=1, source_target_pairs={{0,4},{4,0},{1,5},{5,1},{2,6},{6,2},{3,7},{7,3},{8,12},{12,8},{9,1... | collective-permute-start | bytes 5505032 | tf_op jit(solution)/shard_map/ppermute | solution.py:18
  92.3 15.9 %collective-permute-start.26 = (f32[32,4664]{1,0:T(8,128)S(1)}, f32[32,4664]{1,0:T(8,128)S(1)}, u32[]{:S(2)}, u32[]{:S(2)}) collective-permute-start(f32[32,4664]{1,0:T(8,128)S(1)} %dynamic-slice_add_fusion), channel_id=1, source_target_pairs={{0,8},{8,0},{1,9},{9,1},{2,10},{10,2},{3,11},{11,3},{4,12},{12,4},... | collective-permute-start | bytes 1790984 | tf_op jit(solution)/shard_map/ppermute | solution.py:18
  108.3 10.8 %collective-permute-start.29 = (f32[8,4664]{1,0:T(8,128)S(1)}, f32[8,4664]{1,0:T(8,128)S(1)}, u32[]{:S(2)}, u32[]{:S(2)}) collective-permute-start(f32[8,4664]{1,0:T(8,128)S(1)} %get-tuple-element.80), channel_id=1, source_target_pairs={{0,64},{64,128},{128,192},{192,0},{1,65},{65,129},{129,193},{193,1... | collective-permute-start | bytes 447752 | tf_op jit(solution)/shard_map/ppermute | solution.py:18
  110.1 9.0 %collective-permute-start.30 = (f32[8,4664]{1,0:T(8,128)S(1)}, f32[8,4664]{1,0:T(8,128)S(1)}, u32[]{:S(2)}, u32[]{:S(2)}) collective-permute-start(f32[8,4664]{1,0:T(8,128)S(1)} %get-tuple-element.82), channel_id=1, source_target_pairs={{0,128},{64,192},{128,0},{192,64},{1,129},{65,193},{129,1},{193,65... | collective-permute-start | bytes 447752 | tf_op jit(solution)/shard_map/ppermute | solution.py:18
  112.8 6.8 %collective-permute-start.31 = (f32[8,4664]{1,0:T(8,128)S(1)}, f32[8,4664]{1,0:T(8,128)S(1)}, u32[]{:S(2)}, u32[]{:S(2)}) collective-permute-start(f32[8,4664]{1,0:T(8,128)S(1)} %get-tuple-element.81), channel_id=1, source_target_pairs={{0,192},{64,0},{128,64},{192,128},{1,193},{65,1},{129,65},{193,129... | collective-permute-start | bytes 447752 | tf_op jit(solution)/shard_map/ppermute | solution.py:18
  115.1 26.5 %all-to-all-start = ((bf16[16,96,256]{2,1,0:T(8,128)(2,1)}), bf16[16,96,256]{2,1,0:T(8,128)(2,1)S(1)}, u32[]{:S(2)}, u32[]{:S(2)}) async-start(bf16[16,96,256]{2,1,0:T(8,128)(2,1)} %bitcast.15), calls=%async_computation | async-start | bytes 1572864 | tf_op jit(solution)/shard_map/all_to_all | solution.py:22
  119.7 5.8 %collective-permute-start.32 = (f32[2,4664]{1,0:T(2,128)S(1)}, f32[2,4664]{1,0:T(2,128)S(1)}, u32[]{:S(2)}, u32[]{:S(2)}) collective-permute-start(f32[2,4664]{1,0:T(2,128)S(1)} %get-tuple-element.83), channel_id=1, source_target_pairs={{0,16},{16,32},{32,48},{48,0},{1,17},{17,33},{33,49},{49,1},{2,18}... | collective-permute-start | bytes 111944 | tf_op jit(solution)/shard_map/ppermute | solution.py:18
  121.2 6.4 %collective-permute-start.33 = (f32[2,4664]{1,0:T(2,128)S(1)}, f32[2,4664]{1,0:T(2,128)S(1)}, u32[]{:S(2)}, u32[]{:S(2)}) collective-permute-start(f32[2,4664]{1,0:T(2,128)S(1)} %get-tuple-element.85), channel_id=1, source_target_pairs={{0,32},{16,48},{32,0},{48,16},{1,33},{17,49},{33,1},{49,17},{2,34}... | collective-permute-start | bytes 111944 | tf_op jit(solution)/shard_map/ppermute | solution.py:18
  141.7 22.8 %all-to-all-start.1 = ((bf16[16,96,256]{2,1,0:T(8,128)(2,1)}), bf16[16,96,256]{2,1,0:T(8,128)(2,1)S(1)}, u32[]{:S(2)}, u32[]{:S(2)}) async-start(bf16[16,96,256]{2,1,0:T(8,128)(2,1)} %bitcast.18), calls=%async_computation.1 | async-start | bytes 1572864 | tf_op jit(solution)/shard_map/all_to_all | solution.py:22
  145.3 6.6 %collective-permute-start.35 = (f32[2,4664]{1,0:T(2,128)S(1)}, f32[2,4664]{1,0:T(2,128)S(1)}, u32[]{:S(2)}, u32[]{:S(2)}) collective-permute-start(f32[2,4664]{1,0:T(2,128)S(1)} %add_add_fusion.1), channel_id=1, source_target_pairs={{0,16},{16,32},{32,48},{48,0},{1,17},{17,33},{33,49},{49,1},{2,18}... | collective-permute-start | bytes 111944 | tf_op jit(solution)/shard_map/ppermute | solution.py:18
  147.1 6.5 %collective-permute-start.36 = (f32[2,4664]{1,0:T(2,128)S(1)}, f32[2,4664]{1,0:T(2,128)S(1)}, u32[]{:S(2)}, u32[]{:S(2)}) collective-permute-start(f32[2,4664]{1,0:T(2,128)S(1)} %add_add_fusion.1), channel_id=1, source_target_pairs={{0,32},{16,48},{32,0},{48,16},{1,33},{17,49},{33,1},{49,17},{2,34}... | collective-permute-start | bytes 111944 | tf_op jit(solution)/shard_map/ppermute | solution.py:18
  154.9 5.3 %collective-permute-start.38 = (f32[8,4664]{1,0:T(8,128)S(1)}, f32[8,4664]{1,0:T(8,128)S(1)}, u32[]{:S(2)}, u32[]{:S(2)}) collective-permute-start(f32[8,4664]{1,0:T(8,128)S(1)} %constant_dynamic-update-slice_fusion.6), channel_id=1, source_target_pairs={{0,64},{64,128},{128,192},{192,0},{1,65},{65,129},{129,193},{193,1... | collective-permute-start | bytes 447752 | tf_op jit(solution)/shard_map/ppermute | solution.py:18
  155.6 6.8 %collective-permute-start.39 = (f32[8,4664]{1,0:T(8,128)S(1)}, f32[8,4664]{1,0:T(8,128)S(1)}, u32[]{:S(2)}, u32[]{:S(2)}) collective-permute-start(f32[8,4664]{1,0:T(8,128)S(1)} %constant_dynamic-update-slice_fusion.6), channel_id=1, source_target_pairs={{0,128},{64,192},{128,0},{192,64},{1,129},{65,193},{129,1},{193,65... | collective-permute-start | bytes 447752 | tf_op jit(solution)/shard_map/ppermute | solution.py:18
  157.1 6.8 %collective-permute-start.40 = (f32[8,4664]{1,0:T(8,128)S(1)}, f32[8,4664]{1,0:T(8,128)S(1)}, u32[]{:S(2)}, u32[]{:S(2)}) collective-permute-start(f32[8,4664]{1,0:T(8,128)S(1)} %constant_dynamic-update-slice_fusion.6), channel_id=1, source_target_pairs={{0,192},{64,0},{128,64},{192,128},{1,193},{65,1},{129,65},{193,129... | collective-permute-start | bytes 447752 | tf_op jit(solution)/shard_map/ppermute | solution.py:18
  (19 other events, 186.2 us)

commit v9 on v8

--- a/solution.py
+++ b/solution.py
@@ -80,15 +80,11 @@
     )(codes, scales, factor, out_factor)
 
 
-def tile_kernel(where, *refs):
-    tokens, (ratio, *weights), (first, second), (wide, scaled) = (
-        refs[:7],
-        refs[7:12],
-        refs[12:14],
-        refs[14:],
-    )
+def tile_kernel(count, shifts, where, *refs):
+    tokens, ratio, weights = refs[:count], refs[count], refs[count + 1 : count + 5]
+    first, second, wide, scaled = refs[-4:]
     rows = weights[0].shape[1]
-    half = tokens[1].shape[0]
+    half = first.shape[2]
     x, zl, co = where[0], where[1], where[2]
 
     @pl.when(pl.program_id(0) == 0)
@@ -108,44 +104,56 @@
         scaled[...], wide[...], (((1,), (1,)), ((), ())), preferred_element_type=F32
     ).astype(BF)
     n = 2 * half
-    for k, e in enumerate((0, 3, 1, 2)):
-        first[lax.rem(x + e, 4), 0] = tile[k * n : k * n + half, :]
-        second[lax.rem(x + e, 4), 0] = tile[k * n + half : (k + 1) * n, :]
-
-
-def tile_of(where, tokens, ratio, weights):
+    for k, e in enumerate(shifts):
+        block = 0 if first.shape[0] == 1 else lax.rem(x + e, 4)
+        first[block, 0] = tile[k * n : k * n + half, :]
+        second[block, 0] = tile[k * n + half : (k + 1) * n, :]
+
+
+def tile_of(where, tokens, ratio, weights, shifts, earlier=()):
     width = ratio.shape[1]
-    half = tokens[1].shape[0]
     rows = weights[0].shape[1]
+    total = sum(v.shape[0] for v in tokens)
+    half = total // len(shifts) // 2
+    blocks = 1 if earlier else 4
 
     def place(i, where):
         step = jnp.where(i == 0, 0, jnp.where(i == 1, 3, i - 1))
-        return 0, lax.rem(where[3] + step, 4), 0, 0
+        block = lax.rem(where[0] + shifts[0], 4) if earlier else 0
+        return block, lax.rem(where[3] + step, 4), 0, 0
 
     def whole(value):
         return pl.BlockSpec(value.shape, lambda i, w: (0, 0))
 
+    def body(*refs):
+        tile_kernel(len(tokens), shifts, *refs)
+
     weight = pl.BlockSpec((1, rows, width), lambda i, w: (i, 0, 0))
+    inputs = len(tokens) + 6
     return pl.pallas_call(
-        tile_kernel,
+        body,
         grid_spec=pltpu.PrefetchScalarGridSpec(
             num_scalar_prefetch=1,
             grid=(4,),
-            in_specs=[whole(v) for v in tokens] + [whole(ratio)] + [weight] * 4,
-            out_specs=[pl.BlockSpec((4, 1, half, 4 * rows), place)] * 2,
+            in_specs=[whole(v) for v in tokens]
+            + [whole(ratio)]
+            + [weight] * 4
+            + [pl.BlockSpec(memory_space=pl.ANY)] * len(earlier),
+            out_specs=[pl.BlockSpec((blocks, 1, half, 4 * rows), place)] * 2,
             scratch_shapes=[
                 pltpu.VMEM((4 * rows, width), BF),
-                pltpu.VMEM((8 * half, width), BF),
+                pltpu.VMEM((total, width), BF),
             ],
         ),
         out_shape=[jax.ShapeDtypeStruct((4, 4, half, 4 * rows), BF)] * 2,
+        input_output_aliases={inputs + i: i for i in range(len(earlier))},
         compiler_params=pltpu.CompilerParams(vmem_limit_bytes=40 * 1024 * 1024),
         cost_estimate=pl.CostEstimate(
-            flops=16 * half * 16 * rows * width,
-            bytes_accessed=2 * width * (8 * half + 16 * rows),
+            flops=2 * total * 16 * rows * width,
+            bytes_accessed=2 * width * (total + 16 * rows),
             transcendentals=0,
         ),
-    )(where, *tokens, ratio, *weights)
+    )(where, *tokens, ratio, *weights, *earlier)
 
 
 def on_device(codes, scales, in_factor, out_factor, magnitude, inputs, grad, pre):
@@ -181,14 +189,22 @@
     left_high, right_low = shift(high_half, "x", 1), shift(low_half, "x", -1)
     other_down, other_up = shift(other, "y", 1), shift(other, "y", -1)
     own_far = shift(own_down, "y", 1)
+    other_far = shift(other_up, "y", -1)
     total = after(gather_sum(total, "x"), other_down, other_up, own_far)
     total = gather_sum(total, ("zl", "co"))
-    phase = (left_low, right_high, left_high, right_low, other_down, other_up, own_far, total)
-    phase = lax.optimization_barrier(phase)
-    left_low, right_high, left_high, right_low, other_down, other_up, own_far, total = phase
+    factor_cols = lax.dynamic_slice_in_dim(in_factor, t * features, features, 0)
+    hidden = jnp.dot(inputs, factor_cols, preferred_element_type=F32)
+    mag_sum = jnp.sum(grad.astype(F32) * pre.astype(F32), axis=0).reshape(N_DP, -1)
+    phase = (left_low, right_high, left_high, right_low, total, own_far, other_far)
+    phase = lax.optimization_barrier((*phase, hidden, mag_sum))
+    left_low, right_high, left_high, right_low, total, own_far, other_far, hidden, mag_sum = phase
 
     far_low, far_high = shift(left_low, "x", 1), shift(right_high, "x", -1)
-    other_far = shift(other_up, "y", -1)
+    own_rows = jnp.stack([own, own_down, own_up, own_far])
+    own_swap = shift(own_rows, "co", 1)
+    other_rows = jnp.stack([other, other_down, other_up, other_far])
+    other_swap = shift(other_rows, "co", 1)
+    weights = (own_rows, other_rows, own_swap, other_swap)
     col_norm = jnp.sqrt(total.reshape(-1) + 1e-06)
     ratio = magnitude / col_norm
 
@@ -196,15 +212,17 @@
         return (g.astype(F32) * ratio).astype(BF)
 
     scaled_own = scaled_of(grad)
-    factor_cols = lax.dynamic_slice_in_dim(in_factor, t * features, features, 0)
-    hidden = jnp.dot(inputs, factor_cols, preferred_element_type=F32)
     back = lax.dot_general(
         scaled_own, out_factor, (((1,), (1,)), ((), ())), preferred_element_type=F32
     )
     low = jnp.concatenate([hidden, back], axis=1).astype(BF)
     pieces = [shift(low, "t", k) for k in (1, 2, 3)]
-    phase = lax.optimization_barrier((far_low, far_high, other_far, low, *pieces))
-    far_low, far_high, other_far, low, *pieces = phase
+    where = jnp.stack([x, zl, co, y]).astype(jnp.int32)
+    near = (grad, left_low, left_high, right_low, right_high)
+    tiles = tile_of(where, near, ratio.reshape(1, -1), weights, (0, 3, 1))
+    phase = lax.optimization_barrier((far_low, far_high, low, *pieces, *tiles))
+    far_low, far_high, low, *pieces = phase[:-2]
+    tiles = phase[-2:]
     low = sum((p.astype(F32) for p in pieces), low.astype(F32)).astype(BF)
     hidden, back = low[:, :rank], low[:, rank:]
     in_grad = SCALE * lax.dot_general(
@@ -213,22 +231,14 @@
     out_grad = SCALE * lax.dot_general(
         hidden, scaled_own, (((0,), (0,)), ((), ())), preferred_element_type=F32
     )
-    mag_sum = jnp.sum(grad.astype(F32) * pre.astype(F32), axis=0).reshape(N_DP, -1)
     adapters = jnp.concatenate([out_grad, in_grad, mag_sum], axis=1)
-    own_rows = jnp.stack([own, own_down, own_up, own_far])
-    own_swap = shift(own_rows, "co", 1)
-    other_rows = jnp.stack([other, other_down, other_up, other_far])
-    other_swap = shift(other_rows, "co", 1)
     side = adapters.shape[0] // 2
     keep = lax.dynamic_slice_in_dim(adapters, co * side, side, 0)
     give = lax.dynamic_slice_in_dim(adapters, (1 - co) * side, side, 0)
     adapters = keep + shift(give, "co", 1)
     got = shift(adapters, "zl", 1)
 
-    where = jnp.stack([x, zl, co, y]).astype(jnp.int32)
-    tokens_all = (grad, left_low, left_high, right_low, right_high, far_low, far_high)
-    weights = (own_rows, other_rows, own_swap, other_swap)
-    tiles = tile_of(where, tokens_all, ratio.reshape(1, -1), weights)
+    tiles = tile_of(where, (far_low, far_high), ratio.reshape(1, -1), weights, (2,), tiles)
     adapters, got, *tiles = lax.optimization_barrier((adapters, got, *tiles))
     adapters = adapters + got
     tiles = [swap_all(v.reshape(16, half, part), ("x", "t")) for v in tiles]

time: 172 us -> 189 us (1.099)
  waiting for transfers between devices: 56.9 us -> 64.6 us
  Pallas kernels: 16.1 us -> 21.3 us
  local copies, waits for them, and re-layouts: 8.46 us -> 10.6 us
    ppermute x42, waiting for transfers between devices: 42.6 us -> 50 us  [shift(): return lax.ppermute(value, axis, [(i, (i + step) % n) for i in range(n)])]
    pallas_call x1 -> x2, Pallas kernels: 11.9 us -> 17.1 us  [tile_of(): pl.pallas_call(body, grid_spec=pltpu.PrefetchScalarGridSpec(num_scalar_pr...]
    unnamed x15 -> x41, local copies, waits for them, and re-layouts: 2.62 us -> 4.96 us
  transfers between devices with their start and end apart: 44 -> 44, of which waited for: 25 -> 21; matrix products, arithmetic and copies ran while one was open for 9% -> 5% of each run, Pallas kernels for 10% -> 11%
where the time goes in v9:
time: 189 us; the launch traced here: 186 us
  starting transfers between devices  72.9 us (39%)
  waiting for transfers between devices  64.6 us (34%)
  Pallas kernels  21.3 us (11%)
  other arithmetic  12 us (6%)
  local copies, waits for them, and re-layouts  10.6 us (6%)
  matrix products  3.45 us (2%)
    ppermute x42, starting transfers between devices, shift(): return lax.ppermute(value, axis, [(i, (i + step) % n) for i in range(n)])  65.7 us
    ppermute x42, waiting for transfers between devices, shift(): return lax.ppermute(value, axis, [(i, (i + step) % n) for i in range(n)])  50 us
    pallas_call x2, Pallas kernels, tile_of(): pl.pallas_call(body, grid_spec=pltpu.PrefetchScalarGridSpec(num_scalar_pr...  17.1 us
    all_to_all x2, waiting for transfers between devices, swap_all(): return lax.all_to_all(value, axes, 0, 0, tiled=True)  14.6 us
    all_to_all x2, starting transfers between devices, swap_all(): return lax.all_to_all(value, axes, 0, 0, tiled=True)  7.23 us
    unnamed x41, local copies, waits for them, and re-layouts  4.96 us
    pallas_call x1, Pallas kernels, merge(): pl.pallas_call(body, grid=(steps,), in_specs=[columns(rows), whole(count,...  4.24 us
  transfers between devices with their start and end apart: 44, of which 21 were waited for; matrix products, arithmetic and copies ran while one was open for 5% of the time, Pallas kernels for 11%

profile of v9, /device:TPU:8, one launch (start us, length us, event | category | flops | bytes accessed | tf_op | source)
XLA Modules:
  0.0 186.0 jit_solution(5999187063679355434)
XLA Ops:
  0.6 2.3 %fusion.12 = (bf16[96,3584]{1,0:T(8,128)(2,1)}, bf16[96,3584]{1,0:T(8,128)(2,1)S(1)}) fusion(bf16[192,3584]{1,0:T(8,128)(2,1)} %refs_1_.1), kind=kLoop, calls=%fused_computation.50 | loop fusion | bytes 2752512 | tf_op jit(solution)/shard_map/slice | solution.py:178
  7.0 4.2 %shard_map.111 = (bf16[64,3584]{1,0:T(8,128)(2,1)}, f32[1,3584]{1,0:T(1,128)}) custom-call(s32[64,3584]{1,0:T(8,128)} %refs_0_.1, f32[56,64]{1,0:T(8,128)} %bitcast.52, bf16[64,64]{1,0:T(8,128)(2,1)} %copy.20.refs_2_, bf16[64,3584]{1,0:T(8,128)(2,1)} %refs_3_.1), custom_call_target="tpu_custom_call" | custom-call | flops 234881024 | bytes 1835008 | tf_op jit(solution)/shard_map/pallas_call | solution.py:65
  13.6 2.7 %collective-permute-start.6 = (f32[28,128]{1,0:T(8,128)S(1)}, f32[28,128]{1,0:T(8,128)S(1)}, u32[]{:S(2)}, u32[]{:S(2)}) collective-permute-start(f32[28,128]{1,0:T(8,128)S(1)} %bitcast.49), channel_id=1, source_target_pairs={{0,128},{64,192},{128,0},{192,64},{1,129},{65,193},{129,1},{193,65... | collective-permute-start | bytes 43016 | tf_op jit(solution)/shard_map/ppermute | solution.py:18
  17.0 1.9 %collective-permute-start.2 = (bf16[64,3584]{1,0:T(8,128)(2,1)}, bf16[64,3584]{1,0:T(8,128)(2,1)S(1)}, u32[]{:S(2)}, u32[]{:S(2)}) collective-permute-start(bf16[64,3584]{1,0:T(8,128)(2,1)} %get-tuple-element.45), channel_id=1, source_target_pairs={{0,8},{8,0},{1,9},{9,1},{2,10},{10,2},{3,11},{11,3},{4,12},{12,4},... | collective-permute-start | bytes 1376264 | tf_op jit(solution)/shard_map/ppermute | solution.py:18
  20.9 7.3 %collective-permute-done.2 = bf16[64,3584]{1,0:T(8,128)(2,1)S(1)} collective-permute-done((bf16[64,3584]{1,0:T(8,128)(2,1)}, bf16[64,3584]{1,0:T(8,128)(2,1)S(1)}, u32[]{:S(2)}, u32[]{:S(2)}) %collective-permute-start.2) | collective-permute-done | bytes 458784 | tf_op jit(solution)/shard_map/ppermute | solution.py:18
  35.0 2.7 %collective-permute-start.11 = (f32[28,128]{1,0:T(8,128)S(1)}, f32[28,128]{1,0:T(8,128)S(1)}, u32[]{:S(2)}, u32[]{:S(2)}) collective-permute-start(f32[28,128]{1,0:T(8,128)S(1)} %add_add_fusion.4), channel_id=1, source_target_pairs={{0,32},{16,48},{32,0},{48,16},{1,33},{17,49},{33,1},{49,17},{2,34}... | collective-permute-start | bytes 43016 | tf_op jit(solution)/shard_map/ppermute | solution.py:18
  37.7 2.1 %collective-permute-done.10 = f32[28,128]{1,0:T(8,128)S(1)} collective-permute-done((f32[28,128]{1,0:T(8,128)S(1)}, f32[28,128]{1,0:T(8,128)S(1)}, u32[]{:S(2)}, u32[]{:S(2)}) %collective-permute-start.10) | collective-permute-done | bytes 14368 | tf_op jit(solution)/shard_map/ppermute | solution.py:18
  42.0 1.9 %collective-permute-done.12 = f32[28,128]{1,0:T(8,128)S(1)} collective-permute-done((f32[28,128]{1,0:T(8,128)S(1)}, f32[28,128]{1,0:T(8,128)S(1)}, u32[]{:S(2)}, u32[]{:S(2)}) %collective-permute-start.12) | collective-permute-done | bytes 14368 | tf_op jit(solution)/shard_map/ppermute | solution.py:18
  45.2 4.9 %collective-permute-done.15 = bf16[64,3584]{1,0:T(8,128)(2,1)S(1)} collective-permute-done((bf16[64,3584]{1,0:T(8,128)(2,1)S(1)}, bf16[64,3584]{1,0:T(8,128)(2,1)S(1)}, u32[]{:S(2)}, u32[]{:S(2)}) %collective-permute-start.15) | collective-permute-done | bytes 458784 | tf_op jit(solution)/shard_map/ppermute | solution.py:18
  52.7 2.0 %collective-permute-start.17 = (f32[28,128]{1,0:T(8,128)S(1)}, f32[28,128]{1,0:T(8,128)S(1)}, u32[]{:S(2)}, u32[]{:S(2)}) collective-permute-start(f32[28,128]{1,0:T(8,128)S(1)} %add_add_fusion.3), channel_id=1, source_target_pairs={{0,8},{4,12},{8,0},{12,4},{1,9},{5,13},{9,1},{13,5},{2,10},{6,14},... | collective-permute-start | bytes 43016 | tf_op jit(solution)/shard_map/ppermute | solution.py:18
  56.2 2.9 %collective-permute-start.19 = (bf16[64,3584]{1,0:T(8,128)(2,1)}, bf16[64,3584]{1,0:T(8,128)(2,1)S(1)}, u32[]{:S(2)}, u32[]{:S(2)}) collective-permute-start(bf16[64,3584]{1,0:T(8,128)(2,1)} %copy-done.17), channel_id=1, source_target_pairs={{0,192},{64,0},{128,64},{192,128},{1,193},{65,1},{129,65},{193,129... | collective-permute-start | bytes 1376264 | tf_op jit(solution)/shard_map/ppermute | solution.py:18
  60.4 7.9 %collective-permute-done.19 = bf16[64,3584]{1,0:T(8,128)(2,1)S(1)} collective-permute-done((bf16[64,3584]{1,0:T(8,128)(2,1)}, bf16[64,3584]{1,0:T(8,128)(2,1)S(1)}, u32[]{:S(2)}, u32[]{:S(2)}) %collective-permute-start.19) | collective-permute-done | bytes 458784 | tf_op jit(solution)/shard_map/ppermute | solution.py:18
  69.1 3.1 %pad_maximum_fusion.1.refs_8_.refs_5_ = bf16[4,64,3584]{2,1,0:T(8,128)(2,1)} fusion(bf16[1,64,3584]{2,1,0:T(8,128)(2,1)} %bitcast.47, bf16[1,64,3584]{2,1,0:T(8,128)(2,1)} %bitcast.46, bf16[1,64,3584]{2,1,0:T(8,128)(2,1)} %bitcast.45, bf16[1,64,3584]{2,1,0:T(8,128)(2,1)} %bitcast.42), kind=kLoop, calls=%fused_computation.6 | loop fusion | flops 2752512 | bytes 3670016 | tf_op jit(solution)/shard_map/stack | solution.py:205
  74.4 3.2 %collective-permute-start.21 = (bf16[96,3584]{1,0:T(8,128)(2,1)}, bf16[96,3584]{1,0:T(8,128)(2,1)S(1)}, u32[]{:S(2)}, u32[]{:S(2)}) collective-permute-start(bf16[96,3584]{1,0:T(8,128)(2,1)} %copy-done.2), channel_id=1, source_target_pairs={{0,48},{16,0},{32,16},{48,32},{1,49},{17,1},{33,17},{49,33},{2,50}... | collective-permute-start | bytes 2064392 | tf_op jit(solution)/shard_map/ppermute | solution.py:18
  79.2 3.4 %collective-permute-start.22 = (bf16[192,128]{0,1:T(8,128)(2,1)S(1)}, bf16[192,128]{0,1:T(8,128)(2,1)S(1)}, u32[]{:S(2)}, u32[]{:S(2)}) collective-permute-start(bf16[192,128]{0,1:T(8,128)(2,1)S(1)} %pad_maximum_fusion.4), channel_id=1, source_target_pairs={{0,1},{1,2},{2,3},{3,0},{4,5},{5,6},{6,7},{7,4},{8,9},{9,10},{10,1... | collective-permute-start | bytes 147464 | tf_op jit(solution)/shard_map/ppermute | solution.py:18
  82.6 4.8 %collective-permute-start.23 = (bf16[192,128]{0,1:T(8,128)(2,1)S(1)}, bf16[192,128]{0,1:T(8,128)(2,1)S(1)}, u32[]{:S(2)}, u32[]{:S(2)}) collective-permute-start(bf16[192,128]{0,1:T(8,128)(2,1)S(1)} %pad_maximum_fusion.4), channel_id=1, source_target_pairs={{0,2},{1,3},{2,0},{3,1},{4,6},{5,7},{6,4},{7,5},{8,10},{9,11},{10,... | collective-permute-start | bytes 147464 | tf_op jit(solution)/shard_map/ppermute | solution.py:18
  87.4 2.7 %collective-permute-start.24 = (bf16[192,128]{0,1:T(8,128)(2,1)S(1)}, bf16[192,128]{0,1:T(8,128)(2,1)S(1)}, u32[]{:S(2)}, u32[]{:S(2)}) collective-permute-start(bf16[192,128]{0,1:T(8,128)(2,1)S(1)} %pad_maximum_fusion.4), channel_id=1, source_target_pairs={{0,3},{1,0},{2,1},{3,2},{4,7},{5,4},{6,5},{7,6},{8,11},{9,8},{10,9... | collective-permute-start | bytes 147464 | tf_op jit(solution)/shard_map/ppermute | solution.py:18
  92.3 10.0 %shard_map.112 = (bf16[4,4,96,256]{3,2,1,0:T(8,128)(2,1)}, bf16[4,4,96,256]{3,2,1,0:T(8,128)(2,1)}) custom-call(s32[4]{0:T(128)S(1)} %pad_add_fusion.refs_0_, bf16[192,3584]{1,0:T(8,128)(2,1)S(1)} %copy-done.1, bf16[96,3584]{1,0:T(8,128)(2,1)} %collective-permute-done.refs_2_, bf16[96,3584]{1,0:T(8,128)(2,1)S(1)} %copy-done.5, ...), custom_call_target="tpu_custom_call" | custom-call | flops 4227858432 | bytes 11468800 | tf_op jit(solution)/shard_map/pallas_call | solution.py:133
  104.4 2.4 %collective-permute-done.27 = f32[32,4664]{1,0:T(8,128)} collective-permute-done((f32[32,4664]{1,0:T(8,128)}, f32[32,4664]{1,0:T(8,128)}, u32[]{:S(2)}, u32[]{:S(2)}) %collective-permute-start.27) | collective-permute-done | bytes 597024 | tf_op jit(solution)/shard_map/ppermute | solution.py:18
  106.8 2.0 %dynamic-slice_add_fusion = f32[32,4664]{1,0:T(8,128)} fusion(f32[32,4664]{1,0:T(8,128)} %collective-permute-done.27, f32[64,4664]{1,0:T(8,128)S(1)} %pad_maximum_fusion.2, s32[]{:T(128)S(6)} %select_n.135), kind=kLoop, calls=%fused_computation.14 | loop fusion | flops 149248 | bytes 1790980 | tf_op jit(solution)/shard_map/add | solution.py:238
  109.8 7.1 %shard_map.113 = (bf16[4,4,96,256]{3,2,1,0:T(8,128)(2,1)}, bf16[4,4,96,256]{3,2,1,0:T(8,128)(2,1)}) custom-call(s32[4]{0:T(128)S(1)} %pad_add_fusion.refs_0_, bf16[96,3584]{1,0:T(8,128)(2,1)S(1)} %collective-permute-done.20.refs_1_, bf16[96,3584]{1,0:T(8,128)(2,1)S(1)} %collective-permute-done.21.refs_2_, ...), custom_call_target="tpu_custom_call", output_to_operand_aliasing={{0}: (8, {}), {1}: (9, {})} | custom-call | flops 1409286144 | bytes 8716288 | tf_op jit(solution)/shard_map/pallas_call | solution.py:133
  116.9 7.8 %collective-permute-done.28 = f32[32,4664]{1,0:T(8,128)S(1)} collective-permute-done((f32[32,4664]{1,0:T(8,128)}, f32[32,4664]{1,0:T(8,128)S(1)}, u32[]{:S(2)}, u32[]{:S(2)}) %collective-permute-start.28) | collective-permute-done | bytes 597024 | tf_op jit(solution)/shard_map/ppermute | solution.py:18
  127.7 2.7 %collective-permute-start.30 = (f32[8,4664]{1,0:T(8,128)S(1)}, f32[8,4664]{1,0:T(8,128)S(1)}, u32[]{:S(2)}, u32[]{:S(2)}) collective-permute-start(f32[8,4664]{1,0:T(8,128)S(1)} %get-tuple-element.90), channel_id=1, source_target_pairs={{0,128},{64,192},{128,0},{192,64},{1,129},{65,193},{129,1},{193,65... | collective-permute-start | bytes 447752 | tf_op jit(solution)/shard_map/ppermute | solution.py:18
  130.4 2.3 %collective-permute-start.31 = (f32[8,4664]{1,0:T(8,128)S(1)}, f32[8,4664]{1,0:T(8,128)S(1)}, u32[]{:S(2)}, u32[]{:S(2)}) collective-permute-start(f32[8,4664]{1,0:T(8,128)S(1)} %get-tuple-element.89), channel_id=1, source_target_pairs={{0,192},{64,0},{128,64},{192,128},{1,193},{65,1},{129,65},{193,129... | collective-permute-start | bytes 447752 | tf_op jit(solution)/shard_map/ppermute | solution.py:18
  132.8 3.6 %all-to-all-start = ((bf16[16,96,256]{2,1,0:T(8,128)(2,1)}), bf16[16,96,256]{2,1,0:T(8,128)(2,1)S(1)}, u32[]{:S(2)}, u32[]{:S(2)}) async-start(bf16[16,96,256]{2,1,0:T(8,128)(2,1)} %bitcast.15), calls=%async_computation | async-start | bytes 1572864 | tf_op jit(solution)/shard_map/all_to_all | solution.py:22
  138.4 2.7 %collective-permute-start.33 = (f32[2,4664]{1,0:T(2,128)S(1)}, f32[2,4664]{1,0:T(2,128)S(1)}, u32[]{:S(2)}, u32[]{:S(2)}) collective-permute-start(f32[2,4664]{1,0:T(2,128)S(1)} %get-tuple-element.93), channel_id=1, source_target_pairs={{0,32},{16,48},{32,0},{48,16},{1,33},{17,49},{33,1},{49,17},{2,34}... | collective-permute-start | bytes 111944 | tf_op jit(solution)/shard_map/ppermute | solution.py:18
  145.4 14.6 %all-to-all-done = bf16[16,96,256]{2,1,0:T(8,128)(2,1)S(1)} async-done(((bf16[16,96,256]{2,1,0:T(8,128)(2,1)}), bf16[16,96,256]{2,1,0:T(8,128)(2,1)S(1)}, u32[]{:S(2)}, u32[]{:S(2)}) %all-to-all-start) | async-done | bytes 786464 | tf_op jit(solution)/shard_map/all_to_all | solution.py:22
  160.0 3.6 %all-to-all-start.1 = ((bf16[16,96,256]{2,1,0:T(8,128)(2,1)}), bf16[16,96,256]{2,1,0:T(8,128)(2,1)S(1)}, u32[]{:S(2)}, u32[]{:S(2)}) async-start(bf16[16,96,256]{2,1,0:T(8,128)(2,1)} %bitcast.18), calls=%async_computation.1 | async-start | bytes 1572864 | tf_op jit(solution)/shard_map/all_to_all | solution.py:22
  165.4 2.7 %collective-permute-start.36 = (f32[2,4664]{1,0:T(2,128)S(1)}, f32[2,4664]{1,0:T(2,128)S(1)}, u32[]{:S(2)}, u32[]{:S(2)}) collective-permute-start(f32[2,4664]{1,0:T(2,128)S(1)} %add_add_fusion.1), channel_id=1, source_target_pairs={{0,32},{16,48},{32,0},{48,16},{1,33},{17,49},{33,1},{49,17},{2,34}... | collective-permute-start | bytes 111944 | tf_op jit(solution)/shard_map/ppermute | solution.py:18
  169.8 1.9 %collective-permute-done.35 = f32[2,4664]{1,0:T(2,128)S(1)} collective-permute-done((f32[2,4664]{1,0:T(2,128)S(1)}, f32[2,4664]{1,0:T(2,128)S(1)}, u32[]{:S(2)}, u32[]{:S(2)}) %collective-permute-start.35) | collective-permute-done | bytes 37344 | tf_op jit(solution)/shard_map/ppermute | solution.py:18
  173.1 2.6 %collective-permute-start.39 = (f32[8,4664]{1,0:T(8,128)S(1)}, f32[8,4664]{1,0:T(8,128)S(1)}, u32[]{:S(2)}, u32[]{:S(2)}) collective-permute-start(f32[8,4664]{1,0:T(8,128)S(1)} %constant_dynamic-update-slice_fusion.6), channel_id=1, source_target_pairs={{0,128},{64,192},{128,0},{192,64},{1,129},{65,193},{129,1},{193,65... | collective-permute-start | bytes 447752 | tf_op jit(solution)/shard_map/ppermute | solution.py:18
  177.6 2.2 %collective-permute-done.39 = f32[8,4664]{1,0:T(8,128)S(1)} collective-permute-done((f32[8,4664]{1,0:T(8,128)S(1)}, f32[8,4664]{1,0:T(8,128)S(1)}, u32[]{:S(2)}, u32[]{:S(2)}) %collective-permute-start.39) | collective-permute-done | bytes 149280 | tf_op jit(solution)/shard_map/ppermute | solution.py:18
  (150 shorter events, 56.7 us)
Async XLA Ops:
  3.0 27.8 %collective-permute-start = (bf16[96,3584]{1,0:T(8,128)(2,1)S(1)}, bf16[96,3584]{1,0:T(8,128)(2,1)}, u32[]{:S(2)}, u32[]{:S(2)}) collective-permute-start(bf16[96,3584]{1,0:T(8,128)(2,1)S(1)} %get-tuple-element.50), channel_id=1, source_target_pairs={{0,16},{16,32},{32,48},{48,0},{1,17},{17,33},{33,49},{49,1},{2,18}... | collective-permute-start | bytes 2064392 | tf_op jit(solution)/shard_map/ppermute | solution.py:18
  4.4 26.3 %collective-permute-start.1 = (bf16[96,3584]{1,0:T(8,128)(2,1)}, bf16[96,3584]{1,0:T(8,128)(2,1)S(1)}, u32[]{:S(2)}, u32[]{:S(2)}) collective-permute-start(bf16[96,3584]{1,0:T(8,128)(2,1)} %get-tuple-element.49), channel_id=1, source_target_pairs={{0,48},{16,0},{32,16},{48,32},{1,49},{17,1},{33,17},{49,33},{2,50}... | collective-permute-start | bytes 2064392 | tf_op jit(solution)/shard_map/ppermute | solution.py:18
  17.0 11.2 %collective-permute-start.2 = (bf16[64,3584]{1,0:T(8,128)(2,1)}, bf16[64,3584]{1,0:T(8,128)(2,1)S(1)}, u32[]{:S(2)}, u32[]{:S(2)}) collective-permute-start(bf16[64,3584]{1,0:T(8,128)(2,1)} %get-tuple-element.45), channel_id=1, source_target_pairs={{0,8},{8,0},{1,9},{9,1},{2,10},{10,2},{3,11},{11,3},{4,12},{12,4},... | collective-permute-start | bytes 1376264 | tf_op jit(solution)/shard_map/ppermute | solution.py:18
  18.9 10.8 %collective-permute-start.3 = (bf16[64,3584]{1,0:T(8,128)(2,1)}, bf16[64,3584]{1,0:T(8,128)(2,1)S(1)}, u32[]{:S(2)}, u32[]{:S(2)}) collective-permute-start(bf16[64,3584]{1,0:T(8,128)(2,1)} %get-tuple-element.45), channel_id=1, source_target_pairs={{0,64},{64,128},{128,192},{192,0},{1,65},{65,129},{129,193},{193,1... | collective-permute-start | bytes 1376264 | tf_op jit(solution)/shard_map/ppermute | solution.py:18
  20.1 10.6 %collective-permute-start.4 = (bf16[64,3584]{1,0:T(8,128)(2,1)}, bf16[64,3584]{1,0:T(8,128)(2,1)S(1)}, u32[]{:S(2)}, u32[]{:S(2)}) collective-permute-start(bf16[64,3584]{1,0:T(8,128)(2,1)} %get-tuple-element.45), channel_id=1, source_target_pairs={{0,192},{64,0},{128,64},{192,128},{1,193},{65,1},{129,65},{193,129... | collective-permute-start | bytes 1376264 | tf_op jit(solution)/shard_map/ppermute | solution.py:18
  30.8 14.4 %collective-permute-start.13 = (bf16[64,3584]{1,0:T(8,128)(2,1)S(1)}, bf16[64,3584]{1,0:T(8,128)(2,1)S(1)}, u32[]{:S(2)}, u32[]{:S(2)}) collective-permute-start(bf16[64,3584]{1,0:T(8,128)(2,1)S(1)} %collective-permute-done.2), channel_id=1, source_target_pairs={{0,64},{64,128},{128,192},{192,0},{1,65},{65,129},{129,193},{193,1... | collective-permute-start | bytes 1376264 | tf_op jit(solution)/shard_map/ppermute | solution.py:18
  31.8 13.4 %collective-permute-start.14 = (bf16[64,3584]{1,0:T(8,128)(2,1)S(1)}, bf16[64,3584]{1,0:T(8,128)(2,1)S(1)}, u32[]{:S(2)}, u32[]{:S(2)}) collective-permute-start(bf16[64,3584]{1,0:T(8,128)(2,1)S(1)} %collective-permute-done.2), channel_id=1, source_target_pairs={{0,192},{64,0},{128,64},{192,128},{1,193},{65,1},{129,65},{193,129... | collective-permute-start | bytes 1376264 | tf_op jit(solution)/shard_map/ppermute | solution.py:18
  33.1 17.1 %collective-permute-start.15 = (bf16[64,3584]{1,0:T(8,128)(2,1)S(1)}, bf16[64,3584]{1,0:T(8,128)(2,1)S(1)}, u32[]{:S(2)}, u32[]{:S(2)}) collective-permute-start(bf16[64,3584]{1,0:T(8,128)(2,1)S(1)} %collective-permute-done.3), channel_id=1, source_target_pairs={{0,64},{64,128},{128,192},{192,0},{1,65},{65,129},{129,193},{193,1... | collective-permute-start | bytes 1376264 | tf_op jit(solution)/shard_map/ppermute | solution.py:18
  40.3 20.0 %collective-permute-start.8 = (bf16[96,3584]{1,0:T(8,128)(2,1)}, bf16[96,3584]{1,0:T(8,128)(2,1)S(1)}, u32[]{:S(2)}, u32[]{:S(2)}) collective-permute-start(bf16[96,3584]{1,0:T(8,128)(2,1)} %get-tuple-element.49), channel_id=1, source_target_pairs={{0,16},{16,32},{32,48},{48,0},{1,17},{17,33},{33,49},{49,1},{2,18}... | collective-permute-start | bytes 2064392 | tf_op jit(solution)/shard_map/ppermute | solution.py:18
  43.8 16.6 %collective-permute-start.9 = (bf16[96,3584]{1,0:T(8,128)(2,1)}, bf16[96,3584]{1,0:T(8,128)(2,1)}, u32[]{:S(2)}, u32[]{:S(2)}) collective-permute-start(bf16[96,3584]{1,0:T(8,128)(2,1)} %copy-done.7), channel_id=1, source_target_pairs={{0,48},{16,0},{32,16},{48,32},{1,49},{17,1},{33,17},{49,33},{2,50}... | collective-permute-start | bytes 2064392 | tf_op jit(solution)/shard_map/ppermute | solution.py:18
  52.7 7.7 %collective-permute-start.17 = (f32[28,128]{1,0:T(8,128)S(1)}, f32[28,128]{1,0:T(8,128)S(1)}, u32[]{:S(2)}, u32[]{:S(2)}) collective-permute-start(f32[28,128]{1,0:T(8,128)S(1)} %add_add_fusion.3), channel_id=1, source_target_pairs={{0,8},{4,12},{8,0},{12,4},{1,9},{5,13},{9,1},{13,5},{2,10},{6,14},... | collective-permute-start | bytes 43016 | tf_op jit(solution)/shard_map/ppermute | solution.py:18
  54.7 5.7 %collective-permute-start.18 = (f32[28,128]{1,0:T(8,128)S(1)}, f32[28,128]{1,0:T(8,128)S(1)}, u32[]{:S(2)}, u32[]{:S(2)}) collective-permute-start(f32[28,128]{1,0:T(8,128)S(1)} %add_add_fusion.3), channel_id=1, source_target_pairs={{0,12},{4,0},{8,4},{12,8},{1,13},{5,1},{9,5},{13,9},{2,14},{6,2},{... | collective-permute-start | bytes 43016 | tf_op jit(solution)/shard_map/ppermute | solution.py:18
  56.2 12.2 %collective-permute-start.19 = (bf16[64,3584]{1,0:T(8,128)(2,1)}, bf16[64,3584]{1,0:T(8,128)(2,1)S(1)}, u32[]{:S(2)}, u32[]{:S(2)}) collective-permute-start(bf16[64,3584]{1,0:T(8,128)(2,1)} %copy-done.17), channel_id=1, source_target_pairs={{0,192},{64,0},{128,64},{192,128},{1,193},{65,1},{129,65},{193,129... | collective-permute-start | bytes 1376264 | tf_op jit(solution)/shard_map/ppermute | solution.py:18
  72.2 10.4 %collective-permute-start.26 = (bf16[4,64,3584]{2,1,0:T(8,128)(2,1)}, bf16[4,64,3584]{2,1,0:T(8,128)(2,1)}, u32[]{:S(2)}, u32[]{:S(2)}) collective-permute-start(bf16[4,64,3584]{2,1,0:T(8,128)(2,1)} %pad_maximum_fusion.1.refs_8_.refs_5_), channel_id=1, source_target_pairs={{0,4},{4,0},{1,5},{5,1},{2,6},{6,2},{3,7},{7,3},{8,12},{12,8},{9,1... | collective-permute-start | bytes 5505032 | tf_op jit(solution)/shard_map/ppermute | solution.py:18
  73.7 13.7 %collective-permute-start.25 = (bf16[4,64,3584]{2,1,0:T(8,128)(2,1)}, bf16[4,64,3584]{2,1,0:T(8,128)(2,1)}, u32[]{:S(2)}, u32[]{:S(2)}) collective-permute-start(bf16[4,64,3584]{2,1,0:T(8,128)(2,1)} %pad_maximum_fusion.refs_7_.refs_4_), channel_id=1, source_target_pairs={{0,4},{4,0},{1,5},{5,1},{2,6},{6,2},{3,7},{7,3},{8,12},{12,8},{9,1... | collective-permute-start | bytes 5505032 | tf_op jit(solution)/shard_map/ppermute | solution.py:18
  74.3 28.0 %collective-permute-start.20 = (bf16[96,3584]{1,0:T(8,128)(2,1)}, bf16[96,3584]{1,0:T(8,128)(2,1)S(1)}, u32[]{:S(2)}, u32[]{:S(2)}) collective-permute-start(bf16[96,3584]{1,0:T(8,128)(2,1)} %collective-permute-done.refs_2_), channel_id=1, source_target_pairs={{0,16},{16,32},{32,48},{48,0},{1,17},{17,33},{33,49},{49,1},{2,18}... | collective-permute-start | bytes 2064392 | tf_op jit(solution)/shard_map/ppermute | solution.py:18
  74.4 27.9 %collective-permute-start.21 = (bf16[96,3584]{1,0:T(8,128)(2,1)}, bf16[96,3584]{1,0:T(8,128)(2,1)S(1)}, u32[]{:S(2)}, u32[]{:S(2)}) collective-permute-start(bf16[96,3584]{1,0:T(8,128)(2,1)} %copy-done.2), channel_id=1, source_target_pairs={{0,48},{16,0},{32,16},{48,32},{1,49},{17,1},{33,17},{49,33},{2,50}... | collective-permute-start | bytes 2064392 | tf_op jit(solution)/shard_map/ppermute | solution.py:18
  79.2 23.1 %collective-permute-start.22 = (bf16[192,128]{0,1:T(8,128)(2,1)S(1)}, bf16[192,128]{0,1:T(8,128)(2,1)S(1)}, u32[]{:S(2)}, u32[]{:S(2)}) collective-permute-start(bf16[192,128]{0,1:T(8,128)(2,1)S(1)} %pad_maximum_fusion.4), channel_id=1, source_target_pairs={{0,1},{1,2},{2,3},{3,0},{4,5},{5,6},{6,7},{7,4},{8,9},{9,10},{10,1... | collective-permute-start | bytes 147464 | tf_op jit(solution)/shard_map/ppermute | solution.py:18
  82.6 19.7 %collective-permute-start.23 = (bf16[192,128]{0,1:T(8,128)(2,1)S(1)}, bf16[192,128]{0,1:T(8,128)(2,1)S(1)}, u32[]{:S(2)}, u32[]{:S(2)}) collective-permute-start(bf16[192,128]{0,1:T(8,128)(2,1)S(1)} %pad_maximum_fusion.4), channel_id=1, source_target_pairs={{0,2},{1,3},{2,0},{3,1},{4,6},{5,7},{6,4},{7,5},{8,10},{9,11},{10,... | collective-permute-start | bytes 147464 | tf_op jit(solution)/shard_map/ppermute | solution.py:18
  87.4 14.9 %collective-permute-start.24 = (bf16[192,128]{0,1:T(8,128)(2,1)S(1)}, bf16[192,128]{0,1:T(8,128)(2,1)S(1)}, u32[]{:S(2)}, u32[]{:S(2)}) collective-permute-start(bf16[192,128]{0,1:T(8,128)(2,1)S(1)} %pad_maximum_fusion.4), channel_id=1, source_target_pairs={{0,3},{1,0},{2,1},{3,2},{4,7},{5,4},{6,5},{7,6},{8,11},{9,8},{10,9... | collective-permute-start | bytes 147464 | tf_op jit(solution)/shard_map/ppermute | solution.py:18
  108.8 15.9 %collective-permute-start.28 = (f32[32,4664]{1,0:T(8,128)}, f32[32,4664]{1,0:T(8,128)S(1)}, u32[]{:S(2)}, u32[]{:S(2)}) collective-permute-start(f32[32,4664]{1,0:T(8,128)} %dynamic-slice_add_fusion), channel_id=1, source_target_pairs={{0,8},{8,0},{1,9},{9,1},{2,10},{10,2},{3,11},{11,3},{4,12},{12,4},... | collective-permute-start | bytes 1790984 | tf_op jit(solution)/shard_map/ppermute | solution.py:18
  125.9 10.5 %collective-permute-start.29 = (f32[8,4664]{1,0:T(8,128)S(1)}, f32[8,4664]{1,0:T(8,128)S(1)}, u32[]{:S(2)}, u32[]{:S(2)}) collective-permute-start(f32[8,4664]{1,0:T(8,128)S(1)} %get-tuple-element.88), channel_id=1, source_target_pairs={{0,64},{64,128},{128,192},{192,0},{1,65},{65,129},{129,193},{193,1... | collective-permute-start | bytes 447752 | tf_op jit(solution)/shard_map/ppermute | solution.py:18
  127.7 8.7 %collective-permute-start.30 = (f32[8,4664]{1,0:T(8,128)S(1)}, f32[8,4664]{1,0:T(8,128)S(1)}, u32[]{:S(2)}, u32[]{:S(2)}) collective-permute-start(f32[8,4664]{1,0:T(8,128)S(1)} %get-tuple-element.90), channel_id=1, source_target_pairs={{0,128},{64,192},{128,0},{192,64},{1,129},{65,193},{129,1},{193,65... | collective-permute-start | bytes 447752 | tf_op jit(solution)/shard_map/ppermute | solution.py:18
  130.4 6.9 %collective-permute-start.31 = (f32[8,4664]{1,0:T(8,128)S(1)}, f32[8,4664]{1,0:T(8,128)S(1)}, u32[]{:S(2)}, u32[]{:S(2)}) collective-permute-start(f32[8,4664]{1,0:T(8,128)S(1)} %get-tuple-element.89), channel_id=1, source_target_pairs={{0,192},{64,0},{128,64},{192,128},{1,193},{65,1},{129,65},{193,129... | collective-permute-start | bytes 447752 | tf_op jit(solution)/shard_map/ppermute | solution.py:18
  132.8 27.2 %all-to-all-start = ((bf16[16,96,256]{2,1,0:T(8,128)(2,1)}), bf16[16,96,256]{2,1,0:T(8,128)(2,1)S(1)}, u32[]{:S(2)}, u32[]{:S(2)}) async-start(bf16[16,96,256]{2,1,0:T(8,128)(2,1)} %bitcast.15), calls=%async_computation | async-start | bytes 1572864 | tf_op jit(solution)/shard_map/all_to_all | solution.py:22
  137.5 5.8 %collective-permute-start.32 = (f32[2,4664]{1,0:T(2,128)S(1)}, f32[2,4664]{1,0:T(2,128)S(1)}, u32[]{:S(2)}, u32[]{:S(2)}) collective-permute-start(f32[2,4664]{1,0:T(2,128)S(1)} %get-tuple-element.91), channel_id=1, source_target_pairs={{0,16},{16,32},{32,48},{48,0},{1,17},{17,33},{33,49},{49,1},{2,18}... | collective-permute-start | bytes 111944 | tf_op jit(solution)/shard_map/ppermute | solution.py:18
  138.4 5.5 %collective-permute-start.33 = (f32[2,4664]{1,0:T(2,128)S(1)}, f32[2,4664]{1,0:T(2,128)S(1)}, u32[]{:S(2)}, u32[]{:S(2)}) collective-permute-start(f32[2,4664]{1,0:T(2,128)S(1)} %get-tuple-element.93), channel_id=1, source_target_pairs={{0,32},{16,48},{32,0},{48,16},{1,33},{17,49},{33,1},{49,17},{2,34}... | collective-permute-start | bytes 111944 | tf_op jit(solution)/shard_map/ppermute | solution.py:18
  160.0 21.6 %all-to-all-start.1 = ((bf16[16,96,256]{2,1,0:T(8,128)(2,1)}), bf16[16,96,256]{2,1,0:T(8,128)(2,1)S(1)}, u32[]{:S(2)}, u32[]{:S(2)}) async-start(bf16[16,96,256]{2,1,0:T(8,128)(2,1)} %bitcast.18), calls=%async_computation.1 | async-start | bytes 1572864 | tf_op jit(solution)/shard_map/all_to_all | solution.py:22
  163.6 8.1 %collective-permute-start.35 = (f32[2,4664]{1,0:T(2,128)S(1)}, f32[2,4664]{1,0:T(2,128)S(1)}, u32[]{:S(2)}, u32[]{:S(2)}) collective-permute-start(f32[2,4664]{1,0:T(2,128)S(1)} %add_add_fusion.1), channel_id=1, source_target_pairs={{0,16},{16,32},{32,48},{48,0},{1,17},{17,33},{33,49},{49,1},{2,18}... | collective-permute-start | bytes 111944 | tf_op jit(solution)/shard_map/ppermute | solution.py:18
  165.4 6.9 %collective-permute-start.36 = (f32[2,4664]{1,0:T(2,128)S(1)}, f32[2,4664]{1,0:T(2,128)S(1)}, u32[]{:S(2)}, u32[]{:S(2)}) collective-permute-start(f32[2,4664]{1,0:T(2,128)S(1)} %add_add_fusion.1), channel_id=1, source_target_pairs={{0,32},{16,48},{32,0},{48,16},{1,33},{17,49},{33,1},{49,17},{2,34}... | collective-permute-start | bytes 111944 | tf_op jit(solution)/shard_map/ppermute | solution.py:18
  173.1 6.7 %collective-permute-start.39 = (f32[8,4664]{1,0:T(8,128)S(1)}, f32[8,4664]{1,0:T(8,128)S(1)}, u32[]{:S(2)}, u32[]{:S(2)}) collective-permute-start(f32[8,4664]{1,0:T(8,128)S(1)} %constant_dynamic-update-slice_fusion.6), channel_id=1, source_target_pairs={{0,128},{64,192},{128,0},{192,64},{1,129},{65,193},{129,1},{193,65... | collective-permute-start | bytes 447752 | tf_op jit(solution)/shard_map/ppermute | solution.py:18
  175.7 5.7 %collective-permute-start.40 = (f32[8,4664]{1,0:T(8,128)S(1)}, f32[8,4664]{1,0:T(8,128)S(1)}, u32[]{:S(2)}, u32[]{:S(2)}) collective-permute-start(f32[8,4664]{1,0:T(8,128)S(1)} %constant_dynamic-update-slice_fusion.6), channel_id=1, source_target_pairs={{0,192},{64,0},{128,64},{192,128},{1,193},{65,1},{129,65},{193,129... | collective-permute-start | bytes 447752 | tf_op jit(solution)/shard_map/ppermute | solution.py:18
  (32 other events, 238.8 us)

commit v10 on v8

--- a/solution.py
+++ b/solution.py
@@ -202,10 +202,10 @@
         scaled_own, out_factor, (((1,), (1,)), ((), ())), preferred_element_type=F32
     )
     low = jnp.concatenate([hidden, back], axis=1).astype(BF)
-    pieces = [shift(low, "t", k) for k in (1, 2, 3)]
-    phase = lax.optimization_barrier((far_low, far_high, other_far, low, *pieces))
-    far_low, far_high, other_far, low, *pieces = phase
-    low = sum((p.astype(F32) for p in pieces), low.astype(F32)).astype(BF)
+    pieces = swap_all(jnp.broadcast_to(low[None], (4,) + low.shape), "t")
+    phase = lax.optimization_barrier((far_low, far_high, other_far, pieces))
+    far_low, far_high, other_far, pieces = phase
+    low = jnp.sum(pieces.astype(F32), axis=0).astype(BF)
     hidden, back = low[:, :rank], low[:, rank:]
     in_grad = SCALE * lax.dot_general(
         back, inputs, (((0,), (0,)), ((), ())), preferred_element_type=F32

time: 172 us -> 171 us (level)
  starting transfers between devices: 72.4 us -> 69.6 us
  local copies, waits for them, and re-layouts: 8.46 us -> 10.5 us
    ppermute x42 -> x39, starting transfers between devices: 64.9 us -> 52.9 us  [shift(): return lax.ppermute(value, axis, [(i, (i + step) % n) for i in range(n)])]
    all_to_all x2 -> x3, starting transfers between devices: 7.55 us -> 16.6 us  [swap_all(): return lax.all_to_all(value, axes, 0, 0, tiled=True)]
    ppermute x42 -> x39, waiting for transfers between devices: 42.6 us -> 35.5 us  [shift(): return lax.ppermute(value, axis, [(i, (i + step) % n) for i in range(n)])]
    all_to_all x2 -> x3, waiting for transfers between devices: 14.2 us -> 20.8 us  [swap_all(): return lax.all_to_all(value, axes, 0, 0, tiled=True)]
  transfers between devices with their start and end apart: 44 -> 42, of which waited for: 25 -> 19; matrix products, arithmetic and copies ran while one was open for 9% -> 11% of each run, Pallas kernels for 10% -> 10%
where the time goes in v10:
time: 171 us; the launch traced here: 169 us
  starting transfers between devices  69.6 us (41%)
  waiting for transfers between devices  56.3 us (33%)
  Pallas kernels  16.1 us (9%)
  other arithmetic  11.6 us (7%)
  local copies, waits for them, and re-layouts  10.5 us (6%)
  matrix products  3.55 us (2%)
    ppermute x39, starting transfers between devices, shift(): return lax.ppermute(value, axis, [(i, (i + step) % n) for i in range(n)])  52.9 us
    ppermute x39, waiting for transfers between devices, shift(): return lax.ppermute(value, axis, [(i, (i + step) % n) for i in range(n)])  35.5 us
    all_to_all x3, waiting for transfers between devices, swap_all(): return lax.all_to_all(value, axes, 0, 0, tiled=True)  20.8 us
    all_to_all x3, starting transfers between devices, swap_all(): return lax.all_to_all(value, axes, 0, 0, tiled=True)  16.6 us
    pallas_call x1, Pallas kernels, tile_of(): pl.pallas_call(tile_kernel, grid_spec=pltpu.PrefetchScalarGridSpec(num_sc...  11.9 us
    pallas_call x1, Pallas kernels, merge(): pl.pallas_call(body, grid=(steps,), in_specs=[columns(rows), whole(count,...  4.24 us
  transfers between devices with their start and end apart: 42, of which 19 were waited for; matrix products, arithmetic and copies ran while one was open for 11% of the time, Pallas kernels for 10%

profile of v10, /device:TPU:8, one launch (start us, length us, event | category | flops | bytes accessed | tf_op | source)
XLA Modules:
  0.0 168.7 jit_solution(4936103814451686753)
XLA Ops:
  0.6 2.5 %fusion.13 = (bf16[96,3584]{1,0:T(8,128)(2,1)}, bf16[96,3584]{1,0:T(8,128)(2,1)}) fusion(bf16[192,3584]{1,0:T(8,128)(2,1)} %refs_0_.3), kind=kLoop, calls=%fused_computation.50 | loop fusion | bytes 2752512 | tf_op jit(solution)/shard_map/slice | solution.py:170
  4.7 1.7 %collective-permute-start.1 = (bf16[96,3584]{1,0:T(8,128)(2,1)}, bf16[96,3584]{1,0:T(8,128)(2,1)S(1)}, u32[]{:S(2)}, u32[]{:S(2)}) collective-permute-start(bf16[96,3584]{1,0:T(8,128)(2,1)} %get-tuple-element.42), channel_id=1, source_target_pairs={{0,48},{16,0},{32,16},{48,32},{1,49},{17,1},{33,17},{49,33},{2,50}... | collective-permute-start | bytes 2064392 | tf_op jit(solution)/shard_map/ppermute | solution.py:18
  7.2 4.2 %shard_map.111 = (bf16[64,3584]{1,0:T(8,128)(2,1)}, f32[1,3584]{1,0:T(1,128)}) custom-call(s32[64,3584]{1,0:T(8,128)} %refs_0_.2, f32[56,64]{1,0:T(8,128)} %bitcast.46, bf16[64,64]{1,0:T(8,128)(2,1)} %copy.22.refs_2_, bf16[64,3584]{1,0:T(8,128)(2,1)} %refs_3_.1), custom_call_target="tpu_custom_call" | custom-call | flops 234881024 | bytes 1835008 | tf_op jit(solution)/shard_map/pallas_call | solution.py:65
  12.2 1.7 collective-permute-start.5
  13.8 2.7 %collective-permute-start.6 = (f32[28,128]{1,0:T(8,128)S(1)}, f32[28,128]{1,0:T(8,128)S(1)}, u32[]{:S(2)}, u32[]{:S(2)}) collective-permute-start(f32[28,128]{1,0:T(8,128)S(1)} %bitcast.43), channel_id=1, source_target_pairs={{0,128},{64,192},{128,0},{192,64},{1,129},{65,193},{129,1},{193,65... | collective-permute-start | bytes 43016 | tf_op jit(solution)/shard_map/ppermute | solution.py:18
  17.2 1.9 %collective-permute-start.2 = (bf16[64,3584]{1,0:T(8,128)(2,1)}, bf16[64,3584]{1,0:T(8,128)(2,1)}, u32[]{:S(2)}, u32[]{:S(2)}) collective-permute-start(bf16[64,3584]{1,0:T(8,128)(2,1)} %get-tuple-element.38), channel_id=1, source_target_pairs={{0,8},{8,0},{1,9},{9,1},{2,10},{10,2},{3,11},{11,3},{4,12},{12,4},... | collective-permute-start | bytes 1376264 | tf_op jit(solution)/shard_map/ppermute | solution.py:18
  21.2 7.4 %collective-permute-done.2 = bf16[64,3584]{1,0:T(8,128)(2,1)} collective-permute-done((bf16[64,3584]{1,0:T(8,128)(2,1)}, bf16[64,3584]{1,0:T(8,128)(2,1)}, u32[]{:S(2)}, u32[]{:S(2)}) %collective-permute-start.2) | collective-permute-done | bytes 458784 | tf_op jit(solution)/shard_map/ppermute | solution.py:18
  31.8 3.0 %collective-permute-start.14 = (f32[28,128]{1,0:T(8,128)S(1)}, f32[28,128]{1,0:T(8,128)S(1)}, u32[]{:S(2)}, u32[]{:S(2)}) collective-permute-start(f32[28,128]{1,0:T(8,128)S(1)} %add_add_fusion.4), channel_id=1, source_target_pairs={{0,32},{16,48},{32,0},{48,16},{1,33},{17,49},{33,1},{49,17},{2,34}... | collective-permute-start | bytes 43016 | tf_op jit(solution)/shard_map/ppermute | solution.py:18
  38.0 2.2 %collective-permute-start.12 = (bf16[64,3584]{1,0:T(8,128)(2,1)}, bf16[64,3584]{1,0:T(8,128)(2,1)}, u32[]{:S(2)}, u32[]{:S(2)}) collective-permute-start(bf16[64,3584]{1,0:T(8,128)(2,1)} %collective-permute-done.3), channel_id=1, source_target_pairs={{0,64},{64,128},{128,192},{192,0},{1,65},{65,129},{129,193},{193,1... | collective-permute-start | bytes 1376264 | tf_op jit(solution)/shard_map/ppermute | solution.py:18
  40.2 1.7 %fusion.1 = f32[3584]{0:T(1024)S(1)} fusion(bf16[192,3584]{1,0:T(8,128)(2,1)S(1)} %copy-done.1, bf16[192,3584]{1,0:T(8,128)(2,1)} %param.15), kind=kLoop, calls=%fused_computation.4 | loop fusion | flops 2748928 | bytes 2766848 | tf_op jit(solution)/shard_map/reduce_sum | solution.py:216
  42.6 2.6 %collective-permute-start.9 = (bf16[96,3584]{1,0:T(8,128)(2,1)}, bf16[96,3584]{1,0:T(8,128)(2,1)}, u32[]{:S(2)}, u32[]{:S(2)}) collective-permute-start(bf16[96,3584]{1,0:T(8,128)(2,1)} %get-tuple-element.43), channel_id=1, source_target_pairs={{0,48},{16,0},{32,16},{48,32},{1,49},{17,1},{33,17},{49,33},{2,50}... | collective-permute-start | bytes 2064392 | tf_op jit(solution)/shard_map/ppermute | solution.py:18
  45.3 4.4 %collective-permute-done.10 = bf16[64,3584]{1,0:T(8,128)(2,1)} collective-permute-done((bf16[64,3584]{1,0:T(8,128)(2,1)}, bf16[64,3584]{1,0:T(8,128)(2,1)}, u32[]{:S(2)}, u32[]{:S(2)}) %collective-permute-start.10) | collective-permute-done | bytes 458784 | tf_op jit(solution)/shard_map/ppermute | solution.py:18
  49.7 5.4 %collective-permute-done.12 = bf16[64,3584]{1,0:T(8,128)(2,1)} collective-permute-done((bf16[64,3584]{1,0:T(8,128)(2,1)}, bf16[64,3584]{1,0:T(8,128)(2,1)}, u32[]{:S(2)}, u32[]{:S(2)}) %collective-permute-start.12) | collective-permute-done | bytes 458784 | tf_op jit(solution)/shard_map/ppermute | solution.py:18
  61.1 2.0 %collective-permute-start.20 = (bf16[96,3584]{1,0:T(8,128)(2,1)S(1)}, bf16[96,3584]{1,0:T(8,128)(2,1)}, u32[]{:S(2)}, u32[]{:S(2)}) collective-permute-start(bf16[96,3584]{1,0:T(8,128)(2,1)S(1)} %collective-permute-done.1.refs_4_), channel_id=1, source_target_pairs={{0,48},{16,0},{32,16},{48,32},{1,49},{17,1},{33,17},{49,33},{2,50}... | collective-permute-start | bytes 2064392 | tf_op jit(solution)/shard_map/ppermute | solution.py:18
  63.1 3.0 %collective-permute-start.21 = (bf16[64,3584]{1,0:T(8,128)(2,1)}, bf16[64,3584]{1,0:T(8,128)(2,1)}, u32[]{:S(2)}, u32[]{:S(2)}) collective-permute-start(bf16[64,3584]{1,0:T(8,128)(2,1)} %collective-permute-done.11), channel_id=1, source_target_pairs={{0,192},{64,0},{128,64},{192,128},{1,193},{65,1},{129,65},{193,129... | collective-permute-start | bytes 1376264 | tf_op jit(solution)/shard_map/ppermute | solution.py:18
  66.2 1.6 fusion.5
  68.6 7.6 %all-to-all-start = ((bf16[4,192,128]{2,1,0:T(8,128)(2,1)}), bf16[4,192,128]{2,1,0:T(8,128)(2,1)S(1)}, u32[]{:S(2)}, u32[]{:S(2)}) async-start(bf16[4,192,128]{2,1,0:T(8,128)(2,1)} %broadcast_in_dim.18), calls=%async_computation | async-start | bytes 393216 | tf_op jit(solution)/shard_map/all_to_all | solution.py:22
  76.2 2.9 %pad_maximum_fusion.refs_8_ = bf16[4,64,3584]{2,1,0:T(8,128)(2,1)} fusion(bf16[1,64,3584]{2,1,0:T(8,128)(2,1)} %bitcast.10, bf16[1,64,3584]{2,1,0:T(8,128)(2,1)} %bitcast.41, bf16[1,64,3584]{2,1,0:T(8,128)(2,1)} %bitcast.8, bf16[1,64,3584]{2,1,0:T(8,128)(2,1)} %bitcast.40), kind=kLoop, calls=%fused_computation.5 | loop fusion | flops 2752512 | bytes 3670016 | tf_op jit(solution)/shard_map/stack | solution.py:218
  79.1 7.0 %all-to-all-done = bf16[4,192,128]{2,1,0:T(8,128)(2,1)S(1)} async-done(((bf16[4,192,128]{2,1,0:T(8,128)(2,1)}), bf16[4,192,128]{2,1,0:T(8,128)(2,1)S(1)}, u32[]{:S(2)}, u32[]{:S(2)}) %all-to-all-start) | async-done | bytes 196640 | tf_op jit(solution)/shard_map/all_to_all | solution.py:22
  89.6 2.9 %pad_maximum_fusion.1.refs_9_ = bf16[4,64,3584]{2,1,0:T(8,128)(2,1)} fusion(bf16[1,64,3584]{2,1,0:T(8,128)(2,1)} %bitcast.14, bf16[1,64,3584]{2,1,0:T(8,128)(2,1)} %bitcast.13, bf16[1,64,3584]{2,1,0:T(8,128)(2,1)} %bitcast.12, bf16[1,64,3584]{2,1,0:T(8,128)(2,1)} %bitcast.11), kind=kLoop, calls=%fused_computation.6 | loop fusion | flops 2752512 | bytes 3670016 | tf_op jit(solution)/shard_map/stack | solution.py:220
  96.7 11.9 %shard_map.112 = (bf16[4,4,96,256]{3,2,1,0:T(8,128)(2,1)}, bf16[4,4,96,256]{3,2,1,0:T(8,128)(2,1)}) custom-call(s32[4]{0:T(128)S(1)} %pad_add_fusion.where, bf16[192,3584]{1,0:T(8,128)(2,1)S(1)} %copy-done.1, bf16[96,3584]{1,0:T(8,128)(2,1)S(1)} %collective-permute-done.refs_1_, bf16[96,3584]{1,0:T(8,128)(2,1)} %collective-permute-done.8.refs_2_, ...), custom_call_target="tpu_custom_call" | custom-call | flops 5637144576 | bytes 12845056 | tf_op jit(solution)/shard_map/pallas_call | solution.py:129
  110.2 3.8 %collective-permute-start.27 = (f32[8,4664]{1,0:T(8,128)S(1)}, f32[8,4664]{1,0:T(8,128)S(1)}, u32[]{:S(2)}, u32[]{:S(2)}) collective-permute-start(f32[8,4664]{1,0:T(8,128)S(1)} %get-tuple-element.76), channel_id=1, source_target_pairs={{0,128},{64,192},{128,0},{192,64},{1,129},{65,193},{129,1},{193,65... | collective-permute-start | bytes 447752 | tf_op jit(solution)/shard_map/ppermute | solution.py:18
  114.0 5.4 %all-to-all-start.1 = ((bf16[16,96,256]{2,1,0:T(8,128)(2,1)}), bf16[16,96,256]{2,1,0:T(8,128)(2,1)S(1)}, u32[]{:S(2)}, u32[]{:S(2)}) async-start(bf16[16,96,256]{2,1,0:T(8,128)(2,1)} %bitcast.15), calls=%async_computation.1 | async-start | bytes 1572864 | tf_op jit(solution)/shard_map/all_to_all | solution.py:22
  121.6 2.7 %collective-permute-start.30 = (f32[2,4664]{1,0:T(2,128)S(1)}, f32[2,4664]{1,0:T(2,128)S(1)}, u32[]{:S(2)}, u32[]{:S(2)}) collective-permute-start(f32[2,4664]{1,0:T(2,128)S(1)} %get-tuple-element.79), channel_id=1, source_target_pairs={{0,32},{16,48},{32,0},{48,16},{1,33},{17,49},{33,1},{49,17},{2,34}... | collective-permute-start | bytes 111944 | tf_op jit(solution)/shard_map/ppermute | solution.py:18
  126.1 2.0 %collective-permute-done.30 = f32[2,4664]{1,0:T(2,128)S(1)} collective-permute-done((f32[2,4664]{1,0:T(2,128)S(1)}, f32[2,4664]{1,0:T(2,128)S(1)}, u32[]{:S(2)}, u32[]{:S(2)}) %collective-permute-start.30) | collective-permute-done | bytes 37344 | tf_op jit(solution)/shard_map/ppermute | solution.py:18
  128.3 13.7 %all-to-all-done.1 = bf16[16,96,256]{2,1,0:T(8,128)(2,1)S(1)} async-done(((bf16[16,96,256]{2,1,0:T(8,128)(2,1)}), bf16[16,96,256]{2,1,0:T(8,128)(2,1)S(1)}, u32[]{:S(2)}, u32[]{:S(2)}) %all-to-all-start.1) | async-done | bytes 786464 | tf_op jit(solution)/shard_map/all_to_all | solution.py:22
  142.0 3.6 %all-to-all-start.2 = ((bf16[16,96,256]{2,1,0:T(8,128)(2,1)}), bf16[16,96,256]{2,1,0:T(8,128)(2,1)S(1)}, u32[]{:S(2)}, u32[]{:S(2)}) async-start(bf16[16,96,256]{2,1,0:T(8,128)(2,1)} %bitcast.18), calls=%async_computation.2 | async-start | bytes 1572864 | tf_op jit(solution)/shard_map/all_to_all | solution.py:22
  145.6 1.8 %collective-permute-start.32 = (f32[2,4664]{1,0:T(2,128)S(1)}, f32[2,4664]{1,0:T(2,128)S(1)}, u32[]{:S(2)}, u32[]{:S(2)}) collective-permute-start(f32[2,4664]{1,0:T(2,128)S(1)} %add_add_fusion.1), channel_id=1, source_target_pairs={{0,16},{16,32},{32,48},{48,0},{1,17},{17,33},{33,49},{49,1},{2,18}... | collective-permute-start | bytes 111944 | tf_op jit(solution)/shard_map/ppermute | solution.py:18
  147.4 2.7 %collective-permute-start.33 = (f32[2,4664]{1,0:T(2,128)S(1)}, f32[2,4664]{1,0:T(2,128)S(1)}, u32[]{:S(2)}, u32[]{:S(2)}) collective-permute-start(f32[2,4664]{1,0:T(2,128)S(1)} %add_add_fusion.1), channel_id=1, source_target_pairs={{0,32},{16,48},{32,0},{48,16},{1,33},{17,49},{33,1},{49,17},{2,34}... | collective-permute-start | bytes 111944 | tf_op jit(solution)/shard_map/ppermute | solution.py:18
  151.8 1.9 %collective-permute-done.32 = f32[2,4664]{1,0:T(2,128)S(1)} collective-permute-done((f32[2,4664]{1,0:T(2,128)S(1)}, f32[2,4664]{1,0:T(2,128)S(1)}, u32[]{:S(2)}, u32[]{:S(2)}) %collective-permute-start.32) | collective-permute-done | bytes 37344 | tf_op jit(solution)/shard_map/ppermute | solution.py:18
  158.2 1.9 %collective-permute-done.35 = f32[8,4664]{1,0:T(8,128)S(1)} collective-permute-done((f32[8,4664]{1,0:T(8,128)S(1)}, f32[8,4664]{1,0:T(8,128)S(1)}, u32[]{:S(2)}, u32[]{:S(2)}) %collective-permute-start.35) | collective-permute-done | bytes 149280 | tf_op jit(solution)/shard_map/ppermute | solution.py:18
  160.1 2.4 %collective-permute-done.36 = f32[8,4664]{1,0:T(8,128)S(1)} collective-permute-done((f32[8,4664]{1,0:T(8,128)S(1)}, f32[8,4664]{1,0:T(8,128)S(1)}, u32[]{:S(2)}, u32[]{:S(2)}) %collective-permute-start.36) | collective-permute-done | bytes 149280 | tf_op jit(solution)/shard_map/ppermute | solution.py:18
  (121 shorter events, 45.0 us)
Async XLA Ops:
  3.2 27.7 %collective-permute-start = (bf16[96,3584]{1,0:T(8,128)(2,1)}, bf16[96,3584]{1,0:T(8,128)(2,1)S(1)}, u32[]{:S(2)}, u32[]{:S(2)}) collective-permute-start(bf16[96,3584]{1,0:T(8,128)(2,1)} %get-tuple-element.43), channel_id=1, source_target_pairs={{0,16},{16,32},{32,48},{48,0},{1,17},{17,33},{33,49},{49,1},{2,18}... | collective-permute-start | bytes 2064392 | tf_op jit(solution)/shard_map/ppermute | solution.py:18
  4.7 27.0 %collective-permute-start.1 = (bf16[96,3584]{1,0:T(8,128)(2,1)}, bf16[96,3584]{1,0:T(8,128)(2,1)S(1)}, u32[]{:S(2)}, u32[]{:S(2)}) collective-permute-start(bf16[96,3584]{1,0:T(8,128)(2,1)} %get-tuple-element.42), channel_id=1, source_target_pairs={{0,48},{16,0},{32,16},{48,32},{1,49},{17,1},{33,17},{49,33},{2,50}... | collective-permute-start | bytes 2064392 | tf_op jit(solution)/shard_map/ppermute | solution.py:18
  13.8 5.3 %collective-permute-start.6 = (f32[28,128]{1,0:T(8,128)S(1)}, f32[28,128]{1,0:T(8,128)S(1)}, u32[]{:S(2)}, u32[]{:S(2)}) collective-permute-start(f32[28,128]{1,0:T(8,128)S(1)} %bitcast.43), channel_id=1, source_target_pairs={{0,128},{64,192},{128,0},{192,64},{1,129},{65,193},{129,1},{193,65... | collective-permute-start | bytes 43016 | tf_op jit(solution)/shard_map/ppermute | solution.py:18
  17.2 11.3 %collective-permute-start.2 = (bf16[64,3584]{1,0:T(8,128)(2,1)}, bf16[64,3584]{1,0:T(8,128)(2,1)}, u32[]{:S(2)}, u32[]{:S(2)}) collective-permute-start(bf16[64,3584]{1,0:T(8,128)(2,1)} %get-tuple-element.38), channel_id=1, source_target_pairs={{0,8},{8,0},{1,9},{9,1},{2,10},{10,2},{3,11},{11,3},{4,12},{12,4},... | collective-permute-start | bytes 1376264 | tf_op jit(solution)/shard_map/ppermute | solution.py:18
  19.1 10.9 %collective-permute-start.3 = (bf16[64,3584]{1,0:T(8,128)(2,1)}, bf16[64,3584]{1,0:T(8,128)(2,1)}, u32[]{:S(2)}, u32[]{:S(2)}) collective-permute-start(bf16[64,3584]{1,0:T(8,128)(2,1)} %get-tuple-element.38), channel_id=1, source_target_pairs={{0,64},{64,128},{128,192},{192,0},{1,65},{65,129},{129,193},{193,1... | collective-permute-start | bytes 1376264 | tf_op jit(solution)/shard_map/ppermute | solution.py:18
  20.4 10.5 %collective-permute-start.4 = (bf16[64,3584]{1,0:T(8,128)(2,1)}, bf16[64,3584]{1,0:T(8,128)(2,1)S(1)}, u32[]{:S(2)}, u32[]{:S(2)}) collective-permute-start(bf16[64,3584]{1,0:T(8,128)(2,1)} %get-tuple-element.38), channel_id=1, source_target_pairs={{0,192},{64,0},{128,64},{192,128},{1,193},{65,1},{129,65},{193,129... | collective-permute-start | bytes 1376264 | tf_op jit(solution)/shard_map/ppermute | solution.py:18
  31.7 6.3 %collective-permute-start.13 = (f32[28,128]{1,0:T(8,128)S(1)}, f32[28,128]{1,0:T(8,128)S(1)}, u32[]{:S(2)}, u32[]{:S(2)}) collective-permute-start(f32[28,128]{1,0:T(8,128)S(1)} %add_add_fusion.4), channel_id=1, source_target_pairs={{0,16},{16,32},{32,48},{48,0},{1,17},{17,33},{33,49},{49,1},{2,18}... | collective-permute-start | bytes 43016 | tf_op jit(solution)/shard_map/ppermute | solution.py:18
  31.8 10.1 %collective-permute-start.14 = (f32[28,128]{1,0:T(8,128)S(1)}, f32[28,128]{1,0:T(8,128)S(1)}, u32[]{:S(2)}, u32[]{:S(2)}) collective-permute-start(f32[28,128]{1,0:T(8,128)S(1)} %add_add_fusion.4), channel_id=1, source_target_pairs={{0,32},{16,48},{32,0},{48,16},{1,33},{17,49},{33,1},{49,17},{2,34}... | collective-permute-start | bytes 43016 | tf_op jit(solution)/shard_map/ppermute | solution.py:18
  34.8 7.8 %collective-permute-start.15 = (f32[28,128]{1,0:T(8,128)S(1)}, f32[28,128]{1,0:T(8,128)S(1)}, u32[]{:S(2)}, u32[]{:S(2)}) collective-permute-start(f32[28,128]{1,0:T(8,128)S(1)} %add_add_fusion.4), channel_id=1, source_target_pairs={{0,48},{16,0},{32,16},{48,32},{1,49},{17,1},{33,17},{49,33},{2,50}... | collective-permute-start | bytes 43016 | tf_op jit(solution)/shard_map/ppermute | solution.py:18
  35.9 13.8 %collective-permute-start.10 = (bf16[64,3584]{1,0:T(8,128)(2,1)}, bf16[64,3584]{1,0:T(8,128)(2,1)}, u32[]{:S(2)}, u32[]{:S(2)}) collective-permute-start(bf16[64,3584]{1,0:T(8,128)(2,1)} %collective-permute-done.2), channel_id=1, source_target_pairs={{0,64},{64,128},{128,192},{192,0},{1,65},{65,129},{129,193},{193,1... | collective-permute-start | bytes 1376264 | tf_op jit(solution)/shard_map/ppermute | solution.py:18
  37.3 12.5 %collective-permute-start.11 = (bf16[64,3584]{1,0:T(8,128)(2,1)}, bf16[64,3584]{1,0:T(8,128)(2,1)}, u32[]{:S(2)}, u32[]{:S(2)}) collective-permute-start(bf16[64,3584]{1,0:T(8,128)(2,1)} %collective-permute-done.2), channel_id=1, source_target_pairs={{0,192},{64,0},{128,64},{192,128},{1,193},{65,1},{129,65},{193,129... | collective-permute-start | bytes 1376264 | tf_op jit(solution)/shard_map/ppermute | solution.py:18
  38.0 17.2 %collective-permute-start.12 = (bf16[64,3584]{1,0:T(8,128)(2,1)}, bf16[64,3584]{1,0:T(8,128)(2,1)}, u32[]{:S(2)}, u32[]{:S(2)}) collective-permute-start(bf16[64,3584]{1,0:T(8,128)(2,1)} %collective-permute-done.3), channel_id=1, source_target_pairs={{0,64},{64,128},{128,192},{192,0},{1,65},{65,129},{129,193},{193,1... | collective-permute-start | bytes 1376264 | tf_op jit(solution)/shard_map/ppermute | solution.py:18
  41.9 17.8 %collective-permute-start.8 = (bf16[96,3584]{1,0:T(8,128)(2,1)}, bf16[96,3584]{1,0:T(8,128)(2,1)}, u32[]{:S(2)}, u32[]{:S(2)}) collective-permute-start(bf16[96,3584]{1,0:T(8,128)(2,1)} %get-tuple-element.42), channel_id=1, source_target_pairs={{0,16},{16,32},{32,48},{48,0},{1,17},{17,33},{33,49},{49,1},{2,18}... | collective-permute-start | bytes 2064392 | tf_op jit(solution)/shard_map/ppermute | solution.py:18
  42.6 17.2 %collective-permute-start.9 = (bf16[96,3584]{1,0:T(8,128)(2,1)}, bf16[96,3584]{1,0:T(8,128)(2,1)}, u32[]{:S(2)}, u32[]{:S(2)}) collective-permute-start(bf16[96,3584]{1,0:T(8,128)(2,1)} %get-tuple-element.43), channel_id=1, source_target_pairs={{0,48},{16,0},{32,16},{48,32},{1,49},{17,1},{33,17},{49,33},{2,50}... | collective-permute-start | bytes 2064392 | tf_op jit(solution)/shard_map/ppermute | solution.py:18
  59.8 26.3 %collective-permute-start.19 = (bf16[96,3584]{1,0:T(8,128)(2,1)S(1)}, bf16[96,3584]{1,0:T(8,128)(2,1)}, u32[]{:S(2)}, u32[]{:S(2)}) collective-permute-start(bf16[96,3584]{1,0:T(8,128)(2,1)S(1)} %collective-permute-done.refs_1_), channel_id=1, source_target_pairs={{0,16},{16,32},{32,48},{48,0},{1,17},{17,33},{33,49},{49,1},{2,18}... | collective-permute-start | bytes 2064392 | tf_op jit(solution)/shard_map/ppermute | solution.py:18
  61.1 25.0 %collective-permute-start.20 = (bf16[96,3584]{1,0:T(8,128)(2,1)S(1)}, bf16[96,3584]{1,0:T(8,128)(2,1)}, u32[]{:S(2)}, u32[]{:S(2)}) collective-permute-start(bf16[96,3584]{1,0:T(8,128)(2,1)S(1)} %collective-permute-done.1.refs_4_), channel_id=1, source_target_pairs={{0,48},{16,0},{32,16},{48,32},{1,49},{17,1},{33,17},{49,33},{2,50}... | collective-permute-start | bytes 2064392 | tf_op jit(solution)/shard_map/ppermute | solution.py:18
  63.1 23.0 %collective-permute-start.21 = (bf16[64,3584]{1,0:T(8,128)(2,1)}, bf16[64,3584]{1,0:T(8,128)(2,1)}, u32[]{:S(2)}, u32[]{:S(2)}) collective-permute-start(bf16[64,3584]{1,0:T(8,128)(2,1)} %collective-permute-done.11), channel_id=1, source_target_pairs={{0,192},{64,0},{128,64},{192,128},{1,193},{65,1},{129,65},{193,129... | collective-permute-start | bytes 1376264 | tf_op jit(solution)/shard_map/ppermute | solution.py:18
  68.6 17.5 %all-to-all-start = ((bf16[4,192,128]{2,1,0:T(8,128)(2,1)}), bf16[4,192,128]{2,1,0:T(8,128)(2,1)S(1)}, u32[]{:S(2)}, u32[]{:S(2)}) async-start(bf16[4,192,128]{2,1,0:T(8,128)(2,1)} %broadcast_in_dim.18), calls=%async_computation | async-start | bytes 393216 | tf_op jit(solution)/shard_map/all_to_all | solution.py:22
  79.1 16.2 %collective-permute-start.24 = (bf16[4,64,3584]{2,1,0:T(8,128)(2,1)}, bf16[4,64,3584]{2,1,0:T(8,128)(2,1)}, u32[]{:S(2)}, u32[]{:S(2)}) collective-permute-start(bf16[4,64,3584]{2,1,0:T(8,128)(2,1)} %pad_maximum_fusion.refs_8_), channel_id=1, source_target_pairs={{0,4},{4,0},{1,5},{5,1},{2,6},{6,2},{3,7},{7,3},{8,12},{12,8},{9,1... | collective-permute-start | bytes 5505032 | tf_op jit(solution)/shard_map/ppermute | solution.py:18
  94.3 15.7 %collective-permute-start.23 = (f32[32,4664]{1,0:T(8,128)S(1)}, f32[32,4664]{1,0:T(8,128)S(1)}, u32[]{:S(2)}, u32[]{:S(2)}) collective-permute-start(f32[32,4664]{1,0:T(8,128)S(1)} %dynamic-slice_add_fusion), channel_id=1, source_target_pairs={{0,8},{8,0},{1,9},{9,1},{2,10},{10,2},{3,11},{11,3},{4,12},{12,4},... | collective-permute-start | bytes 1790984 | tf_op jit(solution)/shard_map/ppermute | solution.py:18
  110.1 9.3 %collective-permute-start.26 = (f32[8,4664]{1,0:T(8,128)S(1)}, f32[8,4664]{1,0:T(8,128)S(1)}, u32[]{:S(2)}, u32[]{:S(2)}) collective-permute-start(f32[8,4664]{1,0:T(8,128)S(1)} %get-tuple-element.74), channel_id=1, source_target_pairs={{0,64},{64,128},{128,192},{192,0},{1,65},{65,129},{129,193},{193,1... | collective-permute-start | bytes 447752 | tf_op jit(solution)/shard_map/ppermute | solution.py:18
  110.2 9.3 %collective-permute-start.27 = (f32[8,4664]{1,0:T(8,128)S(1)}, f32[8,4664]{1,0:T(8,128)S(1)}, u32[]{:S(2)}, u32[]{:S(2)}) collective-permute-start(f32[8,4664]{1,0:T(8,128)S(1)} %get-tuple-element.76), channel_id=1, source_target_pairs={{0,128},{64,192},{128,0},{192,64},{1,129},{65,193},{129,1},{193,65... | collective-permute-start | bytes 447752 | tf_op jit(solution)/shard_map/ppermute | solution.py:18
  114.0 6.3 %collective-permute-start.28 = (f32[8,4664]{1,0:T(8,128)S(1)}, f32[8,4664]{1,0:T(8,128)S(1)}, u32[]{:S(2)}, u32[]{:S(2)}) collective-permute-start(f32[8,4664]{1,0:T(8,128)S(1)} %get-tuple-element.75), channel_id=1, source_target_pairs={{0,192},{64,0},{128,64},{192,128},{1,193},{65,1},{129,65},{193,129... | collective-permute-start | bytes 447752 | tf_op jit(solution)/shard_map/ppermute | solution.py:18
  114.0 28.0 %all-to-all-start.1 = ((bf16[16,96,256]{2,1,0:T(8,128)(2,1)}), bf16[16,96,256]{2,1,0:T(8,128)(2,1)S(1)}, u32[]{:S(2)}, u32[]{:S(2)}) async-start(bf16[16,96,256]{2,1,0:T(8,128)(2,1)} %bitcast.15), calls=%async_computation.1 | async-start | bytes 1572864 | tf_op jit(solution)/shard_map/all_to_all | solution.py:22
  120.4 5.7 %collective-permute-start.29 = (f32[2,4664]{1,0:T(2,128)S(1)}, f32[2,4664]{1,0:T(2,128)S(1)}, u32[]{:S(2)}, u32[]{:S(2)}) collective-permute-start(f32[2,4664]{1,0:T(2,128)S(1)} %get-tuple-element.77), channel_id=1, source_target_pairs={{0,16},{16,32},{32,48},{48,0},{1,17},{17,33},{33,49},{49,1},{2,18}... | collective-permute-start | bytes 111944 | tf_op jit(solution)/shard_map/ppermute | solution.py:18
  121.6 6.5 %collective-permute-start.30 = (f32[2,4664]{1,0:T(2,128)S(1)}, f32[2,4664]{1,0:T(2,128)S(1)}, u32[]{:S(2)}, u32[]{:S(2)}) collective-permute-start(f32[2,4664]{1,0:T(2,128)S(1)} %get-tuple-element.79), channel_id=1, source_target_pairs={{0,32},{16,48},{32,0},{48,16},{1,33},{17,49},{33,1},{49,17},{2,34}... | collective-permute-start | bytes 111944 | tf_op jit(solution)/shard_map/ppermute | solution.py:18
  142.0 22.2 %all-to-all-start.2 = ((bf16[16,96,256]{2,1,0:T(8,128)(2,1)}), bf16[16,96,256]{2,1,0:T(8,128)(2,1)S(1)}, u32[]{:S(2)}, u32[]{:S(2)}) async-start(bf16[16,96,256]{2,1,0:T(8,128)(2,1)} %bitcast.18), calls=%async_computation.2 | async-start | bytes 1572864 | tf_op jit(solution)/shard_map/all_to_all | solution.py:22
  145.6 8.1 %collective-permute-start.32 = (f32[2,4664]{1,0:T(2,128)S(1)}, f32[2,4664]{1,0:T(2,128)S(1)}, u32[]{:S(2)}, u32[]{:S(2)}) collective-permute-start(f32[2,4664]{1,0:T(2,128)S(1)} %add_add_fusion.1), channel_id=1, source_target_pairs={{0,16},{16,32},{32,48},{48,0},{1,17},{17,33},{33,49},{49,1},{2,18}... | collective-permute-start | bytes 111944 | tf_op jit(solution)/shard_map/ppermute | solution.py:18
  147.4 7.3 %collective-permute-start.33 = (f32[2,4664]{1,0:T(2,128)S(1)}, f32[2,4664]{1,0:T(2,128)S(1)}, u32[]{:S(2)}, u32[]{:S(2)}) collective-permute-start(f32[2,4664]{1,0:T(2,128)S(1)} %add_add_fusion.1), channel_id=1, source_target_pairs={{0,32},{16,48},{32,0},{48,16},{1,33},{17,49},{33,1},{49,17},{2,34}... | collective-permute-start | bytes 111944 | tf_op jit(solution)/shard_map/ppermute | solution.py:18
  154.8 5.3 %collective-permute-start.35 = (f32[8,4664]{1,0:T(8,128)S(1)}, f32[8,4664]{1,0:T(8,128)S(1)}, u32[]{:S(2)}, u32[]{:S(2)}) collective-permute-start(f32[8,4664]{1,0:T(8,128)S(1)} %constant_dynamic-update-slice_fusion.6), channel_id=1, source_target_pairs={{0,64},{64,128},{128,192},{192,0},{1,65},{65,129},{129,193},{193,1... | collective-permute-start | bytes 447752 | tf_op jit(solution)/shard_map/ppermute | solution.py:18
  155.7 6.8 %collective-permute-start.36 = (f32[8,4664]{1,0:T(8,128)S(1)}, f32[8,4664]{1,0:T(8,128)S(1)}, u32[]{:S(2)}, u32[]{:S(2)}) collective-permute-start(f32[8,4664]{1,0:T(8,128)S(1)} %constant_dynamic-update-slice_fusion.6), channel_id=1, source_target_pairs={{0,128},{64,192},{128,0},{192,64},{1,129},{65,193},{129,1},{193,65... | collective-permute-start | bytes 447752 | tf_op jit(solution)/shard_map/ppermute | solution.py:18
  157.3 6.8 %collective-permute-start.37 = (f32[8,4664]{1,0:T(8,128)S(1)}, f32[8,4664]{1,0:T(8,128)S(1)}, u32[]{:S(2)}, u32[]{:S(2)}) collective-permute-start(f32[8,4664]{1,0:T(8,128)S(1)} %constant_dynamic-update-slice_fusion.6), channel_id=1, source_target_pairs={{0,192},{64,0},{128,64},{192,128},{1,193},{65,1},{129,65},{193,129... | collective-permute-start | bytes 447752 | tf_op jit(solution)/shard_map/ppermute | solution.py:18
  (17 other events, 121.3 us)
